TPU v7x, 256 devices: a whole 4x4x8 slice. The times are simulated.
256 devices in a mesh: lat: 8 (over x, y_lo), lon: 16 (over y_hi, z), rep: 2 (over core).
Axes of the slice: x: 4, y: 4 (y_hi: 2, y_lo: 2; y = y_hi * 2 + y_lo), z: 8, core: 2. Of those that a mesh axis runs over, the one named last changes fastest.
Arguments:
- tokens: bfloat16 [4, 48, 192, 512], P('rep', 'lat', 'lon'), parts along dimension 0, may hold values from -6 to 6
- cotangent: bfloat16 [4, 48, 192, 512], P('rep', 'lat', 'lon'), parts along dimension 0, may hold values from -6 to 6
- region: int32 [4, 48, 192], P('rep', 'lat', 'lon'), parts along dimension 0, may hold values from 1 to 3
- unshifted_norm_gain: float32 [512], replicated, may hold values from 0.5 to 2.7
- unshifted_query_key_value: bfloat16 [512, 1536], replicated, may hold values from -0.9 to 0.9
- out_first: bfloat16 [512, 512], replicated, may hold values from -0.25 to 0.25
- shifted_norm_gain: float32 [512], replicated, may hold values from 0.5 to 2.7
- shifted_query_key_value: bfloat16 [512, 1536], replicated, may hold values from -0.9 to 0.9
- out_second: bfloat16 [512, 512], replicated, may hold values from -0.25 to 0.25
Outputs:
- result: bfloat16 [4, 48, 192, 512], P('rep', 'lat', 'lon'), parts along dimension 0
- token_gradient: bfloat16 [4, 48, 192, 512], P('rep', 'lat', 'lon'), parts along dimension 0
- clip_qkv_first: float32 [1024, 1536], P(('rep', 'lat', 'lon')), parts along dimension 0
- clip_out_first: float32 [1024, 512], P(('rep', 'lat', 'lon')), parts along dimension 0
- clip_qkv_second: float32 [1024, 1536], P(('rep', 'lat', 'lon')), parts along dimension 0
- clip_out_second: float32 [1024, 512], P(('rep', 'lat', 'lon')), parts along dimension 0
There are 2 independent parts, one for each index of `rep`. A program takes and returns all parts, laid end to end along the dimension named above; an argument that names none is the same for every part. Nothing has to cross between parts.
All inputs are finite; a program needn't handle non-finite values.
Results may differ from a plain program's by a relative error of at most 0.038.
Values may be sent and summed in bfloat16 or wider, within the bound.
No kernel may reach another device: no remote copies, remote signals or barrier semaphores. Data moves between devices by JAX's collectives and lax.ppermute only.
A program may use at most 128 MiB of HBM per device.

v0:
```python
import math

import jax
import jax.numpy as jnp
from jax import lax
from jax.sharding import PartitionSpec as P

D = 512
HEADS = 8
HEAD = 64
WLEV = 2
WLAT = 6
WLON = 12


EPSILON = 1e-05
NEGATIVE = -1e30


def extended(block, sides, width, periodic):
    for axis, dim in sides:
        count = lax.axis_size(axis)
        forward = [(i, i + 1) for i in range(count - 1)]
        if periodic:
            forward.append((count - 1, 0))
        backward = [(target, source) for source, target in forward]
        low = lax.ppermute(
            lax.slice_in_dim(block, block.shape[dim] - width, None, axis=dim), axis, forward
        )
        high = lax.ppermute(lax.slice_in_dim(block, 0, width, axis=dim), axis, backward)
        block = jnp.concatenate([low, block, high], axis=dim)
    return block


def as_sent(value):

    def short(part):
        return part.astype(jnp.bfloat16) if part.dtype == jnp.float32 else part

    return jax.tree.map(short, value)


def to_windows(token_field):
    levels, lat_rows, lon_cols = (token_field.shape[0], token_field.shape[1], token_field.shape[2])
    trailing = token_field.shape[3:]
    shaped = token_field.reshape(
        (levels // WLEV, WLEV, lat_rows // WLAT, WLAT, lon_cols // WLON, WLON) + trailing
    )
    axes_order = (2, 0, 4, 1, 3, 5) + tuple(range(6, 6 + len(trailing)))
    shaped = shaped.transpose(axes_order)
    return shaped.reshape(
        (lat_rows // WLAT, levels // WLEV * (lon_cols // WLON), WLEV * WLAT * WLON) + trailing
    )


def from_windows(blocks, levels, lat_rows, lon_cols):
    trailing = blocks.shape[3:]
    shaped = blocks.reshape(
        (lat_rows // WLAT, levels // WLEV, lon_cols // WLON, WLEV, WLAT, WLON) + trailing
    )
    axes_order = (1, 3, 0, 4, 2, 5) + tuple(range(6, 6 + len(trailing)))
    return shaped.transpose(axes_order).reshape((levels, lat_rows, lon_cols) + trailing)


def apply_norm(token_field, gain_vector):
    values = token_field.astype(jnp.float32)
    average = jnp.mean(values, -1, keepdims=True)
    mean_removed = values - average
    inverse_deviation = lax.rsqrt(
        jnp.mean(mean_removed * mean_removed, -1, keepdims=True) + EPSILON
    )
    standardized = mean_removed * inverse_deviation
    return ((standardized * gain_vector).astype(jnp.bfloat16), standardized, inverse_deviation)


def project(token_field, weight):
    flat_rows = token_field.reshape(-1, token_field.shape[-1])
    product = jnp.dot(flat_rows, weight, preferred_element_type=jnp.float32)
    return product.astype(jnp.bfloat16).reshape(token_field.shape[:-1] + (weight.shape[1],))


def versus_operand(token_field, weight):
    flat_rows = token_field.reshape(-1, token_field.shape[-1])
    product = lax.dot_general(
        flat_rows, weight, (((1,), (1,)), ((), ())), preferred_element_type=jnp.float32
    )
    return product.reshape(token_field.shape[:-1] + (weight.shape[0],))


def transposed(left_field, right_field):
    left_rows = left_field.reshape(-1, left_field.shape[-1])
    right_rows = right_field.reshape(-1, right_field.shape[-1])
    return lax.dot_general(
        left_rows, right_rows, (((0,), (0,)), ((), ())), preferred_element_type=jnp.float32
    )


def residual(token_field, attention_result, weight):
    flat_rows = attention_result.reshape(-1, attention_result.shape[-1])
    update = jnp.dot(flat_rows, weight, preferred_element_type=jnp.float32).reshape(
        token_field.shape
    )
    return (token_field.astype(jnp.float32) + update).astype(jnp.bfloat16)


def split_heads(window_block, which_part):
    section = window_block[..., which_part * D : (which_part + 1) * D]
    return section.reshape(section.shape[:-1] + (HEADS, HEAD))


def probabilities(window_block, labels):
    scores = jnp.einsum(
        "wqhd,wkhd->whqk",
        split_heads(window_block, 0),
        split_heads(window_block, 1),
        preferred_element_type=jnp.float32,
    ) * HEAD ** (-0.5)
    allowed = (labels[:, :, None] == labels[:, None, :]) & (labels[:, None, :] > 0)
    scores = jnp.where(allowed[:, None], scores, NEGATIVE)
    row_max = jnp.max(scores, -1, keepdims=True)
    exponent = jnp.exp(scores - row_max)
    return exponent / jnp.sum(exponent, -1, keepdims=True)


def attend(window_block, labels):
    rounded = probabilities(window_block, labels).astype(jnp.bfloat16)
    mixed_out = jnp.einsum(
        "whqk,wkhd->wqhd", rounded, split_heads(window_block, 2), preferred_element_type=jnp.float32
    )
    return mixed_out.reshape(mixed_out.shape[0], mixed_out.shape[1], D).astype(jnp.bfloat16)


def attend_back(window_block, labels, grad_block):
    weights = probabilities(window_block, labels)
    rounded = weights.astype(jnp.bfloat16)
    query_heads = split_heads(window_block, 0)
    key_heads = split_heads(window_block, 1)
    value_heads = split_heads(window_block, 2)
    grad_heads = grad_block.reshape(grad_block.shape[:-1] + (HEADS, HEAD))
    grad_probs = jnp.einsum(
        "wqhd,wkhd->whqk", grad_heads, value_heads, preferred_element_type=jnp.float32
    )
    grad_value = jnp.einsum(
        "whqk,wqhd->wkhd", rounded, grad_heads, preferred_element_type=jnp.float32
    )
    grad_scores = (
        weights * (grad_probs - jnp.sum(grad_probs * weights, -1, keepdims=True)) * HEAD ** (-0.5)
    )
    grad_rounded = grad_scores.astype(jnp.bfloat16)
    grad_query = jnp.einsum(
        "whqk,wkhd->wqhd", grad_rounded, key_heads, preferred_element_type=jnp.float32
    )
    grad_key = jnp.einsum(
        "whqk,wqhd->wkhd", grad_rounded, query_heads, preferred_element_type=jnp.float32
    )
    windows, tokens_in = (grad_query.shape[0], grad_query.shape[1])
    grad_kv = jnp.concatenate(
        [grad_key.reshape(windows, tokens_in, D), grad_value.reshape(windows, tokens_in, D)], -1
    )
    return (grad_query.reshape(windows, tokens_in, D), grad_kv)


def window_attention(projected_tokens, labels):
    levels, lat_rows, lon_cols = labels.shape
    mixed_out = lax.map(
        lambda both: attend(both[0], both[1]), (to_windows(projected_tokens), to_windows(labels))
    )
    return from_windows(mixed_out, levels, lat_rows, lon_cols)


def window_attention_back(projected_tokens, labels, grad_att):
    levels, lat_rows, lon_cols = labels.shape
    grad_query, grad_kv = lax.map(
        lambda trio_in: attend_back(trio_in[0], trio_in[1], trio_in[2]),
        (to_windows(projected_tokens), to_windows(labels), to_windows(grad_att)),
    )
    return (
        from_windows(grad_query, levels, lat_rows, lon_cols),
        from_windows(grad_kv, levels, lat_rows, lon_cols),
    )


def norm_backward_pass(
    normalized_gradient, gain_vector, standardized, inverse_deviation, input_gradient
):
    scaled_tokens = normalized_gradient * gain_vector
    return (
        inverse_deviation
        * (
            scaled_tokens
            - jnp.mean(scaled_tokens, -1, keepdims=True)
            - standardized * jnp.mean(scaled_tokens * standardized, -1, keepdims=True)
        )
        + input_gradient
    )


def widen_block(payload, labels):
    beside_all = (
        extended(payload, (("lon", 2),), WLON // 2, True),
        extended(labels, (("lon", 2),), WLON // 2, True),
    )
    return (
        extended(beside_all[0], (("lat", 1),), WLAT // 2, False),
        extended(as_sent(beside_all[1]), (("lat", 1),), WLAT // 2, False),
    )


def on_device(
    tokens,
    cotangent,
    region,
    unshifted_norm_gain,
    unshifted_query_key_value,
    out_first,
    shifted_norm_gain,
    shifted_query_key_value,
    out_second,
):
    levels, lat_rows, lon_cols, feat_width = tokens.shape
    lat_rim = WLAT // 2
    lon_rim = WLON // 2
    unshifted_normalized, unshifted_standardized, unshifted_inverse_deviation = apply_norm(
        tokens, unshifted_norm_gain
    )
    projected_a = project(unshifted_normalized, unshifted_query_key_value)
    attended_a = window_attention(projected_a, region)
    unshifted_output = residual(tokens, attended_a, out_first)
    shifted_normalized, shifted_standardized, shifted_inverse_deviation = apply_norm(
        unshifted_output, shifted_norm_gain
    )
    wide_normed, wide_region = widen_block(shifted_normalized, region)
    wide_projected = project(wide_normed, shifted_query_key_value)
    wide_attended = window_attention(wide_projected, wide_region)
    attended_b = wide_attended[:, lat_rim : lat_rim + lat_rows, lon_rim : lon_rim + lon_cols]
    result = residual(unshifted_output, attended_b, out_second)
    grad_out_b = transposed(attended_b, cotangent)
    grad_att_b = versus_operand(cotangent, out_second).astype(jnp.bfloat16)
    wide_grad, back_region = widen_block(grad_att_b, region)
    wide_query, wide_kv = window_attention_back(wide_projected, back_region, wide_grad)
    own_query = wide_query[:, lat_rim : lat_rim + lat_rows, lon_rim : lon_rim + lon_cols]
    own_kv = wide_kv[:, lat_rim : lat_rim + lat_rows, lon_rim : lon_rim + lon_cols]
    shifted_projection_gradient = jnp.concatenate([own_query, own_kv], -1).astype(jnp.bfloat16)
    grad_qkv_b = transposed(shifted_normalized, shifted_projection_gradient)
    middle_gradient = norm_backward_pass(
        versus_operand(shifted_projection_gradient, shifted_query_key_value),
        shifted_norm_gain,
        shifted_standardized,
        shifted_inverse_deviation,
        cotangent.astype(jnp.float32),
    )
    grad_mid16 = middle_gradient.astype(jnp.bfloat16)
    grad_out_a = transposed(attended_a, grad_mid16)
    grad_att_a = versus_operand(grad_mid16, out_first).astype(jnp.bfloat16)
    grad_query_a, grad_kv_a = window_attention_back(projected_a, region, grad_att_a)
    unshifted_projection_gradient = jnp.concatenate([grad_query_a, grad_kv_a], -1).astype(
        jnp.bfloat16
    )
    grad_qkv_a = transposed(unshifted_normalized, unshifted_projection_gradient)
    token_gradient = norm_backward_pass(
        versus_operand(unshifted_projection_gradient, unshifted_query_key_value),
        unshifted_norm_gain,
        unshifted_standardized,
        unshifted_inverse_deviation,
        middle_gradient,
    )
    shares = (
        lax.psum_scatter(grad_qkv_a, ("lat", "lon"), scatter_dimension=0, tiled=True),
        lax.psum_scatter(grad_out_a, ("lat", "lon"), scatter_dimension=0, tiled=True),
        lax.psum_scatter(grad_qkv_b, ("lat", "lon"), scatter_dimension=0, tiled=True),
        lax.psum_scatter(grad_out_b, ("lat", "lon"), scatter_dimension=0, tiled=True),
    )
    local_sum = sum((jnp.sum(matrix * matrix) for matrix in shares))
    norm_total = lax.psum(local_sum, ("lat", "lon"))
    factor = jnp.minimum(1.0, math.sqrt(8.0) * D / jnp.sqrt(norm_total))
    return (
        result,
        token_gradient.astype(jnp.bfloat16),
        shares[0] * factor,
        shares[1] * factor,
        shares[2] * factor,
        shares[3] * factor,
    )


def solution(mesh):
    in_specs = (
        P("rep", "lat", "lon", None),
        P("rep", "lat", "lon", None),
        P("rep", "lat", "lon"),
        P(),
        P(),
        P(),
        P(),
        P(),
        P(),
    )
    out_specs = (
        P("rep", "lat", "lon", None),
        P("rep", "lat", "lon", None),
        P(("rep", "lat", "lon"), None),
        P(("rep", "lat", "lon"), None),
        P(("rep", "lat", "lon"), None),
        P(("rep", "lat", "lon"), None),
    )
    return jax.shard_map(
        on_device, mesh=mesh, in_specs=in_specs, out_specs=out_specs, check_vma=False
    )
```

profile of v0, /device:TPU:0, one launch (start us, length us, event | category | flops | bytes accessed | tf_op | source)
XLA Modules:
  0.0 816.7 jit_solution(15567294471619069661)
XLA Ops:
  11.2 1.8 fusion.39
  14.0 1.6 fusion.114
  15.6 1.6 convolution_convert_fusion.6
  19.1 6.8 collective-permute-start.1
  26.0 5.7 collective-permute-start.5
  33.0 5.9 collective-permute-done.4
  40.4 4.5 collective-permute-start.6
  45.0 2.0 collective-permute-start.8
  49.4 4.6 collective-permute-start.2
  56.5 5.0 collective-permute-start.10
  61.7 2.3 convolution_convert_fusion.1
  64.0 3.8 reshape_reshape.4
  67.7 4.7 copy.101
  72.5 6.5 copy.103
  81.0 46.7 %while.5 = (s32[]{:T(128)}, bf16[2,2,144,512]{2,3,1,0:T(8,128)(2,1)}, bf16[2,2,144,1024]{2,3,1,0:T(8,128)(2,1)}, bf16[2,2,144,1536]{2,3,1,0:T(8,128)(2,1)}, s32[...) while((s32[]{:T(128)}, bf16[2,2,144,512]{2,3,1,0:T(8,128)(2,1)}, ...), condition=%wide.region_14.15_spmd, body=%wide.region_10.14_spmd.sunk | while | flops 220240080 | bytes 23087228 | solution.py:173
  81.0 1.5 dynamic-slice_bitcast_fusion.9
  84.4 2.0 fusion.188
  86.6 4.1 fusion.189
  90.6 4.8 fusion.190
  96.3 2.2 fusion.191
  98.5 4.7 fusion.192
  104.4 1.5 dynamic-slice_bitcast_fusion.9
  107.8 2.0 fusion.188
  109.9 4.1 fusion.189
  114.0 4.8 fusion.190
  119.7 2.2 fusion.191
  121.9 4.7 fusion.192
  127.7 2.5 copy.112
  131.7 4.4 copy.115
  142.5 2.9 fusion.60
  145.4 2.9 fusion.61
  148.3 2.4 fusion.62
  151.4 2.3 convolution_bitcast_fusion
  153.7 20.7 %while.4 = (s32[]{:T(128)}, bf16[2,2,144,512]{3,1,2,0:T(2,128)(2,1)}, bf16[2,2,144,1536]{2,3,1,0:T(8,128)(2,1)}, s32[2,2,144]{2,1,0:T(2,128)}, s32[]{:T(128)}) while((s32[]{:T(128)}, bf16[2,2,144,512]{3,1,2,0:T(2,128)(2,1)}, bf16[2,2,144,1536]{2,3,1,0:T(8,128)(2,1)}, s32[2,2,144]{2,1,0:T(2,128)}, s32[]{:T(128)}) %tuple.92), condition=%wide.region_9.10_spmd, body=%wide.region_6.9_spmd.sunk | while | flops 87156144 | bytes 8667181 | solution.py:165
  153.7 1.5 dynamic-slice_bitcast_fusion.8
  156.7 4.0 fusion.176
  160.7 2.0 convolution_convert_fusion.10
  164.0 1.5 dynamic-slice_bitcast_fusion.8
  167.0 4.0 fusion.176
  171.0 2.0 convolution_convert_fusion.10
  174.4 1.7 copy.105
  179.8 3.4 convolution_bitcast_fusion.1
  189.2 1.9 fusion.101
  191.5 255.0 %all-reduce.7.cloned.1.call-done = (f32[512,1536]{1,0:T(8,128)}, f32[512,512]{1,0:T(8,128)}, f32[512,1536]{1,0:T(8,128)}, f32[512,512]{1,0:T(8,128)}) async-done(((f32[512,1536]{1,0:T(8,128)}, f32[512,512]{1,0:T(8,128)}, f32[512,1536]{1,0:T(8,128)}, f32[512,512]{1,0:T(8,128)}), (f32[512,1536]{1,0:T(8,128)}, f32[512,512]{1,0:T(8,128)}, f32[512,1536]{1,0:T(8,128)}, ...) | async-done | bytes 8388624
  446.5 1.4 multiply_reduce_fusion.5
  449.2 1.4 multiply_reduce_fusion.4
  455.4 348.3 %psum.7 = f32[]{:T(128)} all-reduce(f32[]{:T(128)S(6)} %add.65), channel_id=1, replica_groups=mesh['lat'=8,'lon'=16,'rep'=2] {'lat','lon'}, use_global_device_ids=true, to_apply=%region_28.29 | all-reduce | flops 1 | bytes 8 | tf_op jit(solution)/shard_map/psum | solution.py:274
  804.4 1.4 dynamic-slice_multiply_fusion.1
  (223 shorter events, 55.4 us)
Async XLA Ops:
  7.2 54.5 %copy-start = (bf16[512,1536]{1,0:T(8,128)(2,1)S(1)}, bf16[512,1536]{1,0:T(8,128)(2,1)}, u32[]{:S(2)}) copy-start(bf16[512,1536]{1,0:T(8,128)(2,1)} %param.20) | copy-start | bytes 4718596
  7.2 439.3 %all-reduce.7.cloned.1.call-start = ((), (), s32[]{:S(2)}) async-start(), calls=%async_computation | async-start | bytes 16777216
  13.2 2.3 copy-start.19
  13.4 2.2 copy-start.24
  13.7 1.8 copy-start.25
  15.5 1.6 copy-start.44
  15.6 2.8 copy-start.3
  15.6 2.8 copy-start.9
  17.2 1.7 copy-start.40
  18.1 13.6 %copy-start.11 = (bf16[512,512]{1,0:T(8,128)(2,1)S(1)}, bf16[512,512]{1,0:T(8,128)(2,1)}, u32[]{:S(2)}) copy-start(bf16[512,512]{1,0:T(8,128)(2,1)} %param.21) | copy-start | bytes 1572868
  18.1 13.6 %copy-start.13 = (bf16[2,6,12,512]{3,0,2,1:T(2,128)(2,1)S(1)}, bf16[2,6,12,512]{3,0,2,1:T(2,128)(2,1)}, u32[]{:S(2)}) copy-start(bf16[2,6,12,512]{3,0,2,1:T(2,128)(2,1)} %param.14) | copy-start | bytes 442372
  19.1 42.4 %copy-start.7 = (bf16[2,6,12,512]{3,2,1,0:T(8,128)(2,1)}, bf16[2,6,12,512]{3,2,1,0:T(8,128)(2,1)S(1)}, u32[]{:S(2)}) copy-start(bf16[2,6,12,512]{3,2,1,0:T(8,128)(2,1)S(1)} %multiply_convert_fusion.1) | copy-start | bytes 442372
  19.1 28.8 %collective-permute-start.1 = (bf16[2,6,6,512]{3,2,1,0:T(8,128)(2,1)S(1)}, bf16[2,6,6,512]{3,2,1,0:T(8,128)(2,1)S(1)}, u32[]{:S(2)}, u32[]{:S(2)}) collective-permute-start(bf16[2,6,6,512]{3,2,1,0:T(8,128)(2,1)S(1)} %get-tuple-element.184), channel_id=1, source_target_pairs={{2,0},{4,2},{6,4},{8,6},{10,8},{12,10},{14,12},{16,14},{18,16},{20... | collective-permute-start | bytes 221192 | tf_op jit(solution)/shard_map/ppermute | solution.py:30
  26.0 22.0 %collective-permute-start = (bf16[2,6,6,512]{3,2,1,0:T(8,128)(2,1)S(1)}, bf16[2,6,6,512]{3,2,1,0:T(8,128)(2,1)S(1)}, u32[]{:S(2)}, u32[]{:S(2)}) collective-permute-start(bf16[2,6,6,512]{3,2,1,0:T(8,128)(2,1)S(1)} %get-tuple-element.183), channel_id=1, source_target_pairs={{0,2},{2,4},{4,6},{6,8},{8,10},{10,12},{12,14},{14,16},{16,18},{18... | collective-permute-start | bytes 221192 | tf_op jit(solution)/shard_map/ppermute | solution.py:27
  26.0 7.0 collective-permute-start.5
  31.7 7.2 collective-permute-start.4
  39.0 6.0 collective-permute-start.7
  40.4 6.7 collective-permute-start.6
  44.9 9.0 %collective-permute-start.9 = (bf16[2,6,6,512]{3,2,1,0:T(8,128)(2,1)S(1)}, bf16[2,6,6,512]{3,2,1,0:T(8,128)(2,1)S(1)}, u32[]{:S(2)}, u32[]{:S(2)}) collective-permute-start(bf16[2,6,6,512]{3,2,1,0:T(8,128)(2,1)S(1)} %get-tuple-element.182), channel_id=1, source_target_pairs={{2,0},{4,2},{6,4},{8,6},{10,8},{12,10},{14,12},{16,14},{18,16},{20... | collective-permute-start | bytes 221192 | tf_op jit(solution)/shard_map/ppermute | solution.py:30
  45.0 9.3 %collective-permute-start.8 = (bf16[2,6,6,512]{3,2,1,0:T(8,128)(2,1)S(1)}, bf16[2,6,6,512]{3,2,1,0:T(8,128)(2,1)S(1)}, u32[]{:S(2)}, u32[]{:S(2)}) collective-permute-start(bf16[2,6,6,512]{3,2,1,0:T(8,128)(2,1)S(1)} %get-tuple-element.181), channel_id=1, source_target_pairs={{0,2},{2,4},{4,6},{6,8},{8,10},{10,12},{12,14},{14,16},{16,18},{18... | collective-permute-start | bytes 221192 | tf_op jit(solution)/shard_map/ppermute | solution.py:27
  48.1 13.4 %collective-permute-start.3 = (bf16[2,3,24,512]{3,2,1,0:T(8,128)(2,1)S(1)}, bf16[2,3,24,512]{3,2,1,0:T(8,128)(2,1)S(1)}, u32[]{:S(2)}, u32[]{:S(2)}) collective-permute-start(bf16[2,3,24,512]{3,2,1,0:T(8,128)(2,1)S(1)} %get-tuple-element.180), channel_id=1, source_target_pairs={{32,0},{64,32},{96,64},{128,96},{160,128},{192,160},{224,192},{33,... | collective-permute-start | bytes 442376 | tf_op jit(solution)/shard_map/ppermute | solution.py:30
  49.4 12.1 %collective-permute-start.2 = (bf16[2,3,24,512]{3,2,1,0:T(8,128)(2,1)S(1)}, bf16[2,3,24,512]{3,2,1,0:T(8,128)(2,1)S(1)}, u32[]{:S(2)}, u32[]{:S(2)}) collective-permute-start(bf16[2,3,24,512]{3,2,1,0:T(8,128)(2,1)S(1)} %get-tuple-element.179), channel_id=1, source_target_pairs={{0,32},{32,64},{64,96},{96,128},{128,160},{160,192},{192,224},{1,3... | collective-permute-start | bytes 442376 | tf_op jit(solution)/shard_map/ppermute | solution.py:27
  55.2 23.7 %collective-permute-start.11 = (bf16[2,3,24,512]{3,2,1,0:T(8,128)(2,1)}, bf16[2,3,24,512]{3,2,1,0:T(8,128)(2,1)S(1)}, u32[]{:S(2)}, u32[]{:S(2)}) collective-permute-start(bf16[2,3,24,512]{3,2,1,0:T(8,128)(2,1)} %get-tuple-element.178), channel_id=1, source_target_pairs={{32,0},{64,32},{96,64},{128,96},{160,128},{192,160},{224,192},{33,... | collective-permute-start | bytes 442376 | tf_op jit(solution)/shard_map/ppermute | solution.py:30
  56.5 22.5 %collective-permute-start.10 = (bf16[2,3,24,512]{3,2,1,0:T(8,128)(2,1)}, bf16[2,3,24,512]{3,2,1,0:T(8,128)(2,1)S(1)}, u32[]{:S(2)}, u32[]{:S(2)}) collective-permute-start(bf16[2,3,24,512]{3,2,1,0:T(8,128)(2,1)} %get-tuple-element.177), channel_id=1, source_target_pairs={{0,32},{32,64},{64,96},{96,128},{128,160},{160,192},{192,224},{1,3... | collective-permute-start | bytes 442376 | tf_op jit(solution)/shard_map/ppermute | solution.py:27
  84.4 2.0 copy-start.30
  84.4 2.2 copy-start.1
  107.7 2.0 copy-start.30
  107.8 2.2 copy-start.1
  136.1 1.6 copy-start.20
  136.1 1.7 copy-start.41
  137.8 1.7 copy-start.21
  137.8 1.5 copy-start.14
  137.8 1.7 copy-start.10
  140.1 2.4 copy-start.45
  148.3 3.1 copy-start.8
  148.3 3.1 copy-start.22
  174.4 1.9 copy-start.28
  174.4 3.1 copy-start.27
  176.1 1.8 copy-start.26
  176.7 3.0 copy-start.4
  176.7 3.0 copy-start.33
  176.7 3.0 copy-start.39
  176.7 3.0 copy-start.42
  179.8 3.5 copy-start.15
  185.9 1.9 copy-start.12
  189.2 1.9 copy-start.6
  189.2 1.9 copy-start.35
  189.2 1.9 copy-start.37
  (15 other events, 14.4 us)
Sparse Core Ops, SparseCore 0:
  186.0 260.4 all-reduce.6
where the time goes:
time: 819 us; the launch traced here: 817 us
  blocking collectives  348 us (42%)
  waiting for transfers between devices  262 us (32%)
  matrix products  76.6 us (9%)
  local copies, waits for them, and re-layouts  57.7 us (7%)
  starting transfers between devices  32.6 us (4%)
  other arithmetic  20.1 us (2%)
  between operations  18.9 us (2%)
    psum x1, blocking collectives, on_device(): norm_total = lax.psum(local_sum, ('lat', 'lon'))  348 us
    unnamed x2, waiting for transfers between devices  255 us
    sub x5, matrix products, probabilities(): exponent = jnp.exp(scores - row_max)  17.7 us
    ppermute x6, starting transfers between devices, extended(): lax.ppermute(lax.slice_in_dim(block, 0, width, axis=dim), axis, backward)  16.4 us
  transfers between devices with their start and end apart: 13, of which 4 were waited for; matrix products, arithmetic and copies ran while one was open for 3% of the time, Pallas kernels for 0%

commit v1 on v0

v1 whole, which is shorter than its diff:
```python
import math

import jax
import jax.numpy as jnp
from jax import lax
from jax.experimental import pallas as pl
from jax.experimental.pallas import tpu as pltpu
from jax.sharding import PartitionSpec as P

D = 512
HEADS = 8
HEAD = 64
PAIRS = HEADS // 2
WLEV = 2
WLAT = 6
WLON = 12
HLAT = WLAT // 2
HLON = WLON // 2
TOK = WLEV * WLAT * WLON
QUART = TOK // 4
LANES = 128

X, YLO, YHI, Z = 4, 2, 2, 8
Y = YHI * YLO
LAT, LON = X * YLO, YHI * Z
OWN = D // (LAT * LON)
GROUP = 4
WIDE = 4 * D // GROUP
PLANE_ROWS = D // GROUP
LAST_ROWS = PLANE_ROWS // Z
SEND = 2 * D + LANES

EPSILON = 1e-05
NEGATIVE = -1e30
F32 = jnp.float32
BF16 = jnp.bfloat16
VMEM_BYTES = 16 * 1024 * 1024


def dot_nn(a, b):
    return lax.dot_general(a, b, (((1,), (0,)), ((), ())), preferred_element_type=F32)


def dot_nt(a, b):
    return lax.dot_general(a, b, (((1,), (1,)), ((), ())), preferred_element_type=F32)


def dot_tn(a, b):
    return lax.dot_general(a, b, (((0,), (0,)), ((), ())), preferred_element_type=F32)


def norm_parts(values, gain):
    average = jnp.mean(values, -1, keepdims=True)
    centered = values - average
    rstd = lax.rsqrt(jnp.mean(centered * centered, -1, keepdims=True) + EPSILON)
    xhat = centered * rstd
    return (xhat * gain).astype(BF16), xhat, rstd


def norm_back(dnormed, gain, xhat, rstd, incoming):
    s = dnormed * gain
    return (
        rstd * (s - jnp.mean(s, -1, keepdims=True) - xhat * jnp.mean(s * xhat, -1, keepdims=True))
        + incoming
    )


def label_bias(labels):
    lane = lax.broadcasted_iota(jnp.int32, (TOK, LANES), 1).astype(F32)
    hot = jnp.where((lane == labels) & (lane > 0.5), 1.0, 0.0).astype(BF16)
    return (1.0 - dot_nt(hot, hot)) * NEGATIVE


def head_masks():
    lane = lax.broadcasted_iota(jnp.int32, (1, LANES), 1)
    low = (lane < HEAD).astype(F32)
    return low, 1.0 - low


def pair_of(proj, part, pair):
    start = part * D + pair * LANES
    return proj[:, start : start + LANES]


def softmax_rows(scores):
    shifted = jnp.exp(scores - jnp.max(scores, -1, keepdims=True))
    return shifted * (1.0 / jnp.sum(shifted, -1, keepdims=True))


def attention(proj, bias, grad=None, forward=True):
    low, high = head_masks()
    is_low = low > 0.5
    masks = (low.astype(BF16), high.astype(BF16))
    att, dq, dk, dv = [], [], [], []
    for pair in range(PAIRS):
        q = pair_of(proj, 0, pair)
        k = pair_of(proj, 1, pair)
        v = pair_of(proj, 2, pair)
        o_h, dq_h, dk_h, dv_h = [], [], [], []
        for mask in masks:
            probs = softmax_rows(dot_nt(q * (mask * BF16(HEAD**-0.5)), k) + bias)
            p16 = probs.astype(BF16)
            if forward:
                o_h.append(dot_nn(p16, v))
            if grad is not None:
                g = grad[:, pair * LANES : (pair + 1) * LANES]
                dp = dot_nt(g * mask, v)
                delta = jnp.sum(dp * probs, -1, keepdims=True)
                ds16 = (probs * (dp - delta) * HEAD**-0.5).astype(BF16)
                dq_h.append(dot_nn(ds16, k))
                dk_h.append(dot_tn(ds16, q))
                dv_h.append(dot_tn(p16, g))
        if forward:
            att.append(jnp.where(is_low, o_h[0], o_h[1]).astype(BF16))
        if grad is not None:
            dq.append(jnp.where(is_low, dq_h[0], dq_h[1]).astype(BF16))
            dk.append(jnp.where(is_low, dk_h[0], dk_h[1]).astype(BF16))
            dv.append(jnp.where(is_low, dv_h[0], dv_h[1]).astype(BF16))
    attended = jnp.concatenate(att, -1) if forward else None
    dproj = jnp.concatenate(dq + dk + dv, -1) if grad is not None else None
    return attended, dproj


def gather_rows(refs, scratch, column):
    wide = scratch.shape[1]
    for slot, ref in enumerate(refs):
        scratch[slot * QUART : (slot + 1) * QUART, :] = ref[:, column : column + wide].astype(F32)
    return scratch[...]


def scatter_rows(values, scratch, refs, column):
    scratch[...] = values
    wide = scratch.shape[1]
    for slot, ref in enumerate(refs):
        ref[:, column : column + wide] = scratch[slot * QUART : (slot + 1) * QUART, :].astype(BF16)


def regroup(source_of):
    to = lax.broadcasted_iota(jnp.int32, (1, D), 1)
    return (lax.broadcasted_iota(jnp.int32, (D, D), 0) == source_of(to)).astype(F32).astype(BF16)


def row_of(x, y, z, own):
    return (((x * YLO + y % YLO) * YHI + y // YLO) * Z + z) * OWN + own


def order_x(to):
    x = to // OWN % X
    return row_of(x, to // (OWN * X * Z), to // (OWN * X) % Z, to % OWN)


def order_y(to):
    y = to // OWN % Y
    return row_of(to // (OWN * Y * Z), y, to // (OWN * Y) % Z, to % OWN)


def pack(me, left_refs, right_ref, packs):
    for step, ref in enumerate(packs):
        peer = me ^ step
        is_att = peer == GROUP - 1

        @pl.when(is_att)
        def _():
            ref[:, :D] = left_refs[1][...]

        @pl.when(jnp.logical_not(is_att))
        def _():
            ref[:, :D] = left_refs[0][...]

        ref[:, D:] = right_ref[peer]


def store_right(dproj, g16, right_ref):
    for part in range(3):
        right_ref[part] = dproj[:, part * D : (part + 1) * D]
    right_ref[3] = g16


def first_forward(
    wrap, tok, cot, lab, gain, wqkv, wout,
    x0, x1, x2, x3, proj_ref, left_n, left_a, scratch, lab_scratch,
):
    values = tok[...].astype(F32)
    normed, _, _ = norm_parts(values, gain[...])
    proj = dot_nn(normed, wqkv[...]).astype(BF16)
    proj_ref[...] = proj
    labels = lab[...].astype(F32)
    attended, _ = attention(proj, label_bias(labels))
    refs = (x0, x1, x2, x3)
    scatter_rows(values + dot_nn(attended, wout[...]), scratch, refs, 0)
    scatter_rows(cot[...].astype(F32), scratch, refs, D)
    near = lax.broadcasted_iota(jnp.int32, (TOK, LANES), 0) < 2 * QUART
    moved = labels + jnp.where(near, wrap[0].astype(F32), 0.0)
    scatter_rows(moved, lab_scratch, refs, 2 * D)
    order = regroup(order_x)
    left_n[...] = dot_nn(normed, order).astype(BF16)
    left_a[...] = dot_nn(attended, order).astype(BF16)


def second_main(
    x0, x1, x2, x3, gain, wqkv, wout,
    b0, b1, b2, b3, normed_ref, att_ref, right_ref, scratch, lab_scratch,
):
    parts = (x0, x1, x2, x3)
    back = (b0, b1, b2, b3)
    values = gather_rows(parts, scratch, 0)
    g = gather_rows(parts, scratch, D)
    labels = gather_rows(parts, lab_scratch, 2 * D)
    g16 = g.astype(BF16)
    normed, xhat, rstd = norm_parts(values, gain[...])
    normed_ref[...] = normed
    proj = dot_nn(normed, wqkv[...]).astype(BF16)
    datt = dot_nt(g16, wout[...]).astype(BF16)
    attended, dproj = attention(proj, label_bias(labels), grad=datt)
    att_ref[...] = attended
    store_right(dproj, g16, right_ref)
    scatter_rows(values + dot_nn(attended, wout[...]), scratch, back, 0)
    dnormed = dot_nt(dproj, wqkv[...])
    scatter_rows(norm_back(dnormed, gain[...], xhat, rstd, g), scratch, back, D)


def second_pack(me, normed, attended, right, p0, p1, p2, p3, left_n, left_a):
    order = regroup(order_y)
    left_n[...] = dot_nn(normed[...], order).astype(BF16)
    left_a[...] = dot_nn(attended[...], order).astype(BF16)
    pack(me[0], (left_n, left_a), right, (p0, p1, p2, p3))


def first_backward(
    me, b0, b1, b2, b3, lab, wout, proj_ref, left_n, left_a,
    right_ref, p0, p1, p2, p3, scratch,
):
    g16 = gather_rows((b0, b1, b2, b3), scratch, D).astype(BF16)
    datt = dot_nt(g16, wout[...]).astype(BF16)
    _, dproj = attention(
        proj_ref[...], label_bias(lab[...].astype(F32)), grad=datt, forward=False
    )
    store_right(dproj, g16, right_ref)
    pack(me[0], (left_n, left_a), right_ref, (p0, p1, p2, p3))


def first_rest(b0, b1, b2, b3, tok, gain, wqkv, right, tg_ref, scratch):
    g = gather_rows((b0, b1, b2, b3), scratch, D)
    _, xhat, rstd = norm_parts(tok[...].astype(F32), gain[...])
    dnormed = dot_nt(right[0], wqkv[:, :D])
    dnormed += dot_nt(right[1], wqkv[:, D : 2 * D])
    dnormed += dot_nt(right[2], wqkv[:, 2 * D :])
    tg_ref[...] = norm_back(dnormed, gain[...], xhat, rstd, g).astype(BF16)


def weights(me, p0, p1, p2, p3, q0, q1, q2, q3, scratch):
    total = jnp.zeros((D, WIDE), F32)
    for part in (p0, p1, p2, p3):
        total += dot_tn(part[:, :D], part[:, D:])
    scratch[...] = total
    for step, ref in enumerate((q0, q1, q2, q3)):
        first = pl.multiple_of((me[0] ^ step) * PLANE_ROWS, PLANE_ROWS)
        ref[...] = scratch[pl.ds(first, PLANE_ROWS), :].astype(BF16)


def add_rows(a0, a1, a2, a3, b0, b1, b2, b3, out_ref):
    for slot, parts in enumerate(((a0, a1, a2, a3), (b0, b1, b2, b3))):
        total = sum(part[...].astype(F32) for part in parts).astype(BF16)
        for z in range(Z):
            out_ref[z, slot * LAST_ROWS : (slot + 1) * LAST_ROWS, :] = total[
                z * LAST_ROWS : (z + 1) * LAST_ROWS
            ]


PIECE = OWN * WIDE // LANES


def to_owners(parts, send_ref):
    total = jnp.sum(parts[...].astype(F32), 0)
    squares = jnp.sum(total * total, keepdims=True)
    for x in range(X):
        for y in range(Y):
            for slot, row in ((0, x * OWN), (1, LAST_ROWS + y * OWN)):
                for c in range(WIDE // LANES):
                    first = slot * PIECE + c * OWN
                    send_ref[x * Y + y, first : first + OWN, :] = total[
                        row : row + OWN, c * LANES : (c + 1) * LANES
                    ]
            send_ref[x * Y + y, 2 * PIECE :, :] = jnp.broadcast_to(squares, (8, LANES))


def spread(got, tile_ref):
    tile_ref[...] = jnp.broadcast_to(jnp.sum(got[:, 2 * PIECE :, :], 0)[None], tile_ref.shape)


def clipped(where, got, tiles, qkv_a, out_a, qkv_b, out_b):
    total = jnp.sum(tiles[...], 0)[:1, :1]
    factor = jnp.minimum(1.0, math.sqrt(8.0) * D / jnp.sqrt(total))
    x, y = where[0], where[1]
    for k in range(GROUP):
        for slot, source, refs in (
            (0, k * Y + y, (qkv_a, out_a)),
            (1, x * Y + k, (qkv_b, out_b)),
        ):
            ref, column = (refs[0], k * WIDE) if k < 3 else (refs[1], 0)
            for c in range(WIDE // LANES):
                first = slot * PIECE + c * OWN
                ref[:, column + c * LANES : column + (c + 1) * LANES] = (
                    got[source, first : first + OWN, :] * factor
                )


def shape_of(*dims, dtype=BF16):
    return jax.ShapeDtypeStruct(dims, dtype)


def call(kernel, outs, scratch, *args, scalar=False, dtype=F32):
    whole = pl.BlockSpec(memory_space=pltpu.VMEM)
    specs = [whole] * len(args)
    if scalar:
        specs[0] = pl.BlockSpec(memory_space=pltpu.SMEM)
    return pl.pallas_call(
        kernel,
        out_shape=outs,
        in_specs=specs,
        out_specs=[whole] * len(outs),
        scratch_shapes=[pltpu.VMEM(s, dtype) for s in scratch],
        compiler_params=pltpu.CompilerParams(vmem_limit_bytes=VMEM_BYTES),
        name=kernel.__name__,
    )(*args)


def quarters(field):
    trailing = field.shape[3:]
    shaped = field.reshape((WLEV, 2, HLAT, 2, HLON) + trailing)
    order = (1, 3, 0, 2, 4) + tuple(range(5, 5 + len(trailing)))
    return shaped.transpose(order).reshape((4, QUART) + trailing)


def unquarters(field):
    trailing = field.shape[2:]
    shaped = field.reshape((2, 2, WLEV, HLAT, HLON) + trailing)
    order = (2, 0, 3, 1, 4) + tuple(range(5, 5 + len(trailing)))
    return shaped.transpose(order).reshape((WLEV, WLAT, WLON) + trailing)


def moves(lat_count, lon_count):
    tables = []
    for a in range(2):
        for b in range(2):
            table = []
            for i in range(lat_count):
                for j in range(lon_count):
                    ti = (i - (1 - a)) % lat_count
                    tj = (j - (1 - b)) % lon_count
                    table.append((i * lon_count + j, ti * lon_count + tj))
            tables.append(table)
    return tables


def send(parts, tables, back=False):
    out = []
    for part, table in zip(parts, tables):
        if all(s == t for s, t in table):
            out.append(part)
            continue
        pairs = [(t, s) for s, t in table] if back else table
        out.append(lax.ppermute(part, ("lat", "lon"), pairs))
    return out


def index_of(x, y, z):
    return (x * YLO + y % YLO) * LON + y // YLO * Z + z


CHIPS = [(x, y, z) for x in range(X) for y in range(Y) for z in range(Z)]
PLANE = [[index_of(x, y, z) for x in range(X) for y in range(Y)] for z in range(Z)]
COLUMN = [[index_of(x, y, z) for z in range(Z)] for x in range(X) for y in range(Y)]


def swap(packs, axis):
    out = [packs[0]]
    for step in range(1, GROUP):
        pairs = [
            (index_of(x, y, z), index_of(x ^ step, y, z) if axis == "x" else index_of(x, y ^ step, z))
            for x, y, z in CHIPS
        ]
        out.append(lax.ppermute(packs[step], ("lat", "lon"), pairs))
    return out


def exchange(parts, groups):
    return lax.all_to_all(parts, ("lat", "lon"), 0, 0, axis_index_groups=groups)


def after(value, earlier):
    return lax.optimization_barrier((value, earlier))[0]


def on_device(
    tokens,
    cotangent,
    region,
    unshifted_norm_gain,
    unshifted_query_key_value,
    out_first,
    shifted_norm_gain,
    shifted_query_key_value,
    out_second,
):
    tables = moves(LAT, LON)
    lat, lon = lax.axis_index("lat"), lax.axis_index("lon")
    at_x = (lat // YLO).astype(jnp.int32)
    at_y = (lon // Z * YLO + lat % YLO).astype(jnp.int32)
    me_x, me_y = at_x.reshape(1), at_y.reshape(1)
    wrap = jnp.where(lat == 0, 4, 0).astype(jnp.int32).reshape(1)
    gain_a = unshifted_norm_gain.reshape(1, D)
    gain_b = shifted_norm_gain.reshape(1, D)
    tok = quarters(tokens).reshape(TOK, D)
    cot = quarters(cotangent).reshape(TOK, D)
    lab = jnp.broadcast_to(quarters(region).reshape(TOK, 1), (TOK, LANES)).astype(BF16)

    field = shape_of(TOK, D)
    fields = shape_of(GROUP, TOK, D)
    packs = [shape_of(TOK, D + WIDE)] * GROUP
    *x, proj_a, left_n, left_a = call(
        first_forward,
        [shape_of(QUART, SEND)] * 4 + [shape_of(TOK, 3 * D), field, field],
        [(TOK, D), (TOK, LANES)],
        wrap, tok, cot, lab, gain_a, unshifted_query_key_value, out_first,
        scalar=True,
    )
    x = send(x, tables)
    *back, normed_b, att_b, right_b = call(
        second_main,
        [shape_of(QUART, 2 * D)] * 4 + [field, field, fields],
        [(TOK, D), (TOK, LANES)],
        *x, gain_b, shifted_query_key_value, out_second,
    )
    back = send(back, tables, back=True)
    pack_b = call(
        second_pack,
        packs,
        [(TOK, D), (TOK, D)],
        me_y, normed_b, att_b, right_b,
        scalar=True, dtype=BF16,
    )
    pack_b = swap(after(pack_b, back[:3]), "y")
    right_a, *pack_a = call(
        first_backward,
        [fields] + packs,
        [(TOK, D)],
        me_x, *back, lab, out_first, proj_a, left_n, left_a,
        scalar=True,
    )
    pack_a = swap(pack_a, "x")
    (token_gradient,) = call(
        first_rest,
        [field],
        [(TOK, D)],
        *back, tok, gain_a, unshifted_query_key_value, right_a,
    )
    token_gradient = unquarters(token_gradient.reshape(4, QUART, D))
    result = unquarters(jnp.stack(back)[..., :D])

    rows = [shape_of(PLANE_ROWS, WIDE)] * GROUP
    sum_b = swap(call(weights, rows, [(D, WIDE)], me_x, *pack_b, scalar=True), "x")
    sum_a = swap(call(weights, rows, [(D, WIDE)], me_y, *pack_a, scalar=True), "y")
    (sums,) = call(add_rows, [shape_of(Z, 2 * LAST_ROWS, WIDE)], [], *sum_a, *sum_b)
    sums = exchange(sums, COLUMN)
    (pieces,) = call(
        to_owners, [shape_of(X * Y, 2 * PIECE + 8, LANES, dtype=F32)], [], sums
    )
    pieces = exchange(pieces, PLANE)
    (tiles,) = call(spread, [shape_of(Z, 8, LANES, dtype=F32)], [], pieces)
    tiles = exchange(tiles, COLUMN)
    out_qkv, out_out = shape_of(OWN, 3 * D, dtype=F32), shape_of(OWN, D, dtype=F32)
    clips = call(
        clipped, [out_qkv, out_out] * 2, [], jnp.stack([at_x, at_y]), pieces, tiles, scalar=True
    )
    return (result, token_gradient, *clips)


def solution(mesh):
    field = P("rep", "lat", "lon", None)
    rows = P(("rep", "lat", "lon"), None)
    in_specs = (field, field, P("rep", "lat", "lon"), P(), P(), P(), P(), P(), P())
    return jax.shard_map(
        on_device,
        mesh=mesh,
        in_specs=in_specs,
        out_specs=(field, field, rows, rows, rows, rows),
        check_vma=False,
    )
```

time: 819 us -> 118 us (0.14)
  blocking collectives: 348 us -> 13 us
  waiting for transfers between devices: 262 us -> 36.4 us
  matrix products: 76.6 us -> 0 us
  local copies, waits for them, and re-layouts: 57.7 us -> 7.8 us
  other arithmetic: 20.1 us -> 0.79 us
  Pallas kernels: 0 us -> 19.3 us
  between operations: 18.9 us -> 0.9 us
    psum x1 -> x0, blocking collectives: 348 us -> none  [on_device(): norm_total = lax.psum(local_sum, ('lat', 'lon'))]
    unnamed x2 -> x0, waiting for transfers between devices: 255 us -> none
    dot_general x27 -> x0, matrix products: 58.9 us -> none  [the longest x3 12.5 us: attend_back(): jnp.einsum('whqk,wkhd->wqhd', grad_rounded, key_heads, preferred_element_...]
    pallas_call x0 -> x11, Pallas kernels: none -> 19.3 us  [call(): pl.pallas_call(kernel, out_shape=outs, in_specs=specs, out_specs=[whole]...]
    sub x5 -> x0, matrix products: 17.7 us -> none  [probabilities(): exponent = jnp.exp(scores - row_max)]
    ppermute x12 -> x18, waiting for transfers between devices: 7.29 us -> 22.3 us  [the longest x12 12.6 us: swap(): out.append(lax.ppermute(packs[step], ('lat', 'lon'), pairs))]
    all_to_all x0 -> x2, waiting for transfers between devices: none -> 14.1 us  [exchange(): return lax.all_to_all(parts, ('lat', 'lon'), 0, 0, axis_index_groups=groups)]
    all_to_all x0 -> x1, blocking collectives: none -> 13 us  [exchange(): return lax.all_to_all(parts, ('lat', 'lon'), 0, 0, axis_index_groups=groups)]
  transfers between devices with their start and end apart: 13 -> 20, of which waited for: 4 -> 9; matrix products, arithmetic and copies ran while one was open for 3% -> 2% of each run, Pallas kernels for 0% -> 8%
where the time goes in v1:
time: 118 us; the launch traced here: 117 us
  starting transfers between devices  38.8 us (33%)
  waiting for transfers between devices  36.4 us (31%)
  Pallas kernels  19.3 us (16%)
  blocking collectives  13 us (11%)
  local copies, waits for them, and re-layouts  7.8 us (7%)
    pallas_call x11, Pallas kernels, call(): pl.pallas_call(kernel, out_shape=outs, in_specs=specs, out_specs=[whole]...  19.3 us
    ppermute x12, starting transfers between devices, swap(): out.append(lax.ppermute(packs[step], ('lat', 'lon'), pairs))  17.8 us
    all_to_all x2, waiting for transfers between devices, exchange(): return lax.all_to_all(parts, ('lat', 'lon'), 0, 0, axis_index_groups=groups)  14.1 us
    ppermute x6, starting transfers between devices, send(): out.append(lax.ppermute(part, ('lat', 'lon'), pairs))  13.4 us
    all_to_all x1, blocking collectives, exchange(): return lax.all_to_all(parts, ('lat', 'lon'), 0, 0, axis_index_groups=groups)  13 us
    ppermute x12, waiting for transfers between devices, swap(): out.append(lax.ppermute(packs[step], ('lat', 'lon'), pairs))  12.6 us
    ppermute x6, waiting for transfers between devices, send(): out.append(lax.ppermute(part, ('lat', 'lon'), pairs))  9.62 us
    all_to_all x2, starting transfers between devices, exchange(): return lax.all_to_all(parts, ('lat', 'lon'), 0, 0, axis_index_groups=groups)  7.6 us
  transfers between devices with their start and end apart: 20, of which 9 were waited for; matrix products, arithmetic and copies ran while one was open for 2% of the time, Pallas kernels for 8%

profile of v1, /device:TPU:0, one launch (start us, length us, event | category | flops | bytes accessed | tf_op | source)
XLA Modules:
  0.0 117.0 jit_solution(13159560209831020527)
XLA Ops:
  0.6 1.0 copy.33
  1.7 0.7 convert_element_type.9
  2.5 0.1 convert_element_type.12
  2.6 1.0 copy.32
  3.8 1.4 %copy-done = bf16[512,1536]{1,0:T(8,128)(2,1)S(1)} copy-done((bf16[512,1536]{1,0:T(8,128)(2,1)S(1)}, bf16[512,1536]{1,0:T(8,128)(2,1)}, u32[]{:S(2)}) %copy-start) | copy-done | bytes 1572888
  5.2 0.7 copy-done.7
  5.9 1.8 %first_forward.1 = (bf16[36,1152]{1,0:T(8,128)(2,1)S(1)}, bf16[36,1152]{1,0:T(8,128)(2,1)S(1)}, bf16[36,1152]{1,0:T(8,128)(2,1)S(1)}, bf16[36,1152]{1,0:T(8,128)...) custom-call(s32[1]{0:T(128)} %bitcast.wrap, ...), custom_call_target="tpu_custom_call" | custom-call | tf_op jit(solution)/shard_map/first_forward/pallas_call | solution.py:317
  7.7 0.7 copy-done.5
  8.3 8.8 %collective-permute-start = (bf16[36,1152]{1,0:T(8,128)(2,1)S(1)}, bf16[36,1152]{1,0:T(8,128)(2,1)S(1)}, u32[]{:S(2)}, u32[]{:S(2)}) collective-permute-start(bf16[36,1152]{1,0:T(8,128)(2,1)S(1)} %get-tuple-element.45), channel_id=1, source_target_pairs={{0,254},{2,224},{4,226},{6,228},{8,230},{10,232},{12,234},{14,236}... | collective-permute-start | bytes 248840 | tf_op jit(solution)/shard_map/ppermute | solution.py:363
  17.1 0.1 collective-permute-start.1
  17.2 2.5 %collective-permute-start.2 = (bf16[36,1152]{1,0:T(8,128)(2,1)S(1)}, bf16[36,1152]{1,0:T(8,128)(2,1)S(1)}, u32[]{:S(2)}, u32[]{:S(2)}) collective-permute-start(bf16[36,1152]{1,0:T(8,128)(2,1)S(1)} %get-tuple-element.47), channel_id=1, source_target_pairs={{0,30},{2,0},{4,2},{6,4},{8,6},{10,8},{12,10},{14,12},{16,14},{18,... | collective-permute-start | bytes 248840 | tf_op jit(solution)/shard_map/ppermute | solution.py:363
  19.7 1.9 %collective-permute-done.1.x1 = bf16[36,1152]{1,0:T(8,128)(2,1)S(1)} collective-permute-done((bf16[36,1152]{1,0:T(8,128)(2,1)S(1)}, bf16[36,1152]{1,0:T(8,128)(2,1)S(1)}, u32[]{:S(2)}, u32[]{:S(2)}) %collective-permute-start.1) | collective-permute-done | bytes 82976 | tf_op jit(solution)/shard_map/ppermute | solution.py:363
  21.6 0.3 collective-permute-done.2.x2
  21.9 5.5 %second_main.1 = (bf16[36,1024]{1,0:T(8,128)(2,1)S(1)}, bf16[36,1024]{1,0:T(8,128)(2,1)S(1)}, bf16[36,1024]{1,0:T(8,128)(2,1)S(1)}, bf16[36,1024]{1,0:T(8,128)(2...) custom-call(bf16[36,1152]{1,0:T(8,128)(2,1)S(1)} %collective-permute-done.x0, ...), custom_call_target="tpu_custom_call" | custom-call | tf_op jit(solution)/shard_map/second_main/pallas_call | solution.py:317
  27.4 0.9 collective-permute-start.3
  28.3 1.0 collective-permute-start.4
  29.3 1.4 %second_pack.1 = (bf16[144,1024]{1,0:T(8,128)(2,1)S(1)}, bf16[144,1024]{1,0:T(8,128)(2,1)}, bf16[144,1024]{1,0:T(8,128)(2,1)}, bf16[144,1024]{1,0:T(8,128)(2,1)}) custom-call(s32[1]{0:T(128)} %bitcast.17.me, bf16[144,512]{1,0:T(8,128)(2,1)S(1)} %get-tuple-element.65.normed, bf16[144,512]{1,0:T(8,128)(2,1)S(1)} %get-tuple-element.66.attended, ...), custom_call_target="tpu_custom_call" | custom-call | tf_op jit(solution)/shard_map/second_pack/pallas_call | solution.py:317
  30.7 7.5 %collective-permute-done.3.b0 = bf16[36,1024]{1,0:T(8,128)(2,1)S(1)} collective-permute-done((bf16[36,1024]{1,0:T(8,128)(2,1)S(1)}, bf16[36,1024]{1,0:T(8,128)(2,1)S(1)}, u32[]{:S(2)}, u32[]{:S(2)}) %collective-permute-start.3) | collective-permute-done | bytes 73760 | tf_op jit(solution)/shard_map/ppermute | solution.py:363
  38.2 1.5 %collective-permute-start.13 = (bf16[144,1024]{1,0:T(8,128)(2,1)}, bf16[144,1024]{1,0:T(8,128)(2,1)S(1)}, u32[]{:S(2)}, u32[]{:S(2)}) collective-permute-start(bf16[144,1024]{1,0:T(8,128)(2,1)} %get-tuple-element.74), channel_id=1, source_target_pairs={{0,16},{2,18},{4,20},{6,22},{8,24},{10,26},{12,28},{14,30},{32,48}... | collective-permute-start | bytes 884744 | tf_op jit(solution)/shard_map/ppermute | solution.py:383
  39.7 3.2 %collective-permute-start.14 = (bf16[144,1024]{1,0:T(8,128)(2,1)}, bf16[144,1024]{1,0:T(8,128)(2,1)}, u32[]{:S(2)}, u32[]{:S(2)}) collective-permute-start(bf16[144,1024]{1,0:T(8,128)(2,1)} %get-tuple-element.75), channel_id=1, source_target_pairs={{0,48},{2,50},{4,52},{6,54},{8,56},{10,58},{12,60},{14,62},{32,16}... | collective-permute-start | bytes 884744 | tf_op jit(solution)/shard_map/ppermute | solution.py:383
  42.9 0.9 copy-done.6
  43.8 4.5 %first_backward.1 = (bf16[4,144,512]{2,1,0:T(8,128)(2,1)S(1)}, bf16[144,1024]{1,0:T(8,128)(2,1)S(1)}, bf16[144,1024]{1,0:T(8,128)(2,1)S(1)}, bf16[144,1024]{1,0:T(8,128)(2,1)S(1)}, bf16[144,1024]{1,0:T(8,128)(2,1)S(1)}) custom-call(s32[1]{0:T(128)} %bitcast.14.me, bf16[36,1024]{1,0:T(8,128)(2,1)S(1)} %collective-permute-done.3.b0, ...), custom_call_target="tpu_custom_call" | custom-call | tf_op jit(solution)/shard_map/first_backward/pallas_call | solution.py:317
  48.3 0.1 collective-permute-start.6
  48.4 2.6 %collective-permute-start.7 = (bf16[144,1024]{1,0:T(8,128)(2,1)S(1)}, bf16[144,1024]{1,0:T(8,128)(2,1)S(1)}, u32[]{:S(2)}, u32[]{:S(2)}) collective-permute-start(bf16[144,1024]{1,0:T(8,128)(2,1)S(1)} %get-tuple-element.59), channel_id=1, source_target_pairs={{0,128},{2,130},{4,132},{6,134},{8,136},{10,138},{12,140},{14,142}... | collective-permute-start | bytes 884744 | tf_op jit(solution)/shard_map/ppermute | solution.py:383
  51.0 2.1 %collective-permute-start.8 = (bf16[144,1024]{1,0:T(8,128)(2,1)S(1)}, bf16[144,1024]{1,0:T(8,128)(2,1)S(1)}, u32[]{:S(2)}, u32[]{:S(2)}) collective-permute-start(bf16[144,1024]{1,0:T(8,128)(2,1)S(1)} %get-tuple-element.60), channel_id=1, source_target_pairs={{0,192},{2,194},{4,196},{6,198},{8,200},{10,202},{12,204},{14,206}... | collective-permute-start | bytes 884744 | tf_op jit(solution)/shard_map/ppermute | solution.py:383
  53.1 1.8 %weights.3 = (bf16[128,512]{1,0:T(8,128)(2,1)S(1)}, bf16[128,512]{1,0:T(8,128)(2,1)S(1)}, bf16[128,512]{1,0:T(8,128)(2,1)S(1)}, bf16[128,512]{1,0:T(8,128)(2,1)S(1)}) custom-call(s32[1]{0:T(128)} %bitcast.14.me, bf16[144,1024]{1,0:T(8,128)(2,1)S(1)} %get-tuple-element.72.p0, bf16[144,1024]{1,0:T(8,128)(2,1)S(1)} %collective-permute-done.12.p1, ...), custom_call_target="tpu_custom_call" | custom-call | tf_op jit(solution)/shard_map/weights/pallas_call | solution.py:317
  54.9 0.1 collective-permute-start.15
  55.0 4.2 %collective-permute-start.16 = (bf16[128,512]{1,0:T(8,128)(2,1)S(1)}, bf16[128,512]{1,0:T(8,128)(2,1)S(1)}, u32[]{:S(2)}, u32[]{:S(2)}) collective-permute-start(bf16[128,512]{1,0:T(8,128)(2,1)S(1)} %get-tuple-element.78), channel_id=1, source_target_pairs={{0,128},{2,130},{4,132},{6,134},{8,136},{10,138},{12,140},{14,142}... | collective-permute-start | bytes 393224 | tf_op jit(solution)/shard_map/ppermute | solution.py:383
  59.2 0.4 collective-permute-start.17
  59.7 4.6 %collective-permute-done.7.p2 = bf16[144,1024]{1,0:T(8,128)(2,1)S(1)} collective-permute-done((bf16[144,1024]{1,0:T(8,128)(2,1)S(1)}, bf16[144,1024]{1,0:T(8,128)(2,1)S(1)}, u32[]{:S(2)}, u32[]{:S(2)}) %collective-permute-start.7) | collective-permute-done | bytes 294944 | tf_op jit(solution)/shard_map/ppermute | solution.py:383
  64.3 3.9 %collective-permute-done.8.p3 = bf16[144,1024]{1,0:T(8,128)(2,1)S(1)} collective-permute-done((bf16[144,1024]{1,0:T(8,128)(2,1)S(1)}, bf16[144,1024]{1,0:T(8,128)(2,1)S(1)}, u32[]{:S(2)}, u32[]{:S(2)}) %collective-permute-start.8) | collective-permute-done | bytes 294944 | tf_op jit(solution)/shard_map/ppermute | solution.py:383
  68.1 0.8 weights.2
  69.1 2.2 %collective-permute-start.11 = (bf16[128,512]{1,0:T(8,128)(2,1)S(1)}, bf16[128,512]{1,0:T(8,128)(2,1)S(1)}, u32[]{:S(2)}, u32[]{:S(2)}) collective-permute-start(bf16[128,512]{1,0:T(8,128)(2,1)S(1)} %get-tuple-element.64), channel_id=1, source_target_pairs={{0,48},{2,50},{4,52},{6,54},{8,56},{10,58},{12,60},{14,62},{32,16}... | collective-permute-start | bytes 393224 | tf_op jit(solution)/shard_map/ppermute | solution.py:383
  71.3 1.3 %collective-permute-start.9 = (bf16[128,512]{1,0:T(8,128)(2,1)S(1)}, bf16[128,512]{1,0:T(8,128)(2,1)S(1)}, u32[]{:S(2)}, u32[]{:S(2)}) collective-permute-start(bf16[128,512]{1,0:T(8,128)(2,1)S(1)} %get-tuple-element.62), channel_id=1, source_target_pairs={{0,32},{2,34},{4,36},{6,38},{8,40},{10,42},{12,44},{14,46},{32,0},... | collective-permute-start | bytes 393224 | tf_op jit(solution)/shard_map/ppermute | solution.py:383
  72.5 3.1 %collective-permute-done.10.a2 = bf16[128,512]{1,0:T(8,128)(2,1)S(1)} collective-permute-done((bf16[128,512]{1,0:T(8,128)(2,1)S(1)}, bf16[128,512]{1,0:T(8,128)(2,1)S(1)}, u32[]{:S(2)}, u32[]{:S(2)}) %collective-permute-start.10) | collective-permute-done | bytes 131104 | tf_op jit(solution)/shard_map/ppermute | solution.py:383
  75.6 1.1 collective-permute-done.11.a3
  76.7 0.1 add_rows.1
  76.9 13.0 %all_to_all.15.parts = bf16[8,32,512]{2,1,0:T(8,128)(2,1)S(1)} all-to-all(bf16[8,32,512]{2,1,0:T(8,128)(2,1)S(1)} %add_rows.1), channel_id=1, replica_groups={{0,2,4,6,8,10,12,14},{32,34,36,38,40,42,44,46},{16,18,20,22,24,26,28,30..., dimensions={0} | all-to-all | bytes 524288 | tf_op jit(solution)/shard_map/all_to_all | solution.py:388
  89.9 0.9 to_owners.1
  90.8 4.3 %all-to-all-start.1 = ((f32[16,40,128]{2,1,0:T(8,128)}), f32[16,40,128]{2,1,0:T(8,128)S(1)}, u32[]{:S(2)}, u32[]{:S(2)}) async-start(f32[16,40,128]{2,1,0:T(8,128)} %to_owners.1), calls=%async_computation.1 | async-start | bytes 655360 | tf_op jit(solution)/shard_map/all_to_all | solution.py:388
  95.2 8.7 %all-to-all-done.1.got = f32[16,40,128]{2,1,0:T(8,128)S(1)} async-done(((f32[16,40,128]{2,1,0:T(8,128)}), f32[16,40,128]{2,1,0:T(8,128)S(1)}, u32[]{:S(2)}, u32[]{:S(2)}) %all-to-all-start.1) | async-done | bytes 327712 | tf_op jit(solution)/shard_map/all_to_all | solution.py:388
  103.9 0.6 spread.1
  104.5 3.3 %all-to-all-start.2 = ((f32[8,8,128]{2,1,0:T(8,128)}), f32[8,8,128]{2,1,0:T(8,128)S(1)}, u32[]{:S(2)}, u32[]{:S(2)}) async-start(f32[8,8,128]{2,1,0:T(8,128)} %spread.1), calls=%async_computation.2 | async-start | bytes 65536 | tf_op jit(solution)/shard_map/all_to_all | solution.py:388
  107.9 0.8 first_rest.1
  108.7 0.8 copy.28
  109.7 0.8 copy.27
  110.4 5.4 %all-to-all-done.2.tiles = f32[8,8,128]{2,1,0:T(8,128)S(1)} async-done(((f32[8,8,128]{2,1,0:T(8,128)}), f32[8,8,128]{2,1,0:T(8,128)S(1)}, u32[]{:S(2)}, u32[]{:S(2)}) %all-to-all-start.2) | async-done | bytes 32800 | tf_op jit(solution)/shard_map/all_to_all | solution.py:388
  115.8 1.2 %clipped.1 = (f32[4,1536]{1,0:T(4,128)}, f32[4,512]{1,0:T(4,128)}, f32[4,1536]{1,0:T(4,128)}, f32[4,512]{1,0:T(4,128)}) custom-call(s32[2]{0:T(128)S(1)} %pad_add_fusion.where, f32[16,40,128]{2,1,0:T(8,128)S(1)} %all-to-all-done.1.got, f32[8,8,128]{2,1,0:T(8,128)S(1)} %all-to-all-done.2.tiles), custom_call_target="tpu_custom_call" | custom-call | tf_op jit(solution)/shard_map/clipped/pallas_call | solution.py:317
  (40 shorter events, 0.7 us)
Async XLA Ops:
  0.6 3.2 %copy-start.2 = (bf16[512,512]{1,0:T(8,128)(2,1)S(1)}, bf16[512,512]{1,0:T(8,128)(2,1)}, u32[]{:S(2)}) copy-start(bf16[512,512]{1,0:T(8,128)(2,1)} %wout.5) | copy-start | bytes 1572868
  2.6 19.3 %copy-start.4 = (bf16[512,512]{1,0:T(8,128)(2,1)S(1)}, bf16[512,512]{1,0:T(8,128)(2,1)}, u32[]{:S(2)}) copy-start(bf16[512,512]{1,0:T(8,128)(2,1)} %wout.4) | copy-start | bytes 1572868
  2.6 19.3 %copy-start.9 = (f32[512]{0:T(512)S(1)}, f32[512]{0:T(512)}, u32[]{:S(2)}) copy-start(f32[512]{0:T(512)} %param.15) | copy-start | bytes 6148
  3.8 1.4 %copy-start = (bf16[512,1536]{1,0:T(8,128)(2,1)S(1)}, bf16[512,1536]{1,0:T(8,128)(2,1)}, u32[]{:S(2)}) copy-start(bf16[512,1536]{1,0:T(8,128)(2,1)} %wqkv.5) | copy-start | bytes 4718596
  5.2 0.7 copy-start.7
  5.9 16.0 %copy-start.3 = (bf16[512,1536]{1,0:T(8,128)(2,1)S(1)}, bf16[512,1536]{1,0:T(8,128)(2,1)}, u32[]{:S(2)}) copy-start(bf16[512,1536]{1,0:T(8,128)(2,1)} %wqkv.4) | copy-start | bytes 4718596
  7.7 0.7 copy-start.5
  8.3 11.4 %collective-permute-start = (bf16[36,1152]{1,0:T(8,128)(2,1)S(1)}, bf16[36,1152]{1,0:T(8,128)(2,1)S(1)}, u32[]{:S(2)}, u32[]{:S(2)}) collective-permute-start(bf16[36,1152]{1,0:T(8,128)(2,1)S(1)} %get-tuple-element.45), channel_id=1, source_target_pairs={{0,254},{2,224},{4,226},{6,228},{8,230},{10,232},{12,234},{14,236}... | collective-permute-start | bytes 248840 | tf_op jit(solution)/shard_map/ppermute | solution.py:363
  17.1 4.6 %collective-permute-start.1 = (bf16[36,1152]{1,0:T(8,128)(2,1)S(1)}, bf16[36,1152]{1,0:T(8,128)(2,1)S(1)}, u32[]{:S(2)}, u32[]{:S(2)}) collective-permute-start(bf16[36,1152]{1,0:T(8,128)(2,1)S(1)} %get-tuple-element.46), channel_id=1, source_target_pairs={{0,224},{2,226},{4,228},{6,230},{8,232},{10,234},{12,236},{14,238}... | collective-permute-start | bytes 248840 | tf_op jit(solution)/shard_map/ppermute | solution.py:363
  17.2 4.7 %collective-permute-start.2 = (bf16[36,1152]{1,0:T(8,128)(2,1)S(1)}, bf16[36,1152]{1,0:T(8,128)(2,1)S(1)}, u32[]{:S(2)}, u32[]{:S(2)}) collective-permute-start(bf16[36,1152]{1,0:T(8,128)(2,1)S(1)} %get-tuple-element.47), channel_id=1, source_target_pairs={{0,30},{2,0},{4,2},{6,4},{8,6},{10,8},{12,10},{14,12},{16,14},{18,... | collective-permute-start | bytes 248840 | tf_op jit(solution)/shard_map/ppermute | solution.py:363
  27.4 10.8 %collective-permute-start.3 = (bf16[36,1024]{1,0:T(8,128)(2,1)S(1)}, bf16[36,1024]{1,0:T(8,128)(2,1)S(1)}, u32[]{:S(2)}, u32[]{:S(2)}) collective-permute-start(bf16[36,1024]{1,0:T(8,128)(2,1)S(1)} %get-tuple-element.49), channel_id=1, source_target_pairs={{254,0},{224,2},{226,4},{228,6},{230,8},{232,10},{234,12},{236,14}... | collective-permute-start | bytes 221192 | tf_op jit(solution)/shard_map/ppermute | solution.py:363
  28.3 9.9 %collective-permute-start.4 = (bf16[36,1024]{1,0:T(8,128)(2,1)S(1)}, bf16[36,1024]{1,0:T(8,128)(2,1)S(1)}, u32[]{:S(2)}, u32[]{:S(2)}) collective-permute-start(bf16[36,1024]{1,0:T(8,128)(2,1)S(1)} %get-tuple-element.50), channel_id=1, source_target_pairs={{224,0},{226,2},{228,4},{230,6},{232,8},{234,10},{236,12},{238,14}... | collective-permute-start | bytes 221192 | tf_op jit(solution)/shard_map/ppermute | solution.py:363
  29.3 8.9 %collective-permute-start.5 = (bf16[36,1024]{1,0:T(8,128)(2,1)S(1)}, bf16[36,1024]{1,0:T(8,128)(2,1)S(1)}, u32[]{:S(2)}, u32[]{:S(2)}) collective-permute-start(bf16[36,1024]{1,0:T(8,128)(2,1)S(1)} %get-tuple-element.51), channel_id=1, source_target_pairs={{30,0},{0,2},{2,4},{4,6},{6,8},{8,10},{10,12},{12,14},{14,16},{16,... | collective-permute-start | bytes 221192 | tf_op jit(solution)/shard_map/ppermute | solution.py:363
  38.2 12.8 %collective-permute-start.12 = (bf16[144,1024]{1,0:T(8,128)(2,1)}, bf16[144,1024]{1,0:T(8,128)(2,1)S(1)}, u32[]{:S(2)}, u32[]{:S(2)}) collective-permute-start(bf16[144,1024]{1,0:T(8,128)(2,1)} %get-tuple-element.73), channel_id=1, source_target_pairs={{0,32},{2,34},{4,36},{6,38},{8,40},{10,42},{12,44},{14,46},{32,0},... | collective-permute-start | bytes 884744 | tf_op jit(solution)/shard_map/ppermute | solution.py:383
  38.2 14.9 %collective-permute-start.13 = (bf16[144,1024]{1,0:T(8,128)(2,1)}, bf16[144,1024]{1,0:T(8,128)(2,1)S(1)}, u32[]{:S(2)}, u32[]{:S(2)}) collective-permute-start(bf16[144,1024]{1,0:T(8,128)(2,1)} %get-tuple-element.74), channel_id=1, source_target_pairs={{0,16},{2,18},{4,20},{6,22},{8,24},{10,26},{12,28},{14,30},{32,48}... | collective-permute-start | bytes 884744 | tf_op jit(solution)/shard_map/ppermute | solution.py:383
  39.7 13.4 %collective-permute-start.14 = (bf16[144,1024]{1,0:T(8,128)(2,1)}, bf16[144,1024]{1,0:T(8,128)(2,1)}, u32[]{:S(2)}, u32[]{:S(2)}) collective-permute-start(bf16[144,1024]{1,0:T(8,128)(2,1)} %get-tuple-element.75), channel_id=1, source_target_pairs={{0,48},{2,50},{4,52},{6,54},{8,56},{10,58},{12,60},{14,62},{32,16}... | collective-permute-start | bytes 884744 | tf_op jit(solution)/shard_map/ppermute | solution.py:383
  42.9 0.9 copy-start.6
  48.3 10.9 %collective-permute-start.6 = (bf16[144,1024]{1,0:T(8,128)(2,1)S(1)}, bf16[144,1024]{1,0:T(8,128)(2,1)S(1)}, u32[]{:S(2)}, u32[]{:S(2)}) collective-permute-start(bf16[144,1024]{1,0:T(8,128)(2,1)S(1)} %get-tuple-element.58), channel_id=1, source_target_pairs={{0,64},{2,66},{4,68},{6,70},{8,72},{10,74},{12,76},{14,78},{32,96}... | collective-permute-start | bytes 884744 | tf_op jit(solution)/shard_map/ppermute | solution.py:383
  48.4 15.8 %collective-permute-start.7 = (bf16[144,1024]{1,0:T(8,128)(2,1)S(1)}, bf16[144,1024]{1,0:T(8,128)(2,1)S(1)}, u32[]{:S(2)}, u32[]{:S(2)}) collective-permute-start(bf16[144,1024]{1,0:T(8,128)(2,1)S(1)} %get-tuple-element.59), channel_id=1, source_target_pairs={{0,128},{2,130},{4,132},{6,134},{8,136},{10,138},{12,140},{14,142}... | collective-permute-start | bytes 884744 | tf_op jit(solution)/shard_map/ppermute | solution.py:383
  51.0 17.1 %collective-permute-start.8 = (bf16[144,1024]{1,0:T(8,128)(2,1)S(1)}, bf16[144,1024]{1,0:T(8,128)(2,1)S(1)}, u32[]{:S(2)}, u32[]{:S(2)}) collective-permute-start(bf16[144,1024]{1,0:T(8,128)(2,1)S(1)} %get-tuple-element.60), channel_id=1, source_target_pairs={{0,192},{2,194},{4,196},{6,198},{8,200},{10,202},{12,204},{14,206}... | collective-permute-start | bytes 884744 | tf_op jit(solution)/shard_map/ppermute | solution.py:383
  54.9 16.4 %collective-permute-start.15 = (bf16[128,512]{1,0:T(8,128)(2,1)S(1)}, bf16[128,512]{1,0:T(8,128)(2,1)S(1)}, u32[]{:S(2)}, u32[]{:S(2)}) collective-permute-start(bf16[128,512]{1,0:T(8,128)(2,1)S(1)} %get-tuple-element.77), channel_id=1, source_target_pairs={{0,64},{2,66},{4,68},{6,70},{8,72},{10,74},{12,76},{14,78},{32,96}... | collective-permute-start | bytes 393224 | tf_op jit(solution)/shard_map/ppermute | solution.py:383
  55.0 17.5 %collective-permute-start.16 = (bf16[128,512]{1,0:T(8,128)(2,1)S(1)}, bf16[128,512]{1,0:T(8,128)(2,1)S(1)}, u32[]{:S(2)}, u32[]{:S(2)}) collective-permute-start(bf16[128,512]{1,0:T(8,128)(2,1)S(1)} %get-tuple-element.78), channel_id=1, source_target_pairs={{0,128},{2,130},{4,132},{6,134},{8,136},{10,138},{12,140},{14,142}... | collective-permute-start | bytes 393224 | tf_op jit(solution)/shard_map/ppermute | solution.py:383
  59.2 13.3 %collective-permute-start.17 = (bf16[128,512]{1,0:T(8,128)(2,1)S(1)}, bf16[128,512]{1,0:T(8,128)(2,1)S(1)}, u32[]{:S(2)}, u32[]{:S(2)}) collective-permute-start(bf16[128,512]{1,0:T(8,128)(2,1)S(1)} %get-tuple-element.79), channel_id=1, source_target_pairs={{0,192},{2,194},{4,196},{6,198},{8,200},{10,202},{12,204},{14,206}... | collective-permute-start | bytes 393224 | tf_op jit(solution)/shard_map/ppermute | solution.py:383
  69.0 6.7 %collective-permute-start.10 = (bf16[128,512]{1,0:T(8,128)(2,1)S(1)}, bf16[128,512]{1,0:T(8,128)(2,1)S(1)}, u32[]{:S(2)}, u32[]{:S(2)}) collective-permute-start(bf16[128,512]{1,0:T(8,128)(2,1)S(1)} %get-tuple-element.63), channel_id=1, source_target_pairs={{0,16},{2,18},{4,20},{6,22},{8,24},{10,26},{12,28},{14,30},{32,48}... | collective-permute-start | bytes 393224 | tf_op jit(solution)/shard_map/ppermute | solution.py:383
  69.1 7.7 %collective-permute-start.11 = (bf16[128,512]{1,0:T(8,128)(2,1)S(1)}, bf16[128,512]{1,0:T(8,128)(2,1)S(1)}, u32[]{:S(2)}, u32[]{:S(2)}) collective-permute-start(bf16[128,512]{1,0:T(8,128)(2,1)S(1)} %get-tuple-element.64), channel_id=1, source_target_pairs={{0,48},{2,50},{4,52},{6,54},{8,56},{10,58},{12,60},{14,62},{32,16}... | collective-permute-start | bytes 393224 | tf_op jit(solution)/shard_map/ppermute | solution.py:383
  71.3 5.5 %collective-permute-start.9 = (bf16[128,512]{1,0:T(8,128)(2,1)S(1)}, bf16[128,512]{1,0:T(8,128)(2,1)S(1)}, u32[]{:S(2)}, u32[]{:S(2)}) collective-permute-start(bf16[128,512]{1,0:T(8,128)(2,1)S(1)} %get-tuple-element.62), channel_id=1, source_target_pairs={{0,32},{2,34},{4,36},{6,38},{8,40},{10,42},{12,44},{14,46},{32,0},... | collective-permute-start | bytes 393224 | tf_op jit(solution)/shard_map/ppermute | solution.py:383
  76.9 31.0 %copy-start.1 = (bf16[512,1536]{1,0:T(8,128)(2,1)S(1)}, bf16[512,1536]{1,0:T(8,128)(2,1)}, u32[]{:S(2)}) copy-start(bf16[512,1536]{1,0:T(8,128)(2,1)} %wqkv.5) | copy-start | bytes 4718596
  76.9 31.0 %copy-start.8 = (f32[512]{0:T(512)S(1)}, f32[512]{0:T(512)}, u32[]{:S(2)}) copy-start(f32[512]{0:T(512)} %param.12) | copy-start | bytes 6148
  90.8 13.1 %all-to-all-start.1 = ((f32[16,40,128]{2,1,0:T(8,128)}), f32[16,40,128]{2,1,0:T(8,128)S(1)}, u32[]{:S(2)}, u32[]{:S(2)}) async-start(f32[16,40,128]{2,1,0:T(8,128)} %to_owners.1), calls=%async_computation.1 | async-start | bytes 655360 | tf_op jit(solution)/shard_map/all_to_all | solution.py:388
  104.5 11.3 %all-to-all-start.2 = ((f32[8,8,128]{2,1,0:T(8,128)}), f32[8,8,128]{2,1,0:T(8,128)S(1)}, u32[]{:S(2)}, u32[]{:S(2)}) async-start(f32[8,8,128]{2,1,0:T(8,128)} %spread.1), calls=%async_computation.2 | async-start | bytes 65536 | tf_op jit(solution)/shard_map/all_to_all | solution.py:388

commit v2 on v1

--- a/solution.py
+++ b/solution.py
@@ -71,15 +71,9 @@
     return (1.0 - dot_nt(hot, hot)) * NEGATIVE
 
 
-def head_masks():
-    lane = lax.broadcasted_iota(jnp.int32, (1, LANES), 1)
-    low = (lane < HEAD).astype(F32)
-    return low, 1.0 - low
-
-
-def pair_of(proj, part, pair):
+def pair_of(fields, part, pair):
     start = part * D + pair * LANES
-    return proj[:, start : start + LANES]
+    return fields[:, start : start + LANES]
 
 
 def softmax_rows(scores):
@@ -87,38 +81,83 @@
     return shifted * (1.0 / jnp.sum(shifted, -1, keepdims=True))
 
 
-def attention(proj, bias, grad=None, forward=True):
-    low, high = head_masks()
-    is_low = low > 0.5
-    masks = (low.astype(BF16), high.astype(BF16))
+def attention(proj, bias, grad=None, attended=None):
+    lane = lax.broadcasted_iota(jnp.int32, (1, LANES), 1)
+    is_low = lane < HEAD
+    low = is_low.astype(F32)
+    masks = (low.astype(BF16), (1.0 - low).astype(BF16))
+    bias = jnp.concatenate([bias, bias], 0)
+
+    def stacked(field):
+        return jnp.concatenate([field * masks[0], field * masks[1]], 0)
+
+    def merged(both):
+        return jnp.where(is_low, both[:TOK], both[TOK:])
+
     att, dq, dk, dv = [], [], [], []
     for pair in range(PAIRS):
-        q = pair_of(proj, 0, pair)
+        q = stacked(pair_of(proj, 0, pair) * BF16(HEAD**-0.5))
         k = pair_of(proj, 1, pair)
         v = pair_of(proj, 2, pair)
-        o_h, dq_h, dk_h, dv_h = [], [], [], []
-        for mask in masks:
-            probs = softmax_rows(dot_nt(q * (mask * BF16(HEAD**-0.5)), k) + bias)
-            p16 = probs.astype(BF16)
-            if forward:
-                o_h.append(dot_nn(p16, v))
-            if grad is not None:
-                g = grad[:, pair * LANES : (pair + 1) * LANES]
-                dp = dot_nt(g * mask, v)
-                delta = jnp.sum(dp * probs, -1, keepdims=True)
-                ds16 = (probs * (dp - delta) * HEAD**-0.5).astype(BF16)
-                dq_h.append(dot_nn(ds16, k))
-                dk_h.append(dot_tn(ds16, q))
-                dv_h.append(dot_tn(p16, g))
-        if forward:
-            att.append(jnp.where(is_low, o_h[0], o_h[1]).astype(BF16))
+        probs = softmax_rows(dot_nt(q, k) + bias)
+        p16 = probs.astype(BF16)
+        if attended is None:
+            o = merged(dot_nn(p16, v)).astype(BF16)
+            att.append(o)
+        else:
+            o = pair_of(attended, 0, pair)
         if grad is not None:
-            dq.append(jnp.where(is_low, dq_h[0], dq_h[1]).astype(BF16))
-            dk.append(jnp.where(is_low, dk_h[0], dk_h[1]).astype(BF16))
-            dv.append(jnp.where(is_low, dv_h[0], dv_h[1]).astype(BF16))
-    attended = jnp.concatenate(att, -1) if forward else None
+            g = pair_of(grad, 0, pair)
+            g_both = stacked(g)
+            product = g.astype(F32) * o.astype(F32)
+            delta = jnp.concatenate(
+                [
+                    jnp.sum(product * low, -1, keepdims=True),
+                    jnp.sum(product * (1.0 - low), -1, keepdims=True),
+                ],
+                0,
+            )
+            ds16 = (probs * (dot_nt(g_both, v) - delta)).astype(BF16)
+            dq.append((merged(dot_nn(ds16, k)) * HEAD**-0.5).astype(BF16))
+            dk.append(dot_tn(ds16, q).astype(BF16))
+            dv.append(dot_tn(p16, g_both).astype(BF16))
+    if attended is None:
+        attended = jnp.concatenate(att, -1)
     dproj = jnp.concatenate(dq + dk + dv, -1) if grad is not None else None
     return attended, dproj
+
+
+def take_field(ref, scratch):
+    half = HLON * WLEV
+    for row in range(WLAT):
+        values = ref[row].astype(F32).reshape(2 * half, D)
+        for b in range(2):
+            first = (2 * (row // HLAT) + b) * QUART + row % HLAT * half
+            scratch[first : first + half, :] = values[b * half : (b + 1) * half]
+    return scratch[...]
+
+
+def put_field(values, scratch, ref):
+    scratch[...] = values
+    half = HLON * WLEV
+    for row in range(WLAT):
+        for b in range(2):
+            first = (2 * (row // HLAT) + b) * QUART + row % HLAT * half
+            ref[row, b * HLON : (b + 1) * HLON] = (
+                scratch[first : first + half, :].reshape(HLON, WLEV, D).astype(BF16)
+            )
+
+
+def take_labels(region):
+    places = WLAT * WLEV
+    table = region[...].reshape(places, WLON).astype(F32)
+    token = lax.broadcasted_iota(jnp.int32, (TOK, places), 0)
+    slot, rest = token // QUART, token % QUART
+    row = slot // 2 * HLAT + rest // (HLON * WLEV)
+    column = slot % 2 * HLON + rest % (HLON * WLEV) // WLEV
+    place = lax.broadcasted_iota(jnp.int32, (TOK, places), 1)
+    rows = dot_nn((place == row * WLEV + rest % WLEV).astype(F32), table)
+    return jnp.sum(jnp.where(place == column, rows, 0.0), -1, keepdims=True)
 
 
 def gather_rows(refs, scratch, column):
@@ -177,24 +216,34 @@
 
 
 def first_forward(
-    wrap, tok, cot, lab, gain, wqkv, wout,
-    x0, x1, x2, x3, proj_ref, left_n, left_a, scratch, lab_scratch,
+    wrap, region, tok, cot, gain_hbm, wqkv_hbm, wout_hbm,
+    x0, x1, x2, x3, keep_ref, scratch, lab_scratch, gain, wqkv, wout, sems,
 ):
-    values = tok[...].astype(F32)
-    normed, _, _ = norm_parts(values, gain[...])
-    proj = dot_nn(normed, wqkv[...]).astype(BF16)
-    proj_ref[...] = proj
-    labels = lab[...].astype(F32)
-    attended, _ = attention(proj, label_bias(labels))
+    copies = [
+        pltpu.make_async_copy(source, target, sems.at[i])
+        for i, (source, target) in enumerate(((gain_hbm, gain), (wqkv_hbm, wqkv), (wout_hbm, wout)))
+    ]
+    for copy in copies:
+        copy.start()
     refs = (x0, x1, x2, x3)
-    scatter_rows(values + dot_nn(attended, wout[...]), scratch, refs, 0)
-    scatter_rows(cot[...].astype(F32), scratch, refs, D)
+    take_field(cot, scratch)
+    for slot, ref in enumerate(refs):
+        ref[:, D : 2 * D] = scratch[slot * QUART : (slot + 1) * QUART, :].astype(BF16)
+    labels = jnp.broadcast_to(take_labels(region), (TOK, LANES))
     near = lax.broadcasted_iota(jnp.int32, (TOK, LANES), 0) < 2 * QUART
     moved = labels + jnp.where(near, wrap[0].astype(F32), 0.0)
     scatter_rows(moved, lab_scratch, refs, 2 * D)
-    order = regroup(order_x)
-    left_n[...] = dot_nn(normed, order).astype(BF16)
-    left_a[...] = dot_nn(attended, order).astype(BF16)
+    values = take_field(tok, scratch)
+    copies[0].wait()
+    normed, _, _ = norm_parts(values, gain[...])
+    copies[1].wait()
+    proj = dot_nn(normed, wqkv[...]).astype(BF16)
+    keep_ref[:, : 3 * D] = proj
+    keep_ref[:, 4 * D :] = labels.astype(BF16)
+    attended, _ = attention(proj, label_bias(labels))
+    keep_ref[:, 3 * D : 4 * D] = attended
+    copies[2].wait()
+    scatter_rows(values + dot_nn(attended, wout[...]), scratch, refs, 0)
 
 
 def second_main(
@@ -219,33 +268,40 @@
     scatter_rows(norm_back(dnormed, gain[...], xhat, rstd, g), scratch, back, D)
 
 
-def second_pack(me, normed, attended, right, p0, p1, p2, p3, left_n, left_a):
+def second_pack(
+    me, normed, attended, right, tok, gain, keep,
+    p0, p1, p2, p3, first_n, first_a, left_n, left_a, scratch,
+):
     order = regroup(order_y)
     left_n[...] = dot_nn(normed[...], order).astype(BF16)
     left_a[...] = dot_nn(attended[...], order).astype(BF16)
     pack(me[0], (left_n, left_a), right, (p0, p1, p2, p3))
+    order = regroup(order_x)
+    normed, _, _ = norm_parts(take_field(tok, scratch), gain[...])
+    first_n[...] = dot_nn(normed, order).astype(BF16)
+    first_a[...] = dot_nn(keep[:, 3 * D : 4 * D], order).astype(BF16)
 
 
 def first_backward(
-    me, b0, b1, b2, b3, lab, wout, proj_ref, left_n, left_a,
-    right_ref, p0, p1, p2, p3, scratch,
+    me, b0, b1, b2, b3, wout, keep, left_n, left_a, right_ref, p0, p1, p2, p3, scratch
 ):
     g16 = gather_rows((b0, b1, b2, b3), scratch, D).astype(BF16)
     datt = dot_nt(g16, wout[...]).astype(BF16)
-    _, dproj = attention(
-        proj_ref[...], label_bias(lab[...].astype(F32)), grad=datt, forward=False
-    )
+    bias = label_bias(keep[:, 4 * D :].astype(F32))
+    _, dproj = attention(keep[...], bias, grad=datt, attended=keep[:, 3 * D : 4 * D])
     store_right(dproj, g16, right_ref)
     pack(me[0], (left_n, left_a), right_ref, (p0, p1, p2, p3))
 
 
-def first_rest(b0, b1, b2, b3, tok, gain, wqkv, right, tg_ref, scratch):
-    g = gather_rows((b0, b1, b2, b3), scratch, D)
-    _, xhat, rstd = norm_parts(tok[...].astype(F32), gain[...])
+def first_rest(b0, b1, b2, b3, tok, gain, wqkv, right, tg_ref, result_ref, scratch):
+    back = (b0, b1, b2, b3)
+    put_field(gather_rows(back, scratch, 0), scratch, result_ref)
+    _, xhat, rstd = norm_parts(take_field(tok, scratch), gain[...])
+    g = gather_rows(back, scratch, D)
     dnormed = dot_nt(right[0], wqkv[:, :D])
     dnormed += dot_nt(right[1], wqkv[:, D : 2 * D])
     dnormed += dot_nt(right[2], wqkv[:, 2 * D :])
-    tg_ref[...] = norm_back(dnormed, gain[...], xhat, rstd, g).astype(BF16)
+    put_field(norm_back(dnormed, gain[...], xhat, rstd, g), scratch, tg_ref)
 
 
 def weights(me, p0, p1, p2, p3, q0, q1, q2, q3, scratch):
@@ -270,25 +326,36 @@
 PIECE = OWN * WIDE // LANES
 
 
-def to_owners(parts, send_ref):
+def to_owners(parts, send_ref, scratch):
     total = jnp.sum(parts[...].astype(F32), 0)
-    squares = jnp.sum(total * total, keepdims=True)
+    rest = jnp.sum(total * total, keepdims=True)
+    terms = []
+    for _ in range(3):
+        term = rest.astype(BF16).astype(F32)
+        terms.append(term)
+        rest = rest - term
+    terms = jnp.concatenate([jnp.broadcast_to(term, (1, LANES)) for term in terms], 0)
     for x in range(X):
         for y in range(Y):
             for slot, row in ((0, x * OWN), (1, LAST_ROWS + y * OWN)):
                 for c in range(WIDE // LANES):
                     first = slot * PIECE + c * OWN
-                    send_ref[x * Y + y, first : first + OWN, :] = total[
+                    scratch[x * Y + y, first : first + OWN, :] = total[
                         row : row + OWN, c * LANES : (c + 1) * LANES
                     ]
-            send_ref[x * Y + y, 2 * PIECE :, :] = jnp.broadcast_to(squares, (8, LANES))
+            scratch[x * Y + y, 2 * PIECE :, :] = jnp.zeros((16, LANES), F32)
+            scratch[x * Y + y, 2 * PIECE : 2 * PIECE + 3, :] = terms
+    send_ref[...] = scratch[...].astype(BF16)
 
 
 def spread(got, tile_ref):
-    tile_ref[...] = jnp.broadcast_to(jnp.sum(got[:, 2 * PIECE :, :], 0)[None], tile_ref.shape)
-
-
-def clipped(where, got, tiles, qkv_a, out_a, qkv_b, out_b):
+    terms = jnp.sum(got[:, 2 * PIECE :, :].astype(F32), 0)
+    squares = jnp.sum(terms, 0, keepdims=True)
+    tile_ref[...] = jnp.broadcast_to(squares[None], tile_ref.shape)
+
+
+def clipped(where, got, tiles, qkv_a, out_a, qkv_b, out_b, scratch):
+    scratch[...] = got[:, : 2 * PIECE, :].astype(F32)
     total = jnp.sum(tiles[...], 0)[:1, :1]
     factor = jnp.minimum(1.0, math.sqrt(8.0) * D / jnp.sqrt(total))
     x, y = where[0], where[1]
@@ -301,7 +368,7 @@
             for c in range(WIDE // LANES):
                 first = slot * PIECE + c * OWN
                 ref[:, column + c * LANES : column + (c + 1) * LANES] = (
-                    got[source, first : first + OWN, :] * factor
+                    scratch[source, first : first + OWN, :] * factor
                 )
 
 
@@ -309,34 +376,21 @@
     return jax.ShapeDtypeStruct(dims, dtype)
 
 
-def call(kernel, outs, scratch, *args, scalar=False, dtype=F32):
+def call(kernel, outs, scratch, *args, scalar=False, far=0):
     whole = pl.BlockSpec(memory_space=pltpu.VMEM)
-    specs = [whole] * len(args)
+    specs = [whole] * (len(args) - far) + [pl.BlockSpec(memory_space=pl.ANY)] * far
     if scalar:
         specs[0] = pl.BlockSpec(memory_space=pltpu.SMEM)
+    scratch = [pltpu.VMEM(s, F32) if isinstance(s, tuple) else s for s in scratch]
     return pl.pallas_call(
         kernel,
         out_shape=outs,
         in_specs=specs,
         out_specs=[whole] * len(outs),
-        scratch_shapes=[pltpu.VMEM(s, dtype) for s in scratch],
+        scratch_shapes=scratch,
         compiler_params=pltpu.CompilerParams(vmem_limit_bytes=VMEM_BYTES),
         name=kernel.__name__,
     )(*args)
-
-
-def quarters(field):
-    trailing = field.shape[3:]
-    shaped = field.reshape((WLEV, 2, HLAT, 2, HLON) + trailing)
-    order = (1, 3, 0, 2, 4) + tuple(range(5, 5 + len(trailing)))
-    return shaped.transpose(order).reshape((4, QUART) + trailing)
-
-
-def unquarters(field):
-    trailing = field.shape[2:]
-    shaped = field.reshape((2, 2, WLEV, HLAT, HLON) + trailing)
-    order = (2, 0, 3, 1, 4) + tuple(range(5, 5 + len(trailing)))
-    return shaped.transpose(order).reshape((WLEV, WLAT, WLON) + trailing)
 
 
 def moves(lat_count, lon_count):
@@ -411,19 +465,26 @@
     wrap = jnp.where(lat == 0, 4, 0).astype(jnp.int32).reshape(1)
     gain_a = unshifted_norm_gain.reshape(1, D)
     gain_b = shifted_norm_gain.reshape(1, D)
-    tok = quarters(tokens).reshape(TOK, D)
-    cot = quarters(cotangent).reshape(TOK, D)
-    lab = jnp.broadcast_to(quarters(region).reshape(TOK, 1), (TOK, LANES)).astype(BF16)
+    tok = tokens.transpose(1, 2, 0, 3)
+    cot = cotangent.transpose(1, 2, 0, 3)
+    lab = region.transpose(1, 0, 2)
 
     field = shape_of(TOK, D)
     fields = shape_of(GROUP, TOK, D)
     packs = [shape_of(TOK, D + WIDE)] * GROUP
-    *x, proj_a, left_n, left_a = call(
+    *x, keep = call(
         first_forward,
-        [shape_of(QUART, SEND)] * 4 + [shape_of(TOK, 3 * D), field, field],
-        [(TOK, D), (TOK, LANES)],
-        wrap, tok, cot, lab, gain_a, unshifted_query_key_value, out_first,
-        scalar=True,
+        [shape_of(QUART, SEND)] * 4 + [shape_of(TOK, 4 * D + LANES)],
+        [
+            (TOK, D),
+            (TOK, LANES),
+            (1, D),
+            pltpu.VMEM((D, 3 * D), BF16),
+            pltpu.VMEM((D, D), BF16),
+            pltpu.SemaphoreType.DMA((3,)),
+        ],
+        wrap, lab, tok, cot, gain_a, unshifted_query_key_value, out_first,
+        scalar=True, far=3,
     )
     x = send(x, tables)
     *back, normed_b, att_b, right_b = call(
@@ -433,45 +494,49 @@
         *x, gain_b, shifted_query_key_value, out_second,
     )
     back = send(back, tables, back=True)
-    pack_b = call(
+    *pack_b, left_n, left_a = call(
         second_pack,
-        packs,
-        [(TOK, D), (TOK, D)],
-        me_y, normed_b, att_b, right_b,
-        scalar=True, dtype=BF16,
+        packs + [field, field],
+        [pltpu.VMEM((TOK, D), BF16), pltpu.VMEM((TOK, D), BF16), (TOK, D)],
+        me_y, normed_b, att_b, right_b, tok, gain_a, keep,
+        scalar=True,
     )
     pack_b = swap(after(pack_b, back[:3]), "y")
     right_a, *pack_a = call(
         first_backward,
         [fields] + packs,
         [(TOK, D)],
-        me_x, *back, lab, out_first, proj_a, left_n, left_a,
+        me_x, *back, out_first, keep, left_n, left_a,
         scalar=True,
     )
     pack_a = swap(pack_a, "x")
-    (token_gradient,) = call(
+    grid = shape_of(WLAT, WLON, WLEV, D)
+    token_gradient, result = call(
         first_rest,
-        [field],
+        [grid, grid],
         [(TOK, D)],
         *back, tok, gain_a, unshifted_query_key_value, right_a,
     )
-    token_gradient = unquarters(token_gradient.reshape(4, QUART, D))
-    result = unquarters(jnp.stack(back)[..., :D])
+    token_gradient = token_gradient.transpose(2, 0, 1, 3)
+    result = result.transpose(2, 0, 1, 3)
 
     rows = [shape_of(PLANE_ROWS, WIDE)] * GROUP
     sum_b = swap(call(weights, rows, [(D, WIDE)], me_x, *pack_b, scalar=True), "x")
     sum_a = swap(call(weights, rows, [(D, WIDE)], me_y, *pack_a, scalar=True), "y")
     (sums,) = call(add_rows, [shape_of(Z, 2 * LAST_ROWS, WIDE)], [], *sum_a, *sum_b)
     sums = exchange(sums, COLUMN)
-    (pieces,) = call(
-        to_owners, [shape_of(X * Y, 2 * PIECE + 8, LANES, dtype=F32)], [], sums
-    )
+    piece = (X * Y, 2 * PIECE + 16, LANES)
+    (pieces,) = call(to_owners, [shape_of(*piece)], [piece], sums)
     pieces = exchange(pieces, PLANE)
     (tiles,) = call(spread, [shape_of(Z, 8, LANES, dtype=F32)], [], pieces)
     tiles = exchange(tiles, COLUMN)
     out_qkv, out_out = shape_of(OWN, 3 * D, dtype=F32), shape_of(OWN, D, dtype=F32)
     clips = call(
-        clipped, [out_qkv, out_out] * 2, [], jnp.stack([at_x, at_y]), pieces, tiles, scalar=True
+        clipped,
+        [out_qkv, out_out] * 2,
+        [(X * Y, 2 * PIECE, LANES)],
+        jnp.concatenate([me_x, me_y]), pieces, tiles,
+        scalar=True,
     )
     return (result, token_gradient, *clips)
 

time: 118 us -> 115 us (0.975)
  blocking collectives: 13 us -> 25.1 us
  waiting for transfers between devices: 36.4 us -> 27.8 us
  starting transfers between devices: 38.8 us -> 34.6 us
  Pallas kernels: 19.3 us -> 17.1 us
    all_to_all x1 -> x2, blocking collectives: 13 us -> 25.1 us  [exchange(): return lax.all_to_all(parts, ('lat', 'lon'), 0, 0, axis_index_groups=groups)]
    all_to_all x2 -> x1, waiting for transfers between devices: 14.1 us -> 6.26 us  [exchange(): return lax.all_to_all(parts, ('lat', 'lon'), 0, 0, axis_index_groups=groups)]
    unnamed x20 -> x34, local copies, waits for them, and re-layouts: 3.68 us -> 8.81 us
    all_to_all x2 -> x1, starting transfers between devices: 7.6 us -> 3.34 us  [exchange(): return lax.all_to_all(parts, ('lat', 'lon'), 0, 0, axis_index_groups=groups)]
    pallas_call x11, Pallas kernels: 19.3 us -> 17.1 us  [call(): pl.pallas_call(kernel, out_shape=outs, in_specs=specs, out_specs=[whole]...]
    reshape x3 -> x0, local copies, waits for them, and re-layouts: 2.04 us -> none  [the longest x2 1.98 us: quarters(): shaped = field.reshape((WLEV, 2, HLAT, 2, HLON) + trailing)]
    ppermute x6, waiting for transfers between devices: 9.62 us -> 7.88 us  [send(): out.append(lax.ppermute(part, ('lat', 'lon'), pairs))]
    transpose x2 -> x0, local copies, waits for them, and re-layouts: 1.55 us -> none  [unquarters(): return shaped.transpose(order).reshape((WLEV, WLAT, WLON) + trailing)]
  transfers between devices with their start and end apart: 20 -> 19, of which waited for: 9 -> 9; matrix products, arithmetic and copies ran while one was open for 2% -> 0% of each run, Pallas kernels for 8% -> 7%
where the time goes in v2:
time: 115 us; the launch traced here: 114 us
  starting transfers between devices  34.6 us (30%)
  waiting for transfers between devices  27.8 us (24%)
  blocking collectives  25.1 us (22%)
  Pallas kernels  17.1 us (15%)
  local copies, waits for them, and re-layouts  8.81 us (8%)
    all_to_all x2, blocking collectives, exchange(): return lax.all_to_all(parts, ('lat', 'lon'), 0, 0, axis_index_groups=groups)  25.1 us
    ppermute x12, starting transfers between devices, swap(): out.append(lax.ppermute(packs[step], ('lat', 'lon'), pairs))  17.8 us
    pallas_call x11, Pallas kernels, call(): pl.pallas_call(kernel, out_shape=outs, in_specs=specs, out_specs=[whole]...  17.1 us
    ppermute x12, waiting for transfers between devices, swap(): out.append(lax.ppermute(packs[step], ('lat', 'lon'), pairs))  13.6 us
    ppermute x6, starting transfers between devices, send(): out.append(lax.ppermute(part, ('lat', 'lon'), pairs))  13.4 us
    unnamed x34, local copies, waits for them, and re-layouts  8.81 us
    ppermute x6, waiting for transfers between devices, send(): out.append(lax.ppermute(part, ('lat', 'lon'), pairs))  7.88 us
    all_to_all x1, waiting for transfers between devices, exchange(): return lax.all_to_all(parts, ('lat', 'lon'), 0, 0, axis_index_groups=groups)  6.26 us
  transfers between devices with their start and end apart: 19, of which 9 were waited for; matrix products, arithmetic and copies ran while one was open for 0% of the time, Pallas kernels for 7%

profile of v2, /device:TPU:0, one launch (start us, length us, event | category | flops | bytes accessed | tf_op | source)
XLA Modules:
  0.0 114.3 jit_solution(14255942681110368549)
XLA Ops:
  0.7 1.4 %copy-done = bf16[512,1536]{1,0:T(8,128)(2,1)S(1)} copy-done((bf16[512,1536]{1,0:T(8,128)(2,1)S(1)}, bf16[512,1536]{1,0:T(8,128)(2,1)}, u32[]{:S(2)}) %copy-start) | copy-done | bytes 1572888
  2.1 1.0 copy-done.2
  3.1 0.9 copy-done.5
  4.0 0.9 copy-done.12
  4.9 0.7 copy-done.13
  5.6 0.7 copy-done.15
  6.3 2.4 %first_forward.1 = (bf16[36,1152]{1,0:T(8,128)(2,1)S(1)}, bf16[36,1152]{1,0:T(8,128)(2,1)S(1)}, bf16[36,1152]{1,0:T(8,128)(2,1)S(1)}, bf16[36,1152]{1,0:T(8,128)(2,1)S(1)}, bf16[144,2176]{1,0:T(8,128)(2,1)S(1)}) custom-call(s32[1]{0:T(128)} %bitcast.wrap, s32[6,2,12]{2,1,0:T(2,128)S(1)} %bitcast.17, bf16[6,12,2,512]{3,2,1,0:T(2,128)(2,1)S(1)} %bitcast.10, ...), custom_call_target="tpu_custom_call" | custom-call | tf_op jit(solution)/shard_map/first_forward/pallas_call | solution.py:385
  8.7 8.8 %collective-permute-start = (bf16[36,1152]{1,0:T(8,128)(2,1)S(1)}, bf16[36,1152]{1,0:T(8,128)(2,1)S(1)}, u32[]{:S(2)}, u32[]{:S(2)}) collective-permute-start(bf16[36,1152]{1,0:T(8,128)(2,1)S(1)} %get-tuple-element.47), channel_id=1, source_target_pairs={{0,254},{2,224},{4,226},{6,228},{8,230},{10,232},{12,234},{14,236}... | collective-permute-start | bytes 248840 | tf_op jit(solution)/shard_map/ppermute | solution.py:417
  17.5 0.1 collective-permute-start.1
  17.7 2.5 %collective-permute-start.2 = (bf16[36,1152]{1,0:T(8,128)(2,1)S(1)}, bf16[36,1152]{1,0:T(8,128)(2,1)S(1)}, u32[]{:S(2)}, u32[]{:S(2)}) collective-permute-start(bf16[36,1152]{1,0:T(8,128)(2,1)S(1)} %get-tuple-element.49), channel_id=1, source_target_pairs={{0,30},{2,0},{4,2},{6,4},{8,6},{10,8},{12,10},{14,12},{16,14},{18,... | collective-permute-start | bytes 248840 | tf_op jit(solution)/shard_map/ppermute | solution.py:417
  20.2 1.9 %collective-permute-done.1.x1 = bf16[36,1152]{1,0:T(8,128)(2,1)S(1)} collective-permute-done((bf16[36,1152]{1,0:T(8,128)(2,1)S(1)}, bf16[36,1152]{1,0:T(8,128)(2,1)S(1)}, u32[]{:S(2)}, u32[]{:S(2)}) %collective-permute-start.1) | collective-permute-done | bytes 82976 | tf_op jit(solution)/shard_map/ppermute | solution.py:417
  22.1 0.2 collective-permute-done.2.x2
  22.4 4.8 %second_main.1 = (bf16[36,1024]{1,0:T(8,128)(2,1)S(1)}, bf16[36,1024]{1,0:T(8,128)(2,1)S(1)}, bf16[36,1024]{1,0:T(8,128)(2,1)S(1)}, bf16[36,1024]{1,0:T(8,128)(2...) custom-call(bf16[36,1152]{1,0:T(8,128)(2,1)S(1)} %collective-permute-done.x0, ...), custom_call_target="tpu_custom_call" | custom-call | tf_op jit(solution)/shard_map/second_main/pallas_call | solution.py:385
  27.2 0.9 collective-permute-start.3
  28.1 1.0 collective-permute-start.4
  29.1 1.8 %second_pack.1 = (bf16[144,1024]{1,0:T(8,128)(2,1)S(1)}, bf16[144,1024]{1,0:T(8,128)(2,1)}, bf16[144,1024]{1,0:T(8,128)(2,1)}, bf16[144,1024]{1,0:T(8,128)(2,1)}...) custom-call(s32[1]{0:T(128)} %bitcast.7.me, bf16[144,512]{1,0:T(8,128)(2,1)S(1)} %get-tuple-element.56.normed, ...), custom_call_target="tpu_custom_call" | custom-call | tf_op jit(solution)/shard_map/second_pack/pallas_call | solution.py:385
  31.0 0.7 copy-done.8
  31.6 0.7 copy-done.10
  32.3 5.7 %collective-permute-done.3.b0 = bf16[36,1024]{1,0:T(8,128)(2,1)S(1)} collective-permute-done((bf16[36,1024]{1,0:T(8,128)(2,1)S(1)}, bf16[36,1024]{1,0:T(8,128)(2,1)S(1)}, u32[]{:S(2)}, u32[]{:S(2)}) %collective-permute-start.3) | collective-permute-done | bytes 73760 | tf_op jit(solution)/shard_map/ppermute | solution.py:417
  38.0 1.5 %collective-permute-start.13 = (bf16[144,1024]{1,0:T(8,128)(2,1)}, bf16[144,1024]{1,0:T(8,128)(2,1)S(1)}, u32[]{:S(2)}, u32[]{:S(2)}) collective-permute-start(bf16[144,1024]{1,0:T(8,128)(2,1)} %get-tuple-element.78), channel_id=1, source_target_pairs={{0,16},{2,18},{4,20},{6,22},{8,24},{10,26},{12,28},{14,30},{32,48}... | collective-permute-start | bytes 884744 | tf_op jit(solution)/shard_map/ppermute | solution.py:437
  39.5 3.2 %collective-permute-start.14 = (bf16[144,1024]{1,0:T(8,128)(2,1)}, bf16[144,1024]{1,0:T(8,128)(2,1)S(1)}, u32[]{:S(2)}, u32[]{:S(2)}) collective-permute-start(bf16[144,1024]{1,0:T(8,128)(2,1)} %get-tuple-element.79), channel_id=1, source_target_pairs={{0,48},{2,50},{4,52},{6,54},{8,56},{10,58},{12,60},{14,62},{32,16}... | collective-permute-start | bytes 884744 | tf_op jit(solution)/shard_map/ppermute | solution.py:437
  42.7 0.9 copy-done.9
  43.6 0.9 copy-done.11
  44.6 2.7 %first_backward.1 = (bf16[4,144,512]{2,1,0:T(8,128)(2,1)S(1)}, bf16[144,1024]{1,0:T(8,128)(2,1)S(1)}, bf16[144,1024]{1,0:T(8,128)(2,1)S(1)}, bf16[144,1024]{1,0:T(8,128)(2,1)S(1)}, bf16[144,1024]{1,0:T(8,128)(2,1)S(1)}) custom-call(s32[1]{0:T(128)} %bitcast.6.me, bf16[36,1024]{1,0:T(8,128)(2,1)S(1)} %collective-permute-done.3.b0, ...), custom_call_target="tpu_custom_call" | custom-call | tf_op jit(solution)/shard_map/first_backward/pallas_call | solution.py:385
  47.3 0.1 collective-permute-start.6
  47.4 2.6 %collective-permute-start.7 = (bf16[144,1024]{1,0:T(8,128)(2,1)S(1)}, bf16[144,1024]{1,0:T(8,128)(2,1)S(1)}, u32[]{:S(2)}, u32[]{:S(2)}) collective-permute-start(bf16[144,1024]{1,0:T(8,128)(2,1)S(1)} %get-tuple-element.66), channel_id=1, source_target_pairs={{0,128},{2,130},{4,132},{6,134},{8,136},{10,138},{12,140},{14,142}... | collective-permute-start | bytes 884744 | tf_op jit(solution)/shard_map/ppermute | solution.py:437
  49.9 2.1 %collective-permute-start.8 = (bf16[144,1024]{1,0:T(8,128)(2,1)S(1)}, bf16[144,1024]{1,0:T(8,128)(2,1)S(1)}, u32[]{:S(2)}, u32[]{:S(2)}) collective-permute-start(bf16[144,1024]{1,0:T(8,128)(2,1)S(1)} %get-tuple-element.67), channel_id=1, source_target_pairs={{0,192},{2,194},{4,196},{6,198},{8,200},{10,202},{12,204},{14,206}... | collective-permute-start | bytes 884744 | tf_op jit(solution)/shard_map/ppermute | solution.py:437
  52.1 0.7 collective-permute-done.14.p3
  52.8 0.8 weights.3
  53.6 0.2 collective-permute-start.15
  53.8 4.2 %collective-permute-start.16 = (bf16[128,512]{1,0:T(8,128)(2,1)S(1)}, bf16[128,512]{1,0:T(8,128)(2,1)S(1)}, u32[]{:S(2)}, u32[]{:S(2)}) collective-permute-start(bf16[128,512]{1,0:T(8,128)(2,1)S(1)} %get-tuple-element.82), channel_id=1, source_target_pairs={{0,128},{2,130},{4,132},{6,134},{8,136},{10,138},{12,140},{14,142}... | collective-permute-start | bytes 393224 | tf_op jit(solution)/shard_map/ppermute | solution.py:437
  58.0 0.4 collective-permute-start.17
  58.4 4.8 %collective-permute-done.7.p2 = bf16[144,1024]{1,0:T(8,128)(2,1)S(1)} collective-permute-done((bf16[144,1024]{1,0:T(8,128)(2,1)S(1)}, bf16[144,1024]{1,0:T(8,128)(2,1)S(1)}, u32[]{:S(2)}, u32[]{:S(2)}) %collective-permute-start.7) | collective-permute-done | bytes 294944 | tf_op jit(solution)/shard_map/ppermute | solution.py:437
  63.2 3.9 %collective-permute-done.8.p3 = bf16[144,1024]{1,0:T(8,128)(2,1)S(1)} collective-permute-done((bf16[144,1024]{1,0:T(8,128)(2,1)S(1)}, bf16[144,1024]{1,0:T(8,128)(2,1)S(1)}, u32[]{:S(2)}, u32[]{:S(2)}) %collective-permute-start.8) | collective-permute-done | bytes 294944 | tf_op jit(solution)/shard_map/ppermute | solution.py:437
  67.1 0.8 weights.2
  68.0 2.2 %collective-permute-start.11 = (bf16[128,512]{1,0:T(8,128)(2,1)S(1)}, bf16[128,512]{1,0:T(8,128)(2,1)S(1)}, u32[]{:S(2)}, u32[]{:S(2)}) collective-permute-start(bf16[128,512]{1,0:T(8,128)(2,1)S(1)} %get-tuple-element.71), channel_id=1, source_target_pairs={{0,48},{2,50},{4,52},{6,54},{8,56},{10,58},{12,60},{14,62},{32,16}... | collective-permute-start | bytes 393224 | tf_op jit(solution)/shard_map/ppermute | solution.py:437
  70.2 1.3 %collective-permute-start.9 = (bf16[128,512]{1,0:T(8,128)(2,1)S(1)}, bf16[128,512]{1,0:T(8,128)(2,1)S(1)}, u32[]{:S(2)}, u32[]{:S(2)}) collective-permute-start(bf16[128,512]{1,0:T(8,128)(2,1)S(1)} %get-tuple-element.69), channel_id=1, source_target_pairs={{0,32},{2,34},{4,36},{6,38},{8,40},{10,42},{12,44},{14,46},{32,0},... | collective-permute-start | bytes 393224 | tf_op jit(solution)/shard_map/ppermute | solution.py:437
  71.5 3.1 %collective-permute-done.10.a2 = bf16[128,512]{1,0:T(8,128)(2,1)S(1)} collective-permute-done((bf16[128,512]{1,0:T(8,128)(2,1)S(1)}, bf16[128,512]{1,0:T(8,128)(2,1)S(1)}, u32[]{:S(2)}, u32[]{:S(2)}) %collective-permute-start.10) | collective-permute-done | bytes 131104 | tf_op jit(solution)/shard_map/ppermute | solution.py:437
  74.6 1.1 collective-permute-done.11.a3
  75.7 0.1 add_rows.1
  75.8 13.3 %all_to_all.15.parts = bf16[8,32,512]{2,1,0:T(8,128)(2,1)S(1)} all-to-all(bf16[8,32,512]{2,1,0:T(8,128)(2,1)S(1)} %add_rows.1), channel_id=1, replica_groups={{0,2,4,6,8,10,12,14},{32,34,36,38,40,42,44,46},{16,18,20,22,24,26,28,30..., dimensions={0} | all-to-all | bytes 524288 | tf_op jit(solution)/shard_map/all_to_all | solution.py:442
  89.2 0.2 to_owners.1
  89.3 11.8 %all_to_all.16.got = bf16[16,48,128]{2,1,0:T(8,128)(2,1)S(1)} all-to-all(bf16[16,48,128]{2,1,0:T(8,128)(2,1)S(1)} %to_owners.1), channel_id=1, replica_groups={{0,32,16,48,64,96,80,112,128,160,144,176,192,224,208,240},{2,34,18,50,6..., dimensions={0} | all-to-all | bytes 393216 | tf_op jit(solution)/shard_map/all_to_all | solution.py:442
  101.1 0.6 spread.1
  101.8 3.3 %all-to-all-start.2 = ((f32[8,8,128]{2,1,0:T(8,128)}), f32[8,8,128]{2,1,0:T(8,128)S(1)}, u32[]{:S(2)}, u32[]{:S(2)}) async-start(f32[8,8,128]{2,1,0:T(8,128)} %spread.1), calls=%async_computation.2 | async-start | bytes 65536 | tf_op jit(solution)/shard_map/all_to_all | solution.py:442
  105.2 1.6 %first_rest.1 = (bf16[6,12,2,512]{3,2,1,0:T(2,128)(2,1)}, bf16[6,12,2,512]{3,2,1,0:T(2,128)(2,1)}) custom-call(bf16[36,1024]{1,0:T(8,128)(2,1)S(1)} %collective-permute-done.3.b0, bf16[36,1024]{1,0:T(8,128)(2,1)S(1)} %collective-permute-done.4.b1, bf16[36,1024]{1,0:T(8,128)(2,1)S(1)} %collective-permute-done.5.b2, ...), custom_call_target="tpu_custom_call" | custom-call | tf_op jit(solution)/shard_map/first_rest/pallas_call | solution.py:385
  106.8 6.3 %all-to-all-done.2.tiles = f32[8,8,128]{2,1,0:T(8,128)S(1)} async-done(((f32[8,8,128]{2,1,0:T(8,128)}), f32[8,8,128]{2,1,0:T(8,128)S(1)}, u32[]{:S(2)}, u32[]{:S(2)}) %all-to-all-start.2) | async-done | bytes 32800 | tf_op jit(solution)/shard_map/all_to_all | solution.py:442
  113.1 1.2 %clipped.1 = (f32[4,1536]{1,0:T(4,128)}, f32[4,512]{1,0:T(4,128)}, f32[4,1536]{1,0:T(4,128)}, f32[4,512]{1,0:T(4,128)}) custom-call(s32[2]{0:T(128)S(1)} %pad_add_fusion.where, bf16[16,48,128]{2,1,0:T(8,128)(2,1)S(1)} %all_to_all.16.got, f32[8,8,128]{2,1,0:T(8,128)S(1)} %all-to-all-done.2.tiles), custom_call_target="tpu_custom_call" | custom-call | tf_op jit(solution)/shard_map/clipped/pallas_call | solution.py:385
  (38 shorter events, 0.3 us)
Async XLA Ops:
  0.6 21.7 %copy-start.16 = (f32[512]{0:T(512)S(1)}, f32[512]{0:T(512)}, u32[]{:S(2)}) copy-start(f32[512]{0:T(512)} %param.15) | copy-start | bytes 6148
  0.7 1.4 %copy-start = (bf16[512,1536]{1,0:T(8,128)(2,1)S(1)}, bf16[512,1536]{1,0:T(8,128)(2,1)}, u32[]{:S(2)}) copy-start(bf16[512,1536]{1,0:T(8,128)(2,1)} %wqkv.3) | copy-start | bytes 4718596
  2.1 1.0 copy-start.2
  3.1 0.9 copy-start.5
  4.0 0.9 copy-start.12
  4.9 0.7 copy-start.13
  5.6 0.7 copy-start.15
  6.3 16.0 %copy-start.4 = (bf16[512,1536]{1,0:T(8,128)(2,1)S(1)}, bf16[512,1536]{1,0:T(8,128)(2,1)}, u32[]{:S(2)}) copy-start(bf16[512,1536]{1,0:T(8,128)(2,1)} %wqkv.2) | copy-start | bytes 4718596
  6.3 16.0 %copy-start.7 = (bf16[512,512]{1,0:T(8,128)(2,1)S(1)}, bf16[512,512]{1,0:T(8,128)(2,1)}, u32[]{:S(2)}) copy-start(bf16[512,512]{1,0:T(8,128)(2,1)} %wout.2) | copy-start | bytes 1572868
  8.7 20.5 %copy-start.6 = (bf16[2,6,12,512]{3,0,2,1:T(2,128)(2,1)S(1)}, bf16[2,6,12,512]{3,0,2,1:T(2,128)(2,1)}, u32[]{:S(2)}) copy-start(bf16[2,6,12,512]{3,0,2,1:T(2,128)(2,1)} %param.9) | copy-start | bytes 442372
  8.7 20.5 %copy-start.14 = (f32[512]{0:T(512)S(1)}, f32[512]{0:T(512)}, u32[]{:S(2)}) copy-start(f32[512]{0:T(512)} %param.12) | copy-start | bytes 6148
  8.7 11.5 %collective-permute-start = (bf16[36,1152]{1,0:T(8,128)(2,1)S(1)}, bf16[36,1152]{1,0:T(8,128)(2,1)S(1)}, u32[]{:S(2)}, u32[]{:S(2)}) collective-permute-start(bf16[36,1152]{1,0:T(8,128)(2,1)S(1)} %get-tuple-element.47), channel_id=1, source_target_pairs={{0,254},{2,224},{4,226},{6,228},{8,230},{10,232},{12,234},{14,236}... | collective-permute-start | bytes 248840 | tf_op jit(solution)/shard_map/ppermute | solution.py:417
  17.5 4.6 %collective-permute-start.1 = (bf16[36,1152]{1,0:T(8,128)(2,1)S(1)}, bf16[36,1152]{1,0:T(8,128)(2,1)S(1)}, u32[]{:S(2)}, u32[]{:S(2)}) collective-permute-start(bf16[36,1152]{1,0:T(8,128)(2,1)S(1)} %get-tuple-element.48), channel_id=1, source_target_pairs={{0,224},{2,226},{4,228},{6,230},{8,232},{10,234},{12,236},{14,238}... | collective-permute-start | bytes 248840 | tf_op jit(solution)/shard_map/ppermute | solution.py:417
  17.7 4.7 %collective-permute-start.2 = (bf16[36,1152]{1,0:T(8,128)(2,1)S(1)}, bf16[36,1152]{1,0:T(8,128)(2,1)S(1)}, u32[]{:S(2)}, u32[]{:S(2)}) collective-permute-start(bf16[36,1152]{1,0:T(8,128)(2,1)S(1)} %get-tuple-element.49), channel_id=1, source_target_pairs={{0,30},{2,0},{4,2},{6,4},{8,6},{10,8},{12,10},{14,12},{16,14},{18,... | collective-permute-start | bytes 248840 | tf_op jit(solution)/shard_map/ppermute | solution.py:417
  22.3 20.4 %copy-start.3 = (bf16[512,512]{1,0:T(8,128)(2,1)S(1)}, bf16[512,512]{1,0:T(8,128)(2,1)}, u32[]{:S(2)}) copy-start(bf16[512,512]{1,0:T(8,128)(2,1)} %wout.3) | copy-start | bytes 1572868
  27.2 10.8 %collective-permute-start.3 = (bf16[36,1024]{1,0:T(8,128)(2,1)S(1)}, bf16[36,1024]{1,0:T(8,128)(2,1)S(1)}, u32[]{:S(2)}, u32[]{:S(2)}) collective-permute-start(bf16[36,1024]{1,0:T(8,128)(2,1)S(1)} %get-tuple-element.51), channel_id=1, source_target_pairs={{254,0},{224,2},{226,4},{228,6},{230,8},{232,10},{234,12},{236,14}... | collective-permute-start | bytes 221192 | tf_op jit(solution)/shard_map/ppermute | solution.py:417
  28.1 9.9 %collective-permute-start.4 = (bf16[36,1024]{1,0:T(8,128)(2,1)S(1)}, bf16[36,1024]{1,0:T(8,128)(2,1)S(1)}, u32[]{:S(2)}, u32[]{:S(2)}) collective-permute-start(bf16[36,1024]{1,0:T(8,128)(2,1)S(1)} %get-tuple-element.52), channel_id=1, source_target_pairs={{224,0},{226,2},{228,4},{230,6},{232,8},{234,10},{236,12},{238,14}... | collective-permute-start | bytes 221192 | tf_op jit(solution)/shard_map/ppermute | solution.py:417
  29.1 8.9 %collective-permute-start.5 = (bf16[36,1024]{1,0:T(8,128)(2,1)S(1)}, bf16[36,1024]{1,0:T(8,128)(2,1)S(1)}, u32[]{:S(2)}, u32[]{:S(2)}) collective-permute-start(bf16[36,1024]{1,0:T(8,128)(2,1)S(1)} %get-tuple-element.53), channel_id=1, source_target_pairs={{30,0},{0,2},{2,4},{4,6},{6,8},{8,10},{10,12},{12,14},{14,16},{16,... | collective-permute-start | bytes 221192 | tf_op jit(solution)/shard_map/ppermute | solution.py:417
  31.0 0.7 copy-start.8
  31.6 0.7 copy-start.10
  38.0 11.9 %collective-permute-start.12 = (bf16[144,1024]{1,0:T(8,128)(2,1)}, bf16[144,1024]{1,0:T(8,128)(2,1)S(1)}, u32[]{:S(2)}, u32[]{:S(2)}) collective-permute-start(bf16[144,1024]{1,0:T(8,128)(2,1)} %get-tuple-element.77), channel_id=1, source_target_pairs={{0,32},{2,34},{4,36},{6,38},{8,40},{10,42},{12,44},{14,46},{32,0},... | collective-permute-start | bytes 884744 | tf_op jit(solution)/shard_map/ppermute | solution.py:437
  38.0 14.0 %collective-permute-start.13 = (bf16[144,1024]{1,0:T(8,128)(2,1)}, bf16[144,1024]{1,0:T(8,128)(2,1)S(1)}, u32[]{:S(2)}, u32[]{:S(2)}) collective-permute-start(bf16[144,1024]{1,0:T(8,128)(2,1)} %get-tuple-element.78), channel_id=1, source_target_pairs={{0,16},{2,18},{4,20},{6,22},{8,24},{10,26},{12,28},{14,30},{32,48}... | collective-permute-start | bytes 884744 | tf_op jit(solution)/shard_map/ppermute | solution.py:437
  39.5 13.2 %collective-permute-start.14 = (bf16[144,1024]{1,0:T(8,128)(2,1)}, bf16[144,1024]{1,0:T(8,128)(2,1)S(1)}, u32[]{:S(2)}, u32[]{:S(2)}) collective-permute-start(bf16[144,1024]{1,0:T(8,128)(2,1)} %get-tuple-element.79), channel_id=1, source_target_pairs={{0,48},{2,50},{4,52},{6,54},{8,56},{10,58},{12,60},{14,62},{32,16}... | collective-permute-start | bytes 884744 | tf_op jit(solution)/shard_map/ppermute | solution.py:437
  42.7 0.9 copy-start.9
  43.6 0.9 copy-start.11
  47.3 10.7 %collective-permute-start.6 = (bf16[144,1024]{1,0:T(8,128)(2,1)S(1)}, bf16[144,1024]{1,0:T(8,128)(2,1)S(1)}, u32[]{:S(2)}, u32[]{:S(2)}) collective-permute-start(bf16[144,1024]{1,0:T(8,128)(2,1)S(1)} %get-tuple-element.65), channel_id=1, source_target_pairs={{0,64},{2,66},{4,68},{6,70},{8,72},{10,74},{12,76},{14,78},{32,96}... | collective-permute-start | bytes 884744 | tf_op jit(solution)/shard_map/ppermute | solution.py:437
  47.4 15.8 %collective-permute-start.7 = (bf16[144,1024]{1,0:T(8,128)(2,1)S(1)}, bf16[144,1024]{1,0:T(8,128)(2,1)S(1)}, u32[]{:S(2)}, u32[]{:S(2)}) collective-permute-start(bf16[144,1024]{1,0:T(8,128)(2,1)S(1)} %get-tuple-element.66), channel_id=1, source_target_pairs={{0,128},{2,130},{4,132},{6,134},{8,136},{10,138},{12,140},{14,142}... | collective-permute-start | bytes 884744 | tf_op jit(solution)/shard_map/ppermute | solution.py:437
  49.9 17.2 %collective-permute-start.8 = (bf16[144,1024]{1,0:T(8,128)(2,1)S(1)}, bf16[144,1024]{1,0:T(8,128)(2,1)S(1)}, u32[]{:S(2)}, u32[]{:S(2)}) collective-permute-start(bf16[144,1024]{1,0:T(8,128)(2,1)S(1)} %get-tuple-element.67), channel_id=1, source_target_pairs={{0,192},{2,194},{4,196},{6,198},{8,200},{10,202},{12,204},{14,206}... | collective-permute-start | bytes 884744 | tf_op jit(solution)/shard_map/ppermute | solution.py:437
  53.6 16.6 %collective-permute-start.15 = (bf16[128,512]{1,0:T(8,128)(2,1)S(1)}, bf16[128,512]{1,0:T(8,128)(2,1)S(1)}, u32[]{:S(2)}, u32[]{:S(2)}) collective-permute-start(bf16[128,512]{1,0:T(8,128)(2,1)S(1)} %get-tuple-element.81), channel_id=1, source_target_pairs={{0,64},{2,66},{4,68},{6,70},{8,72},{10,74},{12,76},{14,78},{32,96}... | collective-permute-start | bytes 393224 | tf_op jit(solution)/shard_map/ppermute | solution.py:437
  53.8 17.7 %collective-permute-start.16 = (bf16[128,512]{1,0:T(8,128)(2,1)S(1)}, bf16[128,512]{1,0:T(8,128)(2,1)S(1)}, u32[]{:S(2)}, u32[]{:S(2)}) collective-permute-start(bf16[128,512]{1,0:T(8,128)(2,1)S(1)} %get-tuple-element.82), channel_id=1, source_target_pairs={{0,128},{2,130},{4,132},{6,134},{8,136},{10,138},{12,140},{14,142}... | collective-permute-start | bytes 393224 | tf_op jit(solution)/shard_map/ppermute | solution.py:437
  58.0 13.5 %collective-permute-start.17 = (bf16[128,512]{1,0:T(8,128)(2,1)S(1)}, bf16[128,512]{1,0:T(8,128)(2,1)S(1)}, u32[]{:S(2)}, u32[]{:S(2)}) collective-permute-start(bf16[128,512]{1,0:T(8,128)(2,1)S(1)} %get-tuple-element.83), channel_id=1, source_target_pairs={{0,192},{2,194},{4,196},{6,198},{8,200},{10,202},{12,204},{14,206}... | collective-permute-start | bytes 393224 | tf_op jit(solution)/shard_map/ppermute | solution.py:437
  67.9 37.3 %copy-start.1 = (bf16[512,1536]{1,0:T(8,128)(2,1)S(1)}, bf16[512,1536]{1,0:T(8,128)(2,1)}, u32[]{:S(2)}) copy-start(bf16[512,1536]{1,0:T(8,128)(2,1)} %wqkv.3) | copy-start | bytes 4718596
  67.9 6.7 %collective-permute-start.10 = (bf16[128,512]{1,0:T(8,128)(2,1)S(1)}, bf16[128,512]{1,0:T(8,128)(2,1)S(1)}, u32[]{:S(2)}, u32[]{:S(2)}) collective-permute-start(bf16[128,512]{1,0:T(8,128)(2,1)S(1)} %get-tuple-element.70), channel_id=1, source_target_pairs={{0,16},{2,18},{4,20},{6,22},{8,24},{10,26},{12,28},{14,30},{32,48}... | collective-permute-start | bytes 393224 | tf_op jit(solution)/shard_map/ppermute | solution.py:437
  68.0 7.7 %collective-permute-start.11 = (bf16[128,512]{1,0:T(8,128)(2,1)S(1)}, bf16[128,512]{1,0:T(8,128)(2,1)S(1)}, u32[]{:S(2)}, u32[]{:S(2)}) collective-permute-start(bf16[128,512]{1,0:T(8,128)(2,1)S(1)} %get-tuple-element.71), channel_id=1, source_target_pairs={{0,48},{2,50},{4,52},{6,54},{8,56},{10,58},{12,60},{14,62},{32,16}... | collective-permute-start | bytes 393224 | tf_op jit(solution)/shard_map/ppermute | solution.py:437
  70.2 5.5 %collective-permute-start.9 = (bf16[128,512]{1,0:T(8,128)(2,1)S(1)}, bf16[128,512]{1,0:T(8,128)(2,1)S(1)}, u32[]{:S(2)}, u32[]{:S(2)}) collective-permute-start(bf16[128,512]{1,0:T(8,128)(2,1)S(1)} %get-tuple-element.69), channel_id=1, source_target_pairs={{0,32},{2,34},{4,36},{6,38},{8,40},{10,42},{12,44},{14,46},{32,0},... | collective-permute-start | bytes 393224 | tf_op jit(solution)/shard_map/ppermute | solution.py:437
  101.8 11.3 %all-to-all-start.2 = ((f32[8,8,128]{2,1,0:T(8,128)}), f32[8,8,128]{2,1,0:T(8,128)S(1)}, u32[]{:S(2)}, u32[]{:S(2)}) async-start(f32[8,8,128]{2,1,0:T(8,128)} %spread.1), calls=%async_computation.2 | async-start | bytes 65536 | tf_op jit(solution)/shard_map/all_to_all | solution.py:442

commit v3 on v2

--- a/solution.py
+++ b/solution.py
@@ -35,6 +35,7 @@
 F32 = jnp.float32
 BF16 = jnp.bfloat16
 VMEM_BYTES = 16 * 1024 * 1024
+WHOLE_VMEM_BYTES = 62 * 1024 * 1024
 
 
 def dot_nn(a, b):
@@ -239,7 +240,8 @@
     copies[1].wait()
     proj = dot_nn(normed, wqkv[...]).astype(BF16)
     keep_ref[:, : 3 * D] = proj
-    keep_ref[:, 4 * D :] = labels.astype(BF16)
+    keep_ref[:, 4 * D : 5 * D] = normed
+    keep_ref[:, 5 * D :] = labels.astype(BF16)
     attended, _ = attention(proj, label_bias(labels))
     keep_ref[:, 3 * D : 4 * D] = attended
     copies[2].wait()
@@ -268,28 +270,24 @@
     scatter_rows(norm_back(dnormed, gain[...], xhat, rstd, g), scratch, back, D)
 
 
-def second_pack(
-    me, normed, attended, right, tok, gain, keep,
-    p0, p1, p2, p3, first_n, first_a, left_n, left_a, scratch,
-):
+def second_pack(me, normed, attended, right, p0, p1, p2, p3, left_n, left_a):
     order = regroup(order_y)
     left_n[...] = dot_nn(normed[...], order).astype(BF16)
     left_a[...] = dot_nn(attended[...], order).astype(BF16)
     pack(me[0], (left_n, left_a), right, (p0, p1, p2, p3))
-    order = regroup(order_x)
-    normed, _, _ = norm_parts(take_field(tok, scratch), gain[...])
-    first_n[...] = dot_nn(normed, order).astype(BF16)
-    first_a[...] = dot_nn(keep[:, 3 * D : 4 * D], order).astype(BF16)
 
 
 def first_backward(
-    me, b0, b1, b2, b3, wout, keep, left_n, left_a, right_ref, p0, p1, p2, p3, scratch
+    me, b0, b1, b2, b3, wout, keep, right_ref, p0, p1, p2, p3, scratch, left_n, left_a
 ):
     g16 = gather_rows((b0, b1, b2, b3), scratch, D).astype(BF16)
     datt = dot_nt(g16, wout[...]).astype(BF16)
-    bias = label_bias(keep[:, 4 * D :].astype(F32))
+    bias = label_bias(keep[:, 5 * D :].astype(F32))
     _, dproj = attention(keep[...], bias, grad=datt, attended=keep[:, 3 * D : 4 * D])
     store_right(dproj, g16, right_ref)
+    order = regroup(order_x)
+    left_n[...] = dot_nn(keep[:, 4 * D : 5 * D], order).astype(BF16)
+    left_a[...] = dot_nn(keep[:, 3 * D : 4 * D], order).astype(BF16)
     pack(me[0], (left_n, left_a), right_ref, (p0, p1, p2, p3))
 
 
@@ -376,7 +374,7 @@
     return jax.ShapeDtypeStruct(dims, dtype)
 
 
-def call(kernel, outs, scratch, *args, scalar=False, far=0):
+def call(kernel, outs, scratch, *args, scalar=False, far=0, vmem=VMEM_BYTES):
     whole = pl.BlockSpec(memory_space=pltpu.VMEM)
     specs = [whole] * (len(args) - far) + [pl.BlockSpec(memory_space=pl.ANY)] * far
     if scalar:
@@ -388,7 +386,7 @@
         in_specs=specs,
         out_specs=[whole] * len(outs),
         scratch_shapes=scratch,
-        compiler_params=pltpu.CompilerParams(vmem_limit_bytes=VMEM_BYTES),
+        compiler_params=pltpu.CompilerParams(vmem_limit_bytes=vmem),
         name=kernel.__name__,
     )(*args)
 
@@ -474,7 +472,7 @@
     packs = [shape_of(TOK, D + WIDE)] * GROUP
     *x, keep = call(
         first_forward,
-        [shape_of(QUART, SEND)] * 4 + [shape_of(TOK, 4 * D + LANES)],
+        [shape_of(QUART, SEND)] * 4 + [shape_of(TOK, 5 * D + LANES)],
         [
             (TOK, D),
             (TOK, LANES),
@@ -484,7 +482,7 @@
             pltpu.SemaphoreType.DMA((3,)),
         ],
         wrap, lab, tok, cot, gain_a, unshifted_query_key_value, out_first,
-        scalar=True, far=3,
+        scalar=True, far=3, vmem=WHOLE_VMEM_BYTES,
     )
     x = send(x, tables)
     *back, normed_b, att_b, right_b = call(
@@ -494,19 +492,16 @@
         *x, gain_b, shifted_query_key_value, out_second,
     )
     back = send(back, tables, back=True)
-    *pack_b, left_n, left_a = call(
-        second_pack,
-        packs + [field, field],
-        [pltpu.VMEM((TOK, D), BF16), pltpu.VMEM((TOK, D), BF16), (TOK, D)],
-        me_y, normed_b, att_b, right_b, tok, gain_a, keep,
-        scalar=True,
+    half = pltpu.VMEM((TOK, D), BF16)
+    pack_b = call(
+        second_pack, packs, [half, half], me_y, normed_b, att_b, right_b, scalar=True
     )
     pack_b = swap(after(pack_b, back[:3]), "y")
     right_a, *pack_a = call(
         first_backward,
         [fields] + packs,
-        [(TOK, D)],
-        me_x, *back, out_first, keep, left_n, left_a,
+        [(TOK, D), half, half],
+        me_x, *back, out_first, keep,
         scalar=True,
     )
     pack_a = swap(pack_a, "x")

time: 115 us -> 114 us (level)
  local copies, waits for them, and re-layouts: 8.81 us -> 3.87 us
  Pallas kernels: 17.1 us -> 21.1 us
    unnamed x34 -> x22, local copies, waits for them, and re-layouts: 8.81 us -> 3.87 us
    pallas_call x11, Pallas kernels: 17.1 us -> 21.1 us  [call(): pl.pallas_call(kernel, out_shape=outs, in_specs=specs, out_specs=[whole]...]
  transfers between devices with their start and end apart: 19 -> 19, of which waited for: 9 -> 9; matrix products, arithmetic and copies ran while one was open for 0% -> 0% of each run, Pallas kernels for 7% -> 8%
where the time goes in v3:
time: 114 us; the launch traced here: 113 us
  starting transfers between devices  34.3 us (30%)
  waiting for transfers between devices  27.9 us (24%)
  blocking collectives  25 us (22%)
  Pallas kernels  21.1 us (19%)
  local copies, waits for them, and re-layouts  3.87 us (3%)
    all_to_all x2, blocking collectives, exchange(): return lax.all_to_all(parts, ('lat', 'lon'), 0, 0, axis_index_groups=groups)  25 us
    pallas_call x11, Pallas kernels, call(): pl.pallas_call(kernel, out_shape=outs, in_specs=specs, out_specs=[whole]...  21.1 us
    ppermute x12, starting transfers between devices, swap(): out.append(lax.ppermute(packs[step], ('lat', 'lon'), pairs))  17.8 us
    ppermute x6, starting transfers between devices, send(): out.append(lax.ppermute(part, ('lat', 'lon'), pairs))  13.2 us
    ppermute x12, waiting for transfers between devices, swap(): out.append(lax.ppermute(packs[step], ('lat', 'lon'), pairs))  12.7 us
    ppermute x6, waiting for transfers between devices, send(): out.append(lax.ppermute(part, ('lat', 'lon'), pairs))  8.91 us
    all_to_all x1, waiting for transfers between devices, exchange(): return lax.all_to_all(parts, ('lat', 'lon'), 0, 0, axis_index_groups=groups)  6.26 us
    unnamed x22, local copies, waits for them, and re-layouts  3.87 us
  transfers between devices with their start and end apart: 19, of which 9 were waited for; matrix products, arithmetic and copies ran while one was open for 0% of the time, Pallas kernels for 8%

profile of v3, /device:TPU:0, one launch (start us, length us, event | category | flops | bytes accessed | tf_op | source)
XLA Modules:
  0.0 113.1 jit_solution(15600728217466767252)
XLA Ops:
  0.7 5.0 %first_forward.1 = (bf16[36,1152]{1,0:T(8,128)(2,1)}, bf16[36,1152]{1,0:T(8,128)(2,1)}, bf16[36,1152]{1,0:T(8,128)(2,1)}, bf16[36,1152]{1,0:T(8,128)(2,1)}, bf16[144,2688]{1,0:T(8,128)(2,1)}) custom-call(s32[1]{0:T(128)} %bitcast.wrap, s32[6,2,12]{2,1,0:T(2,128)} %bitcast.16, bf16[6,12,2,512]{3,2,1,0:T(2,128)(2,1)} %bitcast.10, ...), custom_call_target="tpu_custom_call" | custom-call | tf_op jit(solution)/shard_map/first_forward/pallas_call | solution.py:383
  5.7 8.8 %collective-permute-start = (bf16[36,1152]{1,0:T(8,128)(2,1)}, bf16[36,1152]{1,0:T(8,128)(2,1)S(1)}, u32[]{:S(2)}, u32[]{:S(2)}) collective-permute-start(bf16[36,1152]{1,0:T(8,128)(2,1)} %get-tuple-element.45), channel_id=1, source_target_pairs={{0,254},{2,224},{4,226},{6,228},{8,230},{10,232},{12,234},{14,236}... | collective-permute-start | bytes 248840 | tf_op jit(solution)/shard_map/ppermute | solution.py:415
  14.5 0.1 collective-permute-start.1
  14.7 2.5 %collective-permute-start.2 = (bf16[36,1152]{1,0:T(8,128)(2,1)}, bf16[36,1152]{1,0:T(8,128)(2,1)S(1)}, u32[]{:S(2)}, u32[]{:S(2)}) collective-permute-start(bf16[36,1152]{1,0:T(8,128)(2,1)} %get-tuple-element.47), channel_id=1, source_target_pairs={{0,30},{2,0},{4,2},{6,4},{8,6},{10,8},{12,10},{14,12},{16,14},{18,... | collective-permute-start | bytes 248840 | tf_op jit(solution)/shard_map/ppermute | solution.py:415
  17.2 0.0 collective-permute-done.x0
  17.2 2.1 %collective-permute-done.1.x1 = bf16[36,1152]{1,0:T(8,128)(2,1)S(1)} collective-permute-done((bf16[36,1152]{1,0:T(8,128)(2,1)}, bf16[36,1152]{1,0:T(8,128)(2,1)S(1)}, u32[]{:S(2)}, u32[]{:S(2)}) %collective-permute-start.1) | collective-permute-done | bytes 82976 | tf_op jit(solution)/shard_map/ppermute | solution.py:415
  19.3 0.4 collective-permute-done.2.x2
  19.7 1.0 copy-done.7
  20.7 0.9 copy-done.8
  21.6 5.4 %second_main.1 = (bf16[36,1024]{1,0:T(8,128)(2,1)}, bf16[36,1024]{1,0:T(8,128)(2,1)S(1)}, bf16[36,1024]{1,0:T(8,128)(2,1)S(1)}, bf16[36,1024]{1,0:T(8,128)(2,1)S...) custom-call(bf16[36,1152]{1,0:T(8,128)(2,1)S(1)} %collective-permute-done.x0, ...), custom_call_target="tpu_custom_call" | custom-call | tf_op jit(solution)/shard_map/second_main/pallas_call | solution.py:383
  27.0 0.8 copy-done.4
  27.8 0.8 collective-permute-start.3
  28.7 0.8 collective-permute-start.4
  29.5 1.1 copy-done.5
  30.6 1.4 %second_pack.1 = (bf16[144,1024]{1,0:T(8,128)(2,1)S(1)}, bf16[144,1024]{1,0:T(8,128)(2,1)}, bf16[144,1024]{1,0:T(8,128)(2,1)}, bf16[144,1024]{1,0:T(8,128)(2,1)}) custom-call(s32[1]{0:T(128)} %bitcast.9.me, bf16[144,512]{1,0:T(8,128)(2,1)S(1)} %get-tuple-element.65.normed, bf16[144,512]{1,0:T(8,128)(2,1)S(1)} %get-tuple-element.66.attended, ...), custom_call_target="tpu_custom_call" | custom-call | tf_op jit(solution)/shard_map/second_pack/pallas_call | solution.py:383
  32.0 6.4 %collective-permute-done.3.b0 = bf16[36,1024]{1,0:T(8,128)(2,1)S(1)} collective-permute-done((bf16[36,1024]{1,0:T(8,128)(2,1)}, bf16[36,1024]{1,0:T(8,128)(2,1)S(1)}, u32[]{:S(2)}, u32[]{:S(2)}) %collective-permute-start.3) | collective-permute-done | bytes 73760 | tf_op jit(solution)/shard_map/ppermute | solution.py:415
  38.5 1.7 %collective-permute-start.13 = (bf16[144,1024]{1,0:T(8,128)(2,1)}, bf16[144,1024]{1,0:T(8,128)(2,1)S(1)}, u32[]{:S(2)}, u32[]{:S(2)}) collective-permute-start(bf16[144,1024]{1,0:T(8,128)(2,1)} %get-tuple-element.74), channel_id=1, source_target_pairs={{0,16},{2,18},{4,20},{6,22},{8,24},{10,26},{12,28},{14,30},{32,48}... | collective-permute-start | bytes 884744 | tf_op jit(solution)/shard_map/ppermute | solution.py:435
  40.2 2.9 %collective-permute-start.14 = (bf16[144,1024]{1,0:T(8,128)(2,1)}, bf16[144,1024]{1,0:T(8,128)(2,1)}, u32[]{:S(2)}, u32[]{:S(2)}) collective-permute-start(bf16[144,1024]{1,0:T(8,128)(2,1)} %get-tuple-element.75), channel_id=1, source_target_pairs={{0,48},{2,50},{4,52},{6,54},{8,56},{10,58},{12,60},{14,62},{32,16}... | collective-permute-start | bytes 884744 | tf_op jit(solution)/shard_map/ppermute | solution.py:435
  43.2 2.9 %first_backward.1 = (bf16[4,144,512]{2,1,0:T(8,128)(2,1)S(1)}, bf16[144,1024]{1,0:T(8,128)(2,1)S(1)}, bf16[144,1024]{1,0:T(8,128)(2,1)S(1)}, bf16[144,1024]{1,0:T(8,128)(2,1)S(1)}, bf16[144,1024]{1,0:T(8,128)(2,1)S(1)}) custom-call(s32[1]{0:T(128)} %bitcast.6.me, bf16[36,1024]{1,0:T(8,128)(2,1)S(1)} %collective-permute-done.3.b0, ...), custom_call_target="tpu_custom_call" | custom-call | tf_op jit(solution)/shard_map/first_backward/pallas_call | solution.py:383
  46.1 0.1 collective-permute-start.6
  46.2 2.7 %collective-permute-start.7 = (bf16[144,1024]{1,0:T(8,128)(2,1)S(1)}, bf16[144,1024]{1,0:T(8,128)(2,1)S(1)}, u32[]{:S(2)}, u32[]{:S(2)}) collective-permute-start(bf16[144,1024]{1,0:T(8,128)(2,1)S(1)} %get-tuple-element.59), channel_id=1, source_target_pairs={{0,128},{2,130},{4,132},{6,134},{8,136},{10,138},{12,140},{14,142}... | collective-permute-start | bytes 884744 | tf_op jit(solution)/shard_map/ppermute | solution.py:435
  48.9 1.9 %collective-permute-start.8 = (bf16[144,1024]{1,0:T(8,128)(2,1)S(1)}, bf16[144,1024]{1,0:T(8,128)(2,1)S(1)}, u32[]{:S(2)}, u32[]{:S(2)}) collective-permute-start(bf16[144,1024]{1,0:T(8,128)(2,1)S(1)} %get-tuple-element.60), channel_id=1, source_target_pairs={{0,192},{2,194},{4,196},{6,198},{8,200},{10,202},{12,204},{14,206}... | collective-permute-start | bytes 884744 | tf_op jit(solution)/shard_map/ppermute | solution.py:435
  50.8 2.6 %collective-permute-done.14.p3 = bf16[144,1024]{1,0:T(8,128)(2,1)} collective-permute-done((bf16[144,1024]{1,0:T(8,128)(2,1)}, bf16[144,1024]{1,0:T(8,128)(2,1)}, u32[]{:S(2)}, u32[]{:S(2)}) %collective-permute-start.14) | collective-permute-done | bytes 294944 | tf_op jit(solution)/shard_map/ppermute | solution.py:435
  53.4 1.8 %weights.3 = (bf16[128,512]{1,0:T(8,128)(2,1)S(1)}, bf16[128,512]{1,0:T(8,128)(2,1)S(1)}, bf16[128,512]{1,0:T(8,128)(2,1)S(1)}, bf16[128,512]{1,0:T(8,128)(2,1)S(1)}) custom-call(s32[1]{0:T(128)} %bitcast.6.me, bf16[144,1024]{1,0:T(8,128)(2,1)S(1)} %get-tuple-element.72.p0, bf16[144,1024]{1,0:T(8,128)(2,1)S(1)} %collective-permute-done.12.p1, ...), custom_call_target="tpu_custom_call" | custom-call | tf_op jit(solution)/shard_map/weights/pallas_call | solution.py:383
  55.2 0.1 collective-permute-start.15
  55.3 4.2 %collective-permute-start.16 = (bf16[128,512]{1,0:T(8,128)(2,1)S(1)}, bf16[128,512]{1,0:T(8,128)(2,1)S(1)}, u32[]{:S(2)}, u32[]{:S(2)}) collective-permute-start(bf16[128,512]{1,0:T(8,128)(2,1)S(1)} %get-tuple-element.78), channel_id=1, source_target_pairs={{0,128},{2,130},{4,132},{6,134},{8,136},{10,138},{12,140},{14,142}... | collective-permute-start | bytes 393224 | tf_op jit(solution)/shard_map/ppermute | solution.py:435
  59.5 0.5 collective-permute-start.17
  60.0 0.4 collective-permute-done.7.p2
  60.4 5.5 %collective-permute-done.8.p3 = bf16[144,1024]{1,0:T(8,128)(2,1)S(1)} collective-permute-done((bf16[144,1024]{1,0:T(8,128)(2,1)S(1)}, bf16[144,1024]{1,0:T(8,128)(2,1)S(1)}, u32[]{:S(2)}, u32[]{:S(2)}) %collective-permute-start.8) | collective-permute-done | bytes 294944 | tf_op jit(solution)/shard_map/ppermute | solution.py:435
  65.9 0.8 weights.2
  66.8 0.0 copy-start
  66.8 0.0 copy-start.6
  66.8 0.0 copy-start.9
  66.8 0.1 collective-permute-start.10
  66.9 2.2 %collective-permute-start.11 = (bf16[128,512]{1,0:T(8,128)(2,1)S(1)}, bf16[128,512]{1,0:T(8,128)(2,1)S(1)}, u32[]{:S(2)}, u32[]{:S(2)}) collective-permute-start(bf16[128,512]{1,0:T(8,128)(2,1)S(1)} %get-tuple-element.64), channel_id=1, source_target_pairs={{0,48},{2,50},{4,52},{6,54},{8,56},{10,58},{12,60},{14,62},{32,16}... | collective-permute-start | bytes 393224 | tf_op jit(solution)/shard_map/ppermute | solution.py:435
  69.1 1.3 %collective-permute-start.9 = (bf16[128,512]{1,0:T(8,128)(2,1)S(1)}, bf16[128,512]{1,0:T(8,128)(2,1)S(1)}, u32[]{:S(2)}, u32[]{:S(2)}) collective-permute-start(bf16[128,512]{1,0:T(8,128)(2,1)S(1)} %get-tuple-element.62), channel_id=1, source_target_pairs={{0,32},{2,34},{4,36},{6,38},{8,40},{10,42},{12,44},{14,46},{32,0},... | collective-permute-start | bytes 393224 | tf_op jit(solution)/shard_map/ppermute | solution.py:435
  70.4 3.1 %collective-permute-done.10.a2 = bf16[128,512]{1,0:T(8,128)(2,1)S(1)} collective-permute-done((bf16[128,512]{1,0:T(8,128)(2,1)S(1)}, bf16[128,512]{1,0:T(8,128)(2,1)S(1)}, u32[]{:S(2)}, u32[]{:S(2)}) %collective-permute-start.10) | collective-permute-done | bytes 131104 | tf_op jit(solution)/shard_map/ppermute | solution.py:435
  73.5 1.1 collective-permute-done.11.a3
  74.6 0.1 add_rows.1
  74.7 12.9 %all_to_all.15.parts = bf16[8,32,512]{2,1,0:T(8,128)(2,1)S(1)} all-to-all(bf16[8,32,512]{2,1,0:T(8,128)(2,1)S(1)} %add_rows.1), channel_id=1, replica_groups={{0,2,4,6,8,10,12,14},{32,34,36,38,40,42,44,46},{16,18,20,22,24,26,28,30..., dimensions={0} | all-to-all | bytes 524288 | tf_op jit(solution)/shard_map/all_to_all | solution.py:440
  87.6 0.2 to_owners.1
  87.8 12.1 %all_to_all.16.got = bf16[16,48,128]{2,1,0:T(8,128)(2,1)S(1)} all-to-all(bf16[16,48,128]{2,1,0:T(8,128)(2,1)S(1)} %to_owners.1), channel_id=1, replica_groups={{0,32,16,48,64,96,80,112,128,160,144,176,192,224,208,240},{2,34,18,50,6..., dimensions={0} | all-to-all | bytes 393216 | tf_op jit(solution)/shard_map/all_to_all | solution.py:440
  99.9 0.6 spread.1
  100.6 3.3 %all-to-all-start.2 = ((f32[8,8,128]{2,1,0:T(8,128)}), f32[8,8,128]{2,1,0:T(8,128)S(1)}, u32[]{:S(2)}, u32[]{:S(2)}) async-start(f32[8,8,128]{2,1,0:T(8,128)} %spread.1), calls=%async_computation.2 | async-start | bytes 65536 | tf_op jit(solution)/shard_map/all_to_all | solution.py:440
  103.9 0.1 pad_add_fusion.where
  104.0 1.6 %first_rest.1 = (bf16[6,12,2,512]{3,2,1,0:T(2,128)(2,1)}, bf16[6,12,2,512]{3,2,1,0:T(2,128)(2,1)}) custom-call(bf16[36,1024]{1,0:T(8,128)(2,1)S(1)} %collective-permute-done.3.b0, bf16[36,1024]{1,0:T(8,128)(2,1)S(1)} %collective-permute-done.4.b1, bf16[36,1024]{1,0:T(8,128)(2,1)S(1)} %collective-permute-done.5.b2, ...), custom_call_target="tpu_custom_call" | custom-call | tf_op jit(solution)/shard_map/first_rest/pallas_call | solution.py:383
  105.6 6.3 %all-to-all-done.2.tiles = f32[8,8,128]{2,1,0:T(8,128)S(1)} async-done(((f32[8,8,128]{2,1,0:T(8,128)}), f32[8,8,128]{2,1,0:T(8,128)S(1)}, u32[]{:S(2)}, u32[]{:S(2)}) %all-to-all-start.2) | async-done | bytes 32800 | tf_op jit(solution)/shard_map/all_to_all | solution.py:440
  111.8 1.2 %clipped.1 = (f32[4,1536]{1,0:T(4,128)}, f32[4,512]{1,0:T(4,128)}, f32[4,1536]{1,0:T(4,128)}, f32[4,512]{1,0:T(4,128)}) custom-call(s32[2]{0:T(128)S(1)} %pad_add_fusion.where, bf16[16,48,128]{2,1,0:T(8,128)(2,1)S(1)} %all_to_all.16.got, f32[8,8,128]{2,1,0:T(8,128)S(1)} %all-to-all-done.2.tiles), custom_call_target="tpu_custom_call" | custom-call | tf_op jit(solution)/shard_map/clipped/pallas_call | solution.py:383
  (26 shorter events, 0.1 us)
Async XLA Ops:
  0.6 19.0 %copy-start.10 = (f32[512]{0:T(512)S(1)}, f32[512]{0:T(512)}, u32[]{:S(2)}) copy-start(f32[512]{0:T(512)} %param.15) | copy-start | bytes 6148
  0.6 19.0 %copy-start.2 = (bf16[512,1536]{1,0:T(8,128)(2,1)S(1)}, bf16[512,1536]{1,0:T(8,128)(2,1)}, u32[]{:S(2)}) copy-start(bf16[512,1536]{1,0:T(8,128)(2,1)} %wqkv.2) | copy-start | bytes 4718596
  5.7 11.5 %collective-permute-start = (bf16[36,1152]{1,0:T(8,128)(2,1)}, bf16[36,1152]{1,0:T(8,128)(2,1)S(1)}, u32[]{:S(2)}, u32[]{:S(2)}) collective-permute-start(bf16[36,1152]{1,0:T(8,128)(2,1)} %get-tuple-element.45), channel_id=1, source_target_pairs={{0,254},{2,224},{4,226},{6,228},{8,230},{10,232},{12,234},{14,236}... | collective-permute-start | bytes 248840 | tf_op jit(solution)/shard_map/ppermute | solution.py:415
  14.5 4.8 %collective-permute-start.1 = (bf16[36,1152]{1,0:T(8,128)(2,1)}, bf16[36,1152]{1,0:T(8,128)(2,1)S(1)}, u32[]{:S(2)}, u32[]{:S(2)}) collective-permute-start(bf16[36,1152]{1,0:T(8,128)(2,1)} %get-tuple-element.46), channel_id=1, source_target_pairs={{0,224},{2,226},{4,228},{6,230},{8,232},{10,234},{12,236},{14,238}... | collective-permute-start | bytes 248840 | tf_op jit(solution)/shard_map/ppermute | solution.py:415
  14.7 5.0 %collective-permute-start.2 = (bf16[36,1152]{1,0:T(8,128)(2,1)}, bf16[36,1152]{1,0:T(8,128)(2,1)S(1)}, u32[]{:S(2)}, u32[]{:S(2)}) collective-permute-start(bf16[36,1152]{1,0:T(8,128)(2,1)} %get-tuple-element.47), channel_id=1, source_target_pairs={{0,30},{2,0},{4,2},{6,4},{8,6},{10,8},{12,10},{14,12},{16,14},{18,... | collective-permute-start | bytes 248840 | tf_op jit(solution)/shard_map/ppermute | solution.py:415
  19.7 1.0 copy-start.7
  20.7 0.9 copy-start.8
  21.6 21.5 %copy-start.1 = (bf16[512,512]{1,0:T(8,128)(2,1)S(1)}, bf16[512,512]{1,0:T(8,128)(2,1)}, u32[]{:S(2)}) copy-start(bf16[512,512]{1,0:T(8,128)(2,1)} %wout.3) | copy-start | bytes 1572868
  21.6 21.5 %copy-start.3 = (bf16[144,2688]{1,0:T(8,128)(2,1)S(1)}, bf16[144,2688]{1,0:T(8,128)(2,1)}, u32[]{:S(2)}) copy-start(bf16[144,2688]{1,0:T(8,128)(2,1)} %get-tuple-element.53.keep) | copy-start | bytes 2322436
  27.0 0.8 copy-start.4
  27.8 10.6 %collective-permute-start.3 = (bf16[36,1024]{1,0:T(8,128)(2,1)}, bf16[36,1024]{1,0:T(8,128)(2,1)S(1)}, u32[]{:S(2)}, u32[]{:S(2)}) collective-permute-start(bf16[36,1024]{1,0:T(8,128)(2,1)} %get-tuple-element.49), channel_id=1, source_target_pairs={{254,0},{224,2},{226,4},{228,6},{230,8},{232,10},{234,12},{236,14}... | collective-permute-start | bytes 221192 | tf_op jit(solution)/shard_map/ppermute | solution.py:415
  28.7 9.8 %collective-permute-start.4 = (bf16[36,1024]{1,0:T(8,128)(2,1)S(1)}, bf16[36,1024]{1,0:T(8,128)(2,1)S(1)}, u32[]{:S(2)}, u32[]{:S(2)}) collective-permute-start(bf16[36,1024]{1,0:T(8,128)(2,1)S(1)} %get-tuple-element.50), channel_id=1, source_target_pairs={{224,0},{226,2},{228,4},{230,6},{232,8},{234,10},{236,12},{238,14}... | collective-permute-start | bytes 221192 | tf_op jit(solution)/shard_map/ppermute | solution.py:415
  29.5 8.9 %collective-permute-start.5 = (bf16[36,1024]{1,0:T(8,128)(2,1)S(1)}, bf16[36,1024]{1,0:T(8,128)(2,1)S(1)}, u32[]{:S(2)}, u32[]{:S(2)}) collective-permute-start(bf16[36,1024]{1,0:T(8,128)(2,1)S(1)} %get-tuple-element.51), channel_id=1, source_target_pairs={{30,0},{0,2},{2,4},{4,6},{6,8},{8,10},{10,12},{12,14},{14,16},{16,... | collective-permute-start | bytes 221192 | tf_op jit(solution)/shard_map/ppermute | solution.py:415
  29.5 1.1 copy-start.5
  38.4 10.5 %collective-permute-start.12 = (bf16[144,1024]{1,0:T(8,128)(2,1)}, bf16[144,1024]{1,0:T(8,128)(2,1)S(1)}, u32[]{:S(2)}, u32[]{:S(2)}) collective-permute-start(bf16[144,1024]{1,0:T(8,128)(2,1)} %get-tuple-element.73), channel_id=1, source_target_pairs={{0,32},{2,34},{4,36},{6,38},{8,40},{10,42},{12,44},{14,46},{32,0},... | collective-permute-start | bytes 884744 | tf_op jit(solution)/shard_map/ppermute | solution.py:435
  38.5 12.4 %collective-permute-start.13 = (bf16[144,1024]{1,0:T(8,128)(2,1)}, bf16[144,1024]{1,0:T(8,128)(2,1)S(1)}, u32[]{:S(2)}, u32[]{:S(2)}) collective-permute-start(bf16[144,1024]{1,0:T(8,128)(2,1)} %get-tuple-element.74), channel_id=1, source_target_pairs={{0,16},{2,18},{4,20},{6,22},{8,24},{10,26},{12,28},{14,30},{32,48}... | collective-permute-start | bytes 884744 | tf_op jit(solution)/shard_map/ppermute | solution.py:435
  40.2 13.2 %collective-permute-start.14 = (bf16[144,1024]{1,0:T(8,128)(2,1)}, bf16[144,1024]{1,0:T(8,128)(2,1)}, u32[]{:S(2)}, u32[]{:S(2)}) collective-permute-start(bf16[144,1024]{1,0:T(8,128)(2,1)} %get-tuple-element.75), channel_id=1, source_target_pairs={{0,48},{2,50},{4,52},{6,54},{8,56},{10,58},{12,60},{14,62},{32,16}... | collective-permute-start | bytes 884744 | tf_op jit(solution)/shard_map/ppermute | solution.py:435
  46.1 13.4 %collective-permute-start.6 = (bf16[144,1024]{1,0:T(8,128)(2,1)S(1)}, bf16[144,1024]{1,0:T(8,128)(2,1)S(1)}, u32[]{:S(2)}, u32[]{:S(2)}) collective-permute-start(bf16[144,1024]{1,0:T(8,128)(2,1)S(1)} %get-tuple-element.58), channel_id=1, source_target_pairs={{0,64},{2,66},{4,68},{6,70},{8,72},{10,74},{12,76},{14,78},{32,96}... | collective-permute-start | bytes 884744 | tf_op jit(solution)/shard_map/ppermute | solution.py:435
  46.2 14.2 %collective-permute-start.7 = (bf16[144,1024]{1,0:T(8,128)(2,1)S(1)}, bf16[144,1024]{1,0:T(8,128)(2,1)S(1)}, u32[]{:S(2)}, u32[]{:S(2)}) collective-permute-start(bf16[144,1024]{1,0:T(8,128)(2,1)S(1)} %get-tuple-element.59), channel_id=1, source_target_pairs={{0,128},{2,130},{4,132},{6,134},{8,136},{10,138},{12,140},{14,142}... | collective-permute-start | bytes 884744 | tf_op jit(solution)/shard_map/ppermute | solution.py:435
  48.9 17.0 %collective-permute-start.8 = (bf16[144,1024]{1,0:T(8,128)(2,1)S(1)}, bf16[144,1024]{1,0:T(8,128)(2,1)S(1)}, u32[]{:S(2)}, u32[]{:S(2)}) collective-permute-start(bf16[144,1024]{1,0:T(8,128)(2,1)S(1)} %get-tuple-element.60), channel_id=1, source_target_pairs={{0,192},{2,194},{4,196},{6,198},{8,200},{10,202},{12,204},{14,206}... | collective-permute-start | bytes 884744 | tf_op jit(solution)/shard_map/ppermute | solution.py:435
  55.2 13.9 %collective-permute-start.15 = (bf16[128,512]{1,0:T(8,128)(2,1)S(1)}, bf16[128,512]{1,0:T(8,128)(2,1)S(1)}, u32[]{:S(2)}, u32[]{:S(2)}) collective-permute-start(bf16[128,512]{1,0:T(8,128)(2,1)S(1)} %get-tuple-element.77), channel_id=1, source_target_pairs={{0,64},{2,66},{4,68},{6,70},{8,72},{10,74},{12,76},{14,78},{32,96}... | collective-permute-start | bytes 393224 | tf_op jit(solution)/shard_map/ppermute | solution.py:435
  55.3 15.1 %collective-permute-start.16 = (bf16[128,512]{1,0:T(8,128)(2,1)S(1)}, bf16[128,512]{1,0:T(8,128)(2,1)S(1)}, u32[]{:S(2)}, u32[]{:S(2)}) collective-permute-start(bf16[128,512]{1,0:T(8,128)(2,1)S(1)} %get-tuple-element.78), channel_id=1, source_target_pairs={{0,128},{2,130},{4,132},{6,134},{8,136},{10,138},{12,140},{14,142}... | collective-permute-start | bytes 393224 | tf_op jit(solution)/shard_map/ppermute | solution.py:435
  59.5 10.9 %collective-permute-start.17 = (bf16[128,512]{1,0:T(8,128)(2,1)S(1)}, bf16[128,512]{1,0:T(8,128)(2,1)S(1)}, u32[]{:S(2)}, u32[]{:S(2)}) collective-permute-start(bf16[128,512]{1,0:T(8,128)(2,1)S(1)} %get-tuple-element.79), channel_id=1, source_target_pairs={{0,192},{2,194},{4,196},{6,198},{8,200},{10,202},{12,204},{14,206}... | collective-permute-start | bytes 393224 | tf_op jit(solution)/shard_map/ppermute | solution.py:435
  66.8 37.2 %copy-start = (bf16[512,1536]{1,0:T(8,128)(2,1)S(1)}, bf16[512,1536]{1,0:T(8,128)(2,1)}, u32[]{:S(2)}) copy-start(bf16[512,1536]{1,0:T(8,128)(2,1)} %wqkv.3) | copy-start | bytes 4718596
  66.8 37.2 %copy-start.6 = (bf16[2,6,12,512]{3,0,2,1:T(2,128)(2,1)S(1)}, bf16[2,6,12,512]{3,0,2,1:T(2,128)(2,1)}, u32[]{:S(2)}) copy-start(bf16[2,6,12,512]{3,0,2,1:T(2,128)(2,1)} %param.9) | copy-start | bytes 442372
  66.8 37.2 %copy-start.9 = (f32[512]{0:T(512)S(1)}, f32[512]{0:T(512)}, u32[]{:S(2)}) copy-start(f32[512]{0:T(512)} %param.12) | copy-start | bytes 6148
  66.8 6.7 %collective-permute-start.10 = (bf16[128,512]{1,0:T(8,128)(2,1)S(1)}, bf16[128,512]{1,0:T(8,128)(2,1)S(1)}, u32[]{:S(2)}, u32[]{:S(2)}) collective-permute-start(bf16[128,512]{1,0:T(8,128)(2,1)S(1)} %get-tuple-element.63), channel_id=1, source_target_pairs={{0,16},{2,18},{4,20},{6,22},{8,24},{10,26},{12,28},{14,30},{32,48}... | collective-permute-start | bytes 393224 | tf_op jit(solution)/shard_map/ppermute | solution.py:435
  66.9 7.7 %collective-permute-start.11 = (bf16[128,512]{1,0:T(8,128)(2,1)S(1)}, bf16[128,512]{1,0:T(8,128)(2,1)S(1)}, u32[]{:S(2)}, u32[]{:S(2)}) collective-permute-start(bf16[128,512]{1,0:T(8,128)(2,1)S(1)} %get-tuple-element.64), channel_id=1, source_target_pairs={{0,48},{2,50},{4,52},{6,54},{8,56},{10,58},{12,60},{14,62},{32,16}... | collective-permute-start | bytes 393224 | tf_op jit(solution)/shard_map/ppermute | solution.py:435
  69.1 5.5 %collective-permute-start.9 = (bf16[128,512]{1,0:T(8,128)(2,1)S(1)}, bf16[128,512]{1,0:T(8,128)(2,1)S(1)}, u32[]{:S(2)}, u32[]{:S(2)}) collective-permute-start(bf16[128,512]{1,0:T(8,128)(2,1)S(1)} %get-tuple-element.62), channel_id=1, source_target_pairs={{0,32},{2,34},{4,36},{6,38},{8,40},{10,42},{12,44},{14,46},{32,0},... | collective-permute-start | bytes 393224 | tf_op jit(solution)/shard_map/ppermute | solution.py:435
  100.6 11.3 %all-to-all-start.2 = ((f32[8,8,128]{2,1,0:T(8,128)}), f32[8,8,128]{2,1,0:T(8,128)S(1)}, u32[]{:S(2)}, u32[]{:S(2)}) async-start(f32[8,8,128]{2,1,0:T(8,128)} %spread.1), calls=%async_computation.2 | async-start | bytes 65536 | tf_op jit(solution)/shard_map/all_to_all | solution.py:440

commit v4 on v3

--- a/solution.py
+++ b/solution.py
@@ -25,9 +25,10 @@
 LAT, LON = X * YLO, YHI * Z
 OWN = D // (LAT * LON)
 GROUP = 4
+LAST = 8
 WIDE = 4 * D // GROUP
 PLANE_ROWS = D // GROUP
-LAST_ROWS = PLANE_ROWS // Z
+LAST_ROWS = PLANE_ROWS // LAST
 SEND = 2 * D + LANES
 
 EPSILON = 1e-05
@@ -35,7 +36,6 @@
 F32 = jnp.float32
 BF16 = jnp.bfloat16
 VMEM_BYTES = 16 * 1024 * 1024
-WHOLE_VMEM_BYTES = 62 * 1024 * 1024
 
 
 def dot_nn(a, b):
@@ -180,18 +180,38 @@
     return (lax.broadcasted_iota(jnp.int32, (D, D), 0) == source_of(to)).astype(F32).astype(BF16)
 
 
-def row_of(x, y, z, own):
-    return (((x * YLO + y % YLO) * YHI + y // YLO) * Z + z) * OWN + own
-
-
-def order_x(to):
-    x = to // OWN % X
-    return row_of(x, to // (OWN * X * Z), to // (OWN * X) % Z, to % OWN)
-
-
-def order_y(to):
-    y = to // OWN % Y
-    return row_of(to // (OWN * Y * Z), y, to // (OWN * Y) % Z, to % OWN)
+def chip_of(lat, lon):
+    return lat // YLO, lon // Z * YLO + lat % YLO, lon % Z
+
+
+def members_first(x, y, z):
+    return x % 2 + z % 2 * 2, y, x // 2 + z // 2 * 2
+
+
+def members_second(x, y, z):
+    s = (x + 3) % 4
+    return s % 2 + y % 2 * 2, y // 2 + z % 2 * 2, s // 2 + z // 2 * 2
+
+
+def chip_first(m1, m2, m3):
+    return m1 % 2 + m3 % 2 * 2, m2, m1 // 2 + m3 // 2 * 2
+
+
+def chip_second(m1, m2, m3):
+    return (m1 % 2 + m3 % 2 * 2 + 1) % 4, m1 // 2 + m2 % 2 * 2, m2 // 2 + m3 // 2 * 2
+
+
+def row_order(chip):
+    def source_of(to):
+        m1, m3, m2 = to // OWN % GROUP, to // (OWN * GROUP) % LAST, to // (OWN * GROUP * LAST)
+        x, y, z = chip(m1, m2, m3)
+        return (((x * YLO + y % YLO) * YHI + y // YLO) * Z + z) * OWN + to % OWN
+
+    return source_of
+
+
+def here(me):
+    return chip_of(me[0], me[1])
 
 
 def pack(me, left_refs, right_ref, packs):
@@ -217,7 +237,7 @@
 
 
 def first_forward(
-    wrap, region, tok, cot, gain_hbm, wqkv_hbm, wout_hbm,
+    me, region, tok, cot, gain_hbm, wqkv_hbm, wout_hbm,
     x0, x1, x2, x3, keep_ref, scratch, lab_scratch, gain, wqkv, wout, sems,
 ):
     copies = [
@@ -232,7 +252,7 @@
         ref[:, D : 2 * D] = scratch[slot * QUART : (slot + 1) * QUART, :].astype(BF16)
     labels = jnp.broadcast_to(take_labels(region), (TOK, LANES))
     near = lax.broadcasted_iota(jnp.int32, (TOK, LANES), 0) < 2 * QUART
-    moved = labels + jnp.where(near, wrap[0].astype(F32), 0.0)
+    moved = labels + jnp.where(near & (me[0] == 0), 4.0, 0.0)
     scatter_rows(moved, lab_scratch, refs, 2 * D)
     values = take_field(tok, scratch)
     copies[0].wait()
@@ -271,10 +291,10 @@
 
 
 def second_pack(me, normed, attended, right, p0, p1, p2, p3, left_n, left_a):
-    order = regroup(order_y)
+    order = regroup(row_order(chip_second))
     left_n[...] = dot_nn(normed[...], order).astype(BF16)
     left_a[...] = dot_nn(attended[...], order).astype(BF16)
-    pack(me[0], (left_n, left_a), right, (p0, p1, p2, p3))
+    pack(members_second(*here(me))[0], (left_n, left_a), right, (p0, p1, p2, p3))
 
 
 def first_backward(
@@ -285,10 +305,10 @@
     bias = label_bias(keep[:, 5 * D :].astype(F32))
     _, dproj = attention(keep[...], bias, grad=datt, attended=keep[:, 3 * D : 4 * D])
     store_right(dproj, g16, right_ref)
-    order = regroup(order_x)
+    order = regroup(row_order(chip_first))
     left_n[...] = dot_nn(keep[:, 4 * D : 5 * D], order).astype(BF16)
     left_a[...] = dot_nn(keep[:, 3 * D : 4 * D], order).astype(BF16)
-    pack(me[0], (left_n, left_a), right_ref, (p0, p1, p2, p3))
+    pack(members_first(*here(me))[0], (left_n, left_a), right_ref, (p0, p1, p2, p3))
 
 
 def first_rest(b0, b1, b2, b3, tok, gain, wqkv, right, tg_ref, result_ref, scratch):
@@ -302,26 +322,38 @@
     put_field(norm_back(dnormed, gain[...], xhat, rstd, g), scratch, tg_ref)
 
 
-def weights(me, p0, p1, p2, p3, q0, q1, q2, q3, scratch):
-    total = jnp.zeros((D, WIDE), F32)
-    for part in (p0, p1, p2, p3):
-        total += dot_tn(part[:, :D], part[:, D:])
-    scratch[...] = total
+def weights(member, p0, p1, p2, p3, q0, q1, q2, q3, scratch):
+    scratch[...] = sum(dot_tn(part[:, :D], part[:, D:]) for part in (p0, p1, p2, p3))
     for step, ref in enumerate((q0, q1, q2, q3)):
-        first = pl.multiple_of((me[0] ^ step) * PLANE_ROWS, PLANE_ROWS)
+        first = pl.multiple_of((member ^ step) * PLANE_ROWS, PLANE_ROWS)
         ref[...] = scratch[pl.ds(first, PLANE_ROWS), :].astype(BF16)
 
 
-def add_rows(a0, a1, a2, a3, b0, b1, b2, b3, out_ref):
-    for slot, parts in enumerate(((a0, a1, a2, a3), (b0, b1, b2, b3))):
-        total = sum(part[...].astype(F32) for part in parts).astype(BF16)
-        for z in range(Z):
-            out_ref[z, slot * LAST_ROWS : (slot + 1) * LAST_ROWS, :] = total[
-                z * LAST_ROWS : (z + 1) * LAST_ROWS
-            ]
+def first_weights(me, *refs):
+    weights(members_first(*here(me))[1], *refs)
+
+
+def second_weights(me, *refs):
+    weights(members_second(*here(me))[1], *refs)
+
+
+def add_rows(me, a0, a1, a2, a3, b0, b1, b2, b3, out_ref, scratch):
+    x, y, z = here(me)
+    flip = members_first(x, y, z)[2] ^ members_second(x, y, z)[2]
+    total = sum(part[...].astype(F32) for part in (a0, a1, a2, a3)).astype(BF16)
+    scratch[...] = sum(part[...].astype(F32) for part in (b0, b1, b2, b3))
+    for last in range(LAST):
+        out_ref[last, :LAST_ROWS, :] = total[last * LAST_ROWS : (last + 1) * LAST_ROWS]
+        first = pl.multiple_of((last ^ flip) * LAST_ROWS, LAST_ROWS)
+        out_ref[last, LAST_ROWS:, :] = scratch[pl.ds(first, LAST_ROWS), :].astype(BF16)
 
 
 PIECE = OWN * WIDE // LANES
+NEAR = [(x, y, z) for z in range(2) for y in range(YLO) for x in range(X)]
+
+
+def near_index(x, y, z):
+    return x + y % YLO * X + z % 2 * X * YLO
 
 
 def to_owners(parts, send_ref, scratch):
@@ -333,16 +365,16 @@
         terms.append(term)
         rest = rest - term
     terms = jnp.concatenate([jnp.broadcast_to(term, (1, LANES)) for term in terms], 0)
-    for x in range(X):
-        for y in range(Y):
-            for slot, row in ((0, x * OWN), (1, LAST_ROWS + y * OWN)):
-                for c in range(WIDE // LANES):
-                    first = slot * PIECE + c * OWN
-                    scratch[x * Y + y, first : first + OWN, :] = total[
-                        row : row + OWN, c * LANES : (c + 1) * LANES
-                    ]
-            scratch[x * Y + y, 2 * PIECE :, :] = jnp.zeros((16, LANES), F32)
-            scratch[x * Y + y, 2 * PIECE : 2 * PIECE + 3, :] = terms
+    for peer, chip in enumerate(NEAR):
+        rows = (members_first(*chip)[0] * OWN, LAST_ROWS + members_second(*chip)[0] * OWN)
+        for slot, row in enumerate(rows):
+            for c in range(WIDE // LANES):
+                first = slot * PIECE + c * OWN
+                scratch[peer, first : first + OWN, :] = total[
+                    row : row + OWN, c * LANES : (c + 1) * LANES
+                ]
+        scratch[peer, 2 * PIECE :, :] = jnp.zeros((16, LANES), F32)
+        scratch[peer, 2 * PIECE : 2 * PIECE + 3, :] = terms
     send_ref[...] = scratch[...].astype(BF16)
 
 
@@ -352,15 +384,17 @@
     tile_ref[...] = jnp.broadcast_to(squares[None], tile_ref.shape)
 
 
-def clipped(where, got, tiles, qkv_a, out_a, qkv_b, out_b, scratch):
+def clipped(me, got, tiles, qkv_a, out_a, qkv_b, out_b, scratch):
     scratch[...] = got[:, : 2 * PIECE, :].astype(F32)
     total = jnp.sum(tiles[...], 0)[:1, :1]
     factor = jnp.minimum(1.0, math.sqrt(8.0) * D / jnp.sqrt(total))
-    x, y = where[0], where[1]
+    chip = here(me)
+    _, *first_rest_of = members_first(*chip)
+    _, *second_rest_of = members_second(*chip)
     for k in range(GROUP):
         for slot, source, refs in (
-            (0, k * Y + y, (qkv_a, out_a)),
-            (1, x * Y + k, (qkv_b, out_b)),
+            (0, near_index(*chip_first(k, *first_rest_of)), (qkv_a, out_a)),
+            (1, near_index(*chip_second(k, *second_rest_of)), (qkv_b, out_b)),
         ):
             ref, column = (refs[0], k * WIDE) if k < 3 else (refs[1], 0)
             for c in range(WIDE // LANES):
@@ -374,7 +408,7 @@
     return jax.ShapeDtypeStruct(dims, dtype)
 
 
-def call(kernel, outs, scratch, *args, scalar=False, far=0, vmem=VMEM_BYTES):
+def call(kernel, outs, scratch, *args, scalar=False, far=0):
     whole = pl.BlockSpec(memory_space=pltpu.VMEM)
     specs = [whole] * (len(args) - far) + [pl.BlockSpec(memory_space=pl.ANY)] * far
     if scalar:
@@ -386,9 +420,13 @@
         in_specs=specs,
         out_specs=[whole] * len(outs),
         scratch_shapes=scratch,
-        compiler_params=pltpu.CompilerParams(vmem_limit_bytes=vmem),
+        compiler_params=pltpu.CompilerParams(vmem_limit_bytes=VMEM_BYTES),
         name=kernel.__name__,
     )(*args)
+
+
+def in_hbm(*arrays):
+    return [pltpu.with_memory_space_constraint(array, pltpu.HBM) for array in arrays]
 
 
 def moves(lat_count, lon_count):
@@ -421,19 +459,40 @@
 
 
 CHIPS = [(x, y, z) for x in range(X) for y in range(Y) for z in range(Z)]
-PLANE = [[index_of(x, y, z) for x in range(X) for y in range(Y)] for z in range(Z)]
-COLUMN = [[index_of(x, y, z) for z in range(Z)] for x in range(X) for y in range(Y)]
-
-
-def swap(packs, axis):
-    out = [packs[0]]
+
+
+def groups_of(key, order):
+    table = {}
+    for chip in sorted(CHIPS, key=order):
+        table.setdefault(key(*chip), []).append(index_of(*chip))
+    return [table[k] for k in sorted(table)]
+
+
+LAST_GROUPS = groups_of(
+    lambda x, y, z: members_first(x, y, z)[:2], lambda chip: members_first(*chip)[2]
+)
+NEAR_GROUPS = groups_of(lambda x, y, z: (y // 2, z // 2), lambda chip: near_index(*chip))
+FAR_GROUPS = groups_of(lambda x, y, z: near_index(x, y, z), lambda chip: chip)
+
+
+def swap(parts, members, chip, level):
+    out = [parts[0]]
     for step in range(1, GROUP):
-        pairs = [
-            (index_of(x, y, z), index_of(x ^ step, y, z) if axis == "x" else index_of(x, y ^ step, z))
-            for x, y, z in CHIPS
-        ]
-        out.append(lax.ppermute(packs[step], ("lat", "lon"), pairs))
+        pairs = []
+        for here_chip in CHIPS:
+            numbers = list(members(*here_chip))
+            numbers[level] ^= step
+            pairs.append((index_of(*here_chip), index_of(*chip(*numbers))))
+        out.append(lax.ppermute(parts[step], ("lat", "lon"), pairs))
     return out
+
+
+def swap_first(parts, level):
+    return swap(parts, members_first, chip_first, level)
+
+
+def swap_second(parts, level):
+    return swap(parts, members_second, chip_second, level)
 
 
 def exchange(parts, groups):
@@ -457,10 +516,7 @@
 ):
     tables = moves(LAT, LON)
     lat, lon = lax.axis_index("lat"), lax.axis_index("lon")
-    at_x = (lat // YLO).astype(jnp.int32)
-    at_y = (lon // Z * YLO + lat % YLO).astype(jnp.int32)
-    me_x, me_y = at_x.reshape(1), at_y.reshape(1)
-    wrap = jnp.where(lat == 0, 4, 0).astype(jnp.int32).reshape(1)
+    me = jnp.stack([lat, lon]).astype(jnp.int32)
     gain_a = unshifted_norm_gain.reshape(1, D)
     gain_b = shifted_norm_gain.reshape(1, D)
     tok = tokens.transpose(1, 2, 0, 3)
@@ -481,8 +537,8 @@
             pltpu.VMEM((D, D), BF16),
             pltpu.SemaphoreType.DMA((3,)),
         ],
-        wrap, lab, tok, cot, gain_a, unshifted_query_key_value, out_first,
-        scalar=True, far=3, vmem=WHOLE_VMEM_BYTES,
+        me, *in_hbm(lab, tok, cot, gain_a, unshifted_query_key_value, out_first),
+        scalar=True, far=3,
     )
     x = send(x, tables)
     *back, normed_b, att_b, right_b = call(
@@ -494,17 +550,17 @@
     back = send(back, tables, back=True)
     half = pltpu.VMEM((TOK, D), BF16)
     pack_b = call(
-        second_pack, packs, [half, half], me_y, normed_b, att_b, right_b, scalar=True
-    )
-    pack_b = swap(after(pack_b, back[:3]), "y")
+        second_pack, packs, [half, half], me, normed_b, att_b, right_b, scalar=True
+    )
+    pack_b = swap_second(after(pack_b, back[:3]), 0)
     right_a, *pack_a = call(
         first_backward,
         [fields] + packs,
         [(TOK, D), half, half],
-        me_x, *back, out_first, keep,
+        me, *back, out_first, keep,
         scalar=True,
     )
-    pack_a = swap(pack_a, "x")
+    pack_a = swap_first(pack_a, 0)
     grid = shape_of(WLAT, WLON, WLEV, D)
     token_gradient, result = call(
         first_rest,
@@ -516,21 +572,27 @@
     result = result.transpose(2, 0, 1, 3)
 
     rows = [shape_of(PLANE_ROWS, WIDE)] * GROUP
-    sum_b = swap(call(weights, rows, [(D, WIDE)], me_x, *pack_b, scalar=True), "x")
-    sum_a = swap(call(weights, rows, [(D, WIDE)], me_y, *pack_a, scalar=True), "y")
-    (sums,) = call(add_rows, [shape_of(Z, 2 * LAST_ROWS, WIDE)], [], *sum_a, *sum_b)
-    sums = exchange(sums, COLUMN)
-    piece = (X * Y, 2 * PIECE + 16, LANES)
+    sum_b = swap_second(call(second_weights, rows, [(D, WIDE)], me, *pack_b, scalar=True), 1)
+    sum_a = swap_first(call(first_weights, rows, [(D, WIDE)], me, *pack_a, scalar=True), 1)
+    (sums,) = call(
+        add_rows,
+        [shape_of(LAST, 2 * LAST_ROWS, WIDE)],
+        [(PLANE_ROWS, WIDE)],
+        me, *sum_a, *sum_b,
+        scalar=True,
+    )
+    sums = exchange(sums, LAST_GROUPS)
+    piece = (len(NEAR), 2 * PIECE + 16, LANES)
     (pieces,) = call(to_owners, [shape_of(*piece)], [piece], sums)
-    pieces = exchange(pieces, PLANE)
-    (tiles,) = call(spread, [shape_of(Z, 8, LANES, dtype=F32)], [], pieces)
-    tiles = exchange(tiles, COLUMN)
+    pieces = exchange(pieces, NEAR_GROUPS)
+    (tiles,) = call(spread, [shape_of(LAST, 8, LANES, dtype=F32)], [], pieces)
+    tiles = exchange(tiles, FAR_GROUPS)
     out_qkv, out_out = shape_of(OWN, 3 * D, dtype=F32), shape_of(OWN, D, dtype=F32)
     clips = call(
         clipped,
         [out_qkv, out_out] * 2,
-        [(X * Y, 2 * PIECE, LANES)],
-        jnp.concatenate([me_x, me_y]), pieces, tiles,
+        [(len(NEAR), 2 * PIECE, LANES)],
+        me, pieces, tiles,
         scalar=True,
     )
     return (result, token_gradient, *clips)

time: 114 us -> 113 us (level)
  local copies, waits for them, and re-layouts: 3.87 us -> 0.04 us
  waiting for transfers between devices: 27.9 us -> 31 us
  blocking collectives: 25 us -> 27.9 us
  starting transfers between devices: 34.3 us -> 31.7 us
    unnamed x22 -> x14, local copies, waits for them, and re-layouts: 3.87 us -> 0.04 us
    ppermute x12, starting transfers between devices: 17.8 us -> 14.3 us  [swap(): out.append(lax.ppermute(parts[step], ('lat', 'lon'), pairs))]
    all_to_all x2, blocking collectives: 25 us -> 27.9 us  [exchange(): return lax.all_to_all(parts, ('lat', 'lon'), 0, 0, axis_index_groups=groups)]
    all_to_all x1, waiting for transfers between devices: 6.26 us -> 8.54 us  [exchange(): return lax.all_to_all(parts, ('lat', 'lon'), 0, 0, axis_index_groups=groups)]
  transfers between devices with their start and end apart: 19 -> 19, of which waited for: 9 -> 11; matrix products, arithmetic and copies ran while one was open for 0% -> 0% of each run, Pallas kernels for 8% -> 8%
where the time goes in v4:
time: 113 us; the launch traced here: 112 us
  starting transfers between devices  31.7 us (28%)
  waiting for transfers between devices  31 us (27%)
  blocking collectives  27.9 us (25%)
  Pallas kernels  20.6 us (18%)
    all_to_all x2, blocking collectives, exchange(): return lax.all_to_all(parts, ('lat', 'lon'), 0, 0, axis_index_groups=groups)  27.9 us
    pallas_call x11, Pallas kernels, call(): pl.pallas_call(kernel, out_shape=outs, in_specs=specs, out_specs=[whole]...  20.6 us
    ppermute x12, starting transfers between devices, swap(): out.append(lax.ppermute(parts[step], ('lat', 'lon'), pairs))  14.3 us
    ppermute x6, starting transfers between devices, send(): out.append(lax.ppermute(part, ('lat', 'lon'), pairs))  13.4 us
    ppermute x12, waiting for transfers between devices, swap(): out.append(lax.ppermute(parts[step], ('lat', 'lon'), pairs))  12.5 us
    ppermute x6, waiting for transfers between devices, send(): out.append(lax.ppermute(part, ('lat', 'lon'), pairs))  9.96 us
    all_to_all x1, waiting for transfers between devices, exchange(): return lax.all_to_all(parts, ('lat', 'lon'), 0, 0, axis_index_groups=groups)  8.54 us
    all_to_all x1, starting transfers between devices, exchange(): return lax.all_to_all(parts, ('lat', 'lon'), 0, 0, axis_index_groups=groups)  3.93 us
  transfers between devices with their start and end apart: 19, of which 11 were waited for; matrix products, arithmetic and copies ran while one was open for 0% of the time, Pallas kernels for 8%

profile of v4, /device:TPU:0, one launch (start us, length us, event | category | flops | bytes accessed | tf_op | source)
XLA Modules:
  0.0 112.0 jit_solution(5442907017907750022)
XLA Ops:
  0.7 0.1 pad_add_fusion.me
  0.7 4.1 %first_forward.1 = (bf16[36,1152]{1,0:T(8,128)(2,1)S(1)}, bf16[36,1152]{1,0:T(8,128)(2,1)S(1)}, bf16[36,1152]{1,0:T(8,128)(2,1)S(1)}, bf16[36,1152]{1,0:T(8,128)(2,1)S(1)}, bf16[144,2688]{1,0:T(8,128)(2,1)S(1)}) custom-call(s32[2]{0:T(128)S(1)} %pad_add_fusion.me, s32[6,2,12]{2,1,0:T(2,128)} %bitcast.15, bf16[6,12,2,512]{3,2,1,0:T(2,128)(2,1)} %bitcast.9, ...), custom_call_target="tpu_custom_call" | custom-call | tf_op jit(solution)/shard_map/first_forward/pallas_call | solution.py:417
  4.9 8.8 %collective-permute-start = (bf16[36,1152]{1,0:T(8,128)(2,1)S(1)}, bf16[36,1152]{1,0:T(8,128)(2,1)S(1)}, u32[]{:S(2)}, u32[]{:S(2)}) collective-permute-start(bf16[36,1152]{1,0:T(8,128)(2,1)S(1)} %get-tuple-element.45), channel_id=1, source_target_pairs={{0,254},{2,224},{4,226},{6,228},{8,230},{10,232},{12,234},{14,236}... | collective-permute-start | bytes 248840 | tf_op jit(solution)/shard_map/ppermute | solution.py:453
  13.7 0.1 collective-permute-start.1
  13.8 2.5 %collective-permute-start.2 = (bf16[36,1152]{1,0:T(8,128)(2,1)S(1)}, bf16[36,1152]{1,0:T(8,128)(2,1)S(1)}, u32[]{:S(2)}, u32[]{:S(2)}) collective-permute-start(bf16[36,1152]{1,0:T(8,128)(2,1)S(1)} %get-tuple-element.47), channel_id=1, source_target_pairs={{0,30},{2,0},{4,2},{6,4},{8,6},{10,8},{12,10},{14,12},{16,14},{18,... | collective-permute-start | bytes 248840 | tf_op jit(solution)/shard_map/ppermute | solution.py:453
  16.3 0.0 collective-permute-done.x0
  16.3 1.9 %collective-permute-done.1.x1 = bf16[36,1152]{1,0:T(8,128)(2,1)S(1)} collective-permute-done((bf16[36,1152]{1,0:T(8,128)(2,1)S(1)}, bf16[36,1152]{1,0:T(8,128)(2,1)S(1)}, u32[]{:S(2)}, u32[]{:S(2)}) %collective-permute-start.1) | collective-permute-done | bytes 82976 | tf_op jit(solution)/shard_map/ppermute | solution.py:453
  18.2 0.3 collective-permute-done.2.x2
  18.5 4.8 %second_main.1 = (bf16[36,1024]{1,0:T(8,128)(2,1)S(1)}, bf16[36,1024]{1,0:T(8,128)(2,1)S(1)}, bf16[36,1024]{1,0:T(8,128)(2,1)S(1)}, bf16[36,1024]{1,0:T(8,128)(2...) custom-call(bf16[36,1152]{1,0:T(8,128)(2,1)S(1)} %collective-permute-done.x0, ...), custom_call_target="tpu_custom_call" | custom-call | tf_op jit(solution)/shard_map/second_main/pallas_call | solution.py:417
  23.3 0.9 collective-permute-start.3
  24.2 1.0 collective-permute-start.4
  25.3 1.1 second_pack.1
  26.4 7.8 %collective-permute-done.3.b0 = bf16[36,1024]{1,0:T(8,128)(2,1)S(1)} collective-permute-done((bf16[36,1024]{1,0:T(8,128)(2,1)S(1)}, bf16[36,1024]{1,0:T(8,128)(2,1)S(1)}, u32[]{:S(2)}, u32[]{:S(2)}) %collective-permute-start.3) | collective-permute-done | bytes 73760 | tf_op jit(solution)/shard_map/ppermute | solution.py:453
  34.2 0.0 collective-permute-done.5.b2
  34.2 1.1 %collective-permute-start.12 = (bf16[144,1024]{1,0:T(8,128)(2,1)S(1)}, bf16[144,1024]{1,0:T(8,128)(2,1)S(1)}, u32[]{:S(2)}, u32[]{:S(2)}) collective-permute-start(bf16[144,1024]{1,0:T(8,128)(2,1)S(1)} %get-tuple-element.73), channel_id=1, source_target_pairs={{0,192},{2,194},{4,196},{6,198},{8,200},{10,202},{12,204},{14,206}... | collective-permute-start | bytes 884744 | tf_op jit(solution)/shard_map/ppermute | solution.py:486
  35.3 1.7 %collective-permute-start.13 = (bf16[144,1024]{1,0:T(8,128)(2,1)S(1)}, bf16[144,1024]{1,0:T(8,128)(2,1)S(1)}, u32[]{:S(2)}, u32[]{:S(2)}) collective-permute-start(bf16[144,1024]{1,0:T(8,128)(2,1)S(1)} %get-tuple-element.74), channel_id=1, source_target_pairs={{0,32},{2,34},{4,36},{6,38},{8,40},{10,42},{12,44},{14,46},{32,0},... | collective-permute-start | bytes 884744 | tf_op jit(solution)/shard_map/ppermute | solution.py:486
  37.0 1.8 %collective-permute-start.14 = (bf16[144,1024]{1,0:T(8,128)(2,1)S(1)}, bf16[144,1024]{1,0:T(8,128)(2,1)S(1)}, u32[]{:S(2)}, u32[]{:S(2)}) collective-permute-start(bf16[144,1024]{1,0:T(8,128)(2,1)S(1)} %get-tuple-element.75), channel_id=1, source_target_pairs={{0,224},{2,226},{4,228},{6,230},{8,232},{10,234},{12,236},{14,238}... | collective-permute-start | bytes 884744 | tf_op jit(solution)/shard_map/ppermute | solution.py:486
  38.9 3.5 %first_backward.1 = (bf16[4,144,512]{2,1,0:T(8,128)(2,1)S(1)}, bf16[144,1024]{1,0:T(8,128)(2,1)S(1)}, bf16[144,1024]{1,0:T(8,128)(2,1)S(1)}, bf16[144,1024]{1,0:T(8,128)(2,1)S(1)}, bf16[144,1024]{1,0:T(8,128)(2,1)S(1)}) custom-call(s32[2]{0:T(128)S(1)} %pad_add_fusion.me, bf16[36,1024]{1,0:T(8,128)(2,1)S(1)} %collective-permute-done.3.b0, ...), custom_call_target="tpu_custom_call" | custom-call | tf_op jit(solution)/shard_map/first_backward/pallas_call | solution.py:417
  42.3 0.1 collective-permute-start.6
  42.4 0.1 collective-permute-start.7
  42.5 1.8 %collective-permute-done.12.refs_1_ = bf16[144,1024]{1,0:T(8,128)(2,1)S(1)} collective-permute-done((bf16[144,1024]{1,0:T(8,128)(2,1)S(1)}, bf16[144,1024]{1,0:T(8,128)(2,1)S(1)}, u32[]{:S(2)}, u32[]{:S(2)}) %collective-permute-start.12) | collective-permute-done | bytes 294944 | tf_op jit(solution)/shard_map/ppermute | solution.py:486
  44.3 1.6 %collective-permute-start.8 = (bf16[144,1024]{1,0:T(8,128)(2,1)S(1)}, bf16[144,1024]{1,0:T(8,128)(2,1)S(1)}, u32[]{:S(2)}, u32[]{:S(2)}) collective-permute-start(bf16[144,1024]{1,0:T(8,128)(2,1)S(1)} %get-tuple-element.60), channel_id=1, source_target_pairs={{0,66},{2,64},{4,70},{6,68},{8,74},{10,72},{12,78},{14,76},{32,98}... | collective-permute-start | bytes 884744 | tf_op jit(solution)/shard_map/ppermute | solution.py:486
  45.9 2.9 %collective-permute-done.13.refs_2_ = bf16[144,1024]{1,0:T(8,128)(2,1)S(1)} collective-permute-done((bf16[144,1024]{1,0:T(8,128)(2,1)S(1)}, bf16[144,1024]{1,0:T(8,128)(2,1)S(1)}, u32[]{:S(2)}, u32[]{:S(2)}) %collective-permute-start.13) | collective-permute-done | bytes 294944 | tf_op jit(solution)/shard_map/ppermute | solution.py:486
  48.8 1.4 %second_weights.1 = (bf16[128,512]{1,0:T(8,128)(2,1)S(1)}, bf16[128,512]{1,0:T(8,128)(2,1)S(1)}, bf16[128,512]{1,0:T(8,128)(2,1)S(1)}, bf16[128,512]{1,0:T(8,128)(2,1)S(1)}) custom-call(s32[2]{0:T(128)S(1)} %pad_add_fusion.me, bf16[144,1024]{1,0:T(8,128)(2,1)S(1)} %get-tuple-element.72.refs_0_, bf16[144,1024]{1,0:T(8,128)(2,1)S(1)} %collective-permute-done.12.refs_1_, ...), custom_call_target="tpu_custom_call" | custom-call | tf_op jit(solution)/shard_map/second_weights/pallas_call | solution.py:417
  50.2 0.7 collective-permute-start.15
  50.9 0.0 collective-permute-start.16
  50.9 0.8 collective-permute-done.6.refs_1_
  51.7 3.5 %collective-permute-start.17 = (bf16[128,512]{1,0:T(8,128)(2,1)S(1)}, bf16[128,512]{1,0:T(8,128)(2,1)S(1)}, u32[]{:S(2)}, u32[]{:S(2)}) collective-permute-start(bf16[128,512]{1,0:T(8,128)(2,1)S(1)} %get-tuple-element.79), channel_id=1, source_target_pairs={{0,18},{2,16},{4,22},{6,20},{8,26},{10,24},{12,30},{14,28},{32,50}... | collective-permute-start | bytes 393224 | tf_op jit(solution)/shard_map/ppermute | solution.py:486
  55.3 2.4 %collective-permute-done.8.refs_3_ = bf16[144,1024]{1,0:T(8,128)(2,1)S(1)} collective-permute-done((bf16[144,1024]{1,0:T(8,128)(2,1)S(1)}, bf16[144,1024]{1,0:T(8,128)(2,1)S(1)}, u32[]{:S(2)}, u32[]{:S(2)}) %collective-permute-start.8) | collective-permute-done | bytes 294944 | tf_op jit(solution)/shard_map/ppermute | solution.py:486
  57.7 1.4 %first_weights.1 = (bf16[128,512]{1,0:T(8,128)(2,1)S(1)}, bf16[128,512]{1,0:T(8,128)(2,1)S(1)}, bf16[128,512]{1,0:T(8,128)(2,1)S(1)}, bf16[128,512]{1,0:T(8,128)(2,1)S(1)}) custom-call(s32[2]{0:T(128)S(1)} %pad_add_fusion.me, bf16[144,1024]{1,0:T(8,128)(2,1)S(1)} %get-tuple-element.57.refs_0_, bf16[144,1024]{1,0:T(8,128)(2,1)S(1)} %collective-permute-done.6.refs_1_, ...), custom_call_target="tpu_custom_call" | custom-call | tf_op jit(solution)/shard_map/first_weights/pallas_call | solution.py:417
  59.1 0.0 copy-start
  59.1 0.0 copy-start.3
  59.1 0.0 copy-start.5
  59.1 0.6 collective-permute-start.10
  59.7 2.5 %collective-permute-start.11 = (bf16[128,512]{1,0:T(8,128)(2,1)S(1)}, bf16[128,512]{1,0:T(8,128)(2,1)S(1)}, u32[]{:S(2)}, u32[]{:S(2)}) collective-permute-start(bf16[128,512]{1,0:T(8,128)(2,1)S(1)} %get-tuple-element.64), channel_id=1, source_target_pairs={{0,48},{2,50},{4,52},{6,54},{8,56},{10,58},{12,60},{14,62},{32,16}... | collective-permute-start | bytes 393224 | tf_op jit(solution)/shard_map/ppermute | solution.py:486
  62.2 0.4 collective-permute-start.9
  62.7 3.1 %collective-permute-done.10.a2 = bf16[128,512]{1,0:T(8,128)(2,1)S(1)} collective-permute-done((bf16[128,512]{1,0:T(8,128)(2,1)S(1)}, bf16[128,512]{1,0:T(8,128)(2,1)S(1)}, u32[]{:S(2)}, u32[]{:S(2)}) %collective-permute-start.10) | collective-permute-done | bytes 131104 | tf_op jit(solution)/shard_map/ppermute | solution.py:486
  65.8 1.3 %collective-permute-done.11.a3 = bf16[128,512]{1,0:T(8,128)(2,1)S(1)} collective-permute-done((bf16[128,512]{1,0:T(8,128)(2,1)S(1)}, bf16[128,512]{1,0:T(8,128)(2,1)S(1)}, u32[]{:S(2)}, u32[]{:S(2)}) %collective-permute-start.11) | collective-permute-done | bytes 131104 | tf_op jit(solution)/shard_map/ppermute | solution.py:486
  67.1 0.1 collective-permute-done.9.a1
  67.2 0.7 add_rows.1
  68.0 15.4 %all_to_all.15.parts = bf16[8,32,512]{2,1,0:T(8,128)(2,1)S(1)} all-to-all(bf16[8,32,512]{2,1,0:T(8,128)(2,1)S(1)} %add_rows.1), channel_id=1, replica_groups={{0,128,4,132,8,136,12,140},{32,160,36,164,40,168,44,172},{16,144,20,148..., dimensions={0} | all-to-all | bytes 524288 | tf_op jit(solution)/shard_map/all_to_all | solution.py:499
  83.3 0.2 to_owners.1
  83.5 12.5 %all_to_all.16.got = bf16[16,48,128]{2,1,0:T(8,128)(2,1)S(1)} all-to-all(bf16[16,48,128]{2,1,0:T(8,128)(2,1)S(1)} %to_owners.1), channel_id=1, replica_groups={{0,64,128,192,32,96,160,224,2,66,130,194,34,98,162,226},{4,68,132,196,3..., dimensions={0} | all-to-all | bytes 393216 | tf_op jit(solution)/shard_map/all_to_all | solution.py:499
  96.0 0.6 spread.1
  96.7 3.9 %all-to-all-start.2 = ((f32[8,8,128]{2,1,0:T(8,128)}), f32[8,8,128]{2,1,0:T(8,128)S(1)}, u32[]{:S(2)}, u32[]{:S(2)}) async-start(f32[8,8,128]{2,1,0:T(8,128)} %spread.1), calls=%async_computation.2 | async-start | bytes 65536 | tf_op jit(solution)/shard_map/all_to_all | solution.py:499
  100.6 1.6 %first_rest.1 = (bf16[6,12,2,512]{3,2,1,0:T(2,128)(2,1)}, bf16[6,12,2,512]{3,2,1,0:T(2,128)(2,1)}) custom-call(bf16[36,1024]{1,0:T(8,128)(2,1)S(1)} %collective-permute-done.3.b0, bf16[36,1024]{1,0:T(8,128)(2,1)S(1)} %collective-permute-done.4.b1, bf16[36,1024]{1,0:T(8,128)(2,1)S(1)} %collective-permute-done.5.b2, ...), custom_call_target="tpu_custom_call" | custom-call | tf_op jit(solution)/shard_map/first_rest/pallas_call | solution.py:417
  102.2 8.5 %all-to-all-done.2.tiles = f32[8,8,128]{2,1,0:T(8,128)S(1)} async-done(((f32[8,8,128]{2,1,0:T(8,128)}), f32[8,8,128]{2,1,0:T(8,128)S(1)}, u32[]{:S(2)}, u32[]{:S(2)}) %all-to-all-start.2) | async-done | bytes 32800 | tf_op jit(solution)/shard_map/all_to_all | solution.py:499
  110.8 1.2 %clipped.1 = (f32[4,1536]{1,0:T(4,128)}, f32[4,512]{1,0:T(4,128)}, f32[4,1536]{1,0:T(4,128)}, f32[4,512]{1,0:T(4,128)}) custom-call(s32[2]{0:T(128)S(1)} %pad_add_fusion.me, bf16[16,48,128]{2,1,0:T(8,128)(2,1)S(1)} %all_to_all.16.got, f32[8,8,128]{2,1,0:T(8,128)S(1)} %all-to-all-done.2.tiles), custom_call_target="tpu_custom_call" | custom-call | tf_op jit(solution)/shard_map/clipped/pallas_call | solution.py:417
  (18 shorter events, 0.0 us)
Async XLA Ops:
  0.6 17.9 %copy-start.6 = (f32[512]{0:T(512)S(1)}, f32[512]{0:T(512)}, u32[]{:S(2)}) copy-start(f32[512]{0:T(512)} %param.15) | copy-start | bytes 6148
  0.6 17.9 %copy-start.2 = (bf16[512,1536]{1,0:T(8,128)(2,1)S(1)}, bf16[512,1536]{1,0:T(8,128)(2,1)}, u32[]{:S(2)}) copy-start(bf16[512,1536]{1,0:T(8,128)(2,1)} %wqkv.2) | copy-start | bytes 4718596
  0.7 17.9 %copy-start.4 = (bf16[512,512]{1,0:T(8,128)(2,1)S(1)}, bf16[512,512]{1,0:T(8,128)(2,1)}, u32[]{:S(2)}) copy-start(bf16[512,512]{1,0:T(8,128)(2,1)} %wout.2) | copy-start | bytes 1572868
  4.9 11.5 %collective-permute-start = (bf16[36,1152]{1,0:T(8,128)(2,1)S(1)}, bf16[36,1152]{1,0:T(8,128)(2,1)S(1)}, u32[]{:S(2)}, u32[]{:S(2)}) collective-permute-start(bf16[36,1152]{1,0:T(8,128)(2,1)S(1)} %get-tuple-element.45), channel_id=1, source_target_pairs={{0,254},{2,224},{4,226},{6,228},{8,230},{10,232},{12,234},{14,236}... | collective-permute-start | bytes 248840 | tf_op jit(solution)/shard_map/ppermute | solution.py:453
  13.7 4.6 %collective-permute-start.1 = (bf16[36,1152]{1,0:T(8,128)(2,1)S(1)}, bf16[36,1152]{1,0:T(8,128)(2,1)S(1)}, u32[]{:S(2)}, u32[]{:S(2)}) collective-permute-start(bf16[36,1152]{1,0:T(8,128)(2,1)S(1)} %get-tuple-element.46), channel_id=1, source_target_pairs={{0,224},{2,226},{4,228},{6,230},{8,232},{10,234},{12,236},{14,238}... | collective-permute-start | bytes 248840 | tf_op jit(solution)/shard_map/ppermute | solution.py:453
  13.8 4.7 %collective-permute-start.2 = (bf16[36,1152]{1,0:T(8,128)(2,1)S(1)}, bf16[36,1152]{1,0:T(8,128)(2,1)S(1)}, u32[]{:S(2)}, u32[]{:S(2)}) collective-permute-start(bf16[36,1152]{1,0:T(8,128)(2,1)S(1)} %get-tuple-element.47), channel_id=1, source_target_pairs={{0,30},{2,0},{4,2},{6,4},{8,6},{10,8},{12,10},{14,12},{16,14},{18,... | collective-permute-start | bytes 248840 | tf_op jit(solution)/shard_map/ppermute | solution.py:453
  18.5 20.4 %copy-start.1 = (bf16[512,512]{1,0:T(8,128)(2,1)S(1)}, bf16[512,512]{1,0:T(8,128)(2,1)}, u32[]{:S(2)}) copy-start(bf16[512,512]{1,0:T(8,128)(2,1)} %wout.3) | copy-start | bytes 1572868
  23.3 10.8 %collective-permute-start.3 = (bf16[36,1024]{1,0:T(8,128)(2,1)S(1)}, bf16[36,1024]{1,0:T(8,128)(2,1)S(1)}, u32[]{:S(2)}, u32[]{:S(2)}) collective-permute-start(bf16[36,1024]{1,0:T(8,128)(2,1)S(1)} %get-tuple-element.49), channel_id=1, source_target_pairs={{254,0},{224,2},{226,4},{228,6},{230,8},{232,10},{234,12},{236,14}... | collective-permute-start | bytes 221192 | tf_op jit(solution)/shard_map/ppermute | solution.py:453
  24.2 9.9 %collective-permute-start.4 = (bf16[36,1024]{1,0:T(8,128)(2,1)S(1)}, bf16[36,1024]{1,0:T(8,128)(2,1)S(1)}, u32[]{:S(2)}, u32[]{:S(2)}) collective-permute-start(bf16[36,1024]{1,0:T(8,128)(2,1)S(1)} %get-tuple-element.50), channel_id=1, source_target_pairs={{224,0},{226,2},{228,4},{230,6},{232,8},{234,10},{236,12},{238,14}... | collective-permute-start | bytes 221192 | tf_op jit(solution)/shard_map/ppermute | solution.py:453
  25.3 8.9 %collective-permute-start.5 = (bf16[36,1024]{1,0:T(8,128)(2,1)S(1)}, bf16[36,1024]{1,0:T(8,128)(2,1)S(1)}, u32[]{:S(2)}, u32[]{:S(2)}) collective-permute-start(bf16[36,1024]{1,0:T(8,128)(2,1)S(1)} %get-tuple-element.51), channel_id=1, source_target_pairs={{30,0},{0,2},{2,4},{4,6},{6,8},{8,10},{10,12},{12,14},{14,16},{16,... | collective-permute-start | bytes 221192 | tf_op jit(solution)/shard_map/ppermute | solution.py:453
  34.2 10.2 %collective-permute-start.12 = (bf16[144,1024]{1,0:T(8,128)(2,1)S(1)}, bf16[144,1024]{1,0:T(8,128)(2,1)S(1)}, u32[]{:S(2)}, u32[]{:S(2)}) collective-permute-start(bf16[144,1024]{1,0:T(8,128)(2,1)S(1)} %get-tuple-element.73), channel_id=1, source_target_pairs={{0,192},{2,194},{4,196},{6,198},{8,200},{10,202},{12,204},{14,206}... | collective-permute-start | bytes 884744 | tf_op jit(solution)/shard_map/ppermute | solution.py:486
  35.3 13.5 %collective-permute-start.13 = (bf16[144,1024]{1,0:T(8,128)(2,1)S(1)}, bf16[144,1024]{1,0:T(8,128)(2,1)S(1)}, u32[]{:S(2)}, u32[]{:S(2)}) collective-permute-start(bf16[144,1024]{1,0:T(8,128)(2,1)S(1)} %get-tuple-element.74), channel_id=1, source_target_pairs={{0,32},{2,34},{4,36},{6,38},{8,40},{10,42},{12,44},{14,46},{32,0},... | collective-permute-start | bytes 884744 | tf_op jit(solution)/shard_map/ppermute | solution.py:486
  37.0 11.8 %collective-permute-start.14 = (bf16[144,1024]{1,0:T(8,128)(2,1)S(1)}, bf16[144,1024]{1,0:T(8,128)(2,1)S(1)}, u32[]{:S(2)}, u32[]{:S(2)}) collective-permute-start(bf16[144,1024]{1,0:T(8,128)(2,1)S(1)} %get-tuple-element.75), channel_id=1, source_target_pairs={{0,224},{2,226},{4,228},{6,230},{8,232},{10,234},{12,236},{14,238}... | collective-permute-start | bytes 884744 | tf_op jit(solution)/shard_map/ppermute | solution.py:486
  42.3 9.4 %collective-permute-start.6 = (bf16[144,1024]{1,0:T(8,128)(2,1)S(1)}, bf16[144,1024]{1,0:T(8,128)(2,1)S(1)}, u32[]{:S(2)}, u32[]{:S(2)}) collective-permute-start(bf16[144,1024]{1,0:T(8,128)(2,1)S(1)} %get-tuple-element.58), channel_id=1, source_target_pairs={{0,64},{2,66},{4,68},{6,70},{8,72},{10,74},{12,76},{14,78},{32,96}... | collective-permute-start | bytes 884744 | tf_op jit(solution)/shard_map/ppermute | solution.py:486
  42.4 12.8 %collective-permute-start.7 = (bf16[144,1024]{1,0:T(8,128)(2,1)S(1)}, bf16[144,1024]{1,0:T(8,128)(2,1)S(1)}, u32[]{:S(2)}, u32[]{:S(2)}) collective-permute-start(bf16[144,1024]{1,0:T(8,128)(2,1)S(1)} %get-tuple-element.59), channel_id=1, source_target_pairs={{0,2},{2,0},{4,6},{6,4},{8,10},{10,8},{12,14},{14,12},{32,34},{34,... | collective-permute-start | bytes 884744 | tf_op jit(solution)/shard_map/ppermute | solution.py:486
  44.3 13.4 %collective-permute-start.8 = (bf16[144,1024]{1,0:T(8,128)(2,1)S(1)}, bf16[144,1024]{1,0:T(8,128)(2,1)S(1)}, u32[]{:S(2)}, u32[]{:S(2)}) collective-permute-start(bf16[144,1024]{1,0:T(8,128)(2,1)S(1)} %get-tuple-element.60), channel_id=1, source_target_pairs={{0,66},{2,64},{4,70},{6,68},{8,74},{10,72},{12,78},{14,76},{32,98}... | collective-permute-start | bytes 884744 | tf_op jit(solution)/shard_map/ppermute | solution.py:486
  50.2 12.1 %collective-permute-start.15 = (bf16[128,512]{1,0:T(8,128)(2,1)S(1)}, bf16[128,512]{1,0:T(8,128)(2,1)S(1)}, u32[]{:S(2)}, u32[]{:S(2)}) collective-permute-start(bf16[128,512]{1,0:T(8,128)(2,1)S(1)} %get-tuple-element.77), channel_id=1, source_target_pairs={{0,16},{2,18},{4,20},{6,22},{8,24},{10,26},{12,28},{14,30},{32,48}... | collective-permute-start | bytes 393224 | tf_op jit(solution)/shard_map/ppermute | solution.py:486
  50.9 11.8 %collective-permute-start.16 = (bf16[128,512]{1,0:T(8,128)(2,1)S(1)}, bf16[128,512]{1,0:T(8,128)(2,1)S(1)}, u32[]{:S(2)}, u32[]{:S(2)}) collective-permute-start(bf16[128,512]{1,0:T(8,128)(2,1)S(1)} %get-tuple-element.78), channel_id=1, source_target_pairs={{0,2},{2,0},{4,6},{6,4},{8,10},{10,8},{12,14},{14,12},{32,34},{34,... | collective-permute-start | bytes 393224 | tf_op jit(solution)/shard_map/ppermute | solution.py:486
  51.7 11.0 %collective-permute-start.17 = (bf16[128,512]{1,0:T(8,128)(2,1)S(1)}, bf16[128,512]{1,0:T(8,128)(2,1)S(1)}, u32[]{:S(2)}, u32[]{:S(2)}) collective-permute-start(bf16[128,512]{1,0:T(8,128)(2,1)S(1)} %get-tuple-element.79), channel_id=1, source_target_pairs={{0,18},{2,16},{4,22},{6,20},{8,26},{10,24},{12,30},{14,28},{32,50}... | collective-permute-start | bytes 393224 | tf_op jit(solution)/shard_map/ppermute | solution.py:486
  59.1 41.5 %copy-start = (bf16[512,1536]{1,0:T(8,128)(2,1)S(1)}, bf16[512,1536]{1,0:T(8,128)(2,1)}, u32[]{:S(2)}) copy-start(bf16[512,1536]{1,0:T(8,128)(2,1)} %wqkv.3) | copy-start | bytes 4718596
  59.1 41.5 %copy-start.3 = (bf16[2,6,12,512]{3,0,2,1:T(2,128)(2,1)S(1)}, bf16[2,6,12,512]{3,0,2,1:T(2,128)(2,1)}, u32[]{:S(2)}) copy-start(bf16[2,6,12,512]{3,0,2,1:T(2,128)(2,1)} %param.9) | copy-start | bytes 442372
  59.1 41.5 %copy-start.5 = (f32[512]{0:T(512)S(1)}, f32[512]{0:T(512)}, u32[]{:S(2)}) copy-start(f32[512]{0:T(512)} %param.12) | copy-start | bytes 6148
  59.1 6.7 %collective-permute-start.10 = (bf16[128,512]{1,0:T(8,128)(2,1)S(1)}, bf16[128,512]{1,0:T(8,128)(2,1)S(1)}, u32[]{:S(2)}, u32[]{:S(2)}) collective-permute-start(bf16[128,512]{1,0:T(8,128)(2,1)S(1)} %get-tuple-element.63), channel_id=1, source_target_pairs={{0,16},{2,18},{4,20},{6,22},{8,24},{10,26},{12,28},{14,30},{32,48}... | collective-permute-start | bytes 393224 | tf_op jit(solution)/shard_map/ppermute | solution.py:486
  59.7 7.3 %collective-permute-start.11 = (bf16[128,512]{1,0:T(8,128)(2,1)S(1)}, bf16[128,512]{1,0:T(8,128)(2,1)S(1)}, u32[]{:S(2)}, u32[]{:S(2)}) collective-permute-start(bf16[128,512]{1,0:T(8,128)(2,1)S(1)} %get-tuple-element.64), channel_id=1, source_target_pairs={{0,48},{2,50},{4,52},{6,54},{8,56},{10,58},{12,60},{14,62},{32,16}... | collective-permute-start | bytes 393224 | tf_op jit(solution)/shard_map/ppermute | solution.py:486
  62.2 5.0 %collective-permute-start.9 = (bf16[128,512]{1,0:T(8,128)(2,1)S(1)}, bf16[128,512]{1,0:T(8,128)(2,1)S(1)}, u32[]{:S(2)}, u32[]{:S(2)}) collective-permute-start(bf16[128,512]{1,0:T(8,128)(2,1)S(1)} %get-tuple-element.62), channel_id=1, source_target_pairs={{0,32},{2,34},{4,36},{6,38},{8,40},{10,42},{12,44},{14,46},{32,0},... | collective-permute-start | bytes 393224 | tf_op jit(solution)/shard_map/ppermute | solution.py:486
  96.7 14.1 %all-to-all-start.2 = ((f32[8,8,128]{2,1,0:T(8,128)}), f32[8,8,128]{2,1,0:T(8,128)S(1)}, u32[]{:S(2)}, u32[]{:S(2)}) async-start(f32[8,8,128]{2,1,0:T(8,128)} %spread.1), calls=%async_computation.2 | async-start | bytes 65536 | tf_op jit(solution)/shard_map/all_to_all | solution.py:499

commit v5 on v4

--- a/solution.py
+++ b/solution.py
@@ -189,8 +189,8 @@
 
 
 def members_second(x, y, z):
-    s = (x + 3) % 4
-    return s % 2 + y % 2 * 2, y // 2 + z % 2 * 2, s // 2 + z // 2 * 2
+    s, w = (x + X - 1) % X, (z + Z - 1) % Z
+    return s % 2 + y % 2 * 2, y // 2 + w % 2 * 2, s // 2 + w // 2 * 2
 
 
 def chip_first(m1, m2, m3):
@@ -198,7 +198,8 @@
 
 
 def chip_second(m1, m2, m3):
-    return (m1 % 2 + m3 % 2 * 2 + 1) % 4, m1 // 2 + m2 % 2 * 2, m2 // 2 + m3 // 2 * 2
+    s, w = m1 % 2 + m3 % 2 * 2, m2 // 2 + m3 // 2 * 2
+    return (s + 1) % X, m1 // 2 + m2 % 2 * 2, (w + 1) % Z
 
 
 def row_order(chip):
@@ -338,13 +339,13 @@
 
 
 def add_rows(me, a0, a1, a2, a3, b0, b1, b2, b3, out_ref, scratch):
-    x, y, z = here(me)
-    flip = members_first(x, y, z)[2] ^ members_second(x, y, z)[2]
+    m1, m2, _ = members_first(*here(me))
     total = sum(part[...].astype(F32) for part in (a0, a1, a2, a3)).astype(BF16)
     scratch[...] = sum(part[...].astype(F32) for part in (b0, b1, b2, b3))
     for last in range(LAST):
         out_ref[last, :LAST_ROWS, :] = total[last * LAST_ROWS : (last + 1) * LAST_ROWS]
-        first = pl.multiple_of((last ^ flip) * LAST_ROWS, LAST_ROWS)
+        place = members_second(*chip_first(m1, m2, last))[2]
+        first = pl.multiple_of(place * LAST_ROWS, LAST_ROWS)
         out_ref[last, LAST_ROWS:, :] = scratch[pl.ds(first, LAST_ROWS), :].astype(BF16)
 
 
@@ -384,24 +385,27 @@
     tile_ref[...] = jnp.broadcast_to(squares[None], tile_ref.shape)
 
 
-def clipped(me, got, tiles, qkv_a, out_a, qkv_b, out_b, scratch):
+def collect(me, got, rows_a, rows_b, scratch):
     scratch[...] = got[:, : 2 * PIECE, :].astype(F32)
+    chip = here(me)
+    _, *numbers_a = members_first(*chip)
+    _, *numbers_b = members_second(*chip)
+    for k in range(GROUP):
+        for slot, source, ref in (
+            (0, near_index(*chip_first(k, *numbers_a)), rows_a),
+            (1, near_index(*chip_second(k, *numbers_b)), rows_b),
+        ):
+            for c in range(WIDE // LANES):
+                first, column = slot * PIECE + c * OWN, k * WIDE + c * LANES
+                ref[:, column : column + LANES] = scratch[source, first : first + OWN, :]
+
+
+def clipped(tiles, rows_a, rows_b, qkv_a, out_a, qkv_b, out_b):
     total = jnp.sum(tiles[...], 0)[:1, :1]
     factor = jnp.minimum(1.0, math.sqrt(8.0) * D / jnp.sqrt(total))
-    chip = here(me)
-    _, *first_rest_of = members_first(*chip)
-    _, *second_rest_of = members_second(*chip)
-    for k in range(GROUP):
-        for slot, source, refs in (
-            (0, near_index(*chip_first(k, *first_rest_of)), (qkv_a, out_a)),
-            (1, near_index(*chip_second(k, *second_rest_of)), (qkv_b, out_b)),
-        ):
-            ref, column = (refs[0], k * WIDE) if k < 3 else (refs[1], 0)
-            for c in range(WIDE // LANES):
-                first = slot * PIECE + c * OWN
-                ref[:, column + c * LANES : column + (c + 1) * LANES] = (
-                    scratch[source, first : first + OWN, :] * factor
-                )
+    for rows, qkv, out in ((rows_a, qkv_a, out_a), (rows_b, qkv_b, out_b)):
+        qkv[...] = rows[:, : 3 * D] * factor
+        out[...] = rows[:, 3 * D :] * factor
 
 
 def shape_of(*dims, dtype=BF16):
@@ -425,6 +429,10 @@
     )(*args)
 
 
+def in_vmem(*arrays):
+    return [pltpu.with_memory_space_constraint(array, pltpu.VMEM) for array in arrays]
+
+
 def in_hbm(*arrays):
     return [pltpu.with_memory_space_constraint(array, pltpu.HBM) for array in arrays]
 
@@ -476,14 +484,14 @@
 
 
 def swap(parts, members, chip, level):
-    out = [parts[0]]
-    for step in range(1, GROUP):
+    out = list(parts)
+    for step in (3, 1, 2):
         pairs = []
         for here_chip in CHIPS:
             numbers = list(members(*here_chip))
             numbers[level] ^= step
             pairs.append((index_of(*here_chip), index_of(*chip(*numbers))))
-        out.append(lax.ppermute(parts[step], ("lat", "lon"), pairs))
+        out[step] = lax.ppermute(parts[step], ("lat", "lon"), pairs)
     return out
 
 
@@ -572,8 +580,8 @@
     result = result.transpose(2, 0, 1, 3)
 
     rows = [shape_of(PLANE_ROWS, WIDE)] * GROUP
-    sum_b = swap_second(call(second_weights, rows, [(D, WIDE)], me, *pack_b, scalar=True), 1)
-    sum_a = swap_first(call(first_weights, rows, [(D, WIDE)], me, *pack_a, scalar=True), 1)
+    sum_b = swap_second(call(second_weights, rows, [(D, WIDE)], me, *in_vmem(*pack_b), scalar=True), 1)
+    sum_a = swap_first(call(first_weights, rows, [(D, WIDE)], me, *in_vmem(*pack_a), scalar=True), 1)
     (sums,) = call(
         add_rows,
         [shape_of(LAST, 2 * LAST_ROWS, WIDE)],
@@ -586,15 +594,12 @@
     (pieces,) = call(to_owners, [shape_of(*piece)], [piece], sums)
     pieces = exchange(pieces, NEAR_GROUPS)
     (tiles,) = call(spread, [shape_of(LAST, 8, LANES, dtype=F32)], [], pieces)
+    pieces = after(pieces, tiles)
     tiles = exchange(tiles, FAR_GROUPS)
+    own = shape_of(OWN, 4 * D, dtype=F32)
+    mine = call(collect, [own, own], [(len(NEAR), 2 * PIECE, LANES)], me, pieces, scalar=True)
     out_qkv, out_out = shape_of(OWN, 3 * D, dtype=F32), shape_of(OWN, D, dtype=F32)
-    clips = call(
-        clipped,
-        [out_qkv, out_out] * 2,
-        [(len(NEAR), 2 * PIECE, LANES)],
-        me, pieces, tiles,
-        scalar=True,
-    )
+    clips = call(clipped, [out_qkv, out_out] * 2, [], tiles, *mine)
     return (result, token_gradient, *clips)
 
 

time: 113 us -> 110 us (0.973)
  waiting for transfers between devices: 31 us -> 27 us
  starting transfers between devices: 31.7 us -> 34.3 us
  blocking collectives: 27.9 us -> 25.8 us
    ppermute x12, waiting for transfers between devices: 12.5 us -> 9.09 us  [swap(): out[step] = lax.ppermute(parts[step], ('lat', 'lon'), pairs)]
    all_to_all x2, blocking collectives: 27.9 us -> 25.8 us  [exchange(): return lax.all_to_all(parts, ('lat', 'lon'), 0, 0, axis_index_groups=groups)]
    ppermute x12, starting transfers between devices: 14.3 us -> 16.3 us  [swap(): out[step] = lax.ppermute(parts[step], ('lat', 'lon'), pairs)]
    pallas_call x11 -> x12, Pallas kernels: 20.6 us -> 20.6 us  [call(): pl.pallas_call(kernel, out_shape=outs, in_specs=specs, out_specs=[whole]...]
  transfers between devices with their start and end apart: 19 -> 19, of which waited for: 11 -> 8; matrix products, arithmetic and copies ran while one was open for 0% -> 0% of each run, Pallas kernels for 8% -> 9%
where the time goes in v5:
time: 110 us; the launch traced here: 109 us
  starting transfers between devices  34.3 us (31%)
  waiting for transfers between devices  27 us (25%)
  blocking collectives  25.8 us (23%)
  Pallas kernels  20.6 us (19%)
    all_to_all x2, blocking collectives, exchange(): return lax.all_to_all(parts, ('lat', 'lon'), 0, 0, axis_index_groups=groups)  25.8 us
    pallas_call x12, Pallas kernels, call(): pl.pallas_call(kernel, out_shape=outs, in_specs=specs, out_specs=[whole]...  20.6 us
    ppermute x12, starting transfers between devices, swap(): out[step] = lax.ppermute(parts[step], ('lat', 'lon'), pairs)  16.3 us
    ppermute x6, starting transfers between devices, send(): out.append(lax.ppermute(part, ('lat', 'lon'), pairs))  13.4 us
    ppermute x6, waiting for transfers between devices, send(): out.append(lax.ppermute(part, ('lat', 'lon'), pairs))  9.95 us
    ppermute x12, waiting for transfers between devices, swap(): out[step] = lax.ppermute(parts[step], ('lat', 'lon'), pairs)  9.09 us
    all_to_all x1, waiting for transfers between devices, exchange(): return lax.all_to_all(parts, ('lat', 'lon'), 0, 0, axis_index_groups=groups)  7.91 us
    all_to_all x1, starting transfers between devices, exchange(): return lax.all_to_all(parts, ('lat', 'lon'), 0, 0, axis_index_groups=groups)  4.55 us
  transfers between devices with their start and end apart: 19, of which 8 were waited for; matrix products, arithmetic and copies ran while one was open for 0% of the time, Pallas kernels for 9%

profile of v5, /device:TPU:0, one launch (start us, length us, event | category | flops | bytes accessed | tf_op | source)
XLA Modules:
  0.0 108.6 jit_solution(2782947993594036771)
XLA Ops:
  0.7 0.1 pad_add_fusion.me
  0.7 4.1 %first_forward.1 = (bf16[36,1152]{1,0:T(8,128)(2,1)S(1)}, bf16[36,1152]{1,0:T(8,128)(2,1)S(1)}, bf16[36,1152]{1,0:T(8,128)(2,1)S(1)}, bf16[36,1152]{1,0:T(8,128)(2,1)S(1)}, bf16[144,2688]{1,0:T(8,128)(2,1)S(1)}) custom-call(s32[2]{0:T(128)S(1)} %pad_add_fusion.me, s32[6,2,12]{2,1,0:T(2,128)} %bitcast.15, bf16[6,12,2,512]{3,2,1,0:T(2,128)(2,1)} %bitcast.9, ...), custom_call_target="tpu_custom_call" | custom-call | tf_op jit(solution)/shard_map/first_forward/pallas_call | solution.py:421
  4.9 8.8 %collective-permute-start = (bf16[36,1152]{1,0:T(8,128)(2,1)S(1)}, bf16[36,1152]{1,0:T(8,128)(2,1)S(1)}, u32[]{:S(2)}, u32[]{:S(2)}) collective-permute-start(bf16[36,1152]{1,0:T(8,128)(2,1)S(1)} %get-tuple-element.48), channel_id=1, source_target_pairs={{0,254},{2,224},{4,226},{6,228},{8,230},{10,232},{12,234},{14,236}... | collective-permute-start | bytes 248840 | tf_op jit(solution)/shard_map/ppermute | solution.py:461
  13.7 0.1 collective-permute-start.1
  13.8 2.5 %collective-permute-start.2 = (bf16[36,1152]{1,0:T(8,128)(2,1)S(1)}, bf16[36,1152]{1,0:T(8,128)(2,1)S(1)}, u32[]{:S(2)}, u32[]{:S(2)}) collective-permute-start(bf16[36,1152]{1,0:T(8,128)(2,1)S(1)} %get-tuple-element.50), channel_id=1, source_target_pairs={{0,30},{2,0},{4,2},{6,4},{8,6},{10,8},{12,10},{14,12},{16,14},{18,... | collective-permute-start | bytes 248840 | tf_op jit(solution)/shard_map/ppermute | solution.py:461
  16.3 0.0 collective-permute-done.x0
  16.3 1.9 %collective-permute-done.1.x1 = bf16[36,1152]{1,0:T(8,128)(2,1)S(1)} collective-permute-done((bf16[36,1152]{1,0:T(8,128)(2,1)S(1)}, bf16[36,1152]{1,0:T(8,128)(2,1)S(1)}, u32[]{:S(2)}, u32[]{:S(2)}) %collective-permute-start.1) | collective-permute-done | bytes 82976 | tf_op jit(solution)/shard_map/ppermute | solution.py:461
  18.2 0.3 collective-permute-done.2.x2
  18.5 4.8 %second_main.1 = (bf16[36,1024]{1,0:T(8,128)(2,1)S(1)}, bf16[36,1024]{1,0:T(8,128)(2,1)S(1)}, bf16[36,1024]{1,0:T(8,128)(2,1)S(1)}, bf16[36,1024]{1,0:T(8,128)(2...) custom-call(bf16[36,1152]{1,0:T(8,128)(2,1)S(1)} %collective-permute-done.x0, ...), custom_call_target="tpu_custom_call" | custom-call | tf_op jit(solution)/shard_map/second_main/pallas_call | solution.py:421
  23.3 0.9 collective-permute-start.3
  24.2 1.0 collective-permute-start.4
  25.3 1.1 %second_pack.1 = (bf16[144,1024]{1,0:T(8,128)(2,1)S(1)}, bf16[144,1024]{1,0:T(8,128)(2,1)S(1)}, bf16[144,1024]{1,0:T(8,128)(2,1)S(1)}, bf16[144,1024]{1,0:T(8,128)(2,1)S(1)}) custom-call(s32[2]{0:T(128)S(1)} %pad_add_fusion.me, bf16[144,512]{1,0:T(8,128)(2,1)S(1)} %get-tuple-element.68.normed, bf16[144,512]{1,0:T(8,128)(2,1)S(1)} %get-tuple-element.69.attended, ...), custom_call_target="tpu_custom_call" | custom-call | tf_op jit(solution)/shard_map/second_pack/pallas_call | solution.py:421
  26.4 7.8 %collective-permute-done.3.b0 = bf16[36,1024]{1,0:T(8,128)(2,1)S(1)} collective-permute-done((bf16[36,1024]{1,0:T(8,128)(2,1)S(1)}, bf16[36,1024]{1,0:T(8,128)(2,1)S(1)}, u32[]{:S(2)}, u32[]{:S(2)}) %collective-permute-start.3) | collective-permute-done | bytes 73760 | tf_op jit(solution)/shard_map/ppermute | solution.py:461
  34.2 0.0 collective-permute-done.5.b2
  34.2 1.1 %collective-permute-start.12 = (bf16[144,1024]{1,0:T(8,128)(2,1)S(1)}, bf16[144,1024]{1,0:T(8,128)(2,1)S(1)}, u32[]{:S(2)}, u32[]{:S(2)}) collective-permute-start(bf16[144,1024]{1,0:T(8,128)(2,1)S(1)} %get-tuple-element.76), channel_id=1, source_target_pairs={{0,192},{2,194},{4,196},{6,198},{8,200},{10,202},{12,204},{14,206}... | collective-permute-start | bytes 884744 | tf_op jit(solution)/shard_map/ppermute | solution.py:494
  35.3 1.7 %collective-permute-start.13 = (bf16[144,1024]{1,0:T(8,128)(2,1)S(1)}, bf16[144,1024]{1,0:T(8,128)(2,1)S(1)}, u32[]{:S(2)}, u32[]{:S(2)}) collective-permute-start(bf16[144,1024]{1,0:T(8,128)(2,1)S(1)} %get-tuple-element.77), channel_id=1, source_target_pairs={{0,32},{2,34},{4,36},{6,38},{8,40},{10,42},{12,44},{14,46},{32,0},... | collective-permute-start | bytes 884744 | tf_op jit(solution)/shard_map/ppermute | solution.py:494
  37.0 1.8 %collective-permute-start.14 = (bf16[144,1024]{1,0:T(8,128)(2,1)S(1)}, bf16[144,1024]{1,0:T(8,128)(2,1)S(1)}, u32[]{:S(2)}, u32[]{:S(2)}) collective-permute-start(bf16[144,1024]{1,0:T(8,128)(2,1)S(1)} %get-tuple-element.78), channel_id=1, source_target_pairs={{0,224},{2,226},{4,228},{6,230},{8,232},{10,234},{12,236},{14,238}... | collective-permute-start | bytes 884744 | tf_op jit(solution)/shard_map/ppermute | solution.py:494
  38.9 3.5 %first_backward.1 = (bf16[4,144,512]{2,1,0:T(8,128)(2,1)S(1)}, bf16[144,1024]{1,0:T(8,128)(2,1)S(1)}, bf16[144,1024]{1,0:T(8,128)(2,1)S(1)}, bf16[144,1024]{1,0:T(8,128)(2,1)S(1)}, bf16[144,1024]{1,0:T(8,128)(2,1)S(1)}) custom-call(s32[2]{0:T(128)S(1)} %pad_add_fusion.me, bf16[36,1024]{1,0:T(8,128)(2,1)S(1)} %collective-permute-done.3.b0, ...), custom_call_target="tpu_custom_call" | custom-call | tf_op jit(solution)/shard_map/first_backward/pallas_call | solution.py:421
  42.3 0.1 collective-permute-start.6
  42.4 0.1 collective-permute-start.7
  42.5 1.8 %collective-permute-done.12.refs_1_ = bf16[144,1024]{1,0:T(8,128)(2,1)S(1)} collective-permute-done((bf16[144,1024]{1,0:T(8,128)(2,1)S(1)}, bf16[144,1024]{1,0:T(8,128)(2,1)S(1)}, u32[]{:S(2)}, u32[]{:S(2)}) %collective-permute-start.12) | collective-permute-done | bytes 294944 | tf_op jit(solution)/shard_map/ppermute | solution.py:494
  44.3 1.6 %collective-permute-start.8 = (bf16[144,1024]{1,0:T(8,128)(2,1)S(1)}, bf16[144,1024]{1,0:T(8,128)(2,1)S(1)}, u32[]{:S(2)}, u32[]{:S(2)}) collective-permute-start(bf16[144,1024]{1,0:T(8,128)(2,1)S(1)} %get-tuple-element.63), channel_id=1, source_target_pairs={{0,66},{2,64},{4,70},{6,68},{8,74},{10,72},{12,78},{14,76},{32,98}... | collective-permute-start | bytes 884744 | tf_op jit(solution)/shard_map/ppermute | solution.py:494
  45.9 2.9 %collective-permute-done.13.refs_2_ = bf16[144,1024]{1,0:T(8,128)(2,1)S(1)} collective-permute-done((bf16[144,1024]{1,0:T(8,128)(2,1)S(1)}, bf16[144,1024]{1,0:T(8,128)(2,1)S(1)}, u32[]{:S(2)}, u32[]{:S(2)}) %collective-permute-start.13) | collective-permute-done | bytes 294944 | tf_op jit(solution)/shard_map/ppermute | solution.py:494
  48.8 1.4 %second_weights.1 = (bf16[128,512]{1,0:T(8,128)(2,1)S(1)}, bf16[128,512]{1,0:T(8,128)(2,1)S(1)}, bf16[128,512]{1,0:T(8,128)(2,1)S(1)}, bf16[128,512]{1,0:T(8,128)(2,1)S(1)}) custom-call(s32[2]{0:T(128)S(1)} %pad_add_fusion.me, bf16[144,1024]{1,0:T(8,128)(2,1)S(1)} %get-tuple-element.75.refs_0_, bf16[144,1024]{1,0:T(8,128)(2,1)S(1)} %collective-permute-done.12.refs_1_, ...), custom_call_target="tpu_custom_call" | custom-call | tf_op jit(solution)/shard_map/second_weights/pallas_call | solution.py:421
  50.2 0.7 collective-permute-start.15
  50.9 1.3 %collective-permute-start.16 = (bf16[128,512]{1,0:T(8,128)(2,1)S(1)}, bf16[128,512]{1,0:T(8,128)(2,1)S(1)}, u32[]{:S(2)}, u32[]{:S(2)}) collective-permute-start(bf16[128,512]{1,0:T(8,128)(2,1)S(1)} %get-tuple-element.81), channel_id=1, source_target_pairs={{0,14},{2,4},{4,2},{6,8},{8,6},{10,12},{12,10},{14,0},{32,46},{34,... | collective-permute-start | bytes 393224 | tf_op jit(solution)/shard_map/ppermute | solution.py:494
  52.2 0.0 collective-permute-done.6.refs_1_
  52.2 4.2 %collective-permute-start.17 = (bf16[128,512]{1,0:T(8,128)(2,1)S(1)}, bf16[128,512]{1,0:T(8,128)(2,1)S(1)}, u32[]{:S(2)}, u32[]{:S(2)}) collective-permute-start(bf16[128,512]{1,0:T(8,128)(2,1)S(1)} %get-tuple-element.82), channel_id=1, source_target_pairs={{0,30},{2,20},{4,18},{6,24},{8,22},{10,28},{12,26},{14,16},{32,62}... | collective-permute-start | bytes 393224 | tf_op jit(solution)/shard_map/ppermute | solution.py:494
  56.5 0.0 collective-permute-done.7.refs_2_
  56.5 1.4 %first_weights.1 = (bf16[128,512]{1,0:T(8,128)(2,1)S(1)}, bf16[128,512]{1,0:T(8,128)(2,1)S(1)}, bf16[128,512]{1,0:T(8,128)(2,1)S(1)}, bf16[128,512]{1,0:T(8,128)(2,1)S(1)}) custom-call(s32[2]{0:T(128)S(1)} %pad_add_fusion.me, bf16[144,1024]{1,0:T(8,128)(2,1)S(1)} %get-tuple-element.60.refs_0_, bf16[144,1024]{1,0:T(8,128)(2,1)S(1)} %collective-permute-done.6.refs_1_, ...), custom_call_target="tpu_custom_call" | custom-call | tf_op jit(solution)/shard_map/first_weights/pallas_call | solution.py:421
  57.8 0.0 copy-start
  57.9 0.0 copy-start.3
  57.9 0.0 copy-start.5
  57.9 0.7 collective-permute-start.10
  58.6 2.2 %collective-permute-start.11 = (bf16[128,512]{1,0:T(8,128)(2,1)S(1)}, bf16[128,512]{1,0:T(8,128)(2,1)S(1)}, u32[]{:S(2)}, u32[]{:S(2)}) collective-permute-start(bf16[128,512]{1,0:T(8,128)(2,1)S(1)} %get-tuple-element.67), channel_id=1, source_target_pairs={{0,48},{2,50},{4,52},{6,54},{8,56},{10,58},{12,60},{14,62},{32,16}... | collective-permute-start | bytes 393224 | tf_op jit(solution)/shard_map/ppermute | solution.py:494
  60.8 0.6 collective-permute-start.9
  61.5 3.1 %collective-permute-done.10.a2 = bf16[128,512]{1,0:T(8,128)(2,1)S(1)} collective-permute-done((bf16[128,512]{1,0:T(8,128)(2,1)S(1)}, bf16[128,512]{1,0:T(8,128)(2,1)S(1)}, u32[]{:S(2)}, u32[]{:S(2)}) %collective-permute-start.10) | collective-permute-done | bytes 131104 | tf_op jit(solution)/shard_map/ppermute | solution.py:494
  64.5 1.3 %collective-permute-done.11.a3 = bf16[128,512]{1,0:T(8,128)(2,1)S(1)} collective-permute-done((bf16[128,512]{1,0:T(8,128)(2,1)S(1)}, bf16[128,512]{1,0:T(8,128)(2,1)S(1)}, u32[]{:S(2)}, u32[]{:S(2)}) %collective-permute-start.11) | collective-permute-done | bytes 131104 | tf_op jit(solution)/shard_map/ppermute | solution.py:494
  65.8 0.7 add_rows.1
  66.6 14.3 %all_to_all.15.parts = bf16[8,32,512]{2,1,0:T(8,128)(2,1)S(1)} all-to-all(bf16[8,32,512]{2,1,0:T(8,128)(2,1)S(1)} %add_rows.1), channel_id=1, replica_groups={{0,128,4,132,8,136,12,140},{32,160,36,164,40,168,44,172},{16,144,20,148..., dimensions={0} | all-to-all | bytes 524288 | tf_op jit(solution)/shard_map/all_to_all | solution.py:507
  80.9 0.2 to_owners.1
  81.1 11.5 %all_to_all.16.got = bf16[16,48,128]{2,1,0:T(8,128)(2,1)S(1)} all-to-all(bf16[16,48,128]{2,1,0:T(8,128)(2,1)S(1)} %to_owners.1), channel_id=1, replica_groups={{0,64,128,192,32,96,160,224,2,66,130,194,34,98,162,226},{4,68,132,196,3..., dimensions={0} | all-to-all | bytes 393216 | tf_op jit(solution)/shard_map/all_to_all | solution.py:507
  92.5 0.6 spread.1
  93.2 4.6 %all-to-all-start.2 = ((f32[8,8,128]{2,1,0:T(8,128)}), f32[8,8,128]{2,1,0:T(8,128)S(1)}, u32[]{:S(2)}, u32[]{:S(2)}) async-start(f32[8,8,128]{2,1,0:T(8,128)} %spread.1), calls=%async_computation.2 | async-start | bytes 65536 | tf_op jit(solution)/shard_map/all_to_all | solution.py:507
  97.8 1.6 %first_rest.1 = (bf16[6,12,2,512]{3,2,1,0:T(2,128)(2,1)}, bf16[6,12,2,512]{3,2,1,0:T(2,128)(2,1)}) custom-call(bf16[36,1024]{1,0:T(8,128)(2,1)S(1)} %collective-permute-done.3.b0, bf16[36,1024]{1,0:T(8,128)(2,1)S(1)} %collective-permute-done.4.b1, bf16[36,1024]{1,0:T(8,128)(2,1)S(1)} %collective-permute-done.5.b2, ...), custom_call_target="tpu_custom_call" | custom-call | tf_op jit(solution)/shard_map/first_rest/pallas_call | solution.py:421
  99.4 0.6 collect.1
  100.0 7.9 %all-to-all-done.2.tiles = f32[8,8,128]{2,1,0:T(8,128)S(1)} async-done(((f32[8,8,128]{2,1,0:T(8,128)}), f32[8,8,128]{2,1,0:T(8,128)S(1)}, u32[]{:S(2)}, u32[]{:S(2)}) %all-to-all-start.2) | async-done | bytes 32800 | tf_op jit(solution)/shard_map/all_to_all | solution.py:507
  107.9 0.7 clipped.1
  (19 shorter events, 0.0 us)
Async XLA Ops:
  0.6 17.9 %copy-start.6 = (f32[512]{0:T(512)S(1)}, f32[512]{0:T(512)}, u32[]{:S(2)}) copy-start(f32[512]{0:T(512)} %param.15) | copy-start | bytes 6148
  0.6 17.9 %copy-start.2 = (bf16[512,1536]{1,0:T(8,128)(2,1)S(1)}, bf16[512,1536]{1,0:T(8,128)(2,1)}, u32[]{:S(2)}) copy-start(bf16[512,1536]{1,0:T(8,128)(2,1)} %wqkv.2) | copy-start | bytes 4718596
  0.7 17.9 %copy-start.4 = (bf16[512,512]{1,0:T(8,128)(2,1)S(1)}, bf16[512,512]{1,0:T(8,128)(2,1)}, u32[]{:S(2)}) copy-start(bf16[512,512]{1,0:T(8,128)(2,1)} %wout.2) | copy-start | bytes 1572868
  4.9 11.5 %collective-permute-start = (bf16[36,1152]{1,0:T(8,128)(2,1)S(1)}, bf16[36,1152]{1,0:T(8,128)(2,1)S(1)}, u32[]{:S(2)}, u32[]{:S(2)}) collective-permute-start(bf16[36,1152]{1,0:T(8,128)(2,1)S(1)} %get-tuple-element.48), channel_id=1, source_target_pairs={{0,254},{2,224},{4,226},{6,228},{8,230},{10,232},{12,234},{14,236}... | collective-permute-start | bytes 248840 | tf_op jit(solution)/shard_map/ppermute | solution.py:461
  13.7 4.6 %collective-permute-start.1 = (bf16[36,1152]{1,0:T(8,128)(2,1)S(1)}, bf16[36,1152]{1,0:T(8,128)(2,1)S(1)}, u32[]{:S(2)}, u32[]{:S(2)}) collective-permute-start(bf16[36,1152]{1,0:T(8,128)(2,1)S(1)} %get-tuple-element.49), channel_id=1, source_target_pairs={{0,224},{2,226},{4,228},{6,230},{8,232},{10,234},{12,236},{14,238}... | collective-permute-start | bytes 248840 | tf_op jit(solution)/shard_map/ppermute | solution.py:461
  13.8 4.7 %collective-permute-start.2 = (bf16[36,1152]{1,0:T(8,128)(2,1)S(1)}, bf16[36,1152]{1,0:T(8,128)(2,1)S(1)}, u32[]{:S(2)}, u32[]{:S(2)}) collective-permute-start(bf16[36,1152]{1,0:T(8,128)(2,1)S(1)} %get-tuple-element.50), channel_id=1, source_target_pairs={{0,30},{2,0},{4,2},{6,4},{8,6},{10,8},{12,10},{14,12},{16,14},{18,... | collective-permute-start | bytes 248840 | tf_op jit(solution)/shard_map/ppermute | solution.py:461
  18.5 20.4 %copy-start.1 = (bf16[512,512]{1,0:T(8,128)(2,1)S(1)}, bf16[512,512]{1,0:T(8,128)(2,1)}, u32[]{:S(2)}) copy-start(bf16[512,512]{1,0:T(8,128)(2,1)} %wout.3) | copy-start | bytes 1572868
  23.3 10.8 %collective-permute-start.3 = (bf16[36,1024]{1,0:T(8,128)(2,1)S(1)}, bf16[36,1024]{1,0:T(8,128)(2,1)S(1)}, u32[]{:S(2)}, u32[]{:S(2)}) collective-permute-start(bf16[36,1024]{1,0:T(8,128)(2,1)S(1)} %get-tuple-element.52), channel_id=1, source_target_pairs={{254,0},{224,2},{226,4},{228,6},{230,8},{232,10},{234,12},{236,14}... | collective-permute-start | bytes 221192 | tf_op jit(solution)/shard_map/ppermute | solution.py:461
  24.2 9.9 %collective-permute-start.4 = (bf16[36,1024]{1,0:T(8,128)(2,1)S(1)}, bf16[36,1024]{1,0:T(8,128)(2,1)S(1)}, u32[]{:S(2)}, u32[]{:S(2)}) collective-permute-start(bf16[36,1024]{1,0:T(8,128)(2,1)S(1)} %get-tuple-element.53), channel_id=1, source_target_pairs={{224,0},{226,2},{228,4},{230,6},{232,8},{234,10},{236,12},{238,14}... | collective-permute-start | bytes 221192 | tf_op jit(solution)/shard_map/ppermute | solution.py:461
  25.3 8.9 %collective-permute-start.5 = (bf16[36,1024]{1,0:T(8,128)(2,1)S(1)}, bf16[36,1024]{1,0:T(8,128)(2,1)S(1)}, u32[]{:S(2)}, u32[]{:S(2)}) collective-permute-start(bf16[36,1024]{1,0:T(8,128)(2,1)S(1)} %get-tuple-element.54), channel_id=1, source_target_pairs={{30,0},{0,2},{2,4},{4,6},{6,8},{8,10},{10,12},{12,14},{14,16},{16,... | collective-permute-start | bytes 221192 | tf_op jit(solution)/shard_map/ppermute | solution.py:461
  34.2 10.2 %collective-permute-start.12 = (bf16[144,1024]{1,0:T(8,128)(2,1)S(1)}, bf16[144,1024]{1,0:T(8,128)(2,1)S(1)}, u32[]{:S(2)}, u32[]{:S(2)}) collective-permute-start(bf16[144,1024]{1,0:T(8,128)(2,1)S(1)} %get-tuple-element.76), channel_id=1, source_target_pairs={{0,192},{2,194},{4,196},{6,198},{8,200},{10,202},{12,204},{14,206}... | collective-permute-start | bytes 884744 | tf_op jit(solution)/shard_map/ppermute | solution.py:494
  35.3 13.5 %collective-permute-start.13 = (bf16[144,1024]{1,0:T(8,128)(2,1)S(1)}, bf16[144,1024]{1,0:T(8,128)(2,1)S(1)}, u32[]{:S(2)}, u32[]{:S(2)}) collective-permute-start(bf16[144,1024]{1,0:T(8,128)(2,1)S(1)} %get-tuple-element.77), channel_id=1, source_target_pairs={{0,32},{2,34},{4,36},{6,38},{8,40},{10,42},{12,44},{14,46},{32,0},... | collective-permute-start | bytes 884744 | tf_op jit(solution)/shard_map/ppermute | solution.py:494
  37.0 11.8 %collective-permute-start.14 = (bf16[144,1024]{1,0:T(8,128)(2,1)S(1)}, bf16[144,1024]{1,0:T(8,128)(2,1)S(1)}, u32[]{:S(2)}, u32[]{:S(2)}) collective-permute-start(bf16[144,1024]{1,0:T(8,128)(2,1)S(1)} %get-tuple-element.78), channel_id=1, source_target_pairs={{0,224},{2,226},{4,228},{6,230},{8,232},{10,234},{12,236},{14,238}... | collective-permute-start | bytes 884744 | tf_op jit(solution)/shard_map/ppermute | solution.py:494
  42.3 9.9 %collective-permute-start.6 = (bf16[144,1024]{1,0:T(8,128)(2,1)S(1)}, bf16[144,1024]{1,0:T(8,128)(2,1)S(1)}, u32[]{:S(2)}, u32[]{:S(2)}) collective-permute-start(bf16[144,1024]{1,0:T(8,128)(2,1)S(1)} %get-tuple-element.61), channel_id=1, source_target_pairs={{0,64},{2,66},{4,68},{6,70},{8,72},{10,74},{12,76},{14,78},{32,96}... | collective-permute-start | bytes 884744 | tf_op jit(solution)/shard_map/ppermute | solution.py:494
  42.4 14.0 %collective-permute-start.7 = (bf16[144,1024]{1,0:T(8,128)(2,1)S(1)}, bf16[144,1024]{1,0:T(8,128)(2,1)S(1)}, u32[]{:S(2)}, u32[]{:S(2)}) collective-permute-start(bf16[144,1024]{1,0:T(8,128)(2,1)S(1)} %get-tuple-element.62), channel_id=1, source_target_pairs={{0,2},{2,0},{4,6},{6,4},{8,10},{10,8},{12,14},{14,12},{32,34},{34,... | collective-permute-start | bytes 884744 | tf_op jit(solution)/shard_map/ppermute | solution.py:494
  44.3 12.1 %collective-permute-start.8 = (bf16[144,1024]{1,0:T(8,128)(2,1)S(1)}, bf16[144,1024]{1,0:T(8,128)(2,1)S(1)}, u32[]{:S(2)}, u32[]{:S(2)}) collective-permute-start(bf16[144,1024]{1,0:T(8,128)(2,1)S(1)} %get-tuple-element.63), channel_id=1, source_target_pairs={{0,66},{2,64},{4,70},{6,68},{8,74},{10,72},{12,78},{14,76},{32,98}... | collective-permute-start | bytes 884744 | tf_op jit(solution)/shard_map/ppermute | solution.py:494
  50.2 10.7 %collective-permute-start.15 = (bf16[128,512]{1,0:T(8,128)(2,1)S(1)}, bf16[128,512]{1,0:T(8,128)(2,1)S(1)}, u32[]{:S(2)}, u32[]{:S(2)}) collective-permute-start(bf16[128,512]{1,0:T(8,128)(2,1)S(1)} %get-tuple-element.80), channel_id=1, source_target_pairs={{0,16},{2,18},{4,20},{6,22},{8,24},{10,26},{12,28},{14,30},{32,48}... | collective-permute-start | bytes 393224 | tf_op jit(solution)/shard_map/ppermute | solution.py:494
  50.9 10.6 %collective-permute-start.16 = (bf16[128,512]{1,0:T(8,128)(2,1)S(1)}, bf16[128,512]{1,0:T(8,128)(2,1)S(1)}, u32[]{:S(2)}, u32[]{:S(2)}) collective-permute-start(bf16[128,512]{1,0:T(8,128)(2,1)S(1)} %get-tuple-element.81), channel_id=1, source_target_pairs={{0,14},{2,4},{4,2},{6,8},{8,6},{10,12},{12,10},{14,0},{32,46},{34,... | collective-permute-start | bytes 393224 | tf_op jit(solution)/shard_map/ppermute | solution.py:494
  52.2 9.2 %collective-permute-start.17 = (bf16[128,512]{1,0:T(8,128)(2,1)S(1)}, bf16[128,512]{1,0:T(8,128)(2,1)S(1)}, u32[]{:S(2)}, u32[]{:S(2)}) collective-permute-start(bf16[128,512]{1,0:T(8,128)(2,1)S(1)} %get-tuple-element.82), channel_id=1, source_target_pairs={{0,30},{2,20},{4,18},{6,24},{8,22},{10,28},{12,26},{14,16},{32,62}... | collective-permute-start | bytes 393224 | tf_op jit(solution)/shard_map/ppermute | solution.py:494
  57.8 39.9 %copy-start = (bf16[512,1536]{1,0:T(8,128)(2,1)S(1)}, bf16[512,1536]{1,0:T(8,128)(2,1)}, u32[]{:S(2)}) copy-start(bf16[512,1536]{1,0:T(8,128)(2,1)} %wqkv.3) | copy-start | bytes 4718596
  57.9 39.9 %copy-start.3 = (bf16[2,6,12,512]{3,0,2,1:T(2,128)(2,1)S(1)}, bf16[2,6,12,512]{3,0,2,1:T(2,128)(2,1)}, u32[]{:S(2)}) copy-start(bf16[2,6,12,512]{3,0,2,1:T(2,128)(2,1)} %param.9) | copy-start | bytes 442372
  57.9 39.9 %copy-start.5 = (f32[512]{0:T(512)S(1)}, f32[512]{0:T(512)}, u32[]{:S(2)}) copy-start(f32[512]{0:T(512)} %param.12) | copy-start | bytes 6148
  57.9 6.7 %collective-permute-start.10 = (bf16[128,512]{1,0:T(8,128)(2,1)S(1)}, bf16[128,512]{1,0:T(8,128)(2,1)S(1)}, u32[]{:S(2)}, u32[]{:S(2)}) collective-permute-start(bf16[128,512]{1,0:T(8,128)(2,1)S(1)} %get-tuple-element.66), channel_id=1, source_target_pairs={{0,16},{2,18},{4,20},{6,22},{8,24},{10,26},{12,28},{14,30},{32,48}... | collective-permute-start | bytes 393224 | tf_op jit(solution)/shard_map/ppermute | solution.py:494
  58.6 7.2 %collective-permute-start.11 = (bf16[128,512]{1,0:T(8,128)(2,1)S(1)}, bf16[128,512]{1,0:T(8,128)(2,1)S(1)}, u32[]{:S(2)}, u32[]{:S(2)}) collective-permute-start(bf16[128,512]{1,0:T(8,128)(2,1)S(1)} %get-tuple-element.67), channel_id=1, source_target_pairs={{0,48},{2,50},{4,52},{6,54},{8,56},{10,58},{12,60},{14,62},{32,16}... | collective-permute-start | bytes 393224 | tf_op jit(solution)/shard_map/ppermute | solution.py:494
  60.8 5.0 %collective-permute-start.9 = (bf16[128,512]{1,0:T(8,128)(2,1)S(1)}, bf16[128,512]{1,0:T(8,128)(2,1)S(1)}, u32[]{:S(2)}, u32[]{:S(2)}) collective-permute-start(bf16[128,512]{1,0:T(8,128)(2,1)S(1)} %get-tuple-element.65), channel_id=1, source_target_pairs={{0,32},{2,34},{4,36},{6,38},{8,40},{10,42},{12,44},{14,46},{32,0},... | collective-permute-start | bytes 393224 | tf_op jit(solution)/shard_map/ppermute | solution.py:494
  93.2 14.7 %all-to-all-start.2 = ((f32[8,8,128]{2,1,0:T(8,128)}), f32[8,8,128]{2,1,0:T(8,128)S(1)}, u32[]{:S(2)}, u32[]{:S(2)}) async-start(f32[8,8,128]{2,1,0:T(8,128)} %spread.1), calls=%async_computation.2 | async-start | bytes 65536 | tf_op jit(solution)/shard_map/all_to_all | solution.py:507

commit v6 on v5

--- a/solution.py
+++ b/solution.py
@@ -184,13 +184,18 @@
     return lat // YLO, lon // Z * YLO + lat % YLO, lon % Z
 
 
+def squares(x, z):
+    return x % 2 + z % 2 * 2, x // 2 + z // 2 * 2
+
+
 def members_first(x, y, z):
-    return x % 2 + z % 2 * 2, y, x // 2 + z // 2 * 2
+    m1, m3 = squares(x, z)
+    return m1, y, m3
 
 
 def members_second(x, y, z):
-    s, w = (x + X - 1) % X, (z + Z - 1) % Z
-    return s % 2 + y % 2 * 2, y // 2 + w % 2 * 2, s // 2 + w // 2 * 2
+    m1, m3 = squares((x + X - 1) % X, (z + Z - 1) % Z)
+    return m1, y, m3
 
 
 def chip_first(m1, m2, m3):
@@ -198,8 +203,8 @@
 
 
 def chip_second(m1, m2, m3):
-    s, w = m1 % 2 + m3 % 2 * 2, m2 // 2 + m3 // 2 * 2
-    return (s + 1) % X, m1 // 2 + m2 % 2 * 2, (w + 1) % Z
+    x, y, z = chip_first(m1, m2, m3)
+    return (x + 1) % X, y, (z + 1) % Z
 
 
 def row_order(chip):
@@ -324,7 +329,10 @@
 
 
 def weights(member, p0, p1, p2, p3, q0, q1, q2, q3, scratch):
-    scratch[...] = sum(dot_tn(part[:, :D], part[:, D:]) for part in (p0, p1, p2, p3))
+    total = jnp.zeros((D, WIDE), F32)
+    for part in (p0, p1, p2, p3):
+        total += dot_tn(part[:, :D], part[:, D:])
+    scratch[...] = total
     for step, ref in enumerate((q0, q1, q2, q3)):
         first = pl.multiple_of((member ^ step) * PLANE_ROWS, PLANE_ROWS)
         ref[...] = scratch[pl.ds(first, PLANE_ROWS), :].astype(BF16)
@@ -338,74 +346,50 @@
     weights(members_second(*here(me))[1], *refs)
 
 
-def add_rows(me, a0, a1, a2, a3, b0, b1, b2, b3, out_ref, scratch):
-    m1, m2, _ = members_first(*here(me))
-    total = sum(part[...].astype(F32) for part in (a0, a1, a2, a3)).astype(BF16)
-    scratch[...] = sum(part[...].astype(F32) for part in (b0, b1, b2, b3))
-    for last in range(LAST):
-        out_ref[last, :LAST_ROWS, :] = total[last * LAST_ROWS : (last + 1) * LAST_ROWS]
-        place = members_second(*chip_first(m1, m2, last))[2]
-        first = pl.multiple_of(place * LAST_ROWS, LAST_ROWS)
-        out_ref[last, LAST_ROWS:, :] = scratch[pl.ds(first, LAST_ROWS), :].astype(BF16)
-
-
 PIECE = OWN * WIDE // LANES
-NEAR = [(x, y, z) for z in range(2) for y in range(YLO) for x in range(X)]
-
-
-def near_index(x, y, z):
-    return x + y % YLO * X + z % 2 * X * YLO
-
-
-def to_owners(parts, send_ref, scratch):
-    total = jnp.sum(parts[...].astype(F32), 0)
-    rest = jnp.sum(total * total, keepdims=True)
-    terms = []
-    for _ in range(3):
-        term = rest.astype(BF16).astype(F32)
-        terms.append(term)
-        rest = rest - term
-    terms = jnp.concatenate([jnp.broadcast_to(term, (1, LANES)) for term in terms], 0)
-    for peer, chip in enumerate(NEAR):
-        rows = (members_first(*chip)[0] * OWN, LAST_ROWS + members_second(*chip)[0] * OWN)
-        for slot, row in enumerate(rows):
+SHEET = [(x, z) for x in range(X) for z in range(Z)]
+
+
+def add_rows(a0, a1, a2, a3, b0, b1, b2, b3, out_ref, scratch):
+    blocks = ((members_first, (a0, a1, a2, a3)), (members_second, (b0, b1, b2, b3)))
+    for slot, (members, parts) in enumerate(blocks):
+        total = sum(part[...].astype(F32) for part in parts)
+        for peer, (x, z) in enumerate(SHEET):
+            m1, _, m3 = members(x, 0, z)
+            row = (m3 * GROUP + m1) * OWN
             for c in range(WIDE // LANES):
                 first = slot * PIECE + c * OWN
                 scratch[peer, first : first + OWN, :] = total[
                     row : row + OWN, c * LANES : (c + 1) * LANES
                 ]
-        scratch[peer, 2 * PIECE :, :] = jnp.zeros((16, LANES), F32)
-        scratch[peer, 2 * PIECE : 2 * PIECE + 3, :] = terms
-    send_ref[...] = scratch[...].astype(BF16)
-
-
-def spread(got, tile_ref):
-    terms = jnp.sum(got[:, 2 * PIECE :, :].astype(F32), 0)
-    squares = jnp.sum(terms, 0, keepdims=True)
-    tile_ref[...] = jnp.broadcast_to(squares[None], tile_ref.shape)
-
-
-def collect(me, got, rows_a, rows_b, scratch):
-    scratch[...] = got[:, : 2 * PIECE, :].astype(F32)
-    chip = here(me)
-    _, *numbers_a = members_first(*chip)
-    _, *numbers_b = members_second(*chip)
-    for k in range(GROUP):
-        for slot, source, ref in (
-            (0, near_index(*chip_first(k, *numbers_a)), rows_a),
-            (1, near_index(*chip_second(k, *numbers_b)), rows_b),
-        ):
-            for c in range(WIDE // LANES):
-                first, column = slot * PIECE + c * OWN, k * WIDE + c * LANES
-                ref[:, column : column + LANES] = scratch[source, first : first + OWN, :]
-
-
-def clipped(tiles, rows_a, rows_b, qkv_a, out_a, qkv_b, out_b):
+    out_ref[...] = scratch[...].astype(BF16)
+
+
+def own_rows(parts, rows_ref, tile_ref):
+    norm = jnp.zeros((1, 1), F32)
+    for slot, members in enumerate((members_first, members_second)):
+        totals = [jnp.zeros((PIECE, LANES), F32)] * GROUP
+        for source, (x, z) in enumerate(SHEET):
+            m1 = members(x, 0, z)[0]
+            piece = parts[source, slot * PIECE : (slot + 1) * PIECE, :]
+            totals[m1] = totals[m1] + piece.astype(F32)
+        for m1, total in enumerate(totals):
+            rows_ref[m1, slot * PIECE : (slot + 1) * PIECE, :] = total
+        norm += jnp.sum(sum(total * total for total in totals), keepdims=True)
+    tile_ref[...] = jnp.broadcast_to(norm[None], tile_ref.shape)
+
+
+def clipped(tiles, rows, qkv_a, out_a, qkv_b, out_b):
     total = jnp.sum(tiles[...], 0)[:1, :1]
     factor = jnp.minimum(1.0, math.sqrt(8.0) * D / jnp.sqrt(total))
-    for rows, qkv, out in ((rows_a, qkv_a, out_a), (rows_b, qkv_b, out_b)):
-        qkv[...] = rows[:, : 3 * D] * factor
-        out[...] = rows[:, 3 * D :] * factor
+    for slot, refs in enumerate(((qkv_a, out_a), (qkv_b, out_b))):
+        for k in range(GROUP):
+            ref, column = (refs[0], k * WIDE) if k < GROUP - 1 else (refs[1], 0)
+            for c in range(WIDE // LANES):
+                first = slot * PIECE + c * OWN
+                ref[:, column + c * LANES : column + (c + 1) * LANES] = (
+                    rows[k, first : first + OWN, :] * factor
+                )
 
 
 def shape_of(*dims, dtype=BF16):
@@ -469,18 +453,7 @@
 CHIPS = [(x, y, z) for x in range(X) for y in range(Y) for z in range(Z)]
 
 
-def groups_of(key, order):
-    table = {}
-    for chip in sorted(CHIPS, key=order):
-        table.setdefault(key(*chip), []).append(index_of(*chip))
-    return [table[k] for k in sorted(table)]
-
-
-LAST_GROUPS = groups_of(
-    lambda x, y, z: members_first(x, y, z)[:2], lambda chip: members_first(*chip)[2]
-)
-NEAR_GROUPS = groups_of(lambda x, y, z: (y // 2, z // 2), lambda chip: near_index(*chip))
-FAR_GROUPS = groups_of(lambda x, y, z: near_index(x, y, z), lambda chip: chip)
+SHEETS = [[index_of(x, y, z) for x, z in SHEET] for y in range(Y)]
 
 
 def swap(parts, members, chip, level):
@@ -582,24 +555,18 @@
     rows = [shape_of(PLANE_ROWS, WIDE)] * GROUP
     sum_b = swap_second(call(second_weights, rows, [(D, WIDE)], me, *in_vmem(*pack_b), scalar=True), 1)
     sum_a = swap_first(call(first_weights, rows, [(D, WIDE)], me, *in_vmem(*pack_a), scalar=True), 1)
-    (sums,) = call(
-        add_rows,
-        [shape_of(LAST, 2 * LAST_ROWS, WIDE)],
-        [(PLANE_ROWS, WIDE)],
-        me, *sum_a, *sum_b,
-        scalar=True,
-    )
-    sums = exchange(sums, LAST_GROUPS)
-    piece = (len(NEAR), 2 * PIECE + 16, LANES)
-    (pieces,) = call(to_owners, [shape_of(*piece)], [piece], sums)
-    pieces = exchange(pieces, NEAR_GROUPS)
-    (tiles,) = call(spread, [shape_of(LAST, 8, LANES, dtype=F32)], [], pieces)
-    pieces = after(pieces, tiles)
-    tiles = exchange(tiles, FAR_GROUPS)
-    own = shape_of(OWN, 4 * D, dtype=F32)
-    mine = call(collect, [own, own], [(len(NEAR), 2 * PIECE, LANES)], me, pieces, scalar=True)
+    piece = (len(SHEET), 2 * PIECE, LANES)
+    (sums,) = call(add_rows, [shape_of(*piece)], [piece], *sum_a, *sum_b)
+    sums = exchange(sums, SHEETS)
+    mine, tiles = call(
+        own_rows,
+        [shape_of(GROUP, 2 * PIECE, LANES, dtype=F32), shape_of(LAT * LON, 1, LANES, dtype=F32)],
+        [],
+        sums,
+    )
+    tiles = lax.all_to_all(tiles, ("lat", "lon"), 0, 0)
     out_qkv, out_out = shape_of(OWN, 3 * D, dtype=F32), shape_of(OWN, D, dtype=F32)
-    clips = call(clipped, [out_qkv, out_out] * 2, [], tiles, *mine)
+    clips = call(clipped, [out_qkv, out_out] * 2, [], tiles, mine)
     return (result, token_gradient, *clips)
 
 

time: 110 us -> 104 us (0.945)
  blocking collectives: 25.8 us -> 16.7 us
  starting transfers between devices: 34.3 us -> 37.2 us
  waiting for transfers between devices: 27 us -> 28.8 us
    all_to_all x2 -> x1, blocking collectives: 25.8 us -> 16.7 us  [exchange(): return lax.all_to_all(parts, ('lat', 'lon'), 0, 0, axis_index_groups=groups)]
    all_to_all x1, starting transfers between devices: 4.55 us -> 7.16 us  [on_device(): tiles = lax.all_to_all(tiles, ('lat', 'lon'), 0, 0)]
    all_to_all x1, waiting for transfers between devices: 7.91 us -> 10.1 us  [on_device(): tiles = lax.all_to_all(tiles, ('lat', 'lon'), 0, 0)]
    pallas_call x12 -> x10, Pallas kernels: 20.6 us -> 19.6 us  [call(): pl.pallas_call(kernel, out_shape=outs, in_specs=specs, out_specs=[whole]...]
  transfers between devices with their start and end apart: 19 -> 19, of which waited for: 8 -> 11; matrix products, arithmetic and copies ran while one was open for 0% -> 0% of each run, Pallas kernels for 9% -> 9%
where the time goes in v6:
time: 104 us; the launch traced here: 103 us
  starting transfers between devices  37.2 us (36%)
  waiting for transfers between devices  28.8 us (28%)
  Pallas kernels  19.6 us (19%)
  blocking collectives  16.7 us (16%)
    pallas_call x10, Pallas kernels, call(): pl.pallas_call(kernel, out_shape=outs, in_specs=specs, out_specs=[whole]...  19.6 us
    all_to_all x1, blocking collectives, exchange(): return lax.all_to_all(parts, ('lat', 'lon'), 0, 0, axis_index_groups=groups)  16.7 us
    ppermute x12, starting transfers between devices, swap(): out[step] = lax.ppermute(parts[step], ('lat', 'lon'), pairs)  16.6 us
    ppermute x6, starting transfers between devices, send(): out.append(lax.ppermute(part, ('lat', 'lon'), pairs))  13.4 us
    all_to_all x1, waiting for transfers between devices, on_device(): tiles = lax.all_to_all(tiles, ('lat', 'lon'), 0, 0)  10.1 us
    ppermute x6, waiting for transfers between devices, send(): out.append(lax.ppermute(part, ('lat', 'lon'), pairs))  9.98 us
    ppermute x12, waiting for transfers between devices, swap(): out[step] = lax.ppermute(parts[step], ('lat', 'lon'), pairs)  8.69 us
    all_to_all x1, starting transfers between devices, on_device(): tiles = lax.all_to_all(tiles, ('lat', 'lon'), 0, 0)  7.16 us
  transfers between devices with their start and end apart: 19, of which 11 were waited for; matrix products, arithmetic and copies ran while one was open for 0% of the time, Pallas kernels for 9%

profile of v6, /device:TPU:0, one launch (start us, length us, event | category | flops | bytes accessed | tf_op | source)
XLA Modules:
  0.0 103.1 jit_solution(11537602526890029623)
XLA Ops:
  0.7 0.1 pad_add_fusion.me
  0.7 4.1 %first_forward.1 = (bf16[36,1152]{1,0:T(8,128)(2,1)S(1)}, bf16[36,1152]{1,0:T(8,128)(2,1)S(1)}, bf16[36,1152]{1,0:T(8,128)(2,1)S(1)}, bf16[36,1152]{1,0:T(8,128)(2,1)S(1)}, bf16[144,2688]{1,0:T(8,128)(2,1)S(1)}) custom-call(s32[2]{0:T(128)S(1)} %pad_add_fusion.me, s32[6,2,12]{2,1,0:T(2,128)} %bitcast.15, bf16[6,12,2,512]{3,2,1,0:T(2,128)(2,1)} %bitcast.9, ...), custom_call_target="tpu_custom_call" | custom-call | tf_op jit(solution)/shard_map/first_forward/pallas_call | solution.py:405
  4.9 8.8 %collective-permute-start = (bf16[36,1152]{1,0:T(8,128)(2,1)S(1)}, bf16[36,1152]{1,0:T(8,128)(2,1)S(1)}, u32[]{:S(2)}, u32[]{:S(2)}) collective-permute-start(bf16[36,1152]{1,0:T(8,128)(2,1)S(1)} %get-tuple-element.47), channel_id=1, source_target_pairs={{0,254},{2,224},{4,226},{6,228},{8,230},{10,232},{12,234},{14,236}... | collective-permute-start | bytes 248840 | tf_op jit(solution)/shard_map/ppermute | solution.py:445
  13.7 0.1 collective-permute-start.1
  13.8 2.5 %collective-permute-start.2 = (bf16[36,1152]{1,0:T(8,128)(2,1)S(1)}, bf16[36,1152]{1,0:T(8,128)(2,1)S(1)}, u32[]{:S(2)}, u32[]{:S(2)}) collective-permute-start(bf16[36,1152]{1,0:T(8,128)(2,1)S(1)} %get-tuple-element.49), channel_id=1, source_target_pairs={{0,30},{2,0},{4,2},{6,4},{8,6},{10,8},{12,10},{14,12},{16,14},{18,... | collective-permute-start | bytes 248840 | tf_op jit(solution)/shard_map/ppermute | solution.py:445
  16.3 0.0 collective-permute-done.x0
  16.3 1.9 %collective-permute-done.1.x1 = bf16[36,1152]{1,0:T(8,128)(2,1)S(1)} collective-permute-done((bf16[36,1152]{1,0:T(8,128)(2,1)S(1)}, bf16[36,1152]{1,0:T(8,128)(2,1)S(1)}, u32[]{:S(2)}, u32[]{:S(2)}) %collective-permute-start.1) | collective-permute-done | bytes 82976 | tf_op jit(solution)/shard_map/ppermute | solution.py:445
  18.2 0.3 collective-permute-done.2.x2
  18.5 4.8 %second_main.1 = (bf16[36,1024]{1,0:T(8,128)(2,1)S(1)}, bf16[36,1024]{1,0:T(8,128)(2,1)S(1)}, bf16[36,1024]{1,0:T(8,128)(2,1)S(1)}, bf16[36,1024]{1,0:T(8,128)(2...) custom-call(bf16[36,1152]{1,0:T(8,128)(2,1)S(1)} %collective-permute-done.x0, ...), custom_call_target="tpu_custom_call" | custom-call | tf_op jit(solution)/shard_map/second_main/pallas_call | solution.py:405
  23.3 0.9 collective-permute-start.3
  24.2 1.0 collective-permute-start.4
  25.3 0.0 collective-permute-start.5
  25.3 1.1 %second_pack.1 = (bf16[144,1024]{1,0:T(8,128)(2,1)S(1)}, bf16[144,1024]{1,0:T(8,128)(2,1)S(1)}, bf16[144,1024]{1,0:T(8,128)(2,1)S(1)}, bf16[144,1024]{1,0:T(8,128)(2,1)S(1)}) custom-call(s32[2]{0:T(128)S(1)} %pad_add_fusion.me, bf16[144,512]{1,0:T(8,128)(2,1)S(1)} %get-tuple-element.67.normed, bf16[144,512]{1,0:T(8,128)(2,1)S(1)} %get-tuple-element.68.attended, ...), custom_call_target="tpu_custom_call" | custom-call | tf_op jit(solution)/shard_map/second_pack/pallas_call | solution.py:405
  26.3 7.8 %collective-permute-done.3.b0 = bf16[36,1024]{1,0:T(8,128)(2,1)S(1)} collective-permute-done((bf16[36,1024]{1,0:T(8,128)(2,1)S(1)}, bf16[36,1024]{1,0:T(8,128)(2,1)S(1)}, u32[]{:S(2)}, u32[]{:S(2)}) %collective-permute-start.3) | collective-permute-done | bytes 73760 | tf_op jit(solution)/shard_map/ppermute | solution.py:445
  34.1 0.0 collective-permute-done.4.b1
  34.2 0.0 collective-permute-done.5.b2
  34.2 1.1 %collective-permute-start.12 = (bf16[144,1024]{1,0:T(8,128)(2,1)S(1)}, bf16[144,1024]{1,0:T(8,128)(2,1)S(1)}, u32[]{:S(2)}, u32[]{:S(2)}) collective-permute-start(bf16[144,1024]{1,0:T(8,128)(2,1)S(1)} %get-tuple-element.75), channel_id=1, source_target_pairs={{0,192},{2,194},{4,196},{6,198},{8,200},{10,202},{12,204},{14,206}... | collective-permute-start | bytes 884744 | tf_op jit(solution)/shard_map/ppermute | solution.py:467
  35.3 0.1 collective-permute-start.13
  35.4 4.7 %collective-permute-start.14 = (bf16[144,1024]{1,0:T(8,128)(2,1)S(1)}, bf16[144,1024]{1,0:T(8,128)(2,1)S(1)}, u32[]{:S(2)}, u32[]{:S(2)}) collective-permute-start(bf16[144,1024]{1,0:T(8,128)(2,1)S(1)} %get-tuple-element.77), channel_id=1, source_target_pairs={{0,206},{2,196},{4,194},{6,200},{8,198},{10,204},{12,202},{14,192}... | collective-permute-start | bytes 884744 | tf_op jit(solution)/shard_map/ppermute | solution.py:467
  40.1 3.5 %first_backward.1 = (bf16[4,144,512]{2,1,0:T(8,128)(2,1)S(1)}, bf16[144,1024]{1,0:T(8,128)(2,1)S(1)}, bf16[144,1024]{1,0:T(8,128)(2,1)S(1)}, bf16[144,1024]{1,0:T(8,128)(2,1)S(1)}, bf16[144,1024]{1,0:T(8,128)(2,1)S(1)}) custom-call(s32[2]{0:T(128)S(1)} %pad_add_fusion.me, bf16[36,1024]{1,0:T(8,128)(2,1)S(1)} %collective-permute-done.3.b0, ...), custom_call_target="tpu_custom_call" | custom-call | tf_op jit(solution)/shard_map/first_backward/pallas_call | solution.py:405
  43.5 0.1 collective-permute-start.6
  43.6 0.1 collective-permute-start.7
  43.7 1.3 %collective-permute-done.12.refs_1_ = bf16[144,1024]{1,0:T(8,128)(2,1)S(1)} collective-permute-done((bf16[144,1024]{1,0:T(8,128)(2,1)S(1)}, bf16[144,1024]{1,0:T(8,128)(2,1)S(1)}, u32[]{:S(2)}, u32[]{:S(2)}) %collective-permute-start.12) | collective-permute-done | bytes 294944 | tf_op jit(solution)/shard_map/ppermute | solution.py:467
  45.0 2.1 %collective-permute-start.8 = (bf16[144,1024]{1,0:T(8,128)(2,1)S(1)}, bf16[144,1024]{1,0:T(8,128)(2,1)S(1)}, u32[]{:S(2)}, u32[]{:S(2)}) collective-permute-start(bf16[144,1024]{1,0:T(8,128)(2,1)S(1)} %get-tuple-element.62), channel_id=1, source_target_pairs={{0,66},{2,64},{4,70},{6,68},{8,74},{10,72},{12,78},{14,76},{32,98}... | collective-permute-start | bytes 884744 | tf_op jit(solution)/shard_map/ppermute | solution.py:467
  47.1 0.0 collective-permute-done.13.refs_2_
  47.1 2.8 %collective-permute-done.14.refs_3_ = bf16[144,1024]{1,0:T(8,128)(2,1)S(1)} collective-permute-done((bf16[144,1024]{1,0:T(8,128)(2,1)S(1)}, bf16[144,1024]{1,0:T(8,128)(2,1)S(1)}, u32[]{:S(2)}, u32[]{:S(2)}) %collective-permute-start.14) | collective-permute-done | bytes 294944 | tf_op jit(solution)/shard_map/ppermute | solution.py:467
  49.9 1.4 %second_weights.1 = (bf16[128,512]{1,0:T(8,128)(2,1)S(1)}, bf16[128,512]{1,0:T(8,128)(2,1)S(1)}, bf16[128,512]{1,0:T(8,128)(2,1)S(1)}, bf16[128,512]{1,0:T(8,128)(2,1)S(1)}) custom-call(s32[2]{0:T(128)S(1)} %pad_add_fusion.me, bf16[144,1024]{1,0:T(8,128)(2,1)S(1)} %get-tuple-element.74.refs_0_, bf16[144,1024]{1,0:T(8,128)(2,1)S(1)} %collective-permute-done.12.refs_1_, ...), custom_call_target="tpu_custom_call" | custom-call | tf_op jit(solution)/shard_map/second_weights/pallas_call | solution.py:405
  51.3 0.5 collective-permute-start.15
  51.7 1.3 %collective-permute-start.16 = (bf16[128,512]{1,0:T(8,128)(2,1)S(1)}, bf16[128,512]{1,0:T(8,128)(2,1)S(1)}, u32[]{:S(2)}, u32[]{:S(2)}) collective-permute-start(bf16[128,512]{1,0:T(8,128)(2,1)S(1)} %get-tuple-element.80), channel_id=1, source_target_pairs={{0,16},{2,18},{4,20},{6,22},{8,24},{10,26},{12,28},{14,30},{32,48}... | collective-permute-start | bytes 393224 | tf_op jit(solution)/shard_map/ppermute | solution.py:467
  53.1 0.0 collective-permute-done.6.refs_1_
  53.1 3.0 %collective-permute-start.17 = (bf16[128,512]{1,0:T(8,128)(2,1)S(1)}, bf16[128,512]{1,0:T(8,128)(2,1)S(1)}, u32[]{:S(2)}, u32[]{:S(2)}) collective-permute-start(bf16[128,512]{1,0:T(8,128)(2,1)S(1)} %get-tuple-element.81), channel_id=1, source_target_pairs={{0,48},{2,50},{4,52},{6,54},{8,56},{10,58},{12,60},{14,62},{32,16}... | collective-permute-start | bytes 393224 | tf_op jit(solution)/shard_map/ppermute | solution.py:467
  56.0 0.0 collective-permute-done.7.refs_2_
  56.1 0.1 collective-permute-done.8.refs_3_
  56.1 1.4 %first_weights.1 = (bf16[128,512]{1,0:T(8,128)(2,1)S(1)}, bf16[128,512]{1,0:T(8,128)(2,1)S(1)}, bf16[128,512]{1,0:T(8,128)(2,1)S(1)}, bf16[128,512]{1,0:T(8,128)(2,1)S(1)}) custom-call(s32[2]{0:T(128)S(1)} %pad_add_fusion.me, bf16[144,1024]{1,0:T(8,128)(2,1)S(1)} %get-tuple-element.59.refs_0_, bf16[144,1024]{1,0:T(8,128)(2,1)S(1)} %collective-permute-done.6.refs_1_, ...), custom_call_target="tpu_custom_call" | custom-call | tf_op jit(solution)/shard_map/first_weights/pallas_call | solution.py:405
  57.5 0.7 collective-permute-start.10
  58.1 2.5 %collective-permute-start.11 = (bf16[128,512]{1,0:T(8,128)(2,1)S(1)}, bf16[128,512]{1,0:T(8,128)(2,1)S(1)}, u32[]{:S(2)}, u32[]{:S(2)}) collective-permute-start(bf16[128,512]{1,0:T(8,128)(2,1)S(1)} %get-tuple-element.66), channel_id=1, source_target_pairs={{0,48},{2,50},{4,52},{6,54},{8,56},{10,58},{12,60},{14,62},{32,16}... | collective-permute-start | bytes 393224 | tf_op jit(solution)/shard_map/ppermute | solution.py:467
  60.7 0.4 collective-permute-start.9
  61.1 0.8 collective-permute-done.17.b3
  61.8 2.3 %collective-permute-done.10.a2 = bf16[128,512]{1,0:T(8,128)(2,1)S(1)} collective-permute-done((bf16[128,512]{1,0:T(8,128)(2,1)S(1)}, bf16[128,512]{1,0:T(8,128)(2,1)S(1)}, u32[]{:S(2)}, u32[]{:S(2)}) %collective-permute-start.10) | collective-permute-done | bytes 131104 | tf_op jit(solution)/shard_map/ppermute | solution.py:467
  64.1 1.3 %collective-permute-done.11.a3 = bf16[128,512]{1,0:T(8,128)(2,1)S(1)} collective-permute-done((bf16[128,512]{1,0:T(8,128)(2,1)S(1)}, bf16[128,512]{1,0:T(8,128)(2,1)S(1)}, u32[]{:S(2)}, u32[]{:S(2)}) %collective-permute-start.11) | collective-permute-done | bytes 131104 | tf_op jit(solution)/shard_map/ppermute | solution.py:467
  65.4 0.2 collective-permute-done.9.a1
  65.6 0.2 add_rows.1
  65.9 16.7 %all_to_all.10.parts = bf16[32,32,128]{2,1,0:T(8,128)(2,1)S(1)} all-to-all(bf16[32,32,128]{2,1,0:T(8,128)(2,1)S(1)} %add_rows.1), channel_id=1, replica_groups={{0,2,4,6,8,10,12,14,64,66,68,70,72,74,76,78,128,130,132,134,136,138,140..., dimensions={0} | all-to-all | bytes 524288 | tf_op jit(solution)/shard_map/all_to_all | solution.py:480
  82.6 0.8 own_rows.1
  83.4 7.2 %all-to-all-start.1 = ((f32[128,1,128]{2,1,0:T(1,128)}), f32[128,1,128]{2,1,0:T(1,128)S(1)}, u32[]{:S(2)}, u32[]{:S(2)}) async-start(f32[128,1,128]{2,1,0:T(1,128)} %get-tuple-element.82), calls=%async_computation.1 | async-start | bytes 131072 | tf_op jit(solution)/shard_map/all_to_all | solution.py:567
  90.6 1.6 %first_rest.1 = (bf16[6,12,2,512]{3,2,1,0:T(2,128)(2,1)}, bf16[6,12,2,512]{3,2,1,0:T(2,128)(2,1)}) custom-call(bf16[36,1024]{1,0:T(8,128)(2,1)S(1)} %collective-permute-done.3.b0, bf16[36,1024]{1,0:T(8,128)(2,1)S(1)} %collective-permute-done.4.b1, bf16[36,1024]{1,0:T(8,128)(2,1)S(1)} %collective-permute-done.5.b2, ...), custom_call_target="tpu_custom_call" | custom-call | tf_op jit(solution)/shard_map/first_rest/pallas_call | solution.py:405
  92.2 10.1 %all-to-all-done.1.tiles = f32[128,1,128]{2,1,0:T(1,128)S(1)} async-done(((f32[128,1,128]{2,1,0:T(1,128)}), f32[128,1,128]{2,1,0:T(1,128)S(1)}, u32[]{:S(2)}, u32[]{:S(2)}) %all-to-all-start.1) | async-done | bytes 65568 | tf_op jit(solution)/shard_map/all_to_all | solution.py:567
  102.3 0.8 clipped.1
  (16 shorter events, 0.0 us)
Async XLA Ops:
  0.6 17.9 %copy-start.6 = (f32[512]{0:T(512)S(1)}, f32[512]{0:T(512)}, u32[]{:S(2)}) copy-start(f32[512]{0:T(512)} %param.15) | copy-start | bytes 6148
  0.6 17.9 %copy-start.2 = (bf16[512,1536]{1,0:T(8,128)(2,1)S(1)}, bf16[512,1536]{1,0:T(8,128)(2,1)}, u32[]{:S(2)}) copy-start(bf16[512,1536]{1,0:T(8,128)(2,1)} %wqkv.2) | copy-start | bytes 4718596
  0.7 17.9 %copy-start.4 = (bf16[512,512]{1,0:T(8,128)(2,1)S(1)}, bf16[512,512]{1,0:T(8,128)(2,1)}, u32[]{:S(2)}) copy-start(bf16[512,512]{1,0:T(8,128)(2,1)} %wout.2) | copy-start | bytes 1572868
  4.9 11.5 %collective-permute-start = (bf16[36,1152]{1,0:T(8,128)(2,1)S(1)}, bf16[36,1152]{1,0:T(8,128)(2,1)S(1)}, u32[]{:S(2)}, u32[]{:S(2)}) collective-permute-start(bf16[36,1152]{1,0:T(8,128)(2,1)S(1)} %get-tuple-element.47), channel_id=1, source_target_pairs={{0,254},{2,224},{4,226},{6,228},{8,230},{10,232},{12,234},{14,236}... | collective-permute-start | bytes 248840 | tf_op jit(solution)/shard_map/ppermute | solution.py:445
  13.7 4.6 %collective-permute-start.1 = (bf16[36,1152]{1,0:T(8,128)(2,1)S(1)}, bf16[36,1152]{1,0:T(8,128)(2,1)S(1)}, u32[]{:S(2)}, u32[]{:S(2)}) collective-permute-start(bf16[36,1152]{1,0:T(8,128)(2,1)S(1)} %get-tuple-element.48), channel_id=1, source_target_pairs={{0,224},{2,226},{4,228},{6,230},{8,232},{10,234},{12,236},{14,238}... | collective-permute-start | bytes 248840 | tf_op jit(solution)/shard_map/ppermute | solution.py:445
  13.8 4.7 %collective-permute-start.2 = (bf16[36,1152]{1,0:T(8,128)(2,1)S(1)}, bf16[36,1152]{1,0:T(8,128)(2,1)S(1)}, u32[]{:S(2)}, u32[]{:S(2)}) collective-permute-start(bf16[36,1152]{1,0:T(8,128)(2,1)S(1)} %get-tuple-element.49), channel_id=1, source_target_pairs={{0,30},{2,0},{4,2},{6,4},{8,6},{10,8},{12,10},{14,12},{16,14},{18,... | collective-permute-start | bytes 248840 | tf_op jit(solution)/shard_map/ppermute | solution.py:445
  18.5 21.6 %copy-start.1 = (bf16[512,512]{1,0:T(8,128)(2,1)S(1)}, bf16[512,512]{1,0:T(8,128)(2,1)}, u32[]{:S(2)}) copy-start(bf16[512,512]{1,0:T(8,128)(2,1)} %wout.3) | copy-start | bytes 1572868
  23.3 10.8 %collective-permute-start.3 = (bf16[36,1024]{1,0:T(8,128)(2,1)S(1)}, bf16[36,1024]{1,0:T(8,128)(2,1)S(1)}, u32[]{:S(2)}, u32[]{:S(2)}) collective-permute-start(bf16[36,1024]{1,0:T(8,128)(2,1)S(1)} %get-tuple-element.51), channel_id=1, source_target_pairs={{254,0},{224,2},{226,4},{228,6},{230,8},{232,10},{234,12},{236,14}... | collective-permute-start | bytes 221192 | tf_op jit(solution)/shard_map/ppermute | solution.py:445
  24.2 9.9 %collective-permute-start.4 = (bf16[36,1024]{1,0:T(8,128)(2,1)S(1)}, bf16[36,1024]{1,0:T(8,128)(2,1)S(1)}, u32[]{:S(2)}, u32[]{:S(2)}) collective-permute-start(bf16[36,1024]{1,0:T(8,128)(2,1)S(1)} %get-tuple-element.52), channel_id=1, source_target_pairs={{224,0},{226,2},{228,4},{230,6},{232,8},{234,10},{236,12},{238,14}... | collective-permute-start | bytes 221192 | tf_op jit(solution)/shard_map/ppermute | solution.py:445
  25.3 8.9 %collective-permute-start.5 = (bf16[36,1024]{1,0:T(8,128)(2,1)S(1)}, bf16[36,1024]{1,0:T(8,128)(2,1)S(1)}, u32[]{:S(2)}, u32[]{:S(2)}) collective-permute-start(bf16[36,1024]{1,0:T(8,128)(2,1)S(1)} %get-tuple-element.53), channel_id=1, source_target_pairs={{30,0},{0,2},{2,4},{4,6},{6,8},{8,10},{10,12},{12,14},{14,16},{16,... | collective-permute-start | bytes 221192 | tf_op jit(solution)/shard_map/ppermute | solution.py:445
  34.2 10.9 %collective-permute-start.12 = (bf16[144,1024]{1,0:T(8,128)(2,1)S(1)}, bf16[144,1024]{1,0:T(8,128)(2,1)S(1)}, u32[]{:S(2)}, u32[]{:S(2)}) collective-permute-start(bf16[144,1024]{1,0:T(8,128)(2,1)S(1)} %get-tuple-element.75), channel_id=1, source_target_pairs={{0,192},{2,194},{4,196},{6,198},{8,200},{10,202},{12,204},{14,206}... | collective-permute-start | bytes 884744 | tf_op jit(solution)/shard_map/ppermute | solution.py:467
  35.3 11.8 %collective-permute-start.13 = (bf16[144,1024]{1,0:T(8,128)(2,1)S(1)}, bf16[144,1024]{1,0:T(8,128)(2,1)S(1)}, u32[]{:S(2)}, u32[]{:S(2)}) collective-permute-start(bf16[144,1024]{1,0:T(8,128)(2,1)S(1)} %get-tuple-element.76), channel_id=1, source_target_pairs={{0,14},{2,4},{4,2},{6,8},{8,6},{10,12},{12,10},{14,0},{32,46},{34,... | collective-permute-start | bytes 884744 | tf_op jit(solution)/shard_map/ppermute | solution.py:467
  35.4 14.5 %collective-permute-start.14 = (bf16[144,1024]{1,0:T(8,128)(2,1)S(1)}, bf16[144,1024]{1,0:T(8,128)(2,1)S(1)}, u32[]{:S(2)}, u32[]{:S(2)}) collective-permute-start(bf16[144,1024]{1,0:T(8,128)(2,1)S(1)} %get-tuple-element.77), channel_id=1, source_target_pairs={{0,206},{2,196},{4,194},{6,200},{8,198},{10,204},{12,202},{14,192}... | collective-permute-start | bytes 884744 | tf_op jit(solution)/shard_map/ppermute | solution.py:467
  43.5 9.5 %collective-permute-start.6 = (bf16[144,1024]{1,0:T(8,128)(2,1)S(1)}, bf16[144,1024]{1,0:T(8,128)(2,1)S(1)}, u32[]{:S(2)}, u32[]{:S(2)}) collective-permute-start(bf16[144,1024]{1,0:T(8,128)(2,1)S(1)} %get-tuple-element.60), channel_id=1, source_target_pairs={{0,64},{2,66},{4,68},{6,70},{8,72},{10,74},{12,76},{14,78},{32,96}... | collective-permute-start | bytes 884744 | tf_op jit(solution)/shard_map/ppermute | solution.py:467
  43.6 12.4 %collective-permute-start.7 = (bf16[144,1024]{1,0:T(8,128)(2,1)S(1)}, bf16[144,1024]{1,0:T(8,128)(2,1)S(1)}, u32[]{:S(2)}, u32[]{:S(2)}) collective-permute-start(bf16[144,1024]{1,0:T(8,128)(2,1)S(1)} %get-tuple-element.61), channel_id=1, source_target_pairs={{0,2},{2,0},{4,6},{6,4},{8,10},{10,8},{12,14},{14,12},{32,34},{34,... | collective-permute-start | bytes 884744 | tf_op jit(solution)/shard_map/ppermute | solution.py:467
  45.0 11.1 %collective-permute-start.8 = (bf16[144,1024]{1,0:T(8,128)(2,1)S(1)}, bf16[144,1024]{1,0:T(8,128)(2,1)S(1)}, u32[]{:S(2)}, u32[]{:S(2)}) collective-permute-start(bf16[144,1024]{1,0:T(8,128)(2,1)S(1)} %get-tuple-element.62), channel_id=1, source_target_pairs={{0,66},{2,64},{4,70},{6,68},{8,74},{10,72},{12,78},{14,76},{32,98}... | collective-permute-start | bytes 884744 | tf_op jit(solution)/shard_map/ppermute | solution.py:467
  51.3 9.4 %collective-permute-start.15 = (bf16[128,512]{1,0:T(8,128)(2,1)S(1)}, bf16[128,512]{1,0:T(8,128)(2,1)S(1)}, u32[]{:S(2)}, u32[]{:S(2)}) collective-permute-start(bf16[128,512]{1,0:T(8,128)(2,1)S(1)} %get-tuple-element.79), channel_id=1, source_target_pairs={{0,32},{2,34},{4,36},{6,38},{8,40},{10,42},{12,44},{14,46},{32,0},... | collective-permute-start | bytes 393224 | tf_op jit(solution)/shard_map/ppermute | solution.py:467
  51.7 9.3 %collective-permute-start.16 = (bf16[128,512]{1,0:T(8,128)(2,1)S(1)}, bf16[128,512]{1,0:T(8,128)(2,1)S(1)}, u32[]{:S(2)}, u32[]{:S(2)}) collective-permute-start(bf16[128,512]{1,0:T(8,128)(2,1)S(1)} %get-tuple-element.80), channel_id=1, source_target_pairs={{0,16},{2,18},{4,20},{6,22},{8,24},{10,26},{12,28},{14,30},{32,48}... | collective-permute-start | bytes 393224 | tf_op jit(solution)/shard_map/ppermute | solution.py:467
  53.1 8.8 %collective-permute-start.17 = (bf16[128,512]{1,0:T(8,128)(2,1)S(1)}, bf16[128,512]{1,0:T(8,128)(2,1)S(1)}, u32[]{:S(2)}, u32[]{:S(2)}) collective-permute-start(bf16[128,512]{1,0:T(8,128)(2,1)S(1)} %get-tuple-element.81), channel_id=1, source_target_pairs={{0,48},{2,50},{4,52},{6,54},{8,56},{10,58},{12,60},{14,62},{32,16}... | collective-permute-start | bytes 393224 | tf_op jit(solution)/shard_map/ppermute | solution.py:467
  56.1 34.5 %copy-start = (bf16[512,1536]{1,0:T(8,128)(2,1)S(1)}, bf16[512,1536]{1,0:T(8,128)(2,1)}, u32[]{:S(2)}) copy-start(bf16[512,1536]{1,0:T(8,128)(2,1)} %wqkv.3) | copy-start | bytes 4718596
  56.1 34.5 %copy-start.3 = (bf16[2,6,12,512]{3,0,2,1:T(2,128)(2,1)S(1)}, bf16[2,6,12,512]{3,0,2,1:T(2,128)(2,1)}, u32[]{:S(2)}) copy-start(bf16[2,6,12,512]{3,0,2,1:T(2,128)(2,1)} %param.9) | copy-start | bytes 442372
  56.1 34.5 %copy-start.5 = (f32[512]{0:T(512)S(1)}, f32[512]{0:T(512)}, u32[]{:S(2)}) copy-start(f32[512]{0:T(512)} %param.12) | copy-start | bytes 6148
  57.5 6.7 %collective-permute-start.10 = (bf16[128,512]{1,0:T(8,128)(2,1)S(1)}, bf16[128,512]{1,0:T(8,128)(2,1)S(1)}, u32[]{:S(2)}, u32[]{:S(2)}) collective-permute-start(bf16[128,512]{1,0:T(8,128)(2,1)S(1)} %get-tuple-element.65), channel_id=1, source_target_pairs={{0,16},{2,18},{4,20},{6,22},{8,24},{10,26},{12,28},{14,30},{32,48}... | collective-permute-start | bytes 393224 | tf_op jit(solution)/shard_map/ppermute | solution.py:467
  58.1 7.3 %collective-permute-start.11 = (bf16[128,512]{1,0:T(8,128)(2,1)S(1)}, bf16[128,512]{1,0:T(8,128)(2,1)S(1)}, u32[]{:S(2)}, u32[]{:S(2)}) collective-permute-start(bf16[128,512]{1,0:T(8,128)(2,1)S(1)} %get-tuple-element.66), channel_id=1, source_target_pairs={{0,48},{2,50},{4,52},{6,54},{8,56},{10,58},{12,60},{14,62},{32,16}... | collective-permute-start | bytes 393224 | tf_op jit(solution)/shard_map/ppermute | solution.py:467
  60.7 5.0 %collective-permute-start.9 = (bf16[128,512]{1,0:T(8,128)(2,1)S(1)}, bf16[128,512]{1,0:T(8,128)(2,1)S(1)}, u32[]{:S(2)}, u32[]{:S(2)}) collective-permute-start(bf16[128,512]{1,0:T(8,128)(2,1)S(1)} %get-tuple-element.64), channel_id=1, source_target_pairs={{0,32},{2,34},{4,36},{6,38},{8,40},{10,42},{12,44},{14,46},{32,0},... | collective-permute-start | bytes 393224 | tf_op jit(solution)/shard_map/ppermute | solution.py:467
  83.4 18.9 %all-to-all-start.1 = ((f32[128,1,128]{2,1,0:T(1,128)}), f32[128,1,128]{2,1,0:T(1,128)S(1)}, u32[]{:S(2)}, u32[]{:S(2)}) async-start(f32[128,1,128]{2,1,0:T(1,128)} %get-tuple-element.82), calls=%async_computation.1 | async-start | bytes 131072 | tf_op jit(solution)/shard_map/all_to_all | solution.py:567

commit v7 on v6

--- a/solution.py
+++ b/solution.py
@@ -180,12 +180,8 @@
     return (lax.broadcasted_iota(jnp.int32, (D, D), 0) == source_of(to)).astype(F32).astype(BF16)
 
 
-def chip_of(lat, lon):
-    return lat // YLO, lon // Z * YLO + lat % YLO, lon % Z
-
-
 def squares(x, z):
-    return x % 2 + z % 2 * 2, x // 2 + z // 2 * 2
+    return (x & 1) + (z & 1) * 2, (x >> 1) + (z >> 1) * 2
 
 
 def members_first(x, y, z):
@@ -194,17 +190,17 @@
 
 
 def members_second(x, y, z):
-    m1, m3 = squares((x + X - 1) % X, (z + Z - 1) % Z)
+    m1, m3 = squares(x + X - 1 & X - 1, z + Z - 1 & Z - 1)
     return m1, y, m3
 
 
 def chip_first(m1, m2, m3):
-    return m1 % 2 + m3 % 2 * 2, m2, m1 // 2 + m3 // 2 * 2
+    return (m1 & 1) + (m3 & 1) * 2, m2, (m1 >> 1) + (m3 >> 1) * 2
 
 
 def chip_second(m1, m2, m3):
     x, y, z = chip_first(m1, m2, m3)
-    return (x + 1) % X, y, (z + 1) % Z
+    return x + 1 & X - 1, y, z + 1 & Z - 1
 
 
 def row_order(chip):
@@ -217,7 +213,8 @@
 
 
 def here(me):
-    return chip_of(me[0], me[1])
+    place = me[0]
+    return place >> 5, (place >> 3 & 1) * 2 + (place >> 4 & 1), place & 7
 
 
 def pack(me, left_refs, right_ref, packs):
@@ -258,7 +255,7 @@
         ref[:, D : 2 * D] = scratch[slot * QUART : (slot + 1) * QUART, :].astype(BF16)
     labels = jnp.broadcast_to(take_labels(region), (TOK, LANES))
     near = lax.broadcasted_iota(jnp.int32, (TOK, LANES), 0) < 2 * QUART
-    moved = labels + jnp.where(near & (me[0] == 0), 4.0, 0.0)
+    moved = labels + jnp.where(near & (me[0] < LON), 4.0, 0.0)
     scatter_rows(moved, lab_scratch, refs, 2 * D)
     values = take_field(tok, scratch)
     copies[0].wait()
@@ -497,7 +494,7 @@
 ):
     tables = moves(LAT, LON)
     lat, lon = lax.axis_index("lat"), lax.axis_index("lon")
-    me = jnp.stack([lat, lon]).astype(jnp.int32)
+    me = (lat * LON + lon).astype(jnp.int32).reshape(1)
     gain_a = unshifted_norm_gain.reshape(1, D)
     gain_b = shifted_norm_gain.reshape(1, D)
     tok = tokens.transpose(1, 2, 0, 3)

time: 104 us -> 103 us (level)
  Pallas kernels: 19.6 us -> 17.4 us
  waiting for transfers between devices: 28.8 us -> 30.4 us
    pallas_call x10, Pallas kernels: 19.6 us -> 17.4 us  [call(): pl.pallas_call(kernel, out_shape=outs, in_specs=specs, out_specs=[whole]...]
    ppermute x12, waiting for transfers between devices: 8.69 us -> 9.76 us  [swap(): out[step] = lax.ppermute(parts[step], ('lat', 'lon'), pairs)]
  transfers between devices with their start and end apart: 19 -> 19, of which waited for: 11 -> 10; matrix products, arithmetic and copies ran while one was open for 0% -> 0% of each run, Pallas kernels for 9% -> 7%
where the time goes in v7:
time: 103 us; the launch traced here: 102 us
  starting transfers between devices  36.7 us (36%)
  waiting for transfers between devices  30.4 us (30%)
  Pallas kernels  17.4 us (17%)
  blocking collectives  16.6 us (16%)
    pallas_call x10, Pallas kernels, call(): pl.pallas_call(kernel, out_shape=outs, in_specs=specs, out_specs=[whole]...  17.4 us
    all_to_all x1, blocking collectives, exchange(): return lax.all_to_all(parts, ('lat', 'lon'), 0, 0, axis_index_groups=groups)  16.6 us
    ppermute x12, starting transfers between devices, swap(): out[step] = lax.ppermute(parts[step], ('lat', 'lon'), pairs)  16 us
    ppermute x6, starting transfers between devices, send(): out.append(lax.ppermute(part, ('lat', 'lon'), pairs))  13.4 us
    ppermute x6, waiting for transfers between devices, send(): out.append(lax.ppermute(part, ('lat', 'lon'), pairs))  10.5 us
    all_to_all x1, waiting for transfers between devices, on_device(): tiles = lax.all_to_all(tiles, ('lat', 'lon'), 0, 0)  10.1 us
    ppermute x12, waiting for transfers between devices, swap(): out[step] = lax.ppermute(parts[step], ('lat', 'lon'), pairs)  9.76 us
    all_to_all x1, starting transfers between devices, on_device(): tiles = lax.all_to_all(tiles, ('lat', 'lon'), 0, 0)  7.25 us
  transfers between devices with their start and end apart: 19, of which 10 were waited for; matrix products, arithmetic and copies ran while one was open for 0% of the time, Pallas kernels for 7%

profile of v7, /device:TPU:0, one launch (start us, length us, event | category | flops | bytes accessed | tf_op | source)
XLA Modules:
  0.0 102.0 jit_solution(9442810082927889)
XLA Ops:
  0.7 4.1 %first_forward.1 = (bf16[36,1152]{1,0:T(8,128)(2,1)S(1)}, bf16[36,1152]{1,0:T(8,128)(2,1)S(1)}, bf16[36,1152]{1,0:T(8,128)(2,1)S(1)}, bf16[36,1152]{1,0:T(8,128)(2,1)S(1)}, bf16[144,2688]{1,0:T(8,128)(2,1)S(1)}) custom-call(s32[1]{0:T(128)} %bitcast.me, s32[6,2,12]{2,1,0:T(2,128)} %bitcast.14, bf16[6,12,2,512]{3,2,1,0:T(2,128)(2,1)} %bitcast.8, ...), custom_call_target="tpu_custom_call" | custom-call | tf_op jit(solution)/shard_map/first_forward/pallas_call | solution.py:402
  4.8 8.8 %collective-permute-start = (bf16[36,1152]{1,0:T(8,128)(2,1)S(1)}, bf16[36,1152]{1,0:T(8,128)(2,1)S(1)}, u32[]{:S(2)}, u32[]{:S(2)}) collective-permute-start(bf16[36,1152]{1,0:T(8,128)(2,1)S(1)} %get-tuple-element.47), channel_id=1, source_target_pairs={{0,254},{2,224},{4,226},{6,228},{8,230},{10,232},{12,234},{14,236}... | collective-permute-start | bytes 248840 | tf_op jit(solution)/shard_map/ppermute | solution.py:442
  13.6 0.1 collective-permute-start.1
  13.8 2.5 %collective-permute-start.2 = (bf16[36,1152]{1,0:T(8,128)(2,1)S(1)}, bf16[36,1152]{1,0:T(8,128)(2,1)S(1)}, u32[]{:S(2)}, u32[]{:S(2)}) collective-permute-start(bf16[36,1152]{1,0:T(8,128)(2,1)S(1)} %get-tuple-element.49), channel_id=1, source_target_pairs={{0,30},{2,0},{4,2},{6,4},{8,6},{10,8},{12,10},{14,12},{16,14},{18,... | collective-permute-start | bytes 248840 | tf_op jit(solution)/shard_map/ppermute | solution.py:442
  16.3 0.0 collective-permute-done.x0
  16.3 1.9 %collective-permute-done.1.x1 = bf16[36,1152]{1,0:T(8,128)(2,1)S(1)} collective-permute-done((bf16[36,1152]{1,0:T(8,128)(2,1)S(1)}, bf16[36,1152]{1,0:T(8,128)(2,1)S(1)}, u32[]{:S(2)}, u32[]{:S(2)}) %collective-permute-start.1) | collective-permute-done | bytes 82976 | tf_op jit(solution)/shard_map/ppermute | solution.py:442
  18.2 0.3 collective-permute-done.2.x2
  18.5 4.8 %second_main.1 = (bf16[36,1024]{1,0:T(8,128)(2,1)S(1)}, bf16[36,1024]{1,0:T(8,128)(2,1)S(1)}, bf16[36,1024]{1,0:T(8,128)(2,1)S(1)}, bf16[36,1024]{1,0:T(8,128)(2...) custom-call(bf16[36,1152]{1,0:T(8,128)(2,1)S(1)} %collective-permute-done.x0, ...), custom_call_target="tpu_custom_call" | custom-call | tf_op jit(solution)/shard_map/second_main/pallas_call | solution.py:402
  23.2 0.9 collective-permute-start.3
  24.2 1.0 %collective-permute-start.4 = (bf16[36,1024]{1,0:T(8,128)(2,1)S(1)}, bf16[36,1024]{1,0:T(8,128)(2,1)S(1)}, u32[]{:S(2)}, u32[]{:S(2)}) collective-permute-start(bf16[36,1024]{1,0:T(8,128)(2,1)S(1)} %get-tuple-element.52), channel_id=1, source_target_pairs={{224,0},{226,2},{228,4},{230,6},{232,8},{234,10},{236,12},{238,14}... | collective-permute-start | bytes 221192 | tf_op jit(solution)/shard_map/ppermute | solution.py:442
  25.2 0.0 collective-permute-start.5
  25.2 0.5 second_pack.1
  25.7 8.4 %collective-permute-done.3.b0 = bf16[36,1024]{1,0:T(8,128)(2,1)S(1)} collective-permute-done((bf16[36,1024]{1,0:T(8,128)(2,1)S(1)}, bf16[36,1024]{1,0:T(8,128)(2,1)S(1)}, u32[]{:S(2)}, u32[]{:S(2)}) %collective-permute-start.3) | collective-permute-done | bytes 73760 | tf_op jit(solution)/shard_map/ppermute | solution.py:442
  34.1 0.0 collective-permute-done.4.b1
  34.1 0.0 collective-permute-done.5.b2
  34.1 1.1 %collective-permute-start.12 = (bf16[144,1024]{1,0:T(8,128)(2,1)S(1)}, bf16[144,1024]{1,0:T(8,128)(2,1)S(1)}, u32[]{:S(2)}, u32[]{:S(2)}) collective-permute-start(bf16[144,1024]{1,0:T(8,128)(2,1)S(1)} %get-tuple-element.75), channel_id=1, source_target_pairs={{0,192},{2,194},{4,196},{6,198},{8,200},{10,202},{12,204},{14,206}... | collective-permute-start | bytes 884744 | tf_op jit(solution)/shard_map/ppermute | solution.py:464
  35.2 0.1 collective-permute-start.13
  35.3 4.7 %collective-permute-start.14 = (bf16[144,1024]{1,0:T(8,128)(2,1)S(1)}, bf16[144,1024]{1,0:T(8,128)(2,1)S(1)}, u32[]{:S(2)}, u32[]{:S(2)}) collective-permute-start(bf16[144,1024]{1,0:T(8,128)(2,1)S(1)} %get-tuple-element.77), channel_id=1, source_target_pairs={{0,206},{2,196},{4,194},{6,200},{8,198},{10,204},{12,202},{14,192}... | collective-permute-start | bytes 884744 | tf_op jit(solution)/shard_map/ppermute | solution.py:464
  40.0 2.9 %first_backward.1 = (bf16[4,144,512]{2,1,0:T(8,128)(2,1)S(1)}, bf16[144,1024]{1,0:T(8,128)(2,1)S(1)}, bf16[144,1024]{1,0:T(8,128)(2,1)S(1)}, bf16[144,1024]{1,0:T(8,128)(2,1)S(1)}, bf16[144,1024]{1,0:T(8,128)(2,1)S(1)}) custom-call(s32[1]{0:T(128)} %bitcast.me, bf16[36,1024]{1,0:T(8,128)(2,1)S(1)} %collective-permute-done.3.b0, ...), custom_call_target="tpu_custom_call" | custom-call | tf_op jit(solution)/shard_map/first_backward/pallas_call | solution.py:402
  42.9 0.1 collective-permute-start.6
  43.0 0.1 collective-permute-start.7
  43.1 1.8 %collective-permute-done.12.refs_1_ = bf16[144,1024]{1,0:T(8,128)(2,1)S(1)} collective-permute-done((bf16[144,1024]{1,0:T(8,128)(2,1)S(1)}, bf16[144,1024]{1,0:T(8,128)(2,1)S(1)}, u32[]{:S(2)}, u32[]{:S(2)}) %collective-permute-start.12) | collective-permute-done | bytes 294944 | tf_op jit(solution)/shard_map/ppermute | solution.py:464
  45.0 1.6 %collective-permute-start.8 = (bf16[144,1024]{1,0:T(8,128)(2,1)S(1)}, bf16[144,1024]{1,0:T(8,128)(2,1)S(1)}, u32[]{:S(2)}, u32[]{:S(2)}) collective-permute-start(bf16[144,1024]{1,0:T(8,128)(2,1)S(1)} %get-tuple-element.62), channel_id=1, source_target_pairs={{0,66},{2,64},{4,70},{6,68},{8,74},{10,72},{12,78},{14,76},{32,98}... | collective-permute-start | bytes 884744 | tf_op jit(solution)/shard_map/ppermute | solution.py:464
  46.5 0.0 collective-permute-done.13.refs_2_
  46.5 3.3 %collective-permute-done.14.refs_3_ = bf16[144,1024]{1,0:T(8,128)(2,1)S(1)} collective-permute-done((bf16[144,1024]{1,0:T(8,128)(2,1)S(1)}, bf16[144,1024]{1,0:T(8,128)(2,1)S(1)}, u32[]{:S(2)}, u32[]{:S(2)}) %collective-permute-start.14) | collective-permute-done | bytes 294944 | tf_op jit(solution)/shard_map/ppermute | solution.py:464
  49.8 0.8 second_weights.1
  50.7 0.5 collective-permute-start.15
  51.1 1.4 %collective-permute-start.16 = (bf16[128,512]{1,0:T(8,128)(2,1)S(1)}, bf16[128,512]{1,0:T(8,128)(2,1)S(1)}, u32[]{:S(2)}, u32[]{:S(2)}) collective-permute-start(bf16[128,512]{1,0:T(8,128)(2,1)S(1)} %get-tuple-element.80), channel_id=1, source_target_pairs={{0,16},{2,18},{4,20},{6,22},{8,24},{10,26},{12,28},{14,30},{32,48}... | collective-permute-start | bytes 393224 | tf_op jit(solution)/shard_map/ppermute | solution.py:464
  52.5 0.0 collective-permute-done.6.refs_1_
  52.5 2.9 %collective-permute-start.17 = (bf16[128,512]{1,0:T(8,128)(2,1)S(1)}, bf16[128,512]{1,0:T(8,128)(2,1)S(1)}, u32[]{:S(2)}, u32[]{:S(2)}) collective-permute-start(bf16[128,512]{1,0:T(8,128)(2,1)S(1)} %get-tuple-element.81), channel_id=1, source_target_pairs={{0,48},{2,50},{4,52},{6,54},{8,56},{10,58},{12,60},{14,62},{32,16}... | collective-permute-start | bytes 393224 | tf_op jit(solution)/shard_map/ppermute | solution.py:464
  55.5 0.0 collective-permute-done.7.refs_2_
  55.5 0.0 collective-permute-done.8.refs_3_
  55.5 0.8 first_weights.1
  56.3 0.7 collective-permute-start.10
  57.0 2.5 %collective-permute-start.11 = (bf16[128,512]{1,0:T(8,128)(2,1)S(1)}, bf16[128,512]{1,0:T(8,128)(2,1)S(1)}, u32[]{:S(2)}, u32[]{:S(2)}) collective-permute-start(bf16[128,512]{1,0:T(8,128)(2,1)S(1)} %get-tuple-element.66), channel_id=1, source_target_pairs={{0,48},{2,50},{4,52},{6,54},{8,56},{10,58},{12,60},{14,62},{32,16}... | collective-permute-start | bytes 393224 | tf_op jit(solution)/shard_map/ppermute | solution.py:464
  59.5 0.0 collective-permute-done.15.b1
  59.5 0.4 collective-permute-start.9
  59.9 1.0 collective-permute-done.17.b3
  60.9 2.1 %collective-permute-done.10.a2 = bf16[128,512]{1,0:T(8,128)(2,1)S(1)} collective-permute-done((bf16[128,512]{1,0:T(8,128)(2,1)S(1)}, bf16[128,512]{1,0:T(8,128)(2,1)S(1)}, u32[]{:S(2)}, u32[]{:S(2)}) %collective-permute-start.10) | collective-permute-done | bytes 131104 | tf_op jit(solution)/shard_map/ppermute | solution.py:464
  63.0 1.3 %collective-permute-done.11.a3 = bf16[128,512]{1,0:T(8,128)(2,1)S(1)} collective-permute-done((bf16[128,512]{1,0:T(8,128)(2,1)S(1)}, bf16[128,512]{1,0:T(8,128)(2,1)S(1)}, u32[]{:S(2)}, u32[]{:S(2)}) %collective-permute-start.11) | collective-permute-done | bytes 131104 | tf_op jit(solution)/shard_map/ppermute | solution.py:464
  64.3 0.2 collective-permute-done.9.a1
  64.5 0.2 add_rows.1
  64.7 16.6 %all_to_all.10.parts = bf16[32,32,128]{2,1,0:T(8,128)(2,1)S(1)} all-to-all(bf16[32,32,128]{2,1,0:T(8,128)(2,1)S(1)} %add_rows.1), channel_id=1, replica_groups={{0,2,4,6,8,10,12,14,64,66,68,70,72,74,76,78,128,130,132,134,136,138,140..., dimensions={0} | all-to-all | bytes 524288 | tf_op jit(solution)/shard_map/all_to_all | solution.py:477
  81.3 0.8 own_rows.1
  82.1 7.3 %all-to-all-start.1 = ((f32[128,1,128]{2,1,0:T(1,128)}), f32[128,1,128]{2,1,0:T(1,128)S(1)}, u32[]{:S(2)}, u32[]{:S(2)}) async-start(f32[128,1,128]{2,1,0:T(1,128)} %get-tuple-element.82), calls=%async_computation.1 | async-start | bytes 131072 | tf_op jit(solution)/shard_map/all_to_all | solution.py:564
  89.4 1.6 %first_rest.1 = (bf16[6,12,2,512]{3,2,1,0:T(2,128)(2,1)}, bf16[6,12,2,512]{3,2,1,0:T(2,128)(2,1)}) custom-call(bf16[36,1024]{1,0:T(8,128)(2,1)S(1)} %collective-permute-done.3.b0, bf16[36,1024]{1,0:T(8,128)(2,1)S(1)} %collective-permute-done.4.b1, bf16[36,1024]{1,0:T(8,128)(2,1)S(1)} %collective-permute-done.5.b2, ...), custom_call_target="tpu_custom_call" | custom-call | tf_op jit(solution)/shard_map/first_rest/pallas_call | solution.py:402
  91.0 10.1 %all-to-all-done.1.tiles = f32[128,1,128]{2,1,0:T(1,128)S(1)} async-done(((f32[128,1,128]{2,1,0:T(1,128)}), f32[128,1,128]{2,1,0:T(1,128)S(1)}, u32[]{:S(2)}, u32[]{:S(2)}) %all-to-all-start.1) | async-done | bytes 65568 | tf_op jit(solution)/shard_map/all_to_all | solution.py:564
  101.2 0.8 clipped.1
  (15 shorter events, 0.0 us)
Async XLA Ops:
  0.6 17.8 %copy-start.6 = (f32[512]{0:T(512)S(1)}, f32[512]{0:T(512)}, u32[]{:S(2)}) copy-start(f32[512]{0:T(512)} %param.15) | copy-start | bytes 6148
  0.6 17.8 %copy-start.2 = (bf16[512,1536]{1,0:T(8,128)(2,1)S(1)}, bf16[512,1536]{1,0:T(8,128)(2,1)}, u32[]{:S(2)}) copy-start(bf16[512,1536]{1,0:T(8,128)(2,1)} %wqkv.2) | copy-start | bytes 4718596
  0.7 17.8 %copy-start.4 = (bf16[512,512]{1,0:T(8,128)(2,1)S(1)}, bf16[512,512]{1,0:T(8,128)(2,1)}, u32[]{:S(2)}) copy-start(bf16[512,512]{1,0:T(8,128)(2,1)} %wout.2) | copy-start | bytes 1572868
  4.8 11.5 %collective-permute-start = (bf16[36,1152]{1,0:T(8,128)(2,1)S(1)}, bf16[36,1152]{1,0:T(8,128)(2,1)S(1)}, u32[]{:S(2)}, u32[]{:S(2)}) collective-permute-start(bf16[36,1152]{1,0:T(8,128)(2,1)S(1)} %get-tuple-element.47), channel_id=1, source_target_pairs={{0,254},{2,224},{4,226},{6,228},{8,230},{10,232},{12,234},{14,236}... | collective-permute-start | bytes 248840 | tf_op jit(solution)/shard_map/ppermute | solution.py:442
  13.6 4.6 %collective-permute-start.1 = (bf16[36,1152]{1,0:T(8,128)(2,1)S(1)}, bf16[36,1152]{1,0:T(8,128)(2,1)S(1)}, u32[]{:S(2)}, u32[]{:S(2)}) collective-permute-start(bf16[36,1152]{1,0:T(8,128)(2,1)S(1)} %get-tuple-element.48), channel_id=1, source_target_pairs={{0,224},{2,226},{4,228},{6,230},{8,232},{10,234},{12,236},{14,238}... | collective-permute-start | bytes 248840 | tf_op jit(solution)/shard_map/ppermute | solution.py:442
  13.8 4.7 %collective-permute-start.2 = (bf16[36,1152]{1,0:T(8,128)(2,1)S(1)}, bf16[36,1152]{1,0:T(8,128)(2,1)S(1)}, u32[]{:S(2)}, u32[]{:S(2)}) collective-permute-start(bf16[36,1152]{1,0:T(8,128)(2,1)S(1)} %get-tuple-element.49), channel_id=1, source_target_pairs={{0,30},{2,0},{4,2},{6,4},{8,6},{10,8},{12,10},{14,12},{16,14},{18,... | collective-permute-start | bytes 248840 | tf_op jit(solution)/shard_map/ppermute | solution.py:442
  18.4 21.6 %copy-start.1 = (bf16[512,512]{1,0:T(8,128)(2,1)S(1)}, bf16[512,512]{1,0:T(8,128)(2,1)}, u32[]{:S(2)}) copy-start(bf16[512,512]{1,0:T(8,128)(2,1)} %wout.3) | copy-start | bytes 1572868
  23.2 10.8 %collective-permute-start.3 = (bf16[36,1024]{1,0:T(8,128)(2,1)S(1)}, bf16[36,1024]{1,0:T(8,128)(2,1)S(1)}, u32[]{:S(2)}, u32[]{:S(2)}) collective-permute-start(bf16[36,1024]{1,0:T(8,128)(2,1)S(1)} %get-tuple-element.51), channel_id=1, source_target_pairs={{254,0},{224,2},{226,4},{228,6},{230,8},{232,10},{234,12},{236,14}... | collective-permute-start | bytes 221192 | tf_op jit(solution)/shard_map/ppermute | solution.py:442
  24.2 9.9 %collective-permute-start.4 = (bf16[36,1024]{1,0:T(8,128)(2,1)S(1)}, bf16[36,1024]{1,0:T(8,128)(2,1)S(1)}, u32[]{:S(2)}, u32[]{:S(2)}) collective-permute-start(bf16[36,1024]{1,0:T(8,128)(2,1)S(1)} %get-tuple-element.52), channel_id=1, source_target_pairs={{224,0},{226,2},{228,4},{230,6},{232,8},{234,10},{236,12},{238,14}... | collective-permute-start | bytes 221192 | tf_op jit(solution)/shard_map/ppermute | solution.py:442
  25.2 8.9 %collective-permute-start.5 = (bf16[36,1024]{1,0:T(8,128)(2,1)S(1)}, bf16[36,1024]{1,0:T(8,128)(2,1)S(1)}, u32[]{:S(2)}, u32[]{:S(2)}) collective-permute-start(bf16[36,1024]{1,0:T(8,128)(2,1)S(1)} %get-tuple-element.53), channel_id=1, source_target_pairs={{30,0},{0,2},{2,4},{4,6},{6,8},{8,10},{10,12},{12,14},{14,16},{16,... | collective-permute-start | bytes 221192 | tf_op jit(solution)/shard_map/ppermute | solution.py:442
  34.1 10.9 %collective-permute-start.12 = (bf16[144,1024]{1,0:T(8,128)(2,1)S(1)}, bf16[144,1024]{1,0:T(8,128)(2,1)S(1)}, u32[]{:S(2)}, u32[]{:S(2)}) collective-permute-start(bf16[144,1024]{1,0:T(8,128)(2,1)S(1)} %get-tuple-element.75), channel_id=1, source_target_pairs={{0,192},{2,194},{4,196},{6,198},{8,200},{10,202},{12,204},{14,206}... | collective-permute-start | bytes 884744 | tf_op jit(solution)/shard_map/ppermute | solution.py:464
  35.2 11.3 %collective-permute-start.13 = (bf16[144,1024]{1,0:T(8,128)(2,1)S(1)}, bf16[144,1024]{1,0:T(8,128)(2,1)S(1)}, u32[]{:S(2)}, u32[]{:S(2)}) collective-permute-start(bf16[144,1024]{1,0:T(8,128)(2,1)S(1)} %get-tuple-element.76), channel_id=1, source_target_pairs={{0,14},{2,4},{4,2},{6,8},{8,6},{10,12},{12,10},{14,0},{32,46},{34,... | collective-permute-start | bytes 884744 | tf_op jit(solution)/shard_map/ppermute | solution.py:464
  35.3 14.5 %collective-permute-start.14 = (bf16[144,1024]{1,0:T(8,128)(2,1)S(1)}, bf16[144,1024]{1,0:T(8,128)(2,1)S(1)}, u32[]{:S(2)}, u32[]{:S(2)}) collective-permute-start(bf16[144,1024]{1,0:T(8,128)(2,1)S(1)} %get-tuple-element.77), channel_id=1, source_target_pairs={{0,206},{2,196},{4,194},{6,200},{8,198},{10,204},{12,202},{14,192}... | collective-permute-start | bytes 884744 | tf_op jit(solution)/shard_map/ppermute | solution.py:464
  42.9 9.6 %collective-permute-start.6 = (bf16[144,1024]{1,0:T(8,128)(2,1)S(1)}, bf16[144,1024]{1,0:T(8,128)(2,1)S(1)}, u32[]{:S(2)}, u32[]{:S(2)}) collective-permute-start(bf16[144,1024]{1,0:T(8,128)(2,1)S(1)} %get-tuple-element.60), channel_id=1, source_target_pairs={{0,64},{2,66},{4,68},{6,70},{8,72},{10,74},{12,76},{14,78},{32,96}... | collective-permute-start | bytes 884744 | tf_op jit(solution)/shard_map/ppermute | solution.py:464
  43.0 12.4 %collective-permute-start.7 = (bf16[144,1024]{1,0:T(8,128)(2,1)S(1)}, bf16[144,1024]{1,0:T(8,128)(2,1)S(1)}, u32[]{:S(2)}, u32[]{:S(2)}) collective-permute-start(bf16[144,1024]{1,0:T(8,128)(2,1)S(1)} %get-tuple-element.61), channel_id=1, source_target_pairs={{0,2},{2,0},{4,6},{6,4},{8,10},{10,8},{12,14},{14,12},{32,34},{34,... | collective-permute-start | bytes 884744 | tf_op jit(solution)/shard_map/ppermute | solution.py:464
  45.0 10.5 %collective-permute-start.8 = (bf16[144,1024]{1,0:T(8,128)(2,1)S(1)}, bf16[144,1024]{1,0:T(8,128)(2,1)S(1)}, u32[]{:S(2)}, u32[]{:S(2)}) collective-permute-start(bf16[144,1024]{1,0:T(8,128)(2,1)S(1)} %get-tuple-element.62), channel_id=1, source_target_pairs={{0,66},{2,64},{4,70},{6,68},{8,74},{10,72},{12,78},{14,76},{32,98}... | collective-permute-start | bytes 884744 | tf_op jit(solution)/shard_map/ppermute | solution.py:464
  50.7 8.9 %collective-permute-start.15 = (bf16[128,512]{1,0:T(8,128)(2,1)S(1)}, bf16[128,512]{1,0:T(8,128)(2,1)S(1)}, u32[]{:S(2)}, u32[]{:S(2)}) collective-permute-start(bf16[128,512]{1,0:T(8,128)(2,1)S(1)} %get-tuple-element.79), channel_id=1, source_target_pairs={{0,32},{2,34},{4,36},{6,38},{8,40},{10,42},{12,44},{14,46},{32,0},... | collective-permute-start | bytes 393224 | tf_op jit(solution)/shard_map/ppermute | solution.py:464
  51.1 8.8 %collective-permute-start.16 = (bf16[128,512]{1,0:T(8,128)(2,1)S(1)}, bf16[128,512]{1,0:T(8,128)(2,1)S(1)}, u32[]{:S(2)}, u32[]{:S(2)}) collective-permute-start(bf16[128,512]{1,0:T(8,128)(2,1)S(1)} %get-tuple-element.80), channel_id=1, source_target_pairs={{0,16},{2,18},{4,20},{6,22},{8,24},{10,26},{12,28},{14,30},{32,48}... | collective-permute-start | bytes 393224 | tf_op jit(solution)/shard_map/ppermute | solution.py:464
  52.5 8.4 %collective-permute-start.17 = (bf16[128,512]{1,0:T(8,128)(2,1)S(1)}, bf16[128,512]{1,0:T(8,128)(2,1)S(1)}, u32[]{:S(2)}, u32[]{:S(2)}) collective-permute-start(bf16[128,512]{1,0:T(8,128)(2,1)S(1)} %get-tuple-element.81), channel_id=1, source_target_pairs={{0,48},{2,50},{4,52},{6,54},{8,56},{10,58},{12,60},{14,62},{32,16}... | collective-permute-start | bytes 393224 | tf_op jit(solution)/shard_map/ppermute | solution.py:464
  55.5 33.9 %copy-start = (bf16[512,1536]{1,0:T(8,128)(2,1)S(1)}, bf16[512,1536]{1,0:T(8,128)(2,1)}, u32[]{:S(2)}) copy-start(bf16[512,1536]{1,0:T(8,128)(2,1)} %wqkv.3) | copy-start | bytes 4718596
  55.5 33.9 %copy-start.3 = (bf16[2,6,12,512]{3,0,2,1:T(2,128)(2,1)S(1)}, bf16[2,6,12,512]{3,0,2,1:T(2,128)(2,1)}, u32[]{:S(2)}) copy-start(bf16[2,6,12,512]{3,0,2,1:T(2,128)(2,1)} %param.9) | copy-start | bytes 442372
  55.5 33.9 %copy-start.5 = (f32[512]{0:T(512)S(1)}, f32[512]{0:T(512)}, u32[]{:S(2)}) copy-start(f32[512]{0:T(512)} %param.12) | copy-start | bytes 6148
  56.3 6.7 %collective-permute-start.10 = (bf16[128,512]{1,0:T(8,128)(2,1)S(1)}, bf16[128,512]{1,0:T(8,128)(2,1)S(1)}, u32[]{:S(2)}, u32[]{:S(2)}) collective-permute-start(bf16[128,512]{1,0:T(8,128)(2,1)S(1)} %get-tuple-element.65), channel_id=1, source_target_pairs={{0,16},{2,18},{4,20},{6,22},{8,24},{10,26},{12,28},{14,30},{32,48}... | collective-permute-start | bytes 393224 | tf_op jit(solution)/shard_map/ppermute | solution.py:464
  57.0 7.3 %collective-permute-start.11 = (bf16[128,512]{1,0:T(8,128)(2,1)S(1)}, bf16[128,512]{1,0:T(8,128)(2,1)S(1)}, u32[]{:S(2)}, u32[]{:S(2)}) collective-permute-start(bf16[128,512]{1,0:T(8,128)(2,1)S(1)} %get-tuple-element.66), channel_id=1, source_target_pairs={{0,48},{2,50},{4,52},{6,54},{8,56},{10,58},{12,60},{14,62},{32,16}... | collective-permute-start | bytes 393224 | tf_op jit(solution)/shard_map/ppermute | solution.py:464
  59.5 5.0 %collective-permute-start.9 = (bf16[128,512]{1,0:T(8,128)(2,1)S(1)}, bf16[128,512]{1,0:T(8,128)(2,1)S(1)}, u32[]{:S(2)}, u32[]{:S(2)}) collective-permute-start(bf16[128,512]{1,0:T(8,128)(2,1)S(1)} %get-tuple-element.64), channel_id=1, source_target_pairs={{0,32},{2,34},{4,36},{6,38},{8,40},{10,42},{12,44},{14,46},{32,0},... | collective-permute-start | bytes 393224 | tf_op jit(solution)/shard_map/ppermute | solution.py:464
  82.1 19.0 %all-to-all-start.1 = ((f32[128,1,128]{2,1,0:T(1,128)}), f32[128,1,128]{2,1,0:T(1,128)S(1)}, u32[]{:S(2)}, u32[]{:S(2)}) async-start(f32[128,1,128]{2,1,0:T(1,128)} %get-tuple-element.82), calls=%async_computation.1 | async-start | bytes 131072 | tf_op jit(solution)/shard_map/all_to_all | solution.py:564

commit v8 on v7

--- a/solution.py
+++ b/solution.py
@@ -240,34 +240,38 @@
 
 
 def first_forward(
-    me, region, tok, cot, gain_hbm, wqkv_hbm, wout_hbm,
-    x0, x1, x2, x3, keep_ref, scratch, lab_scratch, gain, wqkv, wout, sems,
+    me, tok_hbm, gain_hbm, region_hbm, cot_hbm, wqkv_hbm, wout_hbm,
+    x0, x1, x2, x3, keep_ref, scratch, lab_scratch, tok, gain, region, cot, wqkv, wout, sems,
 ):
+    far = (tok_hbm, gain_hbm, region_hbm, cot_hbm, wqkv_hbm, wout_hbm)
     copies = [
         pltpu.make_async_copy(source, target, sems.at[i])
-        for i, (source, target) in enumerate(((gain_hbm, gain), (wqkv_hbm, wqkv), (wout_hbm, wout)))
+        for i, (source, target) in enumerate(zip(far, (tok, gain, region, cot, wqkv, wout)))
     ]
     for copy in copies:
         copy.start()
     refs = (x0, x1, x2, x3)
-    take_field(cot, scratch)
-    for slot, ref in enumerate(refs):
-        ref[:, D : 2 * D] = scratch[slot * QUART : (slot + 1) * QUART, :].astype(BF16)
+    copies[0].wait()
+    values = take_field(tok, scratch)
+    copies[1].wait()
+    normed, _, _ = norm_parts(values, gain[...])
+    copies[2].wait()
     labels = jnp.broadcast_to(take_labels(region), (TOK, LANES))
     near = lax.broadcasted_iota(jnp.int32, (TOK, LANES), 0) < 2 * QUART
     moved = labels + jnp.where(near & (me[0] < LON), 4.0, 0.0)
     scatter_rows(moved, lab_scratch, refs, 2 * D)
-    values = take_field(tok, scratch)
-    copies[0].wait()
-    normed, _, _ = norm_parts(values, gain[...])
-    copies[1].wait()
+    copies[3].wait()
+    take_field(cot, scratch)
+    for slot, ref in enumerate(refs):
+        ref[:, D : 2 * D] = scratch[slot * QUART : (slot + 1) * QUART, :].astype(BF16)
+    copies[4].wait()
     proj = dot_nn(normed, wqkv[...]).astype(BF16)
     keep_ref[:, : 3 * D] = proj
     keep_ref[:, 4 * D : 5 * D] = normed
     keep_ref[:, 5 * D :] = labels.astype(BF16)
     attended, _ = attention(proj, label_bias(labels))
     keep_ref[:, 3 * D : 4 * D] = attended
-    copies[2].wait()
+    copies[5].wait()
     scatter_rows(values + dot_nn(attended, wout[...]), scratch, refs, 0)
 
 
@@ -288,22 +292,26 @@
     attended, dproj = attention(proj, label_bias(labels), grad=datt)
     att_ref[...] = attended
     store_right(dproj, g16, right_ref)
-    scatter_rows(values + dot_nn(attended, wout[...]), scratch, back, 0)
     dnormed = dot_nt(dproj, wqkv[...])
-    scatter_rows(norm_back(dnormed, gain[...], xhat, rstd, g), scratch, back, D)
-
-
-def second_pack(me, normed, attended, right, p0, p1, p2, p3, left_n, left_a):
+    scatter_rows(norm_back(dnormed, gain[...], xhat, rstd, g), scratch, back, 0)
+
+
+def second_pack(
+    me, normed, attended, right, x0, x1, x2, x3, wout,
+    p0, p1, p2, p3, r0, r1, r2, r3, left_n, left_a, scratch,
+):
     order = regroup(row_order(chip_second))
     left_n[...] = dot_nn(normed[...], order).astype(BF16)
     left_a[...] = dot_nn(attended[...], order).astype(BF16)
     pack(members_second(*here(me))[0], (left_n, left_a), right, (p0, p1, p2, p3))
+    values = gather_rows((x0, x1, x2, x3), scratch, 0)
+    scatter_rows(values + dot_nn(attended[...], wout[...]), scratch, (r0, r1, r2, r3), 0)
 
 
 def first_backward(
     me, b0, b1, b2, b3, wout, keep, right_ref, p0, p1, p2, p3, scratch, left_n, left_a
 ):
-    g16 = gather_rows((b0, b1, b2, b3), scratch, D).astype(BF16)
+    g16 = gather_rows((b0, b1, b2, b3), scratch, 0).astype(BF16)
     datt = dot_nt(g16, wout[...]).astype(BF16)
     bias = label_bias(keep[:, 5 * D :].astype(F32))
     _, dproj = attention(keep[...], bias, grad=datt, attended=keep[:, 3 * D : 4 * D])
@@ -314,11 +322,13 @@
     pack(members_first(*here(me))[0], (left_n, left_a), right_ref, (p0, p1, p2, p3))
 
 
-def first_rest(b0, b1, b2, b3, tok, gain, wqkv, right, tg_ref, result_ref, scratch):
-    back = (b0, b1, b2, b3)
-    put_field(gather_rows(back, scratch, 0), scratch, result_ref)
+def place(r0, r1, r2, r3, result_ref, scratch):
+    put_field(gather_rows((r0, r1, r2, r3), scratch, 0), scratch, result_ref)
+
+
+def first_rest(b0, b1, b2, b3, tok, gain, wqkv, right, tg_ref, scratch):
     _, xhat, rstd = norm_parts(take_field(tok, scratch), gain[...])
-    g = gather_rows(back, scratch, D)
+    g = gather_rows((b0, b1, b2, b3), scratch, 0)
     dnormed = dot_nt(right[0], wqkv[:, :D])
     dnormed += dot_nt(right[1], wqkv[:, D : 2 * D])
     dnormed += dot_nt(right[2], wqkv[:, 2 * D :])
@@ -510,25 +520,32 @@
         [
             (TOK, D),
             (TOK, LANES),
+            pltpu.VMEM(tok.shape, BF16),
             (1, D),
+            pltpu.VMEM(lab.shape, jnp.int32),
+            pltpu.VMEM(cot.shape, BF16),
             pltpu.VMEM((D, 3 * D), BF16),
             pltpu.VMEM((D, D), BF16),
-            pltpu.SemaphoreType.DMA((3,)),
+            pltpu.SemaphoreType.DMA((6,)),
         ],
-        me, *in_hbm(lab, tok, cot, gain_a, unshifted_query_key_value, out_first),
-        scalar=True, far=3,
+        me, *in_hbm(tok, gain_a, lab, cot, unshifted_query_key_value, out_first),
+        scalar=True, far=6,
     )
     x = send(x, tables)
     *back, normed_b, att_b, right_b = call(
         second_main,
-        [shape_of(QUART, 2 * D)] * 4 + [field, field, fields],
+        [shape_of(QUART, D)] * 4 + [field, field, fields],
         [(TOK, D), (TOK, LANES)],
         *x, gain_b, shifted_query_key_value, out_second,
     )
     back = send(back, tables, back=True)
     half = pltpu.VMEM((TOK, D), BF16)
-    pack_b = call(
-        second_pack, packs, [half, half], me, normed_b, att_b, right_b, scalar=True
+    *pack_b, r0, r1, r2, r3 = call(
+        second_pack,
+        packs + [pltpu.HBM((QUART, D), BF16)] * 4,
+        [half, half, (TOK, D)],
+        me, normed_b, att_b, right_b, *x, out_second,
+        scalar=True,
     )
     pack_b = swap_second(after(pack_b, back[:3]), 0)
     right_a, *pack_a = call(
@@ -540,21 +557,24 @@
     )
     pack_a = swap_first(pack_a, 0)
     grid = shape_of(WLAT, WLON, WLEV, D)
-    token_gradient, result = call(
+    (token_gradient,) = call(
         first_rest,
-        [grid, grid],
+        [grid],
         [(TOK, D)],
         *back, tok, gain_a, unshifted_query_key_value, right_a,
     )
+    pack_b, token_gradient = lax.optimization_barrier((pack_b, token_gradient))
     token_gradient = token_gradient.transpose(2, 0, 1, 3)
-    result = result.transpose(2, 0, 1, 3)
 
     rows = [shape_of(PLANE_ROWS, WIDE)] * GROUP
     sum_b = swap_second(call(second_weights, rows, [(D, WIDE)], me, *in_vmem(*pack_b), scalar=True), 1)
     sum_a = swap_first(call(first_weights, rows, [(D, WIDE)], me, *in_vmem(*pack_a), scalar=True), 1)
     piece = (len(SHEET), 2 * PIECE, LANES)
     (sums,) = call(add_rows, [shape_of(*piece)], [piece], *sum_a, *sum_b)
-    sums = exchange(sums, SHEETS)
+    res = send(after([r0, r1, r2, r3], sums), tables, back=True)
+    sums, res = lax.optimization_barrier((exchange(sums, SHEETS), res))
+    (result,) = call(place, [grid], [(TOK, D)], *res)
+    result = result.transpose(2, 0, 1, 3)
     mine, tiles = call(
         own_rows,
         [shape_of(GROUP, 2 * PIECE, LANES, dtype=F32), shape_of(LAT * LON, 1, LANES, dtype=F32)],

time: 103 us -> 108 us (1.049)
  blocking collectives: 16.6 us -> 0 us
  starting transfers between devices: 36.7 us -> 50.2 us
  waiting for transfers between devices: 30.4 us -> 36.6 us
  Pallas kernels: 17.4 us -> 19 us
    all_to_all x1 -> x0, blocking collectives: 16.6 us -> none  [exchange(): return lax.all_to_all(parts, ('lat', 'lon'), 0, 0, axis_index_groups=groups)]
    all_to_all x0 -> x1, starting transfers between devices: none -> 7.45 us  [exchange(): return lax.all_to_all(parts, ('lat', 'lon'), 0, 0, axis_index_groups=groups)]
    ppermute x6 -> x9, waiting for transfers between devices: 10.5 us -> 16.3 us  [send(): out.append(lax.ppermute(part, ('lat', 'lon'), pairs))]
    ppermute x6 -> x9, starting transfers between devices: 13.4 us -> 19.1 us  [send(): out.append(lax.ppermute(part, ('lat', 'lon'), pairs))]
    pallas_call x10 -> x11, Pallas kernels: 17.4 us -> 19 us  [call(): pl.pallas_call(kernel, out_shape=outs, in_specs=specs, out_specs=[whole]...]
  transfers between devices with their start and end apart: 19 -> 23, of which waited for: 10 -> 12; matrix products, arithmetic and copies ran while one was open for 0% -> 0% of each run, Pallas kernels for 7% -> 5%
where the time goes in v8:
time: 108 us; the launch traced here: 107 us
  starting transfers between devices  50.2 us (46%)
  waiting for transfers between devices  36.6 us (34%)
  Pallas kernels  19 us (18%)
    ppermute x9, starting transfers between devices, send(): out.append(lax.ppermute(part, ('lat', 'lon'), pairs))  19.1 us
    pallas_call x11, Pallas kernels, call(): pl.pallas_call(kernel, out_shape=outs, in_specs=specs, out_specs=[whole]...  19 us
    ppermute x9, waiting for transfers between devices, send(): out.append(lax.ppermute(part, ('lat', 'lon'), pairs))  16.3 us
    ppermute x12, starting transfers between devices, swap(): out[step] = lax.ppermute(parts[step], ('lat', 'lon'), pairs)  15.8 us
    all_to_all x1, waiting for transfers between devices, on_device(): tiles = lax.all_to_all(tiles, ('lat', 'lon'), 0, 0)  10.9 us
    ppermute x12, waiting for transfers between devices, swap(): out[step] = lax.ppermute(parts[step], ('lat', 'lon'), pairs)  9.38 us
    all_to_all x1, starting transfers between devices, on_device(): tiles = lax.all_to_all(tiles, ('lat', 'lon'), 0, 0)  7.82 us
    all_to_all x1, starting transfers between devices, exchange(): return lax.all_to_all(parts, ('lat', 'lon'), 0, 0, axis_index_groups=groups)  7.45 us
  transfers between devices with their start and end apart: 23, of which 12 were waited for; matrix products, arithmetic and copies ran while one was open for 0% of the time, Pallas kernels for 5%

profile of v8, /device:TPU:0, one launch (start us, length us, event | category | flops | bytes accessed | tf_op | source)
XLA Modules:
  0.0 106.8 jit_solution(7743380898977160969)
XLA Ops:
  0.7 3.3 %first_forward.1 = (bf16[36,1152]{1,0:T(8,128)(2,1)S(1)}, bf16[36,1152]{1,0:T(8,128)(2,1)S(1)}, bf16[36,1152]{1,0:T(8,128)(2,1)S(1)}, bf16[36,1152]{1,0:T(8,128)(2,1)S(1)}, bf16[144,2688]{1,0:T(8,128)(2,1)S(1)}) custom-call(s32[1]{0:T(128)} %bitcast.me, bf16[6,12,2,512]{3,2,1,0:T(2,128)(2,1)} %bitcast.8, f32[1,512]{1,0:T(1,128)} %bitcast.10, ...), custom_call_target="tpu_custom_call" | custom-call | tf_op jit(solution)/shard_map/first_forward/pallas_call | solution.py:412
  4.0 0.0 copy-start.1
  4.0 8.8 %collective-permute-start = (bf16[36,1152]{1,0:T(8,128)(2,1)S(1)}, bf16[36,1152]{1,0:T(8,128)(2,1)S(1)}, u32[]{:S(2)}, u32[]{:S(2)}) collective-permute-start(bf16[36,1152]{1,0:T(8,128)(2,1)S(1)} %get-tuple-element.63), channel_id=1, source_target_pairs={{0,254},{2,224},{4,226},{6,228},{8,230},{10,232},{12,234},{14,236}... | collective-permute-start | bytes 248840 | tf_op jit(solution)/shard_map/ppermute | solution.py:452
  12.9 0.1 collective-permute-start.1
  13.0 2.5 %collective-permute-start.2 = (bf16[36,1152]{1,0:T(8,128)(2,1)S(1)}, bf16[36,1152]{1,0:T(8,128)(2,1)S(1)}, u32[]{:S(2)}, u32[]{:S(2)}) collective-permute-start(bf16[36,1152]{1,0:T(8,128)(2,1)S(1)} %get-tuple-element.65), channel_id=1, source_target_pairs={{0,30},{2,0},{4,2},{6,4},{8,6},{10,8},{12,10},{14,12},{16,14},{18,... | collective-permute-start | bytes 248840 | tf_op jit(solution)/shard_map/ppermute | solution.py:452
  15.5 1.9 %collective-permute-done.1.x1 = bf16[36,1152]{1,0:T(8,128)(2,1)S(1)} collective-permute-done((bf16[36,1152]{1,0:T(8,128)(2,1)S(1)}, bf16[36,1152]{1,0:T(8,128)(2,1)S(1)}, u32[]{:S(2)}, u32[]{:S(2)}) %collective-permute-start.1) | collective-permute-done | bytes 82976 | tf_op jit(solution)/shard_map/ppermute | solution.py:452
  17.4 0.3 collective-permute-done.2.x2
  17.7 4.7 %second_main.1 = (bf16[36,512]{1,0:T(8,128)(2,1)S(1)}, bf16[36,512]{1,0:T(8,128)(2,1)S(1)}, bf16[36,512]{1,0:T(8,128)(2,1)S(1)}, bf16[36,512]{1,0:T(8,128)(2,1)S...) custom-call(bf16[36,1152]{1,0:T(8,128)(2,1)S(1)} %collective-permute-done.x0, ...), custom_call_target="tpu_custom_call" | custom-call | tf_op jit(solution)/shard_map/second_main/pallas_call | solution.py:412
  22.4 0.9 collective-permute-start.3
  23.3 1.0 collective-permute-start.4
  24.3 8.0 %collective-permute-done.3.b0 = bf16[36,512]{1,0:T(8,128)(2,1)S(1)} collective-permute-done((bf16[36,512]{1,0:T(8,128)(2,1)S(1)}, bf16[36,512]{1,0:T(8,128)(2,1)S(1)}, u32[]{:S(2)}, u32[]{:S(2)}) %collective-permute-start.3) | collective-permute-done | bytes 36896 | tf_op jit(solution)/shard_map/ppermute | solution.py:452
  32.3 0.0 collective-permute-done.5.b2
  32.3 3.1 %first_backward.1 = (bf16[4,144,512]{2,1,0:T(8,128)(2,1)S(1)}, bf16[144,1024]{1,0:T(8,128)(2,1)S(1)}, bf16[144,1024]{1,0:T(8,128)(2,1)S(1)}, bf16[144,1024]{1,0:T(8,128)(2,1)S(1)}, bf16[144,1024]{1,0:T(8,128)(2,1)S(1)}) custom-call(s32[1]{0:T(128)} %bitcast.me, bf16[36,512]{1,0:T(8,128)(2,1)S(1)} %collective-permute-done.3.b0, ...), custom_call_target="tpu_custom_call" | custom-call | tf_op jit(solution)/shard_map/first_backward/pallas_call | solution.py:412
  35.4 0.0 copy-start.4
  35.5 0.1 collective-permute-start.6
  35.6 0.1 collective-permute-start.7
  35.7 3.4 %collective-permute-start.8 = (bf16[144,1024]{1,0:T(8,128)(2,1)S(1)}, bf16[144,1024]{1,0:T(8,128)(2,1)S(1)}, u32[]{:S(2)}, u32[]{:S(2)}) collective-permute-start(bf16[144,1024]{1,0:T(8,128)(2,1)S(1)} %get-tuple-element.75), channel_id=1, source_target_pairs={{0,66},{2,64},{4,70},{6,68},{8,74},{10,72},{12,78},{14,76},{32,98}... | collective-permute-start | bytes 884744 | tf_op jit(solution)/shard_map/ppermute | solution.py:474
  39.0 1.4 %second_pack.1 = (bf16[144,1024]{1,0:T(8,128)(2,1)S(1)}, bf16[144,1024]{1,0:T(8,128)(2,1)S(1)}, bf16[144,1024]{1,0:T(8,128)(2,1)S(1)}, bf16[144,1024]{1,0:T(8,12...) custom-call(s32[1]{0:T(128)} %bitcast.me, ...), custom_call_target="tpu_custom_call" | custom-call | tf_op jit(solution)/shard_map/second_pack/pallas_call | solution.py:412
  40.4 1.6 %collective-permute-start.12 = (bf16[144,1024]{1,0:T(8,128)(2,1)S(1)}, bf16[144,1024]{1,0:T(8,128)(2,1)S(1)}, u32[]{:S(2)}, u32[]{:S(2)}) collective-permute-start(bf16[144,1024]{1,0:T(8,128)(2,1)S(1)} %get-tuple-element.88), channel_id=1, source_target_pairs={{0,192},{2,194},{4,196},{6,198},{8,200},{10,202},{12,204},{14,206}... | collective-permute-start | bytes 884744 | tf_op jit(solution)/shard_map/ppermute | solution.py:474
  42.0 0.0 collective-permute-start.13
  42.0 3.4 %collective-permute-done.6.refs_1_ = bf16[144,1024]{1,0:T(8,128)(2,1)S(1)} collective-permute-done((bf16[144,1024]{1,0:T(8,128)(2,1)S(1)}, bf16[144,1024]{1,0:T(8,128)(2,1)S(1)}, u32[]{:S(2)}, u32[]{:S(2)}) %collective-permute-start.6) | collective-permute-done | bytes 294944 | tf_op jit(solution)/shard_map/ppermute | solution.py:474
  45.4 1.1 %collective-permute-start.14 = (bf16[144,1024]{1,0:T(8,128)(2,1)S(1)}, bf16[144,1024]{1,0:T(8,128)(2,1)S(1)}, u32[]{:S(2)}, u32[]{:S(2)}) collective-permute-start(bf16[144,1024]{1,0:T(8,128)(2,1)S(1)} %get-tuple-element.90), channel_id=1, source_target_pairs={{0,206},{2,196},{4,194},{6,200},{8,198},{10,204},{12,202},{14,192}... | collective-permute-start | bytes 884744 | tf_op jit(solution)/shard_map/ppermute | solution.py:474
  46.5 2.4 %collective-permute-done.8.refs_3_ = bf16[144,1024]{1,0:T(8,128)(2,1)S(1)} collective-permute-done((bf16[144,1024]{1,0:T(8,128)(2,1)S(1)}, bf16[144,1024]{1,0:T(8,128)(2,1)S(1)}, u32[]{:S(2)}, u32[]{:S(2)}) %collective-permute-start.8) | collective-permute-done | bytes 294944 | tf_op jit(solution)/shard_map/ppermute | solution.py:474
  48.9 0.8 first_weights.1
  49.8 0.1 collective-permute-start.9
  49.9 1.6 %first_rest.1 = bf16[6,12,2,512]{3,2,1,0:T(2,128)(2,1)} custom-call(bf16[36,512]{1,0:T(8,128)(2,1)S(1)} %collective-permute-done.3.b0, bf16[36,512]{1,0:T(8,128)(2,1)S(1)} %collective-permute-done.4.b1, bf16[36,512]{1,0:T(8,128)(2,1)S(1)} %collective-permute-done.5.b2, bf16[36,512]{1,0:T(8,128)(2,1)S(1)} %get-tuple-element.70.b3, ...), custom_call_target="tpu_custom_call" | custom-call | tf_op jit(solution)/shard_map/first_rest/pallas_call | solution.py:412
  51.5 2.1 %collective-permute-start.10 = (bf16[128,512]{1,0:T(8,128)(2,1)S(1)}, bf16[128,512]{1,0:T(8,128)(2,1)S(1)}, u32[]{:S(2)}, u32[]{:S(2)}) collective-permute-start(bf16[128,512]{1,0:T(8,128)(2,1)S(1)} %get-tuple-element.78), channel_id=1, source_target_pairs={{0,16},{2,18},{4,20},{6,22},{8,24},{10,26},{12,28},{14,30},{32,48}... | collective-permute-start | bytes 393224 | tf_op jit(solution)/shard_map/ppermute | solution.py:474
  53.5 2.6 %collective-permute-start.11 = (bf16[128,512]{1,0:T(8,128)(2,1)S(1)}, bf16[128,512]{1,0:T(8,128)(2,1)S(1)}, u32[]{:S(2)}, u32[]{:S(2)}) collective-permute-start(bf16[128,512]{1,0:T(8,128)(2,1)S(1)} %get-tuple-element.79), channel_id=1, source_target_pairs={{0,48},{2,50},{4,52},{6,54},{8,56},{10,58},{12,60},{14,62},{32,16}... | collective-permute-start | bytes 393224 | tf_op jit(solution)/shard_map/ppermute | solution.py:474
  56.1 0.8 second_weights.1
  57.0 0.1 collective-permute-start.15
  57.1 2.1 %collective-permute-start.16 = (bf16[128,512]{1,0:T(8,128)(2,1)S(1)}, bf16[128,512]{1,0:T(8,128)(2,1)S(1)}, u32[]{:S(2)}, u32[]{:S(2)}) collective-permute-start(bf16[128,512]{1,0:T(8,128)(2,1)S(1)} %get-tuple-element.98), channel_id=1, source_target_pairs={{0,16},{2,18},{4,20},{6,22},{8,24},{10,26},{12,28},{14,30},{32,48}... | collective-permute-start | bytes 393224 | tf_op jit(solution)/shard_map/ppermute | solution.py:474
  59.2 2.6 %collective-permute-start.17 = (bf16[128,512]{1,0:T(8,128)(2,1)S(1)}, bf16[128,512]{1,0:T(8,128)(2,1)S(1)}, u32[]{:S(2)}, u32[]{:S(2)}) collective-permute-start(bf16[128,512]{1,0:T(8,128)(2,1)S(1)} %get-tuple-element.99), channel_id=1, source_target_pairs={{0,48},{2,50},{4,52},{6,54},{8,56},{10,58},{12,60},{14,62},{32,16}... | collective-permute-start | bytes 393224 | tf_op jit(solution)/shard_map/ppermute | solution.py:474
  61.8 0.1 collective-permute-done.11.a3
  61.9 0.1 collective-permute-done.15.b1
  62.0 1.6 %collective-permute-done.16.b2 = bf16[128,512]{1,0:T(8,128)(2,1)S(1)} collective-permute-done((bf16[128,512]{1,0:T(8,128)(2,1)S(1)}, bf16[128,512]{1,0:T(8,128)(2,1)S(1)}, u32[]{:S(2)}, u32[]{:S(2)}) %collective-permute-start.16) | collective-permute-done | bytes 131104 | tf_op jit(solution)/shard_map/ppermute | solution.py:474
  63.6 1.7 %collective-permute-done.17.b3 = bf16[128,512]{1,0:T(8,128)(2,1)S(1)} collective-permute-done((bf16[128,512]{1,0:T(8,128)(2,1)S(1)}, bf16[128,512]{1,0:T(8,128)(2,1)S(1)}, u32[]{:S(2)}, u32[]{:S(2)}) %collective-permute-start.17) | collective-permute-done | bytes 131104 | tf_op jit(solution)/shard_map/ppermute | solution.py:474
  65.4 0.9 add_rows.1
  66.3 7.5 %all-to-all-start = ((bf16[32,32,128]{2,1,0:T(8,128)(2,1)}), bf16[32,32,128]{2,1,0:T(8,128)(2,1)S(1)}, u32[]{:S(2)}, u32[]{:S(2)}) async-start(bf16[32,32,128]{2,1,0:T(8,128)(2,1)} %add_rows.1), calls=%async_computation | async-start | bytes 524288 | tf_op jit(solution)/shard_map/all_to_all | solution.py:487
  73.7 0.3 collective-permute-start.18
  74.1 3.9 %collective-permute-start.19 = (bf16[36,512]{1,0:T(8,128)(2,1)S(1)}, bf16[36,512]{1,0:T(8,128)(2,1)S(1)}, u32[]{:S(2)}, u32[]{:S(2)}) collective-permute-start(bf16[36,512]{1,0:T(8,128)(2,1)S(1)} %copy-done.9), channel_id=1, source_target_pairs={{224,0},{226,2},{228,4},{230,6},{232,8},{234,10},{236,12},{238,14}... | collective-permute-start | bytes 110600 | tf_op jit(solution)/shard_map/ppermute | solution.py:452
  78.0 1.5 %collective-permute-start.20 = (bf16[36,512]{1,0:T(8,128)(2,1)S(1)}, bf16[36,512]{1,0:T(8,128)(2,1)S(1)}, u32[]{:S(2)}, u32[]{:S(2)}) collective-permute-start(bf16[36,512]{1,0:T(8,128)(2,1)S(1)} %copy-done.8), channel_id=1, source_target_pairs={{30,0},{0,2},{2,4},{4,6},{6,8},{8,10},{10,12},{12,14},{14,16},{16,... | collective-permute-start | bytes 110600 | tf_op jit(solution)/shard_map/ppermute | solution.py:452
  79.4 5.2 %collective-permute-done.18.r0 = bf16[36,512]{1,0:T(8,128)(2,1)S(1)} collective-permute-done((bf16[36,512]{1,0:T(8,128)(2,1)S(1)}, bf16[36,512]{1,0:T(8,128)(2,1)S(1)}, u32[]{:S(2)}, u32[]{:S(2)}) %collective-permute-start.18) | collective-permute-done | bytes 36896 | tf_op jit(solution)/shard_map/ppermute | solution.py:452
  84.6 1.0 collective-permute-done.20.r2
  85.6 0.8 own_rows.1
  86.4 7.8 %all-to-all-start.1 = ((f32[128,1,128]{2,1,0:T(1,128)}), f32[128,1,128]{2,1,0:T(1,128)S(1)}, u32[]{:S(2)}, u32[]{:S(2)}) async-start(f32[128,1,128]{2,1,0:T(1,128)} %get-tuple-element.114), calls=%async_computation.1 | async-start | bytes 131072 | tf_op jit(solution)/shard_map/all_to_all | solution.py:584
  94.2 0.8 place.1
  95.0 10.9 %all-to-all-done.1.tiles = f32[128,1,128]{2,1,0:T(1,128)S(1)} async-done(((f32[128,1,128]{2,1,0:T(1,128)}), f32[128,1,128]{2,1,0:T(1,128)S(1)}, u32[]{:S(2)}, u32[]{:S(2)}) %all-to-all-start.1) | async-done | bytes 65568 | tf_op jit(solution)/shard_map/all_to_all | solution.py:584
  106.0 0.8 clipped.1
  (31 shorter events, 0.1 us)
Async XLA Ops:
  0.6 17.0 %copy-start.7 = (f32[512]{0:T(512)S(1)}, f32[512]{0:T(512)}, u32[]{:S(2)}) copy-start(f32[512]{0:T(512)} %param.15) | copy-start | bytes 6148
  0.6 17.0 %copy-start.3 = (bf16[512,1536]{1,0:T(8,128)(2,1)S(1)}, bf16[512,1536]{1,0:T(8,128)(2,1)}, u32[]{:S(2)}) copy-start(bf16[512,1536]{1,0:T(8,128)(2,1)} %wqkv.2) | copy-start | bytes 4718596
  0.7 17.0 %copy-start.2 = (bf16[512,512]{1,0:T(8,128)(2,1)S(1)}, bf16[512,512]{1,0:T(8,128)(2,1)}, u32[]{:S(2)}) copy-start(bf16[512,512]{1,0:T(8,128)(2,1)} %wout.5) | copy-start | bytes 1572868
  4.0 28.3 %copy-start.1 = (bf16[512,512]{1,0:T(8,128)(2,1)S(1)}, bf16[512,512]{1,0:T(8,128)(2,1)}, u32[]{:S(2)}) copy-start(bf16[512,512]{1,0:T(8,128)(2,1)} %wout.4) | copy-start | bytes 1572868
  4.0 11.5 %collective-permute-start = (bf16[36,1152]{1,0:T(8,128)(2,1)S(1)}, bf16[36,1152]{1,0:T(8,128)(2,1)S(1)}, u32[]{:S(2)}, u32[]{:S(2)}) collective-permute-start(bf16[36,1152]{1,0:T(8,128)(2,1)S(1)} %get-tuple-element.63), channel_id=1, source_target_pairs={{0,254},{2,224},{4,226},{6,228},{8,230},{10,232},{12,234},{14,236}... | collective-permute-start | bytes 248840 | tf_op jit(solution)/shard_map/ppermute | solution.py:452
  12.9 4.6 %collective-permute-start.1 = (bf16[36,1152]{1,0:T(8,128)(2,1)S(1)}, bf16[36,1152]{1,0:T(8,128)(2,1)S(1)}, u32[]{:S(2)}, u32[]{:S(2)}) collective-permute-start(bf16[36,1152]{1,0:T(8,128)(2,1)S(1)} %get-tuple-element.64), channel_id=1, source_target_pairs={{0,224},{2,226},{4,228},{6,230},{8,232},{10,234},{12,236},{14,238}... | collective-permute-start | bytes 248840 | tf_op jit(solution)/shard_map/ppermute | solution.py:452
  13.0 4.7 %collective-permute-start.2 = (bf16[36,1152]{1,0:T(8,128)(2,1)S(1)}, bf16[36,1152]{1,0:T(8,128)(2,1)S(1)}, u32[]{:S(2)}, u32[]{:S(2)}) collective-permute-start(bf16[36,1152]{1,0:T(8,128)(2,1)S(1)} %get-tuple-element.65), channel_id=1, source_target_pairs={{0,30},{2,0},{4,2},{6,4},{8,6},{10,8},{12,10},{14,12},{16,14},{18,... | collective-permute-start | bytes 248840 | tf_op jit(solution)/shard_map/ppermute | solution.py:452
  22.4 9.9 %collective-permute-start.3 = (bf16[36,512]{1,0:T(8,128)(2,1)S(1)}, bf16[36,512]{1,0:T(8,128)(2,1)S(1)}, u32[]{:S(2)}, u32[]{:S(2)}) collective-permute-start(bf16[36,512]{1,0:T(8,128)(2,1)S(1)} %get-tuple-element.67), channel_id=1, source_target_pairs={{254,0},{224,2},{226,4},{228,6},{230,8},{232,10},{234,12},{236,14}... | collective-permute-start | bytes 110600 | tf_op jit(solution)/shard_map/ppermute | solution.py:452
  23.3 9.0 %collective-permute-start.4 = (bf16[36,512]{1,0:T(8,128)(2,1)S(1)}, bf16[36,512]{1,0:T(8,128)(2,1)S(1)}, u32[]{:S(2)}, u32[]{:S(2)}) collective-permute-start(bf16[36,512]{1,0:T(8,128)(2,1)S(1)} %get-tuple-element.68), channel_id=1, source_target_pairs={{224,0},{226,2},{228,4},{230,6},{232,8},{234,10},{236,12},{238,14}... | collective-permute-start | bytes 110600 | tf_op jit(solution)/shard_map/ppermute | solution.py:452
  24.3 8.0 %collective-permute-start.5 = (bf16[36,512]{1,0:T(8,128)(2,1)S(1)}, bf16[36,512]{1,0:T(8,128)(2,1)S(1)}, u32[]{:S(2)}, u32[]{:S(2)}) collective-permute-start(bf16[36,512]{1,0:T(8,128)(2,1)S(1)} %get-tuple-element.69), channel_id=1, source_target_pairs={{30,0},{0,2},{2,4},{4,6},{6,8},{8,10},{10,12},{12,14},{14,16},{16,... | collective-permute-start | bytes 110600 | tf_op jit(solution)/shard_map/ppermute | solution.py:452
  35.4 14.4 %copy-start = (bf16[512,1536]{1,0:T(8,128)(2,1)S(1)}, bf16[512,1536]{1,0:T(8,128)(2,1)}, u32[]{:S(2)}) copy-start(bf16[512,1536]{1,0:T(8,128)(2,1)} %wqkv.3) | copy-start | bytes 4718596
  35.4 14.4 %copy-start.4 = (bf16[2,6,12,512]{3,0,2,1:T(2,128)(2,1)S(1)}, bf16[2,6,12,512]{3,0,2,1:T(2,128)(2,1)}, u32[]{:S(2)}) copy-start(bf16[2,6,12,512]{3,0,2,1:T(2,128)(2,1)} %param.9) | copy-start | bytes 442372
  35.4 14.4 %copy-start.6 = (f32[512]{0:T(512)S(1)}, f32[512]{0:T(512)}, u32[]{:S(2)}) copy-start(f32[512]{0:T(512)} %param.12) | copy-start | bytes 6148
  35.5 10.0 %collective-permute-start.6 = (bf16[144,1024]{1,0:T(8,128)(2,1)S(1)}, bf16[144,1024]{1,0:T(8,128)(2,1)S(1)}, u32[]{:S(2)}, u32[]{:S(2)}) collective-permute-start(bf16[144,1024]{1,0:T(8,128)(2,1)S(1)} %get-tuple-element.73), channel_id=1, source_target_pairs={{0,64},{2,66},{4,68},{6,70},{8,72},{10,74},{12,76},{14,78},{32,96}... | collective-permute-start | bytes 884744 | tf_op jit(solution)/shard_map/ppermute | solution.py:474
  35.6 11.0 %collective-permute-start.7 = (bf16[144,1024]{1,0:T(8,128)(2,1)S(1)}, bf16[144,1024]{1,0:T(8,128)(2,1)S(1)}, u32[]{:S(2)}, u32[]{:S(2)}) collective-permute-start(bf16[144,1024]{1,0:T(8,128)(2,1)S(1)} %get-tuple-element.74), channel_id=1, source_target_pairs={{0,2},{2,0},{4,6},{6,4},{8,10},{10,8},{12,14},{14,12},{32,34},{34,... | collective-permute-start | bytes 884744 | tf_op jit(solution)/shard_map/ppermute | solution.py:474
  35.7 13.3 %collective-permute-start.8 = (bf16[144,1024]{1,0:T(8,128)(2,1)S(1)}, bf16[144,1024]{1,0:T(8,128)(2,1)S(1)}, u32[]{:S(2)}, u32[]{:S(2)}) collective-permute-start(bf16[144,1024]{1,0:T(8,128)(2,1)S(1)} %get-tuple-element.75), channel_id=1, source_target_pairs={{0,66},{2,64},{4,70},{6,68},{8,74},{10,72},{12,78},{14,76},{32,98}... | collective-permute-start | bytes 884744 | tf_op jit(solution)/shard_map/ppermute | solution.py:474
  40.4 13.1 %collective-permute-start.12 = (bf16[144,1024]{1,0:T(8,128)(2,1)S(1)}, bf16[144,1024]{1,0:T(8,128)(2,1)S(1)}, u32[]{:S(2)}, u32[]{:S(2)}) collective-permute-start(bf16[144,1024]{1,0:T(8,128)(2,1)S(1)} %get-tuple-element.88), channel_id=1, source_target_pairs={{0,192},{2,194},{4,196},{6,198},{8,200},{10,202},{12,204},{14,206}... | collective-permute-start | bytes 884744 | tf_op jit(solution)/shard_map/ppermute | solution.py:474
  42.0 14.1 %collective-permute-start.13 = (bf16[144,1024]{1,0:T(8,128)(2,1)S(1)}, bf16[144,1024]{1,0:T(8,128)(2,1)S(1)}, u32[]{:S(2)}, u32[]{:S(2)}) collective-permute-start(bf16[144,1024]{1,0:T(8,128)(2,1)S(1)} %get-tuple-element.89), channel_id=1, source_target_pairs={{0,14},{2,4},{4,2},{6,8},{8,6},{10,12},{12,10},{14,0},{32,46},{34,... | collective-permute-start | bytes 884744 | tf_op jit(solution)/shard_map/ppermute | solution.py:474
  45.4 10.7 %collective-permute-start.14 = (bf16[144,1024]{1,0:T(8,128)(2,1)S(1)}, bf16[144,1024]{1,0:T(8,128)(2,1)S(1)}, u32[]{:S(2)}, u32[]{:S(2)}) collective-permute-start(bf16[144,1024]{1,0:T(8,128)(2,1)S(1)} %get-tuple-element.90), channel_id=1, source_target_pairs={{0,206},{2,196},{4,194},{6,200},{8,198},{10,204},{12,202},{14,192}... | collective-permute-start | bytes 884744 | tf_op jit(solution)/shard_map/ppermute | solution.py:474
  49.8 9.4 %collective-permute-start.9 = (bf16[128,512]{1,0:T(8,128)(2,1)S(1)}, bf16[128,512]{1,0:T(8,128)(2,1)S(1)}, u32[]{:S(2)}, u32[]{:S(2)}) collective-permute-start(bf16[128,512]{1,0:T(8,128)(2,1)S(1)} %get-tuple-element.77), channel_id=1, source_target_pairs={{0,32},{2,34},{4,36},{6,38},{8,40},{10,42},{12,44},{14,46},{32,0},... | collective-permute-start | bytes 393224 | tf_op jit(solution)/shard_map/ppermute | solution.py:474
  51.5 22.3 %copy-start.10 = (bf16[36,512]{1,0:T(8,128)(2,1)S(1)}, bf16[36,512]{1,0:T(8,128)(2,1)}, u32[]{:S(2)}) copy-start(bf16[36,512]{1,0:T(8,128)(2,1)} %get-tuple-element.104) | copy-start | bytes 110596
  51.5 22.6 %copy-start.9 = (bf16[36,512]{1,0:T(8,128)(2,1)S(1)}, bf16[36,512]{1,0:T(8,128)(2,1)}, u32[]{:S(2)}) copy-start(bf16[36,512]{1,0:T(8,128)(2,1)} %get-tuple-element.105) | copy-start | bytes 110596
  51.5 26.5 %copy-start.8 = (bf16[36,512]{1,0:T(8,128)(2,1)S(1)}, bf16[36,512]{1,0:T(8,128)(2,1)}, u32[]{:S(2)}) copy-start(bf16[36,512]{1,0:T(8,128)(2,1)} %get-tuple-element.106) | copy-start | bytes 110596
  51.5 10.3 %collective-permute-start.10 = (bf16[128,512]{1,0:T(8,128)(2,1)S(1)}, bf16[128,512]{1,0:T(8,128)(2,1)S(1)}, u32[]{:S(2)}, u32[]{:S(2)}) collective-permute-start(bf16[128,512]{1,0:T(8,128)(2,1)S(1)} %get-tuple-element.78), channel_id=1, source_target_pairs={{0,16},{2,18},{4,20},{6,22},{8,24},{10,26},{12,28},{14,30},{32,48}... | collective-permute-start | bytes 393224 | tf_op jit(solution)/shard_map/ppermute | solution.py:474
  53.5 40.7 %copy-start.5 = (bf16[36,512]{1,0:T(8,128)(2,1)S(1)}, bf16[36,512]{1,0:T(8,128)(2,1)}, u32[]{:S(2)}) copy-start(bf16[36,512]{1,0:T(8,128)(2,1)} %get-tuple-element.111.r3) | copy-start | bytes 110596
  53.5 8.4 %collective-permute-start.11 = (bf16[128,512]{1,0:T(8,128)(2,1)S(1)}, bf16[128,512]{1,0:T(8,128)(2,1)S(1)}, u32[]{:S(2)}, u32[]{:S(2)}) collective-permute-start(bf16[128,512]{1,0:T(8,128)(2,1)S(1)} %get-tuple-element.79), channel_id=1, source_target_pairs={{0,48},{2,50},{4,52},{6,54},{8,56},{10,58},{12,60},{14,62},{32,16}... | collective-permute-start | bytes 393224 | tf_op jit(solution)/shard_map/ppermute | solution.py:474
  57.0 5.1 %collective-permute-start.15 = (bf16[128,512]{1,0:T(8,128)(2,1)S(1)}, bf16[128,512]{1,0:T(8,128)(2,1)S(1)}, u32[]{:S(2)}, u32[]{:S(2)}) collective-permute-start(bf16[128,512]{1,0:T(8,128)(2,1)S(1)} %get-tuple-element.97), channel_id=1, source_target_pairs={{0,32},{2,34},{4,36},{6,38},{8,40},{10,42},{12,44},{14,46},{32,0},... | collective-permute-start | bytes 393224 | tf_op jit(solution)/shard_map/ppermute | solution.py:474
  57.1 6.6 %collective-permute-start.16 = (bf16[128,512]{1,0:T(8,128)(2,1)S(1)}, bf16[128,512]{1,0:T(8,128)(2,1)S(1)}, u32[]{:S(2)}, u32[]{:S(2)}) collective-permute-start(bf16[128,512]{1,0:T(8,128)(2,1)S(1)} %get-tuple-element.98), channel_id=1, source_target_pairs={{0,16},{2,18},{4,20},{6,22},{8,24},{10,26},{12,28},{14,30},{32,48}... | collective-permute-start | bytes 393224 | tf_op jit(solution)/shard_map/ppermute | solution.py:474
  59.2 6.2 %collective-permute-start.17 = (bf16[128,512]{1,0:T(8,128)(2,1)S(1)}, bf16[128,512]{1,0:T(8,128)(2,1)S(1)}, u32[]{:S(2)}, u32[]{:S(2)}) collective-permute-start(bf16[128,512]{1,0:T(8,128)(2,1)S(1)} %get-tuple-element.99), channel_id=1, source_target_pairs={{0,48},{2,50},{4,52},{6,54},{8,56},{10,58},{12,60},{14,62},{32,16}... | collective-permute-start | bytes 393224 | tf_op jit(solution)/shard_map/ppermute | solution.py:474
  66.3 19.3 %all-to-all-start = ((bf16[32,32,128]{2,1,0:T(8,128)(2,1)}), bf16[32,32,128]{2,1,0:T(8,128)(2,1)S(1)}, u32[]{:S(2)}, u32[]{:S(2)}) async-start(bf16[32,32,128]{2,1,0:T(8,128)(2,1)} %add_rows.1), calls=%async_computation | async-start | bytes 524288 | tf_op jit(solution)/shard_map/all_to_all | solution.py:487
  73.7 10.9 %collective-permute-start.18 = (bf16[36,512]{1,0:T(8,128)(2,1)S(1)}, bf16[36,512]{1,0:T(8,128)(2,1)S(1)}, u32[]{:S(2)}, u32[]{:S(2)}) collective-permute-start(bf16[36,512]{1,0:T(8,128)(2,1)S(1)} %copy-done.10), channel_id=1, source_target_pairs={{254,0},{224,2},{226,4},{228,6},{230,8},{232,10},{234,12},{236,14}... | collective-permute-start | bytes 110600 | tf_op jit(solution)/shard_map/ppermute | solution.py:452
  74.1 10.5 %collective-permute-start.19 = (bf16[36,512]{1,0:T(8,128)(2,1)S(1)}, bf16[36,512]{1,0:T(8,128)(2,1)S(1)}, u32[]{:S(2)}, u32[]{:S(2)}) collective-permute-start(bf16[36,512]{1,0:T(8,128)(2,1)S(1)} %copy-done.9), channel_id=1, source_target_pairs={{224,0},{226,2},{228,4},{230,6},{232,8},{234,10},{236,12},{238,14}... | collective-permute-start | bytes 110600 | tf_op jit(solution)/shard_map/ppermute | solution.py:452
  78.0 7.6 %collective-permute-start.20 = (bf16[36,512]{1,0:T(8,128)(2,1)S(1)}, bf16[36,512]{1,0:T(8,128)(2,1)S(1)}, u32[]{:S(2)}, u32[]{:S(2)}) collective-permute-start(bf16[36,512]{1,0:T(8,128)(2,1)S(1)} %copy-done.8), channel_id=1, source_target_pairs={{30,0},{0,2},{2,4},{4,6},{6,8},{8,10},{10,12},{12,14},{14,16},{16,... | collective-permute-start | bytes 110600 | tf_op jit(solution)/shard_map/ppermute | solution.py:452
  86.4 19.6 %all-to-all-start.1 = ((f32[128,1,128]{2,1,0:T(1,128)}), f32[128,1,128]{2,1,0:T(1,128)S(1)}, u32[]{:S(2)}, u32[]{:S(2)}) async-start(f32[128,1,128]{2,1,0:T(1,128)} %get-tuple-element.114), calls=%async_computation.1 | async-start | bytes 131072 | tf_op jit(solution)/shard_map/all_to_all | solution.py:584

commit v9 on v7

--- a/solution.py
+++ b/solution.py
@@ -240,34 +240,38 @@
 
 
 def first_forward(
-    me, region, tok, cot, gain_hbm, wqkv_hbm, wout_hbm,
-    x0, x1, x2, x3, keep_ref, scratch, lab_scratch, gain, wqkv, wout, sems,
+    me, tok_hbm, gain_hbm, region_hbm, cot_hbm, wqkv_hbm, wout_hbm,
+    x0, x1, x2, x3, keep_ref, scratch, lab_scratch, tok, gain, region, cot, wqkv, wout, sems,
 ):
+    far = (tok_hbm, gain_hbm, region_hbm, cot_hbm, wqkv_hbm, wout_hbm)
     copies = [
         pltpu.make_async_copy(source, target, sems.at[i])
-        for i, (source, target) in enumerate(((gain_hbm, gain), (wqkv_hbm, wqkv), (wout_hbm, wout)))
+        for i, (source, target) in enumerate(zip(far, (tok, gain, region, cot, wqkv, wout)))
     ]
     for copy in copies:
         copy.start()
     refs = (x0, x1, x2, x3)
-    take_field(cot, scratch)
-    for slot, ref in enumerate(refs):
-        ref[:, D : 2 * D] = scratch[slot * QUART : (slot + 1) * QUART, :].astype(BF16)
+    copies[0].wait()
+    values = take_field(tok, scratch)
+    copies[1].wait()
+    normed, _, _ = norm_parts(values, gain[...])
+    copies[2].wait()
     labels = jnp.broadcast_to(take_labels(region), (TOK, LANES))
     near = lax.broadcasted_iota(jnp.int32, (TOK, LANES), 0) < 2 * QUART
     moved = labels + jnp.where(near & (me[0] < LON), 4.0, 0.0)
     scatter_rows(moved, lab_scratch, refs, 2 * D)
-    values = take_field(tok, scratch)
-    copies[0].wait()
-    normed, _, _ = norm_parts(values, gain[...])
-    copies[1].wait()
+    copies[3].wait()
+    take_field(cot, scratch)
+    for slot, ref in enumerate(refs):
+        ref[:, D : 2 * D] = scratch[slot * QUART : (slot + 1) * QUART, :].astype(BF16)
+    copies[4].wait()
     proj = dot_nn(normed, wqkv[...]).astype(BF16)
     keep_ref[:, : 3 * D] = proj
     keep_ref[:, 4 * D : 5 * D] = normed
     keep_ref[:, 5 * D :] = labels.astype(BF16)
     attended, _ = attention(proj, label_bias(labels))
     keep_ref[:, 3 * D : 4 * D] = attended
-    copies[2].wait()
+    copies[5].wait()
     scatter_rows(values + dot_nn(attended, wout[...]), scratch, refs, 0)
 
 
@@ -453,9 +457,9 @@
 SHEETS = [[index_of(x, y, z) for x, z in SHEET] for y in range(Y)]
 
 
-def swap(parts, members, chip, level):
+def swap(parts, members, chip, level, steps):
     out = list(parts)
-    for step in (3, 1, 2):
+    for step in steps:
         pairs = []
         for here_chip in CHIPS:
             numbers = list(members(*here_chip))
@@ -465,12 +469,12 @@
     return out
 
 
-def swap_first(parts, level):
-    return swap(parts, members_first, chip_first, level)
-
-
-def swap_second(parts, level):
-    return swap(parts, members_second, chip_second, level)
+def swap_first(parts, level, steps):
+    return swap(parts, members_first, chip_first, level, steps)
+
+
+def swap_second(parts, level, steps):
+    return swap(parts, members_second, chip_second, level, steps)
 
 
 def exchange(parts, groups):
@@ -510,13 +514,16 @@
         [
             (TOK, D),
             (TOK, LANES),
+            pltpu.VMEM(tok.shape, BF16),
             (1, D),
+            pltpu.VMEM(lab.shape, jnp.int32),
+            pltpu.VMEM(cot.shape, BF16),
             pltpu.VMEM((D, 3 * D), BF16),
             pltpu.VMEM((D, D), BF16),
-            pltpu.SemaphoreType.DMA((3,)),
+            pltpu.SemaphoreType.DMA((6,)),
         ],
-        me, *in_hbm(lab, tok, cot, gain_a, unshifted_query_key_value, out_first),
-        scalar=True, far=3,
+        me, *in_hbm(tok, gain_a, lab, cot, unshifted_query_key_value, out_first),
+        scalar=True, far=6,
     )
     x = send(x, tables)
     *back, normed_b, att_b, right_b = call(
@@ -530,7 +537,7 @@
     pack_b = call(
         second_pack, packs, [half, half], me, normed_b, att_b, right_b, scalar=True
     )
-    pack_b = swap_second(after(pack_b, back[:3]), 0)
+    pack_b = swap_second(after(pack_b, back[:3]), 0, (3, 1, 2))
     right_a, *pack_a = call(
         first_backward,
         [fields] + packs,
@@ -538,7 +545,7 @@
         me, *back, out_first, keep,
         scalar=True,
     )
-    pack_a = swap_first(pack_a, 0)
+    pack_a = swap_first(pack_a, 0, (3, 1, 2))
     grid = shape_of(WLAT, WLON, WLEV, D)
     token_gradient, result = call(
         first_rest,
@@ -550,8 +557,10 @@
     result = result.transpose(2, 0, 1, 3)
 
     rows = [shape_of(PLANE_ROWS, WIDE)] * GROUP
-    sum_b = swap_second(call(second_weights, rows, [(D, WIDE)], me, *in_vmem(*pack_b), scalar=True), 1)
-    sum_a = swap_first(call(first_weights, rows, [(D, WIDE)], me, *in_vmem(*pack_a), scalar=True), 1)
+    sum_b = call(second_weights, rows, [(D, WIDE)], me, *in_vmem(*pack_b), scalar=True)
+    sum_b = swap_second(sum_b, 1, (2, 1, 3))
+    sum_a = call(first_weights, rows, [(D, WIDE)], me, *in_vmem(*pack_a), scalar=True)
+    sum_a = swap_first(sum_a, 1, (1, 2, 3))
     piece = (len(SHEET), 2 * PIECE, LANES)
     (sums,) = call(add_rows, [shape_of(*piece)], [piece], *sum_a, *sum_b)
     sums = exchange(sums, SHEETS)

time: 103 us -> 102 us (level)
  no operation moved by 1% of the time
where the time goes in v9:
time: 102 us; the launch traced here: 101 us
  starting transfers between devices  36.7 us (36%)
  waiting for transfers between devices  30.4 us (30%)
  Pallas kernels  16.6 us (16%)
  blocking collectives  16.6 us (16%)
    all_to_all x1, blocking collectives, exchange(): return lax.all_to_all(parts, ('lat', 'lon'), 0, 0, axis_index_groups=groups)  16.6 us
    pallas_call x10, Pallas kernels, call(): pl.pallas_call(kernel, out_shape=outs, in_specs=specs, out_specs=[whole]...  16.6 us
    ppermute x12, starting transfers between devices, swap(): out[step] = lax.ppermute(parts[step], ('lat', 'lon'), pairs)  16 us
    ppermute x6, starting transfers between devices, send(): out.append(lax.ppermute(part, ('lat', 'lon'), pairs))  13.4 us
    ppermute x6, waiting for transfers between devices, send(): out.append(lax.ppermute(part, ('lat', 'lon'), pairs))  10.5 us
    all_to_all x1, waiting for transfers between devices, on_device(): tiles = lax.all_to_all(tiles, ('lat', 'lon'), 0, 0)  10.1 us
    ppermute x12, waiting for transfers between devices, swap(): out[step] = lax.ppermute(parts[step], ('lat', 'lon'), pairs)  9.76 us
    all_to_all x1, starting transfers between devices, on_device(): tiles = lax.all_to_all(tiles, ('lat', 'lon'), 0, 0)  7.28 us
  transfers between devices with their start and end apart: 19, of which 10 were waited for; matrix products, arithmetic and copies ran while one was open for 0% of the time, Pallas kernels for 7%

profile of v9, /device:TPU:0, one launch (start us, length us, event | category | flops | bytes accessed | tf_op | source)
XLA Modules:
  0.0 101.2 jit_solution(9808101564036127034)
XLA Ops:
  0.7 3.3 %first_forward.1 = (bf16[36,1152]{1,0:T(8,128)(2,1)S(1)}, bf16[36,1152]{1,0:T(8,128)(2,1)S(1)}, bf16[36,1152]{1,0:T(8,128)(2,1)S(1)}, bf16[36,1152]{1,0:T(8,128)(2,1)S(1)}, bf16[144,2688]{1,0:T(8,128)(2,1)S(1)}) custom-call(s32[1]{0:T(128)} %bitcast.me, bf16[6,12,2,512]{3,2,1,0:T(2,128)(2,1)} %bitcast.8, f32[1,512]{1,0:T(1,128)} %bitcast.10, ...), custom_call_target="tpu_custom_call" | custom-call | tf_op jit(solution)/shard_map/first_forward/pallas_call | solution.py:406
  4.0 8.8 %collective-permute-start = (bf16[36,1152]{1,0:T(8,128)(2,1)S(1)}, bf16[36,1152]{1,0:T(8,128)(2,1)S(1)}, u32[]{:S(2)}, u32[]{:S(2)}) collective-permute-start(bf16[36,1152]{1,0:T(8,128)(2,1)S(1)} %get-tuple-element.47), channel_id=1, source_target_pairs={{0,254},{2,224},{4,226},{6,228},{8,230},{10,232},{12,234},{14,236}... | collective-permute-start | bytes 248840 | tf_op jit(solution)/shard_map/ppermute | solution.py:446
  12.8 0.1 collective-permute-start.1
  13.0 2.5 %collective-permute-start.2 = (bf16[36,1152]{1,0:T(8,128)(2,1)S(1)}, bf16[36,1152]{1,0:T(8,128)(2,1)S(1)}, u32[]{:S(2)}, u32[]{:S(2)}) collective-permute-start(bf16[36,1152]{1,0:T(8,128)(2,1)S(1)} %get-tuple-element.49), channel_id=1, source_target_pairs={{0,30},{2,0},{4,2},{6,4},{8,6},{10,8},{12,10},{14,12},{16,14},{18,... | collective-permute-start | bytes 248840 | tf_op jit(solution)/shard_map/ppermute | solution.py:446
  15.5 0.0 collective-permute-done.x0
  15.5 1.9 %collective-permute-done.1.x1 = bf16[36,1152]{1,0:T(8,128)(2,1)S(1)} collective-permute-done((bf16[36,1152]{1,0:T(8,128)(2,1)S(1)}, bf16[36,1152]{1,0:T(8,128)(2,1)S(1)}, u32[]{:S(2)}, u32[]{:S(2)}) %collective-permute-start.1) | collective-permute-done | bytes 82976 | tf_op jit(solution)/shard_map/ppermute | solution.py:446
  17.4 0.3 collective-permute-done.2.x2
  17.7 4.8 %second_main.1 = (bf16[36,1024]{1,0:T(8,128)(2,1)S(1)}, bf16[36,1024]{1,0:T(8,128)(2,1)S(1)}, bf16[36,1024]{1,0:T(8,128)(2,1)S(1)}, bf16[36,1024]{1,0:T(8,128)(2...) custom-call(bf16[36,1152]{1,0:T(8,128)(2,1)S(1)} %collective-permute-done.x0, ...), custom_call_target="tpu_custom_call" | custom-call | tf_op jit(solution)/shard_map/second_main/pallas_call | solution.py:406
  22.5 0.9 collective-permute-start.3
  23.4 1.0 %collective-permute-start.4 = (bf16[36,1024]{1,0:T(8,128)(2,1)S(1)}, bf16[36,1024]{1,0:T(8,128)(2,1)S(1)}, u32[]{:S(2)}, u32[]{:S(2)}) collective-permute-start(bf16[36,1024]{1,0:T(8,128)(2,1)S(1)} %get-tuple-element.52), channel_id=1, source_target_pairs={{224,0},{226,2},{228,4},{230,6},{232,8},{234,10},{236,12},{238,14}... | collective-permute-start | bytes 221192 | tf_op jit(solution)/shard_map/ppermute | solution.py:446
  24.4 0.0 collective-permute-start.5
  24.4 0.5 second_pack.1
  24.9 8.4 %collective-permute-done.3.b0 = bf16[36,1024]{1,0:T(8,128)(2,1)S(1)} collective-permute-done((bf16[36,1024]{1,0:T(8,128)(2,1)S(1)}, bf16[36,1024]{1,0:T(8,128)(2,1)S(1)}, u32[]{:S(2)}, u32[]{:S(2)}) %collective-permute-start.3) | collective-permute-done | bytes 73760 | tf_op jit(solution)/shard_map/ppermute | solution.py:446
  33.3 0.0 collective-permute-done.4.b1
  33.3 0.0 collective-permute-done.5.b2
  33.3 1.1 %collective-permute-start.12 = (bf16[144,1024]{1,0:T(8,128)(2,1)S(1)}, bf16[144,1024]{1,0:T(8,128)(2,1)S(1)}, u32[]{:S(2)}, u32[]{:S(2)}) collective-permute-start(bf16[144,1024]{1,0:T(8,128)(2,1)S(1)} %get-tuple-element.75), channel_id=1, source_target_pairs={{0,192},{2,194},{4,196},{6,198},{8,200},{10,202},{12,204},{14,206}... | collective-permute-start | bytes 884744 | tf_op jit(solution)/shard_map/ppermute | solution.py:468
  34.4 0.1 collective-permute-start.13
  34.5 4.7 %collective-permute-start.14 = (bf16[144,1024]{1,0:T(8,128)(2,1)S(1)}, bf16[144,1024]{1,0:T(8,128)(2,1)S(1)}, u32[]{:S(2)}, u32[]{:S(2)}) collective-permute-start(bf16[144,1024]{1,0:T(8,128)(2,1)S(1)} %get-tuple-element.77), channel_id=1, source_target_pairs={{0,206},{2,196},{4,194},{6,200},{8,198},{10,204},{12,202},{14,192}... | collective-permute-start | bytes 884744 | tf_op jit(solution)/shard_map/ppermute | solution.py:468
  39.2 2.9 %first_backward.1 = (bf16[4,144,512]{2,1,0:T(8,128)(2,1)S(1)}, bf16[144,1024]{1,0:T(8,128)(2,1)S(1)}, bf16[144,1024]{1,0:T(8,128)(2,1)S(1)}, bf16[144,1024]{1,0:T(8,128)(2,1)S(1)}, bf16[144,1024]{1,0:T(8,128)(2,1)S(1)}) custom-call(s32[1]{0:T(128)} %bitcast.me, bf16[36,1024]{1,0:T(8,128)(2,1)S(1)} %collective-permute-done.3.b0, ...), custom_call_target="tpu_custom_call" | custom-call | tf_op jit(solution)/shard_map/first_backward/pallas_call | solution.py:406
  42.2 0.1 collective-permute-start.6
  42.3 0.1 collective-permute-start.7
  42.4 1.8 %collective-permute-done.12.refs_1_ = bf16[144,1024]{1,0:T(8,128)(2,1)S(1)} collective-permute-done((bf16[144,1024]{1,0:T(8,128)(2,1)S(1)}, bf16[144,1024]{1,0:T(8,128)(2,1)S(1)}, u32[]{:S(2)}, u32[]{:S(2)}) %collective-permute-start.12) | collective-permute-done | bytes 294944 | tf_op jit(solution)/shard_map/ppermute | solution.py:468
  44.2 1.6 %collective-permute-start.8 = (bf16[144,1024]{1,0:T(8,128)(2,1)S(1)}, bf16[144,1024]{1,0:T(8,128)(2,1)S(1)}, u32[]{:S(2)}, u32[]{:S(2)}) collective-permute-start(bf16[144,1024]{1,0:T(8,128)(2,1)S(1)} %get-tuple-element.62), channel_id=1, source_target_pairs={{0,66},{2,64},{4,70},{6,68},{8,74},{10,72},{12,78},{14,76},{32,98}... | collective-permute-start | bytes 884744 | tf_op jit(solution)/shard_map/ppermute | solution.py:468
  45.7 0.0 collective-permute-done.13.refs_2_
  45.7 3.3 %collective-permute-done.14.refs_3_ = bf16[144,1024]{1,0:T(8,128)(2,1)S(1)} collective-permute-done((bf16[144,1024]{1,0:T(8,128)(2,1)S(1)}, bf16[144,1024]{1,0:T(8,128)(2,1)S(1)}, u32[]{:S(2)}, u32[]{:S(2)}) %collective-permute-start.14) | collective-permute-done | bytes 294944 | tf_op jit(solution)/shard_map/ppermute | solution.py:468
  49.0 0.8 second_weights.1
  49.9 0.5 collective-permute-start.15
  50.3 1.4 %collective-permute-start.16 = (bf16[128,512]{1,0:T(8,128)(2,1)S(1)}, bf16[128,512]{1,0:T(8,128)(2,1)S(1)}, u32[]{:S(2)}, u32[]{:S(2)}) collective-permute-start(bf16[128,512]{1,0:T(8,128)(2,1)S(1)} %get-tuple-element.80), channel_id=1, source_target_pairs={{0,16},{2,18},{4,20},{6,22},{8,24},{10,26},{12,28},{14,30},{32,48}... | collective-permute-start | bytes 393224 | tf_op jit(solution)/shard_map/ppermute | solution.py:468
  51.7 0.0 collective-permute-done.6.refs_1_
  51.7 2.9 %collective-permute-start.17 = (bf16[128,512]{1,0:T(8,128)(2,1)S(1)}, bf16[128,512]{1,0:T(8,128)(2,1)S(1)}, u32[]{:S(2)}, u32[]{:S(2)}) collective-permute-start(bf16[128,512]{1,0:T(8,128)(2,1)S(1)} %get-tuple-element.81), channel_id=1, source_target_pairs={{0,48},{2,50},{4,52},{6,54},{8,56},{10,58},{12,60},{14,62},{32,16}... | collective-permute-start | bytes 393224 | tf_op jit(solution)/shard_map/ppermute | solution.py:468
  54.7 0.0 collective-permute-done.7.refs_2_
  54.7 0.0 collective-permute-done.8.refs_3_
  54.7 0.8 first_weights.1
  55.6 0.7 collective-permute-start.10
  56.2 2.5 %collective-permute-start.11 = (bf16[128,512]{1,0:T(8,128)(2,1)S(1)}, bf16[128,512]{1,0:T(8,128)(2,1)S(1)}, u32[]{:S(2)}, u32[]{:S(2)}) collective-permute-start(bf16[128,512]{1,0:T(8,128)(2,1)S(1)} %get-tuple-element.66), channel_id=1, source_target_pairs={{0,48},{2,50},{4,52},{6,54},{8,56},{10,58},{12,60},{14,62},{32,16}... | collective-permute-start | bytes 393224 | tf_op jit(solution)/shard_map/ppermute | solution.py:468
  58.7 0.0 collective-permute-done.15.b1
  58.7 0.4 collective-permute-start.9
  59.1 1.0 collective-permute-done.17.b3
  60.1 2.1 %collective-permute-done.10.a2 = bf16[128,512]{1,0:T(8,128)(2,1)S(1)} collective-permute-done((bf16[128,512]{1,0:T(8,128)(2,1)S(1)}, bf16[128,512]{1,0:T(8,128)(2,1)S(1)}, u32[]{:S(2)}, u32[]{:S(2)}) %collective-permute-start.10) | collective-permute-done | bytes 131104 | tf_op jit(solution)/shard_map/ppermute | solution.py:468
  62.2 1.3 %collective-permute-done.11.a3 = bf16[128,512]{1,0:T(8,128)(2,1)S(1)} collective-permute-done((bf16[128,512]{1,0:T(8,128)(2,1)S(1)}, bf16[128,512]{1,0:T(8,128)(2,1)S(1)}, u32[]{:S(2)}, u32[]{:S(2)}) %collective-permute-start.11) | collective-permute-done | bytes 131104 | tf_op jit(solution)/shard_map/ppermute | solution.py:468
  63.5 0.2 collective-permute-done.9.a1
  63.7 0.2 add_rows.1
  63.9 16.6 %all_to_all.10.parts = bf16[32,32,128]{2,1,0:T(8,128)(2,1)S(1)} all-to-all(bf16[32,32,128]{2,1,0:T(8,128)(2,1)S(1)} %add_rows.1), channel_id=1, replica_groups={{0,2,4,6,8,10,12,14,64,66,68,70,72,74,76,78,128,130,132,134,136,138,140..., dimensions={0} | all-to-all | bytes 524288 | tf_op jit(solution)/shard_map/all_to_all | solution.py:481
  80.5 0.8 own_rows.1
  81.4 7.3 %all-to-all-start.1 = ((f32[128,1,128]{2,1,0:T(1,128)}), f32[128,1,128]{2,1,0:T(1,128)S(1)}, u32[]{:S(2)}, u32[]{:S(2)}) async-start(f32[128,1,128]{2,1,0:T(1,128)} %get-tuple-element.82), calls=%async_computation.1 | async-start | bytes 131072 | tf_op jit(solution)/shard_map/all_to_all | solution.py:573
  88.7 1.6 %first_rest.1 = (bf16[6,12,2,512]{3,2,1,0:T(2,128)(2,1)}, bf16[6,12,2,512]{3,2,1,0:T(2,128)(2,1)}) custom-call(bf16[36,1024]{1,0:T(8,128)(2,1)S(1)} %collective-permute-done.3.b0, bf16[36,1024]{1,0:T(8,128)(2,1)S(1)} %collective-permute-done.4.b1, bf16[36,1024]{1,0:T(8,128)(2,1)S(1)} %collective-permute-done.5.b2, ...), custom_call_target="tpu_custom_call" | custom-call | tf_op jit(solution)/shard_map/first_rest/pallas_call | solution.py:406
  90.3 10.1 %all-to-all-done.1.tiles = f32[128,1,128]{2,1,0:T(1,128)S(1)} async-done(((f32[128,1,128]{2,1,0:T(1,128)}), f32[128,1,128]{2,1,0:T(1,128)S(1)}, u32[]{:S(2)}, u32[]{:S(2)}) %all-to-all-start.1) | async-done | bytes 65568 | tf_op jit(solution)/shard_map/all_to_all | solution.py:573
  100.4 0.8 clipped.1
  (15 shorter events, 0.0 us)
Async XLA Ops:
  0.6 17.0 %copy-start.6 = (f32[512]{0:T(512)S(1)}, f32[512]{0:T(512)}, u32[]{:S(2)}) copy-start(f32[512]{0:T(512)} %param.15) | copy-start | bytes 6148
  0.6 17.0 %copy-start.2 = (bf16[512,1536]{1,0:T(8,128)(2,1)S(1)}, bf16[512,1536]{1,0:T(8,128)(2,1)}, u32[]{:S(2)}) copy-start(bf16[512,1536]{1,0:T(8,128)(2,1)} %wqkv.2) | copy-start | bytes 4718596
  0.7 17.0 %copy-start.4 = (bf16[512,512]{1,0:T(8,128)(2,1)S(1)}, bf16[512,512]{1,0:T(8,128)(2,1)}, u32[]{:S(2)}) copy-start(bf16[512,512]{1,0:T(8,128)(2,1)} %wout.2) | copy-start | bytes 1572868
  4.0 11.5 %collective-permute-start = (bf16[36,1152]{1,0:T(8,128)(2,1)S(1)}, bf16[36,1152]{1,0:T(8,128)(2,1)S(1)}, u32[]{:S(2)}, u32[]{:S(2)}) collective-permute-start(bf16[36,1152]{1,0:T(8,128)(2,1)S(1)} %get-tuple-element.47), channel_id=1, source_target_pairs={{0,254},{2,224},{4,226},{6,228},{8,230},{10,232},{12,234},{14,236}... | collective-permute-start | bytes 248840 | tf_op jit(solution)/shard_map/ppermute | solution.py:446
  12.8 4.6 %collective-permute-start.1 = (bf16[36,1152]{1,0:T(8,128)(2,1)S(1)}, bf16[36,1152]{1,0:T(8,128)(2,1)S(1)}, u32[]{:S(2)}, u32[]{:S(2)}) collective-permute-start(bf16[36,1152]{1,0:T(8,128)(2,1)S(1)} %get-tuple-element.48), channel_id=1, source_target_pairs={{0,224},{2,226},{4,228},{6,230},{8,232},{10,234},{12,236},{14,238}... | collective-permute-start | bytes 248840 | tf_op jit(solution)/shard_map/ppermute | solution.py:446
  13.0 4.7 %collective-permute-start.2 = (bf16[36,1152]{1,0:T(8,128)(2,1)S(1)}, bf16[36,1152]{1,0:T(8,128)(2,1)S(1)}, u32[]{:S(2)}, u32[]{:S(2)}) collective-permute-start(bf16[36,1152]{1,0:T(8,128)(2,1)S(1)} %get-tuple-element.49), channel_id=1, source_target_pairs={{0,30},{2,0},{4,2},{6,4},{8,6},{10,8},{12,10},{14,12},{16,14},{18,... | collective-permute-start | bytes 248840 | tf_op jit(solution)/shard_map/ppermute | solution.py:446
  17.7 21.6 %copy-start.1 = (bf16[512,512]{1,0:T(8,128)(2,1)S(1)}, bf16[512,512]{1,0:T(8,128)(2,1)}, u32[]{:S(2)}) copy-start(bf16[512,512]{1,0:T(8,128)(2,1)} %wout.3) | copy-start | bytes 1572868
  22.5 10.8 %collective-permute-start.3 = (bf16[36,1024]{1,0:T(8,128)(2,1)S(1)}, bf16[36,1024]{1,0:T(8,128)(2,1)S(1)}, u32[]{:S(2)}, u32[]{:S(2)}) collective-permute-start(bf16[36,1024]{1,0:T(8,128)(2,1)S(1)} %get-tuple-element.51), channel_id=1, source_target_pairs={{254,0},{224,2},{226,4},{228,6},{230,8},{232,10},{234,12},{236,14}... | collective-permute-start | bytes 221192 | tf_op jit(solution)/shard_map/ppermute | solution.py:446
  23.4 9.9 %collective-permute-start.4 = (bf16[36,1024]{1,0:T(8,128)(2,1)S(1)}, bf16[36,1024]{1,0:T(8,128)(2,1)S(1)}, u32[]{:S(2)}, u32[]{:S(2)}) collective-permute-start(bf16[36,1024]{1,0:T(8,128)(2,1)S(1)} %get-tuple-element.52), channel_id=1, source_target_pairs={{224,0},{226,2},{228,4},{230,6},{232,8},{234,10},{236,12},{238,14}... | collective-permute-start | bytes 221192 | tf_op jit(solution)/shard_map/ppermute | solution.py:446
  24.4 8.9 %collective-permute-start.5 = (bf16[36,1024]{1,0:T(8,128)(2,1)S(1)}, bf16[36,1024]{1,0:T(8,128)(2,1)S(1)}, u32[]{:S(2)}, u32[]{:S(2)}) collective-permute-start(bf16[36,1024]{1,0:T(8,128)(2,1)S(1)} %get-tuple-element.53), channel_id=1, source_target_pairs={{30,0},{0,2},{2,4},{4,6},{6,8},{8,10},{10,12},{12,14},{14,16},{16,... | collective-permute-start | bytes 221192 | tf_op jit(solution)/shard_map/ppermute | solution.py:446
  33.3 10.9 %collective-permute-start.12 = (bf16[144,1024]{1,0:T(8,128)(2,1)S(1)}, bf16[144,1024]{1,0:T(8,128)(2,1)S(1)}, u32[]{:S(2)}, u32[]{:S(2)}) collective-permute-start(bf16[144,1024]{1,0:T(8,128)(2,1)S(1)} %get-tuple-element.75), channel_id=1, source_target_pairs={{0,192},{2,194},{4,196},{6,198},{8,200},{10,202},{12,204},{14,206}... | collective-permute-start | bytes 884744 | tf_op jit(solution)/shard_map/ppermute | solution.py:468
  34.4 11.3 %collective-permute-start.13 = (bf16[144,1024]{1,0:T(8,128)(2,1)S(1)}, bf16[144,1024]{1,0:T(8,128)(2,1)S(1)}, u32[]{:S(2)}, u32[]{:S(2)}) collective-permute-start(bf16[144,1024]{1,0:T(8,128)(2,1)S(1)} %get-tuple-element.76), channel_id=1, source_target_pairs={{0,14},{2,4},{4,2},{6,8},{8,6},{10,12},{12,10},{14,0},{32,46},{34,... | collective-permute-start | bytes 884744 | tf_op jit(solution)/shard_map/ppermute | solution.py:468
  34.5 14.5 %collective-permute-start.14 = (bf16[144,1024]{1,0:T(8,128)(2,1)S(1)}, bf16[144,1024]{1,0:T(8,128)(2,1)S(1)}, u32[]{:S(2)}, u32[]{:S(2)}) collective-permute-start(bf16[144,1024]{1,0:T(8,128)(2,1)S(1)} %get-tuple-element.77), channel_id=1, source_target_pairs={{0,206},{2,196},{4,194},{6,200},{8,198},{10,204},{12,202},{14,192}... | collective-permute-start | bytes 884744 | tf_op jit(solution)/shard_map/ppermute | solution.py:468
  42.2 9.6 %collective-permute-start.6 = (bf16[144,1024]{1,0:T(8,128)(2,1)S(1)}, bf16[144,1024]{1,0:T(8,128)(2,1)S(1)}, u32[]{:S(2)}, u32[]{:S(2)}) collective-permute-start(bf16[144,1024]{1,0:T(8,128)(2,1)S(1)} %get-tuple-element.60), channel_id=1, source_target_pairs={{0,64},{2,66},{4,68},{6,70},{8,72},{10,74},{12,76},{14,78},{32,96}... | collective-permute-start | bytes 884744 | tf_op jit(solution)/shard_map/ppermute | solution.py:468
  42.3 12.4 %collective-permute-start.7 = (bf16[144,1024]{1,0:T(8,128)(2,1)S(1)}, bf16[144,1024]{1,0:T(8,128)(2,1)S(1)}, u32[]{:S(2)}, u32[]{:S(2)}) collective-permute-start(bf16[144,1024]{1,0:T(8,128)(2,1)S(1)} %get-tuple-element.61), channel_id=1, source_target_pairs={{0,2},{2,0},{4,6},{6,4},{8,10},{10,8},{12,14},{14,12},{32,34},{34,... | collective-permute-start | bytes 884744 | tf_op jit(solution)/shard_map/ppermute | solution.py:468
  44.2 10.5 %collective-permute-start.8 = (bf16[144,1024]{1,0:T(8,128)(2,1)S(1)}, bf16[144,1024]{1,0:T(8,128)(2,1)S(1)}, u32[]{:S(2)}, u32[]{:S(2)}) collective-permute-start(bf16[144,1024]{1,0:T(8,128)(2,1)S(1)} %get-tuple-element.62), channel_id=1, source_target_pairs={{0,66},{2,64},{4,70},{6,68},{8,74},{10,72},{12,78},{14,76},{32,98}... | collective-permute-start | bytes 884744 | tf_op jit(solution)/shard_map/ppermute | solution.py:468
  49.9 8.9 %collective-permute-start.15 = (bf16[128,512]{1,0:T(8,128)(2,1)S(1)}, bf16[128,512]{1,0:T(8,128)(2,1)S(1)}, u32[]{:S(2)}, u32[]{:S(2)}) collective-permute-start(bf16[128,512]{1,0:T(8,128)(2,1)S(1)} %get-tuple-element.79), channel_id=1, source_target_pairs={{0,32},{2,34},{4,36},{6,38},{8,40},{10,42},{12,44},{14,46},{32,0},... | collective-permute-start | bytes 393224 | tf_op jit(solution)/shard_map/ppermute | solution.py:468
  50.3 8.8 %collective-permute-start.16 = (bf16[128,512]{1,0:T(8,128)(2,1)S(1)}, bf16[128,512]{1,0:T(8,128)(2,1)S(1)}, u32[]{:S(2)}, u32[]{:S(2)}) collective-permute-start(bf16[128,512]{1,0:T(8,128)(2,1)S(1)} %get-tuple-element.80), channel_id=1, source_target_pairs={{0,16},{2,18},{4,20},{6,22},{8,24},{10,26},{12,28},{14,30},{32,48}... | collective-permute-start | bytes 393224 | tf_op jit(solution)/shard_map/ppermute | solution.py:468
  51.7 8.4 %collective-permute-start.17 = (bf16[128,512]{1,0:T(8,128)(2,1)S(1)}, bf16[128,512]{1,0:T(8,128)(2,1)S(1)}, u32[]{:S(2)}, u32[]{:S(2)}) collective-permute-start(bf16[128,512]{1,0:T(8,128)(2,1)S(1)} %get-tuple-element.81), channel_id=1, source_target_pairs={{0,48},{2,50},{4,52},{6,54},{8,56},{10,58},{12,60},{14,62},{32,16}... | collective-permute-start | bytes 393224 | tf_op jit(solution)/shard_map/ppermute | solution.py:468
  54.7 33.9 %copy-start = (bf16[512,1536]{1,0:T(8,128)(2,1)S(1)}, bf16[512,1536]{1,0:T(8,128)(2,1)}, u32[]{:S(2)}) copy-start(bf16[512,1536]{1,0:T(8,128)(2,1)} %wqkv.3) | copy-start | bytes 4718596
  54.7 33.9 %copy-start.3 = (bf16[2,6,12,512]{3,0,2,1:T(2,128)(2,1)S(1)}, bf16[2,6,12,512]{3,0,2,1:T(2,128)(2,1)}, u32[]{:S(2)}) copy-start(bf16[2,6,12,512]{3,0,2,1:T(2,128)(2,1)} %param.9) | copy-start | bytes 442372
  54.7 34.0 %copy-start.5 = (f32[512]{0:T(512)S(1)}, f32[512]{0:T(512)}, u32[]{:S(2)}) copy-start(f32[512]{0:T(512)} %param.12) | copy-start | bytes 6148
  55.6 6.7 %collective-permute-start.10 = (bf16[128,512]{1,0:T(8,128)(2,1)S(1)}, bf16[128,512]{1,0:T(8,128)(2,1)S(1)}, u32[]{:S(2)}, u32[]{:S(2)}) collective-permute-start(bf16[128,512]{1,0:T(8,128)(2,1)S(1)} %get-tuple-element.65), channel_id=1, source_target_pairs={{0,16},{2,18},{4,20},{6,22},{8,24},{10,26},{12,28},{14,30},{32,48}... | collective-permute-start | bytes 393224 | tf_op jit(solution)/shard_map/ppermute | solution.py:468
  56.2 7.3 %collective-permute-start.11 = (bf16[128,512]{1,0:T(8,128)(2,1)S(1)}, bf16[128,512]{1,0:T(8,128)(2,1)S(1)}, u32[]{:S(2)}, u32[]{:S(2)}) collective-permute-start(bf16[128,512]{1,0:T(8,128)(2,1)S(1)} %get-tuple-element.66), channel_id=1, source_target_pairs={{0,48},{2,50},{4,52},{6,54},{8,56},{10,58},{12,60},{14,62},{32,16}... | collective-permute-start | bytes 393224 | tf_op jit(solution)/shard_map/ppermute | solution.py:468
  58.7 5.0 %collective-permute-start.9 = (bf16[128,512]{1,0:T(8,128)(2,1)S(1)}, bf16[128,512]{1,0:T(8,128)(2,1)S(1)}, u32[]{:S(2)}, u32[]{:S(2)}) collective-permute-start(bf16[128,512]{1,0:T(8,128)(2,1)S(1)} %get-tuple-element.64), channel_id=1, source_target_pairs={{0,32},{2,34},{4,36},{6,38},{8,40},{10,42},{12,44},{14,46},{32,0},... | collective-permute-start | bytes 393224 | tf_op jit(solution)/shard_map/ppermute | solution.py:468
  81.4 19.0 %all-to-all-start.1 = ((f32[128,1,128]{2,1,0:T(1,128)}), f32[128,1,128]{2,1,0:T(1,128)S(1)}, u32[]{:S(2)}, u32[]{:S(2)}) async-start(f32[128,1,128]{2,1,0:T(1,128)} %get-tuple-element.82), calls=%async_computation.1 | async-start | bytes 131072 | tf_op jit(solution)/shard_map/all_to_all | solution.py:573

commit v10 on v9

--- a/solution.py
+++ b/solution.py
@@ -437,13 +437,10 @@
 
 
 def send(parts, tables, back=False):
-    out = []
-    for part, table in zip(parts, tables):
-        if all(s == t for s, t in table):
-            out.append(part)
-            continue
-        pairs = [(t, s) for s, t in table] if back else table
-        out.append(lax.ppermute(part, ("lat", "lon"), pairs))
+    out = list(parts)
+    for slot in (2, 0, 1):
+        pairs = [(t, s) for s, t in tables[slot]] if back else tables[slot]
+        out[slot] = lax.ppermute(parts[slot], ("lat", "lon"), pairs)
     return out
 
 

time: 102 us -> 102 us (level)
  no operation moved by 1% of the time
where the time goes in v10:
time: 102 us; the launch traced here: 101 us
  starting transfers between devices  36.7 us (36%)
  waiting for transfers between devices  30.4 us (30%)
  Pallas kernels  16.6 us (16%)
  blocking collectives  16.6 us (16%)
    all_to_all x1, blocking collectives, exchange(): return lax.all_to_all(parts, ('lat', 'lon'), 0, 0, axis_index_groups=groups)  16.6 us
    pallas_call x10, Pallas kernels, call(): pl.pallas_call(kernel, out_shape=outs, in_specs=specs, out_specs=[whole]...  16.6 us
    ppermute x12, starting transfers between devices, swap(): out[step] = lax.ppermute(parts[step], ('lat', 'lon'), pairs)  16 us
    ppermute x6, starting transfers between devices, send(): out[slot] = lax.ppermute(parts[slot], ('lat', 'lon'), pairs)  13.4 us
    ppermute x6, waiting for transfers between devices, send(): out[slot] = lax.ppermute(parts[slot], ('lat', 'lon'), pairs)  10.5 us
    all_to_all x1, waiting for transfers between devices, on_device(): tiles = lax.all_to_all(tiles, ('lat', 'lon'), 0, 0)  10.1 us
    ppermute x12, waiting for transfers between devices, swap(): out[step] = lax.ppermute(parts[step], ('lat', 'lon'), pairs)  9.76 us
    all_to_all x1, starting transfers between devices, on_device(): tiles = lax.all_to_all(tiles, ('lat', 'lon'), 0, 0)  7.28 us
  transfers between devices with their start and end apart: 19, of which 10 were waited for; matrix products, arithmetic and copies ran while one was open for 0% of the time, Pallas kernels for 7%

profile of v10, /device:TPU:0, one launch (start us, length us, event | category | flops | bytes accessed | tf_op | source)
XLA Modules:
  0.0 101.2 jit_solution(9808101564036127034)
XLA Ops:
  0.7 3.3 %first_forward.1 = (bf16[36,1152]{1,0:T(8,128)(2,1)S(1)}, bf16[36,1152]{1,0:T(8,128)(2,1)S(1)}, bf16[36,1152]{1,0:T(8,128)(2,1)S(1)}, bf16[36,1152]{1,0:T(8,128)(2,1)S(1)}, bf16[144,2688]{1,0:T(8,128)(2,1)S(1)}) custom-call(s32[1]{0:T(128)} %bitcast.me, bf16[6,12,2,512]{3,2,1,0:T(2,128)(2,1)} %bitcast.8, f32[1,512]{1,0:T(1,128)} %bitcast.10, ...), custom_call_target="tpu_custom_call" | custom-call | tf_op jit(solution)/shard_map/first_forward/pallas_call | solution.py:406
  4.0 8.8 %collective-permute-start = (bf16[36,1152]{1,0:T(8,128)(2,1)S(1)}, bf16[36,1152]{1,0:T(8,128)(2,1)S(1)}, u32[]{:S(2)}, u32[]{:S(2)}) collective-permute-start(bf16[36,1152]{1,0:T(8,128)(2,1)S(1)} %get-tuple-element.47), channel_id=1, source_target_pairs={{0,254},{2,224},{4,226},{6,228},{8,230},{10,232},{12,234},{14,236}... | collective-permute-start | bytes 248840 | tf_op jit(solution)/shard_map/ppermute | solution.py:443
  12.8 0.1 collective-permute-start.1
  13.0 2.5 %collective-permute-start.2 = (bf16[36,1152]{1,0:T(8,128)(2,1)S(1)}, bf16[36,1152]{1,0:T(8,128)(2,1)S(1)}, u32[]{:S(2)}, u32[]{:S(2)}) collective-permute-start(bf16[36,1152]{1,0:T(8,128)(2,1)S(1)} %get-tuple-element.49), channel_id=1, source_target_pairs={{0,30},{2,0},{4,2},{6,4},{8,6},{10,8},{12,10},{14,12},{16,14},{18,... | collective-permute-start | bytes 248840 | tf_op jit(solution)/shard_map/ppermute | solution.py:443
  15.5 0.0 collective-permute-done.x0
  15.5 1.9 %collective-permute-done.1.x1 = bf16[36,1152]{1,0:T(8,128)(2,1)S(1)} collective-permute-done((bf16[36,1152]{1,0:T(8,128)(2,1)S(1)}, bf16[36,1152]{1,0:T(8,128)(2,1)S(1)}, u32[]{:S(2)}, u32[]{:S(2)}) %collective-permute-start.1) | collective-permute-done | bytes 82976 | tf_op jit(solution)/shard_map/ppermute | solution.py:443
  17.4 0.3 collective-permute-done.2.x2
  17.7 4.8 %second_main.1 = (bf16[36,1024]{1,0:T(8,128)(2,1)S(1)}, bf16[36,1024]{1,0:T(8,128)(2,1)S(1)}, bf16[36,1024]{1,0:T(8,128)(2,1)S(1)}, bf16[36,1024]{1,0:T(8,128)(2...) custom-call(bf16[36,1152]{1,0:T(8,128)(2,1)S(1)} %collective-permute-done.x0, ...), custom_call_target="tpu_custom_call" | custom-call | tf_op jit(solution)/shard_map/second_main/pallas_call | solution.py:406
  22.5 0.9 collective-permute-start.3
  23.4 1.0 %collective-permute-start.4 = (bf16[36,1024]{1,0:T(8,128)(2,1)S(1)}, bf16[36,1024]{1,0:T(8,128)(2,1)S(1)}, u32[]{:S(2)}, u32[]{:S(2)}) collective-permute-start(bf16[36,1024]{1,0:T(8,128)(2,1)S(1)} %get-tuple-element.52), channel_id=1, source_target_pairs={{224,0},{226,2},{228,4},{230,6},{232,8},{234,10},{236,12},{238,14}... | collective-permute-start | bytes 221192 | tf_op jit(solution)/shard_map/ppermute | solution.py:443
  24.4 0.0 collective-permute-start.5
  24.4 0.5 second_pack.1
  24.9 8.4 %collective-permute-done.3.b0 = bf16[36,1024]{1,0:T(8,128)(2,1)S(1)} collective-permute-done((bf16[36,1024]{1,0:T(8,128)(2,1)S(1)}, bf16[36,1024]{1,0:T(8,128)(2,1)S(1)}, u32[]{:S(2)}, u32[]{:S(2)}) %collective-permute-start.3) | collective-permute-done | bytes 73760 | tf_op jit(solution)/shard_map/ppermute | solution.py:443
  33.3 0.0 collective-permute-done.4.b1
  33.3 0.0 collective-permute-done.5.b2
  33.3 1.1 %collective-permute-start.12 = (bf16[144,1024]{1,0:T(8,128)(2,1)S(1)}, bf16[144,1024]{1,0:T(8,128)(2,1)S(1)}, u32[]{:S(2)}, u32[]{:S(2)}) collective-permute-start(bf16[144,1024]{1,0:T(8,128)(2,1)S(1)} %get-tuple-element.75), channel_id=1, source_target_pairs={{0,192},{2,194},{4,196},{6,198},{8,200},{10,202},{12,204},{14,206}... | collective-permute-start | bytes 884744 | tf_op jit(solution)/shard_map/ppermute | solution.py:465
  34.4 0.1 collective-permute-start.13
  34.5 4.7 %collective-permute-start.14 = (bf16[144,1024]{1,0:T(8,128)(2,1)S(1)}, bf16[144,1024]{1,0:T(8,128)(2,1)S(1)}, u32[]{:S(2)}, u32[]{:S(2)}) collective-permute-start(bf16[144,1024]{1,0:T(8,128)(2,1)S(1)} %get-tuple-element.77), channel_id=1, source_target_pairs={{0,206},{2,196},{4,194},{6,200},{8,198},{10,204},{12,202},{14,192}... | collective-permute-start | bytes 884744 | tf_op jit(solution)/shard_map/ppermute | solution.py:465
  39.2 2.9 %first_backward.1 = (bf16[4,144,512]{2,1,0:T(8,128)(2,1)S(1)}, bf16[144,1024]{1,0:T(8,128)(2,1)S(1)}, bf16[144,1024]{1,0:T(8,128)(2,1)S(1)}, bf16[144,1024]{1,0:T(8,128)(2,1)S(1)}, bf16[144,1024]{1,0:T(8,128)(2,1)S(1)}) custom-call(s32[1]{0:T(128)} %bitcast.me, bf16[36,1024]{1,0:T(8,128)(2,1)S(1)} %collective-permute-done.3.b0, ...), custom_call_target="tpu_custom_call" | custom-call | tf_op jit(solution)/shard_map/first_backward/pallas_call | solution.py:406
  42.2 0.1 collective-permute-start.6
  42.3 0.1 collective-permute-start.7
  42.4 1.8 %collective-permute-done.12.refs_1_ = bf16[144,1024]{1,0:T(8,128)(2,1)S(1)} collective-permute-done((bf16[144,1024]{1,0:T(8,128)(2,1)S(1)}, bf16[144,1024]{1,0:T(8,128)(2,1)S(1)}, u32[]{:S(2)}, u32[]{:S(2)}) %collective-permute-start.12) | collective-permute-done | bytes 294944 | tf_op jit(solution)/shard_map/ppermute | solution.py:465
  44.2 1.6 %collective-permute-start.8 = (bf16[144,1024]{1,0:T(8,128)(2,1)S(1)}, bf16[144,1024]{1,0:T(8,128)(2,1)S(1)}, u32[]{:S(2)}, u32[]{:S(2)}) collective-permute-start(bf16[144,1024]{1,0:T(8,128)(2,1)S(1)} %get-tuple-element.62), channel_id=1, source_target_pairs={{0,66},{2,64},{4,70},{6,68},{8,74},{10,72},{12,78},{14,76},{32,98}... | collective-permute-start | bytes 884744 | tf_op jit(solution)/shard_map/ppermute | solution.py:465
  45.7 0.0 collective-permute-done.13.refs_2_
  45.7 3.3 %collective-permute-done.14.refs_3_ = bf16[144,1024]{1,0:T(8,128)(2,1)S(1)} collective-permute-done((bf16[144,1024]{1,0:T(8,128)(2,1)S(1)}, bf16[144,1024]{1,0:T(8,128)(2,1)S(1)}, u32[]{:S(2)}, u32[]{:S(2)}) %collective-permute-start.14) | collective-permute-done | bytes 294944 | tf_op jit(solution)/shard_map/ppermute | solution.py:465
  49.0 0.8 second_weights.1
  49.9 0.5 collective-permute-start.15
  50.3 1.4 %collective-permute-start.16 = (bf16[128,512]{1,0:T(8,128)(2,1)S(1)}, bf16[128,512]{1,0:T(8,128)(2,1)S(1)}, u32[]{:S(2)}, u32[]{:S(2)}) collective-permute-start(bf16[128,512]{1,0:T(8,128)(2,1)S(1)} %get-tuple-element.80), channel_id=1, source_target_pairs={{0,16},{2,18},{4,20},{6,22},{8,24},{10,26},{12,28},{14,30},{32,48}... | collective-permute-start | bytes 393224 | tf_op jit(solution)/shard_map/ppermute | solution.py:465
  51.7 0.0 collective-permute-done.6.refs_1_
  51.7 2.9 %collective-permute-start.17 = (bf16[128,512]{1,0:T(8,128)(2,1)S(1)}, bf16[128,512]{1,0:T(8,128)(2,1)S(1)}, u32[]{:S(2)}, u32[]{:S(2)}) collective-permute-start(bf16[128,512]{1,0:T(8,128)(2,1)S(1)} %get-tuple-element.81), channel_id=1, source_target_pairs={{0,48},{2,50},{4,52},{6,54},{8,56},{10,58},{12,60},{14,62},{32,16}... | collective-permute-start | bytes 393224 | tf_op jit(solution)/shard_map/ppermute | solution.py:465
  54.7 0.0 collective-permute-done.7.refs_2_
  54.7 0.0 collective-permute-done.8.refs_3_
  54.7 0.8 first_weights.1
  55.6 0.7 collective-permute-start.10
  56.2 2.5 %collective-permute-start.11 = (bf16[128,512]{1,0:T(8,128)(2,1)S(1)}, bf16[128,512]{1,0:T(8,128)(2,1)S(1)}, u32[]{:S(2)}, u32[]{:S(2)}) collective-permute-start(bf16[128,512]{1,0:T(8,128)(2,1)S(1)} %get-tuple-element.66), channel_id=1, source_target_pairs={{0,48},{2,50},{4,52},{6,54},{8,56},{10,58},{12,60},{14,62},{32,16}... | collective-permute-start | bytes 393224 | tf_op jit(solution)/shard_map/ppermute | solution.py:465
  58.7 0.0 collective-permute-done.15.b1
  58.7 0.4 collective-permute-start.9
  59.1 1.0 collective-permute-done.17.b3
  60.1 2.1 %collective-permute-done.10.a2 = bf16[128,512]{1,0:T(8,128)(2,1)S(1)} collective-permute-done((bf16[128,512]{1,0:T(8,128)(2,1)S(1)}, bf16[128,512]{1,0:T(8,128)(2,1)S(1)}, u32[]{:S(2)}, u32[]{:S(2)}) %collective-permute-start.10) | collective-permute-done | bytes 131104 | tf_op jit(solution)/shard_map/ppermute | solution.py:465
  62.2 1.3 %collective-permute-done.11.a3 = bf16[128,512]{1,0:T(8,128)(2,1)S(1)} collective-permute-done((bf16[128,512]{1,0:T(8,128)(2,1)S(1)}, bf16[128,512]{1,0:T(8,128)(2,1)S(1)}, u32[]{:S(2)}, u32[]{:S(2)}) %collective-permute-start.11) | collective-permute-done | bytes 131104 | tf_op jit(solution)/shard_map/ppermute | solution.py:465
  63.5 0.2 collective-permute-done.9.a1
  63.7 0.2 add_rows.1
  63.9 16.6 %all_to_all.10.parts = bf16[32,32,128]{2,1,0:T(8,128)(2,1)S(1)} all-to-all(bf16[32,32,128]{2,1,0:T(8,128)(2,1)S(1)} %add_rows.1), channel_id=1, replica_groups={{0,2,4,6,8,10,12,14,64,66,68,70,72,74,76,78,128,130,132,134,136,138,140..., dimensions={0} | all-to-all | bytes 524288 | tf_op jit(solution)/shard_map/all_to_all | solution.py:478
  80.5 0.8 own_rows.1
  81.4 7.3 %all-to-all-start.1 = ((f32[128,1,128]{2,1,0:T(1,128)}), f32[128,1,128]{2,1,0:T(1,128)S(1)}, u32[]{:S(2)}, u32[]{:S(2)}) async-start(f32[128,1,128]{2,1,0:T(1,128)} %get-tuple-element.82), calls=%async_computation.1 | async-start | bytes 131072 | tf_op jit(solution)/shard_map/all_to_all | solution.py:570
  88.7 1.6 %first_rest.1 = (bf16[6,12,2,512]{3,2,1,0:T(2,128)(2,1)}, bf16[6,12,2,512]{3,2,1,0:T(2,128)(2,1)}) custom-call(bf16[36,1024]{1,0:T(8,128)(2,1)S(1)} %collective-permute-done.3.b0, bf16[36,1024]{1,0:T(8,128)(2,1)S(1)} %collective-permute-done.4.b1, bf16[36,1024]{1,0:T(8,128)(2,1)S(1)} %collective-permute-done.5.b2, ...), custom_call_target="tpu_custom_call" | custom-call | tf_op jit(solution)/shard_map/first_rest/pallas_call | solution.py:406
  90.3 10.1 %all-to-all-done.1.tiles = f32[128,1,128]{2,1,0:T(1,128)S(1)} async-done(((f32[128,1,128]{2,1,0:T(1,128)}), f32[128,1,128]{2,1,0:T(1,128)S(1)}, u32[]{:S(2)}, u32[]{:S(2)}) %all-to-all-start.1) | async-done | bytes 65568 | tf_op jit(solution)/shard_map/all_to_all | solution.py:570
  100.4 0.8 clipped.1
  (15 shorter events, 0.0 us)
Async XLA Ops:
  0.6 17.0 %copy-start.6 = (f32[512]{0:T(512)S(1)}, f32[512]{0:T(512)}, u32[]{:S(2)}) copy-start(f32[512]{0:T(512)} %param.15) | copy-start | bytes 6148
  0.6 17.0 %copy-start.2 = (bf16[512,1536]{1,0:T(8,128)(2,1)S(1)}, bf16[512,1536]{1,0:T(8,128)(2,1)}, u32[]{:S(2)}) copy-start(bf16[512,1536]{1,0:T(8,128)(2,1)} %wqkv.2) | copy-start | bytes 4718596
  0.7 17.0 %copy-start.4 = (bf16[512,512]{1,0:T(8,128)(2,1)S(1)}, bf16[512,512]{1,0:T(8,128)(2,1)}, u32[]{:S(2)}) copy-start(bf16[512,512]{1,0:T(8,128)(2,1)} %wout.2) | copy-start | bytes 1572868
  4.0 11.5 %collective-permute-start = (bf16[36,1152]{1,0:T(8,128)(2,1)S(1)}, bf16[36,1152]{1,0:T(8,128)(2,1)S(1)}, u32[]{:S(2)}, u32[]{:S(2)}) collective-permute-start(bf16[36,1152]{1,0:T(8,128)(2,1)S(1)} %get-tuple-element.47), channel_id=1, source_target_pairs={{0,254},{2,224},{4,226},{6,228},{8,230},{10,232},{12,234},{14,236}... | collective-permute-start | bytes 248840 | tf_op jit(solution)/shard_map/ppermute | solution.py:443
  12.8 4.6 %collective-permute-start.1 = (bf16[36,1152]{1,0:T(8,128)(2,1)S(1)}, bf16[36,1152]{1,0:T(8,128)(2,1)S(1)}, u32[]{:S(2)}, u32[]{:S(2)}) collective-permute-start(bf16[36,1152]{1,0:T(8,128)(2,1)S(1)} %get-tuple-element.48), channel_id=1, source_target_pairs={{0,224},{2,226},{4,228},{6,230},{8,232},{10,234},{12,236},{14,238}... | collective-permute-start | bytes 248840 | tf_op jit(solution)/shard_map/ppermute | solution.py:443
  13.0 4.7 %collective-permute-start.2 = (bf16[36,1152]{1,0:T(8,128)(2,1)S(1)}, bf16[36,1152]{1,0:T(8,128)(2,1)S(1)}, u32[]{:S(2)}, u32[]{:S(2)}) collective-permute-start(bf16[36,1152]{1,0:T(8,128)(2,1)S(1)} %get-tuple-element.49), channel_id=1, source_target_pairs={{0,30},{2,0},{4,2},{6,4},{8,6},{10,8},{12,10},{14,12},{16,14},{18,... | collective-permute-start | bytes 248840 | tf_op jit(solution)/shard_map/ppermute | solution.py:443
  17.7 21.6 %copy-start.1 = (bf16[512,512]{1,0:T(8,128)(2,1)S(1)}, bf16[512,512]{1,0:T(8,128)(2,1)}, u32[]{:S(2)}) copy-start(bf16[512,512]{1,0:T(8,128)(2,1)} %wout.3) | copy-start | bytes 1572868
  22.5 10.8 %collective-permute-start.3 = (bf16[36,1024]{1,0:T(8,128)(2,1)S(1)}, bf16[36,1024]{1,0:T(8,128)(2,1)S(1)}, u32[]{:S(2)}, u32[]{:S(2)}) collective-permute-start(bf16[36,1024]{1,0:T(8,128)(2,1)S(1)} %get-tuple-element.51), channel_id=1, source_target_pairs={{254,0},{224,2},{226,4},{228,6},{230,8},{232,10},{234,12},{236,14}... | collective-permute-start | bytes 221192 | tf_op jit(solution)/shard_map/ppermute | solution.py:443
  23.4 9.9 %collective-permute-start.4 = (bf16[36,1024]{1,0:T(8,128)(2,1)S(1)}, bf16[36,1024]{1,0:T(8,128)(2,1)S(1)}, u32[]{:S(2)}, u32[]{:S(2)}) collective-permute-start(bf16[36,1024]{1,0:T(8,128)(2,1)S(1)} %get-tuple-element.52), channel_id=1, source_target_pairs={{224,0},{226,2},{228,4},{230,6},{232,8},{234,10},{236,12},{238,14}... | collective-permute-start | bytes 221192 | tf_op jit(solution)/shard_map/ppermute | solution.py:443
  24.4 8.9 %collective-permute-start.5 = (bf16[36,1024]{1,0:T(8,128)(2,1)S(1)}, bf16[36,1024]{1,0:T(8,128)(2,1)S(1)}, u32[]{:S(2)}, u32[]{:S(2)}) collective-permute-start(bf16[36,1024]{1,0:T(8,128)(2,1)S(1)} %get-tuple-element.53), channel_id=1, source_target_pairs={{30,0},{0,2},{2,4},{4,6},{6,8},{8,10},{10,12},{12,14},{14,16},{16,... | collective-permute-start | bytes 221192 | tf_op jit(solution)/shard_map/ppermute | solution.py:443
  33.3 10.9 %collective-permute-start.12 = (bf16[144,1024]{1,0:T(8,128)(2,1)S(1)}, bf16[144,1024]{1,0:T(8,128)(2,1)S(1)}, u32[]{:S(2)}, u32[]{:S(2)}) collective-permute-start(bf16[144,1024]{1,0:T(8,128)(2,1)S(1)} %get-tuple-element.75), channel_id=1, source_target_pairs={{0,192},{2,194},{4,196},{6,198},{8,200},{10,202},{12,204},{14,206}... | collective-permute-start | bytes 884744 | tf_op jit(solution)/shard_map/ppermute | solution.py:465
  34.4 11.3 %collective-permute-start.13 = (bf16[144,1024]{1,0:T(8,128)(2,1)S(1)}, bf16[144,1024]{1,0:T(8,128)(2,1)S(1)}, u32[]{:S(2)}, u32[]{:S(2)}) collective-permute-start(bf16[144,1024]{1,0:T(8,128)(2,1)S(1)} %get-tuple-element.76), channel_id=1, source_target_pairs={{0,14},{2,4},{4,2},{6,8},{8,6},{10,12},{12,10},{14,0},{32,46},{34,... | collective-permute-start | bytes 884744 | tf_op jit(solution)/shard_map/ppermute | solution.py:465
  34.5 14.5 %collective-permute-start.14 = (bf16[144,1024]{1,0:T(8,128)(2,1)S(1)}, bf16[144,1024]{1,0:T(8,128)(2,1)S(1)}, u32[]{:S(2)}, u32[]{:S(2)}) collective-permute-start(bf16[144,1024]{1,0:T(8,128)(2,1)S(1)} %get-tuple-element.77), channel_id=1, source_target_pairs={{0,206},{2,196},{4,194},{6,200},{8,198},{10,204},{12,202},{14,192}... | collective-permute-start | bytes 884744 | tf_op jit(solution)/shard_map/ppermute | solution.py:465
  42.2 9.6 %collective-permute-start.6 = (bf16[144,1024]{1,0:T(8,128)(2,1)S(1)}, bf16[144,1024]{1,0:T(8,128)(2,1)S(1)}, u32[]{:S(2)}, u32[]{:S(2)}) collective-permute-start(bf16[144,1024]{1,0:T(8,128)(2,1)S(1)} %get-tuple-element.60), channel_id=1, source_target_pairs={{0,64},{2,66},{4,68},{6,70},{8,72},{10,74},{12,76},{14,78},{32,96}... | collective-permute-start | bytes 884744 | tf_op jit(solution)/shard_map/ppermute | solution.py:465
  42.3 12.4 %collective-permute-start.7 = (bf16[144,1024]{1,0:T(8,128)(2,1)S(1)}, bf16[144,1024]{1,0:T(8,128)(2,1)S(1)}, u32[]{:S(2)}, u32[]{:S(2)}) collective-permute-start(bf16[144,1024]{1,0:T(8,128)(2,1)S(1)} %get-tuple-element.61), channel_id=1, source_target_pairs={{0,2},{2,0},{4,6},{6,4},{8,10},{10,8},{12,14},{14,12},{32,34},{34,... | collective-permute-start | bytes 884744 | tf_op jit(solution)/shard_map/ppermute | solution.py:465
  44.2 10.5 %collective-permute-start.8 = (bf16[144,1024]{1,0:T(8,128)(2,1)S(1)}, bf16[144,1024]{1,0:T(8,128)(2,1)S(1)}, u32[]{:S(2)}, u32[]{:S(2)}) collective-permute-start(bf16[144,1024]{1,0:T(8,128)(2,1)S(1)} %get-tuple-element.62), channel_id=1, source_target_pairs={{0,66},{2,64},{4,70},{6,68},{8,74},{10,72},{12,78},{14,76},{32,98}... | collective-permute-start | bytes 884744 | tf_op jit(solution)/shard_map/ppermute | solution.py:465
  49.9 8.9 %collective-permute-start.15 = (bf16[128,512]{1,0:T(8,128)(2,1)S(1)}, bf16[128,512]{1,0:T(8,128)(2,1)S(1)}, u32[]{:S(2)}, u32[]{:S(2)}) collective-permute-start(bf16[128,512]{1,0:T(8,128)(2,1)S(1)} %get-tuple-element.79), channel_id=1, source_target_pairs={{0,32},{2,34},{4,36},{6,38},{8,40},{10,42},{12,44},{14,46},{32,0},... | collective-permute-start | bytes 393224 | tf_op jit(solution)/shard_map/ppermute | solution.py:465
  50.3 8.8 %collective-permute-start.16 = (bf16[128,512]{1,0:T(8,128)(2,1)S(1)}, bf16[128,512]{1,0:T(8,128)(2,1)S(1)}, u32[]{:S(2)}, u32[]{:S(2)}) collective-permute-start(bf16[128,512]{1,0:T(8,128)(2,1)S(1)} %get-tuple-element.80), channel_id=1, source_target_pairs={{0,16},{2,18},{4,20},{6,22},{8,24},{10,26},{12,28},{14,30},{32,48}... | collective-permute-start | bytes 393224 | tf_op jit(solution)/shard_map/ppermute | solution.py:465
  51.7 8.4 %collective-permute-start.17 = (bf16[128,512]{1,0:T(8,128)(2,1)S(1)}, bf16[128,512]{1,0:T(8,128)(2,1)S(1)}, u32[]{:S(2)}, u32[]{:S(2)}) collective-permute-start(bf16[128,512]{1,0:T(8,128)(2,1)S(1)} %get-tuple-element.81), channel_id=1, source_target_pairs={{0,48},{2,50},{4,52},{6,54},{8,56},{10,58},{12,60},{14,62},{32,16}... | collective-permute-start | bytes 393224 | tf_op jit(solution)/shard_map/ppermute | solution.py:465
  54.7 33.9 %copy-start = (bf16[512,1536]{1,0:T(8,128)(2,1)S(1)}, bf16[512,1536]{1,0:T(8,128)(2,1)}, u32[]{:S(2)}) copy-start(bf16[512,1536]{1,0:T(8,128)(2,1)} %wqkv.3) | copy-start | bytes 4718596
  54.7 33.9 %copy-start.3 = (bf16[2,6,12,512]{3,0,2,1:T(2,128)(2,1)S(1)}, bf16[2,6,12,512]{3,0,2,1:T(2,128)(2,1)}, u32[]{:S(2)}) copy-start(bf16[2,6,12,512]{3,0,2,1:T(2,128)(2,1)} %param.9) | copy-start | bytes 442372
  54.7 34.0 %copy-start.5 = (f32[512]{0:T(512)S(1)}, f32[512]{0:T(512)}, u32[]{:S(2)}) copy-start(f32[512]{0:T(512)} %param.12) | copy-start | bytes 6148
  55.6 6.7 %collective-permute-start.10 = (bf16[128,512]{1,0:T(8,128)(2,1)S(1)}, bf16[128,512]{1,0:T(8,128)(2,1)S(1)}, u32[]{:S(2)}, u32[]{:S(2)}) collective-permute-start(bf16[128,512]{1,0:T(8,128)(2,1)S(1)} %get-tuple-element.65), channel_id=1, source_target_pairs={{0,16},{2,18},{4,20},{6,22},{8,24},{10,26},{12,28},{14,30},{32,48}... | collective-permute-start | bytes 393224 | tf_op jit(solution)/shard_map/ppermute | solution.py:465
  56.2 7.3 %collective-permute-start.11 = (bf16[128,512]{1,0:T(8,128)(2,1)S(1)}, bf16[128,512]{1,0:T(8,128)(2,1)S(1)}, u32[]{:S(2)}, u32[]{:S(2)}) collective-permute-start(bf16[128,512]{1,0:T(8,128)(2,1)S(1)} %get-tuple-element.66), channel_id=1, source_target_pairs={{0,48},{2,50},{4,52},{6,54},{8,56},{10,58},{12,60},{14,62},{32,16}... | collective-permute-start | bytes 393224 | tf_op jit(solution)/shard_map/ppermute | solution.py:465
  58.7 5.0 %collective-permute-start.9 = (bf16[128,512]{1,0:T(8,128)(2,1)S(1)}, bf16[128,512]{1,0:T(8,128)(2,1)S(1)}, u32[]{:S(2)}, u32[]{:S(2)}) collective-permute-start(bf16[128,512]{1,0:T(8,128)(2,1)S(1)} %get-tuple-element.64), channel_id=1, source_target_pairs={{0,32},{2,34},{4,36},{6,38},{8,40},{10,42},{12,44},{14,46},{32,0},... | collective-permute-start | bytes 393224 | tf_op jit(solution)/shard_map/ppermute | solution.py:465
  81.4 19.0 %all-to-all-start.1 = ((f32[128,1,128]{2,1,0:T(1,128)}), f32[128,1,128]{2,1,0:T(1,128)S(1)}, u32[]{:S(2)}, u32[]{:S(2)}) async-start(f32[128,1,128]{2,1,0:T(1,128)} %get-tuple-element.82), calls=%async_computation.1 | async-start | bytes 131072 | tf_op jit(solution)/shard_map/all_to_all | solution.py:570

commit v11 on v10

--- a/solution.py
+++ b/solution.py
@@ -276,7 +276,7 @@
 
 
 def second_main(
-    x0, x1, x2, x3, gain, wqkv, wout,
+    x2, x0, x1, x3, gain, wqkv, wout,
     b0, b1, b2, b3, normed_ref, att_ref, right_ref, scratch, lab_scratch,
 ):
     parts = (x0, x1, x2, x3)
@@ -305,7 +305,7 @@
 
 
 def first_backward(
-    me, b0, b1, b2, b3, wout, keep, right_ref, p0, p1, p2, p3, scratch, left_n, left_a
+    me, b2, b0, b1, b3, wout, keep, right_ref, p0, p1, p2, p3, scratch, left_n, left_a
 ):
     g16 = gather_rows((b0, b1, b2, b3), scratch, D).astype(BF16)
     datt = dot_nt(g16, wout[...]).astype(BF16)
@@ -318,7 +318,7 @@
     pack(members_first(*here(me))[0], (left_n, left_a), right_ref, (p0, p1, p2, p3))
 
 
-def first_rest(b0, b1, b2, b3, tok, gain, wqkv, right, tg_ref, result_ref, scratch):
+def first_rest(b2, b0, b1, b3, tok, gain, wqkv, right, tg_ref, result_ref, scratch):
     back = (b0, b1, b2, b3)
     put_field(gather_rows(back, scratch, 0), scratch, result_ref)
     _, xhat, rstd = norm_parts(take_field(tok, scratch), gain[...])
@@ -438,10 +438,18 @@
 
 def send(parts, tables, back=False):
     out = list(parts)
-    for slot in (2, 0, 1):
+    for slot in range(3):
         pairs = [(t, s) for s, t in tables[slot]] if back else tables[slot]
         out[slot] = lax.ppermute(parts[slot], ("lat", "lon"), pairs)
     return out
+
+
+def longest_first(parts):
+    return [parts[slot] for slot in (2, 0, 1, 3)]
+
+
+def two_hops_first(parts):
+    return [parts[step] for step in (0, 3, 1, 2)]
 
 
 def index_of(x, y, z):
@@ -527,7 +535,7 @@
         second_main,
         [shape_of(QUART, 2 * D)] * 4 + [field, field, fields],
         [(TOK, D), (TOK, LANES)],
-        *x, gain_b, shifted_query_key_value, out_second,
+        *longest_first(x), gain_b, shifted_query_key_value, out_second,
     )
     back = send(back, tables, back=True)
     half = pltpu.VMEM((TOK, D), BF16)
@@ -539,7 +547,7 @@
         first_backward,
         [fields] + packs,
         [(TOK, D), half, half],
-        me, *back, out_first, keep,
+        me, *longest_first(back), out_first, keep,
         scalar=True,
     )
     pack_a = swap_first(pack_a, 0, (3, 1, 2))
@@ -548,15 +556,15 @@
         first_rest,
         [grid, grid],
         [(TOK, D)],
-        *back, tok, gain_a, unshifted_query_key_value, right_a,
+        *longest_first(back), tok, gain_a, unshifted_query_key_value, right_a,
     )
     token_gradient = token_gradient.transpose(2, 0, 1, 3)
     result = result.transpose(2, 0, 1, 3)
 
     rows = [shape_of(PLANE_ROWS, WIDE)] * GROUP
-    sum_b = call(second_weights, rows, [(D, WIDE)], me, *in_vmem(*pack_b), scalar=True)
+    sum_b = call(second_weights, rows, [(D, WIDE)], me, *in_vmem(*two_hops_first(pack_b)), scalar=True)
     sum_b = swap_second(sum_b, 1, (2, 1, 3))
-    sum_a = call(first_weights, rows, [(D, WIDE)], me, *in_vmem(*pack_a), scalar=True)
+    sum_a = call(first_weights, rows, [(D, WIDE)], me, *in_vmem(*two_hops_first(pack_a)), scalar=True)
     sum_a = swap_first(sum_a, 1, (1, 2, 3))
     piece = (len(SHEET), 2 * PIECE, LANES)
     (sums,) = call(add_rows, [shape_of(*piece)], [piece], *sum_a, *sum_b)

time: 102 us -> 104 us (1.020)
  waiting for transfers between devices: 30.4 us -> 36.8 us
  starting transfers between devices: 36.7 us -> 32 us
    ppermute x6, waiting for transfers between devices: 10.5 us -> 14.1 us  [send(): out[slot] = lax.ppermute(parts[slot], ('lat', 'lon'), pairs)]
    ppermute x12, waiting for transfers between devices: 9.76 us -> 12.6 us  [swap(): out[step] = lax.ppermute(parts[step], ('lat', 'lon'), pairs)]
    ppermute x12, starting transfers between devices: 16 us -> 13.5 us  [swap(): out[step] = lax.ppermute(parts[step], ('lat', 'lon'), pairs)]
    ppermute x6, starting transfers between devices: 13.4 us -> 11.6 us  [send(): out[slot] = lax.ppermute(parts[slot], ('lat', 'lon'), pairs)]
  transfers between devices with their start and end apart: 19 -> 19, of which waited for: 10 -> 11; matrix products, arithmetic and copies ran while one was open for 0% -> 0% of each run, Pallas kernels for 7% -> 6%
where the time goes in v11:
time: 104 us; the launch traced here: 103 us
  waiting for transfers between devices  36.8 us (35%)
  starting transfers between devices  32 us (31%)
  blocking collectives  16.7 us (16%)
  Pallas kernels  16.6 us (16%)
    all_to_all x1, blocking collectives, exchange(): return lax.all_to_all(parts, ('lat', 'lon'), 0, 0, axis_index_groups=groups)  16.7 us
    pallas_call x10, Pallas kernels, call(): pl.pallas_call(kernel, out_shape=outs, in_specs=specs, out_specs=[whole]...  16.6 us
    ppermute x6, waiting for transfers between devices, send(): out[slot] = lax.ppermute(parts[slot], ('lat', 'lon'), pairs)  14.1 us
    ppermute x12, starting transfers between devices, swap(): out[step] = lax.ppermute(parts[step], ('lat', 'lon'), pairs)  13.5 us
    ppermute x12, waiting for transfers between devices, swap(): out[step] = lax.ppermute(parts[step], ('lat', 'lon'), pairs)  12.6 us
    ppermute x6, starting transfers between devices, send(): out[slot] = lax.ppermute(parts[slot], ('lat', 'lon'), pairs)  11.6 us
    all_to_all x1, waiting for transfers between devices, on_device(): tiles = lax.all_to_all(tiles, ('lat', 'lon'), 0, 0)  10.1 us
    all_to_all x1, starting transfers between devices, on_device(): tiles = lax.all_to_all(tiles, ('lat', 'lon'), 0, 0)  6.91 us
  transfers between devices with their start and end apart: 19, of which 11 were waited for; matrix products, arithmetic and copies ran while one was open for 0% of the time, Pallas kernels for 6%

profile of v11, /device:TPU:0, one launch (start us, length us, event | category | flops | bytes accessed | tf_op | source)
XLA Modules:
  0.0 103.0 jit_solution(12360633011115748221)
XLA Ops:
  0.7 3.3 %first_forward.1 = (bf16[36,1152]{1,0:T(8,128)(2,1)S(1)}, bf16[36,1152]{1,0:T(8,128)(2,1)S(1)}, bf16[36,1152]{1,0:T(8,128)(2,1)S(1)}, bf16[36,1152]{1,0:T(8,128)(2,1)S(1)}, bf16[144,2688]{1,0:T(8,128)(2,1)S(1)}) custom-call(s32[1]{0:T(128)} %bitcast.me, bf16[6,12,2,512]{3,2,1,0:T(2,128)(2,1)} %bitcast.8, f32[1,512]{1,0:T(1,128)} %bitcast.10, ...), custom_call_target="tpu_custom_call" | custom-call | tf_op jit(solution)/shard_map/first_forward/pallas_call | solution.py:406
  4.0 6.8 %collective-permute-start = (bf16[36,1152]{1,0:T(8,128)(2,1)S(1)}, bf16[36,1152]{1,0:T(8,128)(2,1)S(1)}, u32[]{:S(2)}, u32[]{:S(2)}) collective-permute-start(bf16[36,1152]{1,0:T(8,128)(2,1)S(1)} %get-tuple-element.47), channel_id=1, source_target_pairs={{0,30},{2,0},{4,2},{6,4},{8,6},{10,8},{12,10},{14,12},{16,14},{18,... | collective-permute-start | bytes 248840 | tf_op jit(solution)/shard_map/ppermute | solution.py:443
  10.8 3.0 %collective-permute-start.1 = (bf16[36,1152]{1,0:T(8,128)(2,1)S(1)}, bf16[36,1152]{1,0:T(8,128)(2,1)S(1)}, u32[]{:S(2)}, u32[]{:S(2)}) collective-permute-start(bf16[36,1152]{1,0:T(8,128)(2,1)S(1)} %get-tuple-element.48), channel_id=1, source_target_pairs={{0,254},{2,224},{4,226},{6,228},{8,230},{10,232},{12,234},{14,236}... | collective-permute-start | bytes 248840 | tf_op jit(solution)/shard_map/ppermute | solution.py:443
  13.9 0.1 collective-permute-start.2
  14.0 0.0 collective-permute-done.x2
  14.0 2.3 %collective-permute-done.1.x0 = bf16[36,1152]{1,0:T(8,128)(2,1)S(1)} collective-permute-done((bf16[36,1152]{1,0:T(8,128)(2,1)S(1)}, bf16[36,1152]{1,0:T(8,128)(2,1)S(1)}, u32[]{:S(2)}, u32[]{:S(2)}) %collective-permute-start.1) | collective-permute-done | bytes 82976 | tf_op jit(solution)/shard_map/ppermute | solution.py:443
  16.3 2.1 %collective-permute-done.2.x1 = bf16[36,1152]{1,0:T(8,128)(2,1)S(1)} collective-permute-done((bf16[36,1152]{1,0:T(8,128)(2,1)S(1)}, bf16[36,1152]{1,0:T(8,128)(2,1)S(1)}, u32[]{:S(2)}, u32[]{:S(2)}) %collective-permute-start.2) | collective-permute-done | bytes 82976 | tf_op jit(solution)/shard_map/ppermute | solution.py:443
  18.4 0.0 copy-start.1
  18.4 4.8 %second_main.1 = (bf16[36,1024]{1,0:T(8,128)(2,1)S(1)}, bf16[36,1024]{1,0:T(8,128)(2,1)S(1)}, bf16[36,1024]{1,0:T(8,128)(2,1)S(1)}, bf16[36,1024]{1,0:T(8,128)(2...) custom-call(bf16[36,1152]{1,0:T(8,128)(2,1)S(1)} %collective-permute-done.x2, ...), custom_call_target="tpu_custom_call" | custom-call | tf_op jit(solution)/shard_map/second_main/pallas_call | solution.py:406
  23.2 1.4 %collective-permute-start.3 = (bf16[36,1024]{1,0:T(8,128)(2,1)S(1)}, bf16[36,1024]{1,0:T(8,128)(2,1)S(1)}, u32[]{:S(2)}, u32[]{:S(2)}) collective-permute-start(bf16[36,1024]{1,0:T(8,128)(2,1)S(1)} %get-tuple-element.51), channel_id=1, source_target_pairs={{30,0},{0,2},{2,4},{4,6},{6,8},{8,10},{10,12},{12,14},{14,16},{16,... | collective-permute-start | bytes 221192 | tf_op jit(solution)/shard_map/ppermute | solution.py:443
  24.6 0.0 collective-permute-start.4
  24.6 0.3 collective-permute-start.5
  24.9 0.5 second_pack.1
  25.4 6.0 %collective-permute-done.3.b2 = bf16[36,1024]{1,0:T(8,128)(2,1)S(1)} collective-permute-done((bf16[36,1024]{1,0:T(8,128)(2,1)S(1)}, bf16[36,1024]{1,0:T(8,128)(2,1)S(1)}, u32[]{:S(2)}, u32[]{:S(2)}) %collective-permute-start.3) | collective-permute-done | bytes 73760 | tf_op jit(solution)/shard_map/ppermute | solution.py:443
  31.4 3.7 %collective-permute-done.4.b0 = bf16[36,1024]{1,0:T(8,128)(2,1)S(1)} collective-permute-done((bf16[36,1024]{1,0:T(8,128)(2,1)S(1)}, bf16[36,1024]{1,0:T(8,128)(2,1)S(1)}, u32[]{:S(2)}, u32[]{:S(2)}) %collective-permute-start.4) | collective-permute-done | bytes 73760 | tf_op jit(solution)/shard_map/ppermute | solution.py:443
  35.0 0.0 collective-permute-done.5.b1
  35.0 0.3 collective-permute-start.12
  35.3 2.1 %collective-permute-start.13 = (bf16[144,1024]{1,0:T(8,128)(2,1)S(1)}, bf16[144,1024]{1,0:T(8,128)(2,1)S(1)}, u32[]{:S(2)}, u32[]{:S(2)}) collective-permute-start(bf16[144,1024]{1,0:T(8,128)(2,1)S(1)} %get-tuple-element.76), channel_id=1, source_target_pairs={{0,192},{2,194},{4,196},{6,198},{8,200},{10,202},{12,204},{14,206}... | collective-permute-start | bytes 884744 | tf_op jit(solution)/shard_map/ppermute | solution.py:473
  37.4 3.6 %collective-permute-start.14 = (bf16[144,1024]{1,0:T(8,128)(2,1)S(1)}, bf16[144,1024]{1,0:T(8,128)(2,1)S(1)}, u32[]{:S(2)}, u32[]{:S(2)}) collective-permute-start(bf16[144,1024]{1,0:T(8,128)(2,1)S(1)} %get-tuple-element.77), channel_id=1, source_target_pairs={{0,14},{2,4},{4,2},{6,8},{8,6},{10,12},{12,10},{14,0},{32,46},{34,... | collective-permute-start | bytes 884744 | tf_op jit(solution)/shard_map/ppermute | solution.py:473
  41.0 2.9 %first_backward.1 = (bf16[4,144,512]{2,1,0:T(8,128)(2,1)S(1)}, bf16[144,1024]{1,0:T(8,128)(2,1)S(1)}, bf16[144,1024]{1,0:T(8,128)(2,1)S(1)}, bf16[144,1024]{1,0:T(8,128)(2,1)S(1)}, bf16[144,1024]{1,0:T(8,128)(2,1)S(1)}) custom-call(s32[1]{0:T(128)} %bitcast.me, bf16[36,1024]{1,0:T(8,128)(2,1)S(1)} %collective-permute-done.3.b2, ...), custom_call_target="tpu_custom_call" | custom-call | tf_op jit(solution)/shard_map/first_backward/pallas_call | solution.py:406
  43.9 0.1 collective-permute-start.6
  44.0 0.1 collective-permute-start.7
  44.1 3.6 %collective-permute-done.12.refs_1_ = bf16[144,1024]{1,0:T(8,128)(2,1)S(1)} collective-permute-done((bf16[144,1024]{1,0:T(8,128)(2,1)S(1)}, bf16[144,1024]{1,0:T(8,128)(2,1)S(1)}, u32[]{:S(2)}, u32[]{:S(2)}) %collective-permute-start.12) | collective-permute-done | bytes 294944 | tf_op jit(solution)/shard_map/ppermute | solution.py:473
  47.7 1.1 %collective-permute-done.13.refs_2_ = bf16[144,1024]{1,0:T(8,128)(2,1)S(1)} collective-permute-done((bf16[144,1024]{1,0:T(8,128)(2,1)S(1)}, bf16[144,1024]{1,0:T(8,128)(2,1)S(1)}, u32[]{:S(2)}, u32[]{:S(2)}) %collective-permute-start.13) | collective-permute-done | bytes 294944 | tf_op jit(solution)/shard_map/ppermute | solution.py:473
  48.9 0.0 collective-permute-done.14.refs_3_
  48.9 0.8 second_weights.1
  49.7 0.7 collective-permute-start.15
  50.4 2.0 %collective-permute-start.16 = (bf16[128,512]{1,0:T(8,128)(2,1)S(1)}, bf16[128,512]{1,0:T(8,128)(2,1)S(1)}, u32[]{:S(2)}, u32[]{:S(2)}) collective-permute-start(bf16[128,512]{1,0:T(8,128)(2,1)S(1)} %get-tuple-element.80), channel_id=1, source_target_pairs={{0,16},{2,18},{4,20},{6,22},{8,24},{10,26},{12,28},{14,30},{32,48}... | collective-permute-start | bytes 393224 | tf_op jit(solution)/shard_map/ppermute | solution.py:473
  52.4 1.0 collective-permute-done.6.refs_1_
  53.4 1.1 %collective-permute-start.17 = (bf16[128,512]{1,0:T(8,128)(2,1)S(1)}, bf16[128,512]{1,0:T(8,128)(2,1)S(1)}, u32[]{:S(2)}, u32[]{:S(2)}) collective-permute-start(bf16[128,512]{1,0:T(8,128)(2,1)S(1)} %get-tuple-element.81), channel_id=1, source_target_pairs={{0,48},{2,50},{4,52},{6,54},{8,56},{10,58},{12,60},{14,62},{32,16}... | collective-permute-start | bytes 393224 | tf_op jit(solution)/shard_map/ppermute | solution.py:473
  54.5 1.1 %collective-permute-done.7.refs_2_ = bf16[144,1024]{1,0:T(8,128)(2,1)S(1)} collective-permute-done((bf16[144,1024]{1,0:T(8,128)(2,1)S(1)}, bf16[144,1024]{1,0:T(8,128)(2,1)S(1)}, u32[]{:S(2)}, u32[]{:S(2)}) %collective-permute-start.7) | collective-permute-done | bytes 294944 | tf_op jit(solution)/shard_map/ppermute | solution.py:473
  55.6 0.0 collective-permute-done.8.refs_3_
  55.7 0.8 first_weights.1
  56.5 0.7 collective-permute-start.10
  57.2 0.5 collective-permute-start.11
  57.8 0.0 collective-permute-done.15.b1
  57.8 2.3 %collective-permute-start.9 = (bf16[128,512]{1,0:T(8,128)(2,1)S(1)}, bf16[128,512]{1,0:T(8,128)(2,1)S(1)}, u32[]{:S(2)}, u32[]{:S(2)}) collective-permute-start(bf16[128,512]{1,0:T(8,128)(2,1)S(1)} %get-tuple-element.64), channel_id=1, source_target_pairs={{0,32},{2,34},{4,36},{6,38},{8,40},{10,42},{12,44},{14,46},{32,0},... | collective-permute-start | bytes 393224 | tf_op jit(solution)/shard_map/ppermute | solution.py:473
  60.1 3.5 %collective-permute-done.17.b3 = bf16[128,512]{1,0:T(8,128)(2,1)S(1)} collective-permute-done((bf16[128,512]{1,0:T(8,128)(2,1)S(1)}, bf16[128,512]{1,0:T(8,128)(2,1)S(1)}, u32[]{:S(2)}, u32[]{:S(2)}) %collective-permute-start.17) | collective-permute-done | bytes 131104 | tf_op jit(solution)/shard_map/ppermute | solution.py:473
  63.6 0.0 collective-permute-done.10.a2
  63.6 2.1 %collective-permute-done.11.a3 = bf16[128,512]{1,0:T(8,128)(2,1)S(1)} collective-permute-done((bf16[128,512]{1,0:T(8,128)(2,1)S(1)}, bf16[128,512]{1,0:T(8,128)(2,1)S(1)}, u32[]{:S(2)}, u32[]{:S(2)}) %collective-permute-start.11) | collective-permute-done | bytes 131104 | tf_op jit(solution)/shard_map/ppermute | solution.py:473
  65.7 0.0 collective-permute-done.9.a1
  65.7 0.2 add_rows.1
  65.9 16.7 %all_to_all.10.parts = bf16[32,32,128]{2,1,0:T(8,128)(2,1)S(1)} all-to-all(bf16[32,32,128]{2,1,0:T(8,128)(2,1)S(1)} %add_rows.1), channel_id=1, replica_groups={{0,2,4,6,8,10,12,14,64,66,68,70,72,74,76,78,128,130,132,134,136,138,140..., dimensions={0} | all-to-all | bytes 524288 | tf_op jit(solution)/shard_map/all_to_all | solution.py:486
  82.7 0.8 own_rows.1
  83.5 6.9 %all-to-all-start.1 = ((f32[128,1,128]{2,1,0:T(1,128)}), f32[128,1,128]{2,1,0:T(1,128)S(1)}, u32[]{:S(2)}, u32[]{:S(2)}) async-start(f32[128,1,128]{2,1,0:T(1,128)} %get-tuple-element.82), calls=%async_computation.1 | async-start | bytes 131072 | tf_op jit(solution)/shard_map/all_to_all | solution.py:578
  90.4 1.6 %first_rest.1 = (bf16[6,12,2,512]{3,2,1,0:T(2,128)(2,1)}, bf16[6,12,2,512]{3,2,1,0:T(2,128)(2,1)}) custom-call(bf16[36,1024]{1,0:T(8,128)(2,1)S(1)} %collective-permute-done.3.b2, bf16[36,1024]{1,0:T(8,128)(2,1)S(1)} %collective-permute-done.4.b0, bf16[36,1024]{1,0:T(8,128)(2,1)S(1)} %collective-permute-done.5.b1, ...), custom_call_target="tpu_custom_call" | custom-call | tf_op jit(solution)/shard_map/first_rest/pallas_call | solution.py:406
  92.0 10.1 %all-to-all-done.1.tiles = f32[128,1,128]{2,1,0:T(1,128)S(1)} async-done(((f32[128,1,128]{2,1,0:T(1,128)}), f32[128,1,128]{2,1,0:T(1,128)S(1)}, u32[]{:S(2)}, u32[]{:S(2)}) %all-to-all-start.1) | async-done | bytes 65568 | tf_op jit(solution)/shard_map/all_to_all | solution.py:578
  102.2 0.8 clipped.1
  (15 shorter events, 0.0 us)
Async XLA Ops:
  0.6 17.8 %copy-start.6 = (f32[512]{0:T(512)S(1)}, f32[512]{0:T(512)}, u32[]{:S(2)}) copy-start(f32[512]{0:T(512)} %param.15) | copy-start | bytes 6148
  0.6 17.8 %copy-start.2 = (bf16[512,1536]{1,0:T(8,128)(2,1)S(1)}, bf16[512,1536]{1,0:T(8,128)(2,1)}, u32[]{:S(2)}) copy-start(bf16[512,1536]{1,0:T(8,128)(2,1)} %wqkv.2) | copy-start | bytes 4718596
  0.7 17.8 %copy-start.4 = (bf16[512,512]{1,0:T(8,128)(2,1)S(1)}, bf16[512,512]{1,0:T(8,128)(2,1)}, u32[]{:S(2)}) copy-start(bf16[512,512]{1,0:T(8,128)(2,1)} %wout.2) | copy-start | bytes 1572868
  4.0 10.0 %collective-permute-start = (bf16[36,1152]{1,0:T(8,128)(2,1)S(1)}, bf16[36,1152]{1,0:T(8,128)(2,1)S(1)}, u32[]{:S(2)}, u32[]{:S(2)}) collective-permute-start(bf16[36,1152]{1,0:T(8,128)(2,1)S(1)} %get-tuple-element.47), channel_id=1, source_target_pairs={{0,30},{2,0},{4,2},{6,4},{8,6},{10,8},{12,10},{14,12},{16,14},{18,... | collective-permute-start | bytes 248840 | tf_op jit(solution)/shard_map/ppermute | solution.py:443
  10.8 5.5 %collective-permute-start.1 = (bf16[36,1152]{1,0:T(8,128)(2,1)S(1)}, bf16[36,1152]{1,0:T(8,128)(2,1)S(1)}, u32[]{:S(2)}, u32[]{:S(2)}) collective-permute-start(bf16[36,1152]{1,0:T(8,128)(2,1)S(1)} %get-tuple-element.48), channel_id=1, source_target_pairs={{0,254},{2,224},{4,226},{6,228},{8,230},{10,232},{12,234},{14,236}... | collective-permute-start | bytes 248840 | tf_op jit(solution)/shard_map/ppermute | solution.py:443
  13.9 4.6 %collective-permute-start.2 = (bf16[36,1152]{1,0:T(8,128)(2,1)S(1)}, bf16[36,1152]{1,0:T(8,128)(2,1)S(1)}, u32[]{:S(2)}, u32[]{:S(2)}) collective-permute-start(bf16[36,1152]{1,0:T(8,128)(2,1)S(1)} %get-tuple-element.49), channel_id=1, source_target_pairs={{0,224},{2,226},{4,228},{6,230},{8,232},{10,234},{12,236},{14,238}... | collective-permute-start | bytes 248840 | tf_op jit(solution)/shard_map/ppermute | solution.py:443
  18.4 22.5 %copy-start.1 = (bf16[512,512]{1,0:T(8,128)(2,1)S(1)}, bf16[512,512]{1,0:T(8,128)(2,1)}, u32[]{:S(2)}) copy-start(bf16[512,512]{1,0:T(8,128)(2,1)} %wout.3) | copy-start | bytes 1572868
  23.2 8.1 %collective-permute-start.3 = (bf16[36,1024]{1,0:T(8,128)(2,1)S(1)}, bf16[36,1024]{1,0:T(8,128)(2,1)S(1)}, u32[]{:S(2)}, u32[]{:S(2)}) collective-permute-start(bf16[36,1024]{1,0:T(8,128)(2,1)S(1)} %get-tuple-element.51), channel_id=1, source_target_pairs={{30,0},{0,2},{2,4},{4,6},{6,8},{8,10},{10,12},{12,14},{14,16},{16,... | collective-permute-start | bytes 221192 | tf_op jit(solution)/shard_map/ppermute | solution.py:443
  24.6 10.4 %collective-permute-start.4 = (bf16[36,1024]{1,0:T(8,128)(2,1)S(1)}, bf16[36,1024]{1,0:T(8,128)(2,1)S(1)}, u32[]{:S(2)}, u32[]{:S(2)}) collective-permute-start(bf16[36,1024]{1,0:T(8,128)(2,1)S(1)} %get-tuple-element.52), channel_id=1, source_target_pairs={{254,0},{224,2},{226,4},{228,6},{230,8},{232,10},{234,12},{236,14}... | collective-permute-start | bytes 221192 | tf_op jit(solution)/shard_map/ppermute | solution.py:443
  24.6 10.4 %collective-permute-start.5 = (bf16[36,1024]{1,0:T(8,128)(2,1)S(1)}, bf16[36,1024]{1,0:T(8,128)(2,1)S(1)}, u32[]{:S(2)}, u32[]{:S(2)}) collective-permute-start(bf16[36,1024]{1,0:T(8,128)(2,1)S(1)} %get-tuple-element.53), channel_id=1, source_target_pairs={{224,0},{226,2},{228,4},{230,6},{232,8},{234,10},{236,12},{238,14}... | collective-permute-start | bytes 221192 | tf_op jit(solution)/shard_map/ppermute | solution.py:443
  35.0 12.7 %collective-permute-start.12 = (bf16[144,1024]{1,0:T(8,128)(2,1)S(1)}, bf16[144,1024]{1,0:T(8,128)(2,1)S(1)}, u32[]{:S(2)}, u32[]{:S(2)}) collective-permute-start(bf16[144,1024]{1,0:T(8,128)(2,1)S(1)} %get-tuple-element.75), channel_id=1, source_target_pairs={{0,206},{2,196},{4,194},{6,200},{8,198},{10,204},{12,202},{14,192}... | collective-permute-start | bytes 884744 | tf_op jit(solution)/shard_map/ppermute | solution.py:473
  35.3 13.6 %collective-permute-start.13 = (bf16[144,1024]{1,0:T(8,128)(2,1)S(1)}, bf16[144,1024]{1,0:T(8,128)(2,1)S(1)}, u32[]{:S(2)}, u32[]{:S(2)}) collective-permute-start(bf16[144,1024]{1,0:T(8,128)(2,1)S(1)} %get-tuple-element.76), channel_id=1, source_target_pairs={{0,192},{2,194},{4,196},{6,198},{8,200},{10,202},{12,204},{14,206}... | collective-permute-start | bytes 884744 | tf_op jit(solution)/shard_map/ppermute | solution.py:473
  37.4 11.5 %collective-permute-start.14 = (bf16[144,1024]{1,0:T(8,128)(2,1)S(1)}, bf16[144,1024]{1,0:T(8,128)(2,1)S(1)}, u32[]{:S(2)}, u32[]{:S(2)}) collective-permute-start(bf16[144,1024]{1,0:T(8,128)(2,1)S(1)} %get-tuple-element.77), channel_id=1, source_target_pairs={{0,14},{2,4},{4,2},{6,8},{8,6},{10,12},{12,10},{14,0},{32,46},{34,... | collective-permute-start | bytes 884744 | tf_op jit(solution)/shard_map/ppermute | solution.py:473
  43.9 9.6 %collective-permute-start.6 = (bf16[144,1024]{1,0:T(8,128)(2,1)S(1)}, bf16[144,1024]{1,0:T(8,128)(2,1)S(1)}, u32[]{:S(2)}, u32[]{:S(2)}) collective-permute-start(bf16[144,1024]{1,0:T(8,128)(2,1)S(1)} %get-tuple-element.60), channel_id=1, source_target_pairs={{0,66},{2,64},{4,70},{6,68},{8,74},{10,72},{12,78},{14,76},{32,98}... | collective-permute-start | bytes 884744 | tf_op jit(solution)/shard_map/ppermute | solution.py:473
  44.0 11.7 %collective-permute-start.7 = (bf16[144,1024]{1,0:T(8,128)(2,1)S(1)}, bf16[144,1024]{1,0:T(8,128)(2,1)S(1)}, u32[]{:S(2)}, u32[]{:S(2)}) collective-permute-start(bf16[144,1024]{1,0:T(8,128)(2,1)S(1)} %get-tuple-element.61), channel_id=1, source_target_pairs={{0,64},{2,66},{4,68},{6,70},{8,72},{10,74},{12,76},{14,78},{32,96}... | collective-permute-start | bytes 884744 | tf_op jit(solution)/shard_map/ppermute | solution.py:473
  47.7 7.9 %collective-permute-start.8 = (bf16[144,1024]{1,0:T(8,128)(2,1)S(1)}, bf16[144,1024]{1,0:T(8,128)(2,1)S(1)}, u32[]{:S(2)}, u32[]{:S(2)}) collective-permute-start(bf16[144,1024]{1,0:T(8,128)(2,1)S(1)} %get-tuple-element.62), channel_id=1, source_target_pairs={{0,2},{2,0},{4,6},{6,4},{8,10},{10,8},{12,14},{14,12},{32,34},{34,... | collective-permute-start | bytes 884744 | tf_op jit(solution)/shard_map/ppermute | solution.py:473
  49.7 8.0 %collective-permute-start.15 = (bf16[128,512]{1,0:T(8,128)(2,1)S(1)}, bf16[128,512]{1,0:T(8,128)(2,1)S(1)}, u32[]{:S(2)}, u32[]{:S(2)}) collective-permute-start(bf16[128,512]{1,0:T(8,128)(2,1)S(1)} %get-tuple-element.79), channel_id=1, source_target_pairs={{0,32},{2,34},{4,36},{6,38},{8,40},{10,42},{12,44},{14,46},{32,0},... | collective-permute-start | bytes 393224 | tf_op jit(solution)/shard_map/ppermute | solution.py:473
  50.4 9.7 %collective-permute-start.16 = (bf16[128,512]{1,0:T(8,128)(2,1)S(1)}, bf16[128,512]{1,0:T(8,128)(2,1)S(1)}, u32[]{:S(2)}, u32[]{:S(2)}) collective-permute-start(bf16[128,512]{1,0:T(8,128)(2,1)S(1)} %get-tuple-element.80), channel_id=1, source_target_pairs={{0,16},{2,18},{4,20},{6,22},{8,24},{10,26},{12,28},{14,30},{32,48}... | collective-permute-start | bytes 393224 | tf_op jit(solution)/shard_map/ppermute | solution.py:473
  53.4 10.2 %collective-permute-start.17 = (bf16[128,512]{1,0:T(8,128)(2,1)S(1)}, bf16[128,512]{1,0:T(8,128)(2,1)S(1)}, u32[]{:S(2)}, u32[]{:S(2)}) collective-permute-start(bf16[128,512]{1,0:T(8,128)(2,1)S(1)} %get-tuple-element.81), channel_id=1, source_target_pairs={{0,48},{2,50},{4,52},{6,54},{8,56},{10,58},{12,60},{14,62},{32,16}... | collective-permute-start | bytes 393224 | tf_op jit(solution)/shard_map/ppermute | solution.py:473
  55.6 34.8 %copy-start = (bf16[512,1536]{1,0:T(8,128)(2,1)S(1)}, bf16[512,1536]{1,0:T(8,128)(2,1)}, u32[]{:S(2)}) copy-start(bf16[512,1536]{1,0:T(8,128)(2,1)} %wqkv.3) | copy-start | bytes 4718596
  55.7 34.8 %copy-start.3 = (bf16[2,6,12,512]{3,0,2,1:T(2,128)(2,1)S(1)}, bf16[2,6,12,512]{3,0,2,1:T(2,128)(2,1)}, u32[]{:S(2)}) copy-start(bf16[2,6,12,512]{3,0,2,1:T(2,128)(2,1)} %param.9) | copy-start | bytes 442372
  55.7 34.8 %copy-start.5 = (f32[512]{0:T(512)S(1)}, f32[512]{0:T(512)}, u32[]{:S(2)}) copy-start(f32[512]{0:T(512)} %param.12) | copy-start | bytes 6148
  56.5 7.1 %collective-permute-start.10 = (bf16[128,512]{1,0:T(8,128)(2,1)S(1)}, bf16[128,512]{1,0:T(8,128)(2,1)S(1)}, u32[]{:S(2)}, u32[]{:S(2)}) collective-permute-start(bf16[128,512]{1,0:T(8,128)(2,1)S(1)} %get-tuple-element.65), channel_id=1, source_target_pairs={{0,16},{2,18},{4,20},{6,22},{8,24},{10,26},{12,28},{14,30},{32,48}... | collective-permute-start | bytes 393224 | tf_op jit(solution)/shard_map/ppermute | solution.py:473
  57.2 8.5 %collective-permute-start.11 = (bf16[128,512]{1,0:T(8,128)(2,1)S(1)}, bf16[128,512]{1,0:T(8,128)(2,1)S(1)}, u32[]{:S(2)}, u32[]{:S(2)}) collective-permute-start(bf16[128,512]{1,0:T(8,128)(2,1)S(1)} %get-tuple-element.66), channel_id=1, source_target_pairs={{0,48},{2,50},{4,52},{6,54},{8,56},{10,58},{12,60},{14,62},{32,16}... | collective-permute-start | bytes 393224 | tf_op jit(solution)/shard_map/ppermute | solution.py:473
  57.8 8.0 %collective-permute-start.9 = (bf16[128,512]{1,0:T(8,128)(2,1)S(1)}, bf16[128,512]{1,0:T(8,128)(2,1)S(1)}, u32[]{:S(2)}, u32[]{:S(2)}) collective-permute-start(bf16[128,512]{1,0:T(8,128)(2,1)S(1)} %get-tuple-element.64), channel_id=1, source_target_pairs={{0,32},{2,34},{4,36},{6,38},{8,40},{10,42},{12,44},{14,46},{32,0},... | collective-permute-start | bytes 393224 | tf_op jit(solution)/shard_map/ppermute | solution.py:473
  83.5 18.7 %all-to-all-start.1 = ((f32[128,1,128]{2,1,0:T(1,128)}), f32[128,1,128]{2,1,0:T(1,128)S(1)}, u32[]{:S(2)}, u32[]{:S(2)}) async-start(f32[128,1,128]{2,1,0:T(1,128)} %get-tuple-element.82), calls=%async_computation.1 | async-start | bytes 131072 | tf_op jit(solution)/shard_map/all_to_all | solution.py:578

commit v12 on v10

--- a/solution.py
+++ b/solution.py
@@ -276,7 +276,7 @@
 
 
 def second_main(
-    x0, x1, x2, x3, gain, wqkv, wout,
+    x2, x0, x1, x3, gain, wqkv, wout,
     b0, b1, b2, b3, normed_ref, att_ref, right_ref, scratch, lab_scratch,
 ):
     parts = (x0, x1, x2, x3)
@@ -527,7 +527,7 @@
         second_main,
         [shape_of(QUART, 2 * D)] * 4 + [field, field, fields],
         [(TOK, D), (TOK, LANES)],
-        *x, gain_b, shifted_query_key_value, out_second,
+        x[2], x[0], x[1], x[3], gain_b, shifted_query_key_value, out_second,
     )
     back = send(back, tables, back=True)
     half = pltpu.VMEM((TOK, D), BF16)

time: 102 us -> 102 us (level)
  waiting for transfers between devices: 30.4 us -> 33 us
  blocking collectives: 16.6 us -> 14.7 us
    ppermute x6, waiting for transfers between devices: 10.5 us -> 12.8 us  [send(): out[slot] = lax.ppermute(parts[slot], ('lat', 'lon'), pairs)]
    all_to_all x1, blocking collectives: 16.6 us -> 14.7 us  [exchange(): return lax.all_to_all(parts, ('lat', 'lon'), 0, 0, axis_index_groups=groups)]
    ppermute x6, starting transfers between devices: 13.4 us -> 11.6 us  [send(): out[slot] = lax.ppermute(parts[slot], ('lat', 'lon'), pairs)]
    ppermute x12, starting transfers between devices: 16 us -> 17.2 us  [swap(): out[step] = lax.ppermute(parts[step], ('lat', 'lon'), pairs)]
  transfers between devices with their start and end apart: 19 -> 19, of which waited for: 10 -> 12; matrix products, arithmetic and copies ran while one was open for 0% -> 0% of each run, Pallas kernels for 7% -> 7%
where the time goes in v12:
time: 102 us; the launch traced here: 101 us
  starting transfers between devices  36.1 us (35%)
  waiting for transfers between devices  33 us (32%)
  Pallas kernels  16.6 us (16%)
  blocking collectives  14.7 us (14%)
    ppermute x12, starting transfers between devices, swap(): out[step] = lax.ppermute(parts[step], ('lat', 'lon'), pairs)  17.2 us
    pallas_call x10, Pallas kernels, call(): pl.pallas_call(kernel, out_shape=outs, in_specs=specs, out_specs=[whole]...  16.6 us
    all_to_all x1, blocking collectives, exchange(): return lax.all_to_all(parts, ('lat', 'lon'), 0, 0, axis_index_groups=groups)  14.7 us
    ppermute x6, waiting for transfers between devices, send(): out[slot] = lax.ppermute(parts[slot], ('lat', 'lon'), pairs)  12.8 us
    ppermute x6, starting transfers between devices, send(): out[slot] = lax.ppermute(parts[slot], ('lat', 'lon'), pairs)  11.6 us
    all_to_all x1, waiting for transfers between devices, on_device(): tiles = lax.all_to_all(tiles, ('lat', 'lon'), 0, 0)  10.1 us
    ppermute x12, waiting for transfers between devices, swap(): out[step] = lax.ppermute(parts[step], ('lat', 'lon'), pairs)  10.1 us
    all_to_all x1, starting transfers between devices, on_device(): tiles = lax.all_to_all(tiles, ('lat', 'lon'), 0, 0)  7.4 us
  transfers between devices with their start and end apart: 19, of which 12 were waited for; matrix products, arithmetic and copies ran while one was open for 0% of the time, Pallas kernels for 7%

profile of v12, /device:TPU:0, one launch (start us, length us, event | category | flops | bytes accessed | tf_op | source)
XLA Modules:
  0.0 101.3 jit_solution(17384358070600980150)
XLA Ops:
  0.7 3.3 %first_forward.1 = (bf16[36,1152]{1,0:T(8,128)(2,1)S(1)}, bf16[36,1152]{1,0:T(8,128)(2,1)S(1)}, bf16[36,1152]{1,0:T(8,128)(2,1)S(1)}, bf16[36,1152]{1,0:T(8,128)(2,1)S(1)}, bf16[144,2688]{1,0:T(8,128)(2,1)S(1)}) custom-call(s32[1]{0:T(128)} %bitcast.me, bf16[6,12,2,512]{3,2,1,0:T(2,128)(2,1)} %bitcast.8, f32[1,512]{1,0:T(1,128)} %bitcast.10, ...), custom_call_target="tpu_custom_call" | custom-call | tf_op jit(solution)/shard_map/first_forward/pallas_call | solution.py:406
  4.0 6.8 %collective-permute-start = (bf16[36,1152]{1,0:T(8,128)(2,1)S(1)}, bf16[36,1152]{1,0:T(8,128)(2,1)S(1)}, u32[]{:S(2)}, u32[]{:S(2)}) collective-permute-start(bf16[36,1152]{1,0:T(8,128)(2,1)S(1)} %get-tuple-element.47), channel_id=1, source_target_pairs={{0,30},{2,0},{4,2},{6,4},{8,6},{10,8},{12,10},{14,12},{16,14},{18,... | collective-permute-start | bytes 248840 | tf_op jit(solution)/shard_map/ppermute | solution.py:443
  10.8 3.0 %collective-permute-start.1 = (bf16[36,1152]{1,0:T(8,128)(2,1)S(1)}, bf16[36,1152]{1,0:T(8,128)(2,1)S(1)}, u32[]{:S(2)}, u32[]{:S(2)}) collective-permute-start(bf16[36,1152]{1,0:T(8,128)(2,1)S(1)} %get-tuple-element.48), channel_id=1, source_target_pairs={{0,254},{2,224},{4,226},{6,228},{8,230},{10,232},{12,234},{14,236}... | collective-permute-start | bytes 248840 | tf_op jit(solution)/shard_map/ppermute | solution.py:443
  13.9 0.1 collective-permute-start.2
  14.0 0.0 collective-permute-done.x2
  14.0 2.3 %collective-permute-done.1.x0 = bf16[36,1152]{1,0:T(8,128)(2,1)S(1)} collective-permute-done((bf16[36,1152]{1,0:T(8,128)(2,1)S(1)}, bf16[36,1152]{1,0:T(8,128)(2,1)S(1)}, u32[]{:S(2)}, u32[]{:S(2)}) %collective-permute-start.1) | collective-permute-done | bytes 82976 | tf_op jit(solution)/shard_map/ppermute | solution.py:443
  16.3 2.1 %collective-permute-done.2.x1 = bf16[36,1152]{1,0:T(8,128)(2,1)S(1)} collective-permute-done((bf16[36,1152]{1,0:T(8,128)(2,1)S(1)}, bf16[36,1152]{1,0:T(8,128)(2,1)S(1)}, u32[]{:S(2)}, u32[]{:S(2)}) %collective-permute-start.2) | collective-permute-done | bytes 82976 | tf_op jit(solution)/shard_map/ppermute | solution.py:443
  18.4 0.0 copy-start.1
  18.4 4.8 %second_main.1 = (bf16[36,1024]{1,0:T(8,128)(2,1)S(1)}, bf16[36,1024]{1,0:T(8,128)(2,1)S(1)}, bf16[36,1024]{1,0:T(8,128)(2,1)S(1)}, bf16[36,1024]{1,0:T(8,128)(2...) custom-call(bf16[36,1152]{1,0:T(8,128)(2,1)S(1)} %collective-permute-done.x2, ...), custom_call_target="tpu_custom_call" | custom-call | tf_op jit(solution)/shard_map/second_main/pallas_call | solution.py:406
  23.2 0.9 collective-permute-start.3
  24.1 0.7 collective-permute-start.4
  24.8 0.0 collective-permute-start.5
  24.8 0.5 second_pack.1
  25.3 8.4 %collective-permute-done.3.b0 = bf16[36,1024]{1,0:T(8,128)(2,1)S(1)} collective-permute-done((bf16[36,1024]{1,0:T(8,128)(2,1)S(1)}, bf16[36,1024]{1,0:T(8,128)(2,1)S(1)}, u32[]{:S(2)}, u32[]{:S(2)}) %collective-permute-start.3) | collective-permute-done | bytes 73760 | tf_op jit(solution)/shard_map/ppermute | solution.py:443
  33.7 0.0 collective-permute-done.4.b1
  33.7 0.0 collective-permute-done.5.b2
  33.7 3.1 %collective-permute-start.12 = (bf16[144,1024]{1,0:T(8,128)(2,1)S(1)}, bf16[144,1024]{1,0:T(8,128)(2,1)S(1)}, u32[]{:S(2)}, u32[]{:S(2)}) collective-permute-start(bf16[144,1024]{1,0:T(8,128)(2,1)S(1)} %get-tuple-element.75), channel_id=1, source_target_pairs={{0,192},{2,194},{4,196},{6,198},{8,200},{10,202},{12,204},{14,206}... | collective-permute-start | bytes 884744 | tf_op jit(solution)/shard_map/ppermute | solution.py:465
  36.8 0.0 collective-permute-start.13
  36.8 2.8 %collective-permute-start.14 = (bf16[144,1024]{1,0:T(8,128)(2,1)S(1)}, bf16[144,1024]{1,0:T(8,128)(2,1)S(1)}, u32[]{:S(2)}, u32[]{:S(2)}) collective-permute-start(bf16[144,1024]{1,0:T(8,128)(2,1)S(1)} %get-tuple-element.77), channel_id=1, source_target_pairs={{0,206},{2,196},{4,194},{6,200},{8,198},{10,204},{12,202},{14,192}... | collective-permute-start | bytes 884744 | tf_op jit(solution)/shard_map/ppermute | solution.py:465
  39.6 2.9 %first_backward.1 = (bf16[4,144,512]{2,1,0:T(8,128)(2,1)S(1)}, bf16[144,1024]{1,0:T(8,128)(2,1)S(1)}, bf16[144,1024]{1,0:T(8,128)(2,1)S(1)}, bf16[144,1024]{1,0:T(8,128)(2,1)S(1)}, bf16[144,1024]{1,0:T(8,128)(2,1)S(1)}) custom-call(s32[1]{0:T(128)} %bitcast.me, bf16[36,1024]{1,0:T(8,128)(2,1)S(1)} %collective-permute-done.3.b0, ...), custom_call_target="tpu_custom_call" | custom-call | tf_op jit(solution)/shard_map/first_backward/pallas_call | solution.py:406
  42.5 0.1 collective-permute-start.6
  42.6 0.1 collective-permute-start.7
  42.8 0.9 collective-permute-done.12.refs_1_
  43.7 2.4 %collective-permute-start.8 = (bf16[144,1024]{1,0:T(8,128)(2,1)S(1)}, bf16[144,1024]{1,0:T(8,128)(2,1)S(1)}, u32[]{:S(2)}, u32[]{:S(2)}) collective-permute-start(bf16[144,1024]{1,0:T(8,128)(2,1)S(1)} %get-tuple-element.62), channel_id=1, source_target_pairs={{0,66},{2,64},{4,70},{6,68},{8,74},{10,72},{12,78},{14,76},{32,98}... | collective-permute-start | bytes 884744 | tf_op jit(solution)/shard_map/ppermute | solution.py:465
  46.1 0.7 collective-permute-done.13.refs_2_
  46.8 3.4 %collective-permute-done.14.refs_3_ = bf16[144,1024]{1,0:T(8,128)(2,1)S(1)} collective-permute-done((bf16[144,1024]{1,0:T(8,128)(2,1)S(1)}, bf16[144,1024]{1,0:T(8,128)(2,1)S(1)}, u32[]{:S(2)}, u32[]{:S(2)}) %collective-permute-start.14) | collective-permute-done | bytes 294944 | tf_op jit(solution)/shard_map/ppermute | solution.py:465
  50.2 0.8 second_weights.1
  51.1 1.2 %collective-permute-start.15 = (bf16[128,512]{1,0:T(8,128)(2,1)S(1)}, bf16[128,512]{1,0:T(8,128)(2,1)S(1)}, u32[]{:S(2)}, u32[]{:S(2)}) collective-permute-start(bf16[128,512]{1,0:T(8,128)(2,1)S(1)} %get-tuple-element.79), channel_id=1, source_target_pairs={{0,32},{2,34},{4,36},{6,38},{8,40},{10,42},{12,44},{14,46},{32,0},... | collective-permute-start | bytes 393224 | tf_op jit(solution)/shard_map/ppermute | solution.py:465
  52.3 1.0 %collective-permute-start.16 = (bf16[128,512]{1,0:T(8,128)(2,1)S(1)}, bf16[128,512]{1,0:T(8,128)(2,1)S(1)}, u32[]{:S(2)}, u32[]{:S(2)}) collective-permute-start(bf16[128,512]{1,0:T(8,128)(2,1)S(1)} %get-tuple-element.80), channel_id=1, source_target_pairs={{0,16},{2,18},{4,20},{6,22},{8,24},{10,26},{12,28},{14,30},{32,48}... | collective-permute-start | bytes 393224 | tf_op jit(solution)/shard_map/ppermute | solution.py:465
  53.3 0.0 collective-permute-done.6.refs_1_
  53.3 2.6 %collective-permute-start.17 = (bf16[128,512]{1,0:T(8,128)(2,1)S(1)}, bf16[128,512]{1,0:T(8,128)(2,1)S(1)}, u32[]{:S(2)}, u32[]{:S(2)}) collective-permute-start(bf16[128,512]{1,0:T(8,128)(2,1)S(1)} %get-tuple-element.81), channel_id=1, source_target_pairs={{0,48},{2,50},{4,52},{6,54},{8,56},{10,58},{12,60},{14,62},{32,16}... | collective-permute-start | bytes 393224 | tf_op jit(solution)/shard_map/ppermute | solution.py:465
  55.9 0.0 collective-permute-done.7.refs_2_
  55.9 0.1 collective-permute-done.8.refs_3_
  56.0 0.8 first_weights.1
  56.8 1.1 %collective-permute-start.10 = (bf16[128,512]{1,0:T(8,128)(2,1)S(1)}, bf16[128,512]{1,0:T(8,128)(2,1)S(1)}, u32[]{:S(2)}, u32[]{:S(2)}) collective-permute-start(bf16[128,512]{1,0:T(8,128)(2,1)S(1)} %get-tuple-element.65), channel_id=1, source_target_pairs={{0,16},{2,18},{4,20},{6,22},{8,24},{10,26},{12,28},{14,30},{32,48}... | collective-permute-start | bytes 393224 | tf_op jit(solution)/shard_map/ppermute | solution.py:465
  57.9 2.7 %collective-permute-start.11 = (bf16[128,512]{1,0:T(8,128)(2,1)S(1)}, bf16[128,512]{1,0:T(8,128)(2,1)S(1)}, u32[]{:S(2)}, u32[]{:S(2)}) collective-permute-start(bf16[128,512]{1,0:T(8,128)(2,1)S(1)} %get-tuple-element.66), channel_id=1, source_target_pairs={{0,48},{2,50},{4,52},{6,54},{8,56},{10,58},{12,60},{14,62},{32,16}... | collective-permute-start | bytes 393224 | tf_op jit(solution)/shard_map/ppermute | solution.py:465
  60.6 0.0 collective-permute-done.15.b1
  60.6 1.2 %collective-permute-done.17.b3 = bf16[128,512]{1,0:T(8,128)(2,1)S(1)} collective-permute-done((bf16[128,512]{1,0:T(8,128)(2,1)S(1)}, bf16[128,512]{1,0:T(8,128)(2,1)S(1)}, u32[]{:S(2)}, u32[]{:S(2)}) %collective-permute-start.17) | collective-permute-done | bytes 131104 | tf_op jit(solution)/shard_map/ppermute | solution.py:465
  61.9 1.5 %collective-permute-done.10.a2 = bf16[128,512]{1,0:T(8,128)(2,1)S(1)} collective-permute-done((bf16[128,512]{1,0:T(8,128)(2,1)S(1)}, bf16[128,512]{1,0:T(8,128)(2,1)S(1)}, u32[]{:S(2)}, u32[]{:S(2)}) %collective-permute-start.10) | collective-permute-done | bytes 131104 | tf_op jit(solution)/shard_map/ppermute | solution.py:465
  63.4 1.3 %collective-permute-done.11.a3 = bf16[128,512]{1,0:T(8,128)(2,1)S(1)} collective-permute-done((bf16[128,512]{1,0:T(8,128)(2,1)S(1)}, bf16[128,512]{1,0:T(8,128)(2,1)S(1)}, u32[]{:S(2)}, u32[]{:S(2)}) %collective-permute-start.11) | collective-permute-done | bytes 131104 | tf_op jit(solution)/shard_map/ppermute | solution.py:465
  64.8 0.8 collective-permute-done.9.a1
  65.6 0.2 add_rows.1
  65.8 14.7 %all_to_all.10.parts = bf16[32,32,128]{2,1,0:T(8,128)(2,1)S(1)} all-to-all(bf16[32,32,128]{2,1,0:T(8,128)(2,1)S(1)} %add_rows.1), channel_id=1, replica_groups={{0,2,4,6,8,10,12,14,64,66,68,70,72,74,76,78,128,130,132,134,136,138,140..., dimensions={0} | all-to-all | bytes 524288 | tf_op jit(solution)/shard_map/all_to_all | solution.py:478
  80.5 0.8 own_rows.1
  81.3 7.4 %all-to-all-start.1 = ((f32[128,1,128]{2,1,0:T(1,128)}), f32[128,1,128]{2,1,0:T(1,128)S(1)}, u32[]{:S(2)}, u32[]{:S(2)}) async-start(f32[128,1,128]{2,1,0:T(1,128)} %get-tuple-element.82), calls=%async_computation.1 | async-start | bytes 131072 | tf_op jit(solution)/shard_map/all_to_all | solution.py:570
  88.8 1.6 %first_rest.1 = (bf16[6,12,2,512]{3,2,1,0:T(2,128)(2,1)}, bf16[6,12,2,512]{3,2,1,0:T(2,128)(2,1)}) custom-call(bf16[36,1024]{1,0:T(8,128)(2,1)S(1)} %collective-permute-done.3.b0, bf16[36,1024]{1,0:T(8,128)(2,1)S(1)} %collective-permute-done.4.b1, bf16[36,1024]{1,0:T(8,128)(2,1)S(1)} %collective-permute-done.5.b2, ...), custom_call_target="tpu_custom_call" | custom-call | tf_op jit(solution)/shard_map/first_rest/pallas_call | solution.py:406
  90.4 10.1 %all-to-all-done.1.tiles = f32[128,1,128]{2,1,0:T(1,128)S(1)} async-done(((f32[128,1,128]{2,1,0:T(1,128)}), f32[128,1,128]{2,1,0:T(1,128)S(1)}, u32[]{:S(2)}, u32[]{:S(2)}) %all-to-all-start.1) | async-done | bytes 65568 | tf_op jit(solution)/shard_map/all_to_all | solution.py:570
  100.5 0.8 clipped.1
  (15 shorter events, 0.0 us)
Async XLA Ops:
  0.6 17.8 %copy-start.6 = (f32[512]{0:T(512)S(1)}, f32[512]{0:T(512)}, u32[]{:S(2)}) copy-start(f32[512]{0:T(512)} %param.15) | copy-start | bytes 6148
  0.6 17.8 %copy-start.2 = (bf16[512,1536]{1,0:T(8,128)(2,1)S(1)}, bf16[512,1536]{1,0:T(8,128)(2,1)}, u32[]{:S(2)}) copy-start(bf16[512,1536]{1,0:T(8,128)(2,1)} %wqkv.2) | copy-start | bytes 4718596
  0.7 17.8 %copy-start.4 = (bf16[512,512]{1,0:T(8,128)(2,1)S(1)}, bf16[512,512]{1,0:T(8,128)(2,1)}, u32[]{:S(2)}) copy-start(bf16[512,512]{1,0:T(8,128)(2,1)} %wout.2) | copy-start | bytes 1572868
  4.0 10.0 %collective-permute-start = (bf16[36,1152]{1,0:T(8,128)(2,1)S(1)}, bf16[36,1152]{1,0:T(8,128)(2,1)S(1)}, u32[]{:S(2)}, u32[]{:S(2)}) collective-permute-start(bf16[36,1152]{1,0:T(8,128)(2,1)S(1)} %get-tuple-element.47), channel_id=1, source_target_pairs={{0,30},{2,0},{4,2},{6,4},{8,6},{10,8},{12,10},{14,12},{16,14},{18,... | collective-permute-start | bytes 248840 | tf_op jit(solution)/shard_map/ppermute | solution.py:443
  10.8 5.5 %collective-permute-start.1 = (bf16[36,1152]{1,0:T(8,128)(2,1)S(1)}, bf16[36,1152]{1,0:T(8,128)(2,1)S(1)}, u32[]{:S(2)}, u32[]{:S(2)}) collective-permute-start(bf16[36,1152]{1,0:T(8,128)(2,1)S(1)} %get-tuple-element.48), channel_id=1, source_target_pairs={{0,254},{2,224},{4,226},{6,228},{8,230},{10,232},{12,234},{14,236}... | collective-permute-start | bytes 248840 | tf_op jit(solution)/shard_map/ppermute | solution.py:443
  13.9 4.6 %collective-permute-start.2 = (bf16[36,1152]{1,0:T(8,128)(2,1)S(1)}, bf16[36,1152]{1,0:T(8,128)(2,1)S(1)}, u32[]{:S(2)}, u32[]{:S(2)}) collective-permute-start(bf16[36,1152]{1,0:T(8,128)(2,1)S(1)} %get-tuple-element.49), channel_id=1, source_target_pairs={{0,224},{2,226},{4,228},{6,230},{8,232},{10,234},{12,236},{14,238}... | collective-permute-start | bytes 248840 | tf_op jit(solution)/shard_map/ppermute | solution.py:443
  18.4 21.2 %copy-start.1 = (bf16[512,512]{1,0:T(8,128)(2,1)S(1)}, bf16[512,512]{1,0:T(8,128)(2,1)}, u32[]{:S(2)}) copy-start(bf16[512,512]{1,0:T(8,128)(2,1)} %wout.3) | copy-start | bytes 1572868
  23.2 10.5 %collective-permute-start.3 = (bf16[36,1024]{1,0:T(8,128)(2,1)S(1)}, bf16[36,1024]{1,0:T(8,128)(2,1)S(1)}, u32[]{:S(2)}, u32[]{:S(2)}) collective-permute-start(bf16[36,1024]{1,0:T(8,128)(2,1)S(1)} %get-tuple-element.51), channel_id=1, source_target_pairs={{254,0},{224,2},{226,4},{228,6},{230,8},{232,10},{234,12},{236,14}... | collective-permute-start | bytes 221192 | tf_op jit(solution)/shard_map/ppermute | solution.py:443
  24.1 9.6 %collective-permute-start.4 = (bf16[36,1024]{1,0:T(8,128)(2,1)S(1)}, bf16[36,1024]{1,0:T(8,128)(2,1)S(1)}, u32[]{:S(2)}, u32[]{:S(2)}) collective-permute-start(bf16[36,1024]{1,0:T(8,128)(2,1)S(1)} %get-tuple-element.52), channel_id=1, source_target_pairs={{224,0},{226,2},{228,4},{230,6},{232,8},{234,10},{236,12},{238,14}... | collective-permute-start | bytes 221192 | tf_op jit(solution)/shard_map/ppermute | solution.py:443
  24.8 8.9 %collective-permute-start.5 = (bf16[36,1024]{1,0:T(8,128)(2,1)S(1)}, bf16[36,1024]{1,0:T(8,128)(2,1)S(1)}, u32[]{:S(2)}, u32[]{:S(2)}) collective-permute-start(bf16[36,1024]{1,0:T(8,128)(2,1)S(1)} %get-tuple-element.53), channel_id=1, source_target_pairs={{30,0},{0,2},{2,4},{4,6},{6,8},{8,10},{10,12},{12,14},{14,16},{16,... | collective-permute-start | bytes 221192 | tf_op jit(solution)/shard_map/ppermute | solution.py:443
  33.7 10.0 %collective-permute-start.12 = (bf16[144,1024]{1,0:T(8,128)(2,1)S(1)}, bf16[144,1024]{1,0:T(8,128)(2,1)S(1)}, u32[]{:S(2)}, u32[]{:S(2)}) collective-permute-start(bf16[144,1024]{1,0:T(8,128)(2,1)S(1)} %get-tuple-element.75), channel_id=1, source_target_pairs={{0,192},{2,194},{4,196},{6,198},{8,200},{10,202},{12,204},{14,206}... | collective-permute-start | bytes 884744 | tf_op jit(solution)/shard_map/ppermute | solution.py:465
  36.8 10.0 %collective-permute-start.13 = (bf16[144,1024]{1,0:T(8,128)(2,1)S(1)}, bf16[144,1024]{1,0:T(8,128)(2,1)S(1)}, u32[]{:S(2)}, u32[]{:S(2)}) collective-permute-start(bf16[144,1024]{1,0:T(8,128)(2,1)S(1)} %get-tuple-element.76), channel_id=1, source_target_pairs={{0,14},{2,4},{4,2},{6,8},{8,6},{10,12},{12,10},{14,0},{32,46},{34,... | collective-permute-start | bytes 884744 | tf_op jit(solution)/shard_map/ppermute | solution.py:465
  36.8 13.4 %collective-permute-start.14 = (bf16[144,1024]{1,0:T(8,128)(2,1)S(1)}, bf16[144,1024]{1,0:T(8,128)(2,1)S(1)}, u32[]{:S(2)}, u32[]{:S(2)}) collective-permute-start(bf16[144,1024]{1,0:T(8,128)(2,1)S(1)} %get-tuple-element.77), channel_id=1, source_target_pairs={{0,206},{2,196},{4,194},{6,200},{8,198},{10,204},{12,202},{14,192}... | collective-permute-start | bytes 884744 | tf_op jit(solution)/shard_map/ppermute | solution.py:465
  42.5 10.7 %collective-permute-start.6 = (bf16[144,1024]{1,0:T(8,128)(2,1)S(1)}, bf16[144,1024]{1,0:T(8,128)(2,1)S(1)}, u32[]{:S(2)}, u32[]{:S(2)}) collective-permute-start(bf16[144,1024]{1,0:T(8,128)(2,1)S(1)} %get-tuple-element.60), channel_id=1, source_target_pairs={{0,64},{2,66},{4,68},{6,70},{8,72},{10,74},{12,76},{14,78},{32,96}... | collective-permute-start | bytes 884744 | tf_op jit(solution)/shard_map/ppermute | solution.py:465
  42.6 13.2 %collective-permute-start.7 = (bf16[144,1024]{1,0:T(8,128)(2,1)S(1)}, bf16[144,1024]{1,0:T(8,128)(2,1)S(1)}, u32[]{:S(2)}, u32[]{:S(2)}) collective-permute-start(bf16[144,1024]{1,0:T(8,128)(2,1)S(1)} %get-tuple-element.61), channel_id=1, source_target_pairs={{0,2},{2,0},{4,6},{6,4},{8,10},{10,8},{12,14},{14,12},{32,34},{34,... | collective-permute-start | bytes 884744 | tf_op jit(solution)/shard_map/ppermute | solution.py:465
  43.7 12.3 %collective-permute-start.8 = (bf16[144,1024]{1,0:T(8,128)(2,1)S(1)}, bf16[144,1024]{1,0:T(8,128)(2,1)S(1)}, u32[]{:S(2)}, u32[]{:S(2)}) collective-permute-start(bf16[144,1024]{1,0:T(8,128)(2,1)S(1)} %get-tuple-element.62), channel_id=1, source_target_pairs={{0,66},{2,64},{4,70},{6,68},{8,74},{10,72},{12,78},{14,76},{32,98}... | collective-permute-start | bytes 884744 | tf_op jit(solution)/shard_map/ppermute | solution.py:465
  51.1 9.5 %collective-permute-start.15 = (bf16[128,512]{1,0:T(8,128)(2,1)S(1)}, bf16[128,512]{1,0:T(8,128)(2,1)S(1)}, u32[]{:S(2)}, u32[]{:S(2)}) collective-permute-start(bf16[128,512]{1,0:T(8,128)(2,1)S(1)} %get-tuple-element.79), channel_id=1, source_target_pairs={{0,32},{2,34},{4,36},{6,38},{8,40},{10,42},{12,44},{14,46},{32,0},... | collective-permute-start | bytes 393224 | tf_op jit(solution)/shard_map/ppermute | solution.py:465
  52.3 8.4 %collective-permute-start.16 = (bf16[128,512]{1,0:T(8,128)(2,1)S(1)}, bf16[128,512]{1,0:T(8,128)(2,1)S(1)}, u32[]{:S(2)}, u32[]{:S(2)}) collective-permute-start(bf16[128,512]{1,0:T(8,128)(2,1)S(1)} %get-tuple-element.80), channel_id=1, source_target_pairs={{0,16},{2,18},{4,20},{6,22},{8,24},{10,26},{12,28},{14,30},{32,48}... | collective-permute-start | bytes 393224 | tf_op jit(solution)/shard_map/ppermute | solution.py:465
  53.3 8.6 %collective-permute-start.17 = (bf16[128,512]{1,0:T(8,128)(2,1)S(1)}, bf16[128,512]{1,0:T(8,128)(2,1)S(1)}, u32[]{:S(2)}, u32[]{:S(2)}) collective-permute-start(bf16[128,512]{1,0:T(8,128)(2,1)S(1)} %get-tuple-element.81), channel_id=1, source_target_pairs={{0,48},{2,50},{4,52},{6,54},{8,56},{10,58},{12,60},{14,62},{32,16}... | collective-permute-start | bytes 393224 | tf_op jit(solution)/shard_map/ppermute | solution.py:465
  55.9 32.8 %copy-start = (bf16[512,1536]{1,0:T(8,128)(2,1)S(1)}, bf16[512,1536]{1,0:T(8,128)(2,1)}, u32[]{:S(2)}) copy-start(bf16[512,1536]{1,0:T(8,128)(2,1)} %wqkv.3) | copy-start | bytes 4718596
  56.0 32.8 %copy-start.3 = (bf16[2,6,12,512]{3,0,2,1:T(2,128)(2,1)S(1)}, bf16[2,6,12,512]{3,0,2,1:T(2,128)(2,1)}, u32[]{:S(2)}) copy-start(bf16[2,6,12,512]{3,0,2,1:T(2,128)(2,1)} %param.9) | copy-start | bytes 442372
  56.0 32.8 %copy-start.5 = (f32[512]{0:T(512)S(1)}, f32[512]{0:T(512)}, u32[]{:S(2)}) copy-start(f32[512]{0:T(512)} %param.12) | copy-start | bytes 6148
  56.8 6.6 %collective-permute-start.10 = (bf16[128,512]{1,0:T(8,128)(2,1)S(1)}, bf16[128,512]{1,0:T(8,128)(2,1)S(1)}, u32[]{:S(2)}, u32[]{:S(2)}) collective-permute-start(bf16[128,512]{1,0:T(8,128)(2,1)S(1)} %get-tuple-element.65), channel_id=1, source_target_pairs={{0,16},{2,18},{4,20},{6,22},{8,24},{10,26},{12,28},{14,30},{32,48}... | collective-permute-start | bytes 393224 | tf_op jit(solution)/shard_map/ppermute | solution.py:465
  57.9 6.8 %collective-permute-start.11 = (bf16[128,512]{1,0:T(8,128)(2,1)S(1)}, bf16[128,512]{1,0:T(8,128)(2,1)S(1)}, u32[]{:S(2)}, u32[]{:S(2)}) collective-permute-start(bf16[128,512]{1,0:T(8,128)(2,1)S(1)} %get-tuple-element.66), channel_id=1, source_target_pairs={{0,48},{2,50},{4,52},{6,54},{8,56},{10,58},{12,60},{14,62},{32,16}... | collective-permute-start | bytes 393224 | tf_op jit(solution)/shard_map/ppermute | solution.py:465
  60.6 5.0 %collective-permute-start.9 = (bf16[128,512]{1,0:T(8,128)(2,1)S(1)}, bf16[128,512]{1,0:T(8,128)(2,1)S(1)}, u32[]{:S(2)}, u32[]{:S(2)}) collective-permute-start(bf16[128,512]{1,0:T(8,128)(2,1)S(1)} %get-tuple-element.64), channel_id=1, source_target_pairs={{0,32},{2,34},{4,36},{6,38},{8,40},{10,42},{12,44},{14,46},{32,0},... | collective-permute-start | bytes 393224 | tf_op jit(solution)/shard_map/ppermute | solution.py:465
  81.3 19.2 %all-to-all-start.1 = ((f32[128,1,128]{2,1,0:T(1,128)}), f32[128,1,128]{2,1,0:T(1,128)S(1)}, u32[]{:S(2)}, u32[]{:S(2)}) async-start(f32[128,1,128]{2,1,0:T(1,128)} %get-tuple-element.82), calls=%async_computation.1 | async-start | bytes 131072 | tf_op jit(solution)/shard_map/all_to_all | solution.py:570

commit v13 on v10

--- a/solution.py
+++ b/solution.py
@@ -297,25 +297,25 @@
     scatter_rows(norm_back(dnormed, gain[...], xhat, rstd, g), scratch, back, D)
 
 
-def second_pack(me, normed, attended, right, p0, p1, p2, p3, left_n, left_a):
+def second_pack(me, normed, attended, right, keep, p0, p1, p2, p3, left_ref, left_n, left_a):
     order = regroup(row_order(chip_second))
     left_n[...] = dot_nn(normed[...], order).astype(BF16)
     left_a[...] = dot_nn(attended[...], order).astype(BF16)
     pack(members_second(*here(me))[0], (left_n, left_a), right, (p0, p1, p2, p3))
+    order = regroup(row_order(chip_first))
+    left_ref[0] = dot_nn(keep[:, 4 * D : 5 * D], order).astype(BF16)
+    left_ref[1] = dot_nn(keep[:, 3 * D : 4 * D], order).astype(BF16)
 
 
 def first_backward(
-    me, b0, b1, b2, b3, wout, keep, right_ref, p0, p1, p2, p3, scratch, left_n, left_a
+    me, b0, b1, b2, b3, wout, keep, left, right_ref, p0, p1, p2, p3, scratch
 ):
     g16 = gather_rows((b0, b1, b2, b3), scratch, D).astype(BF16)
     datt = dot_nt(g16, wout[...]).astype(BF16)
     bias = label_bias(keep[:, 5 * D :].astype(F32))
     _, dproj = attention(keep[...], bias, grad=datt, attended=keep[:, 3 * D : 4 * D])
     store_right(dproj, g16, right_ref)
-    order = regroup(row_order(chip_first))
-    left_n[...] = dot_nn(keep[:, 4 * D : 5 * D], order).astype(BF16)
-    left_a[...] = dot_nn(keep[:, 3 * D : 4 * D], order).astype(BF16)
-    pack(members_first(*here(me))[0], (left_n, left_a), right_ref, (p0, p1, p2, p3))
+    pack(members_first(*here(me))[0], (left.at[0], left.at[1]), right_ref, (p0, p1, p2, p3))
 
 
 def first_rest(b0, b1, b2, b3, tok, gain, wqkv, right, tg_ref, result_ref, scratch):
@@ -531,15 +531,19 @@
     )
     back = send(back, tables, back=True)
     half = pltpu.VMEM((TOK, D), BF16)
-    pack_b = call(
-        second_pack, packs, [half, half], me, normed_b, att_b, right_b, scalar=True
+    *pack_b, left_a = call(
+        second_pack,
+        packs + [shape_of(2, TOK, D)],
+        [half, half],
+        me, normed_b, att_b, right_b, keep,
+        scalar=True,
     )
     pack_b = swap_second(after(pack_b, back[:3]), 0, (3, 1, 2))
     right_a, *pack_a = call(
         first_backward,
         [fields] + packs,
-        [(TOK, D), half, half],
-        me, *back, out_first, keep,
+        [(TOK, D)],
+        me, *back, out_first, keep, left_a,
         scalar=True,
     )
     pack_a = swap_first(pack_a, 0, (3, 1, 2))

time: 102 us -> 103 us (level)
  blocking collectives: 16.6 us -> 18 us
  waiting for transfers between devices: 30.4 us -> 29.3 us
    all_to_all x1, blocking collectives: 16.6 us -> 18 us  [exchange(): return lax.all_to_all(parts, ('lat', 'lon'), 0, 0, axis_index_groups=groups)]
  transfers between devices with their start and end apart: 19 -> 19, of which waited for: 10 -> 9; matrix products, arithmetic and copies ran while one was open for 0% -> 0% of each run, Pallas kernels for 7% -> 7%
where the time goes in v13:
time: 103 us; the launch traced here: 102 us
  starting transfers between devices  37 us (36%)
  waiting for transfers between devices  29.3 us (28%)
  blocking collectives  18 us (17%)
  Pallas kernels  16.8 us (16%)
    all_to_all x1, blocking collectives, exchange(): return lax.all_to_all(parts, ('lat', 'lon'), 0, 0, axis_index_groups=groups)  18 us
    ppermute x12, starting transfers between devices, swap(): out[step] = lax.ppermute(parts[step], ('lat', 'lon'), pairs)  17 us
    pallas_call x10, Pallas kernels, call(): pl.pallas_call(kernel, out_shape=outs, in_specs=specs, out_specs=[whole]...  16.8 us
    ppermute x6, starting transfers between devices, send(): out[slot] = lax.ppermute(parts[slot], ('lat', 'lon'), pairs)  13.4 us
    ppermute x6, waiting for transfers between devices, send(): out[slot] = lax.ppermute(parts[slot], ('lat', 'lon'), pairs)  10.2 us
    all_to_all x1, waiting for transfers between devices, on_device(): tiles = lax.all_to_all(tiles, ('lat', 'lon'), 0, 0)  10.1 us
    ppermute x12, waiting for transfers between devices, swap(): out[step] = lax.ppermute(parts[step], ('lat', 'lon'), pairs)  8.97 us
    all_to_all x1, starting transfers between devices, on_device(): tiles = lax.all_to_all(tiles, ('lat', 'lon'), 0, 0)  6.59 us
  transfers between devices with their start and end apart: 19, of which 9 were waited for; matrix products, arithmetic and copies ran while one was open for 0% of the time, Pallas kernels for 7%

profile of v13, /device:TPU:0, one launch (start us, length us, event | category | flops | bytes accessed | tf_op | source)
XLA Modules:
  0.0 101.9 jit_solution(4225413934177168495)
XLA Ops:
  0.7 3.3 %first_forward.1 = (bf16[36,1152]{1,0:T(8,128)(2,1)S(1)}, bf16[36,1152]{1,0:T(8,128)(2,1)S(1)}, bf16[36,1152]{1,0:T(8,128)(2,1)S(1)}, bf16[36,1152]{1,0:T(8,128)(2,1)S(1)}, bf16[144,2688]{1,0:T(8,128)(2,1)S(1)}) custom-call(s32[1]{0:T(128)} %bitcast.me, bf16[6,12,2,512]{3,2,1,0:T(2,128)(2,1)} %bitcast.8, f32[1,512]{1,0:T(1,128)} %bitcast.10, ...), custom_call_target="tpu_custom_call" | custom-call | tf_op jit(solution)/shard_map/first_forward/pallas_call | solution.py:406
  4.0 8.8 %collective-permute-start = (bf16[36,1152]{1,0:T(8,128)(2,1)S(1)}, bf16[36,1152]{1,0:T(8,128)(2,1)S(1)}, u32[]{:S(2)}, u32[]{:S(2)}) collective-permute-start(bf16[36,1152]{1,0:T(8,128)(2,1)S(1)} %get-tuple-element.48), channel_id=1, source_target_pairs={{0,254},{2,224},{4,226},{6,228},{8,230},{10,232},{12,234},{14,236}... | collective-permute-start | bytes 248840 | tf_op jit(solution)/shard_map/ppermute | solution.py:443
  12.8 0.1 collective-permute-start.1
  13.0 2.5 %collective-permute-start.2 = (bf16[36,1152]{1,0:T(8,128)(2,1)S(1)}, bf16[36,1152]{1,0:T(8,128)(2,1)S(1)}, u32[]{:S(2)}, u32[]{:S(2)}) collective-permute-start(bf16[36,1152]{1,0:T(8,128)(2,1)S(1)} %get-tuple-element.50), channel_id=1, source_target_pairs={{0,30},{2,0},{4,2},{6,4},{8,6},{10,8},{12,10},{14,12},{16,14},{18,... | collective-permute-start | bytes 248840 | tf_op jit(solution)/shard_map/ppermute | solution.py:443
  15.5 0.0 collective-permute-done.x0
  15.5 1.9 %collective-permute-done.1.x1 = bf16[36,1152]{1,0:T(8,128)(2,1)S(1)} collective-permute-done((bf16[36,1152]{1,0:T(8,128)(2,1)S(1)}, bf16[36,1152]{1,0:T(8,128)(2,1)S(1)}, u32[]{:S(2)}, u32[]{:S(2)}) %collective-permute-start.1) | collective-permute-done | bytes 82976 | tf_op jit(solution)/shard_map/ppermute | solution.py:443
  17.4 0.3 collective-permute-done.2.x2
  17.7 4.8 %second_main.1 = (bf16[36,1024]{1,0:T(8,128)(2,1)S(1)}, bf16[36,1024]{1,0:T(8,128)(2,1)S(1)}, bf16[36,1024]{1,0:T(8,128)(2,1)S(1)}, bf16[36,1024]{1,0:T(8,128)(2...) custom-call(bf16[36,1152]{1,0:T(8,128)(2,1)S(1)} %collective-permute-done.x0, ...), custom_call_target="tpu_custom_call" | custom-call | tf_op jit(solution)/shard_map/second_main/pallas_call | solution.py:406
  22.5 0.9 collective-permute-start.3
  23.4 1.0 %collective-permute-start.4 = (bf16[36,1024]{1,0:T(8,128)(2,1)S(1)}, bf16[36,1024]{1,0:T(8,128)(2,1)S(1)}, u32[]{:S(2)}, u32[]{:S(2)}) collective-permute-start(bf16[36,1024]{1,0:T(8,128)(2,1)S(1)} %get-tuple-element.53), channel_id=1, source_target_pairs={{224,0},{226,2},{228,4},{230,6},{232,8},{234,10},{236,12},{238,14}... | collective-permute-start | bytes 221192 | tf_op jit(solution)/shard_map/ppermute | solution.py:443
  24.4 0.0 collective-permute-start.5
  24.4 0.9 second_pack.1
  25.3 8.0 %collective-permute-done.3.b0 = bf16[36,1024]{1,0:T(8,128)(2,1)S(1)} collective-permute-done((bf16[36,1024]{1,0:T(8,128)(2,1)S(1)}, bf16[36,1024]{1,0:T(8,128)(2,1)S(1)}, u32[]{:S(2)}, u32[]{:S(2)}) %collective-permute-start.3) | collective-permute-done | bytes 73760 | tf_op jit(solution)/shard_map/ppermute | solution.py:443
  33.3 0.0 collective-permute-done.4.b1
  33.3 0.0 collective-permute-done.5.b2
  33.3 1.1 %collective-permute-start.12 = (bf16[144,1024]{1,0:T(8,128)(2,1)S(1)}, bf16[144,1024]{1,0:T(8,128)(2,1)S(1)}, u32[]{:S(2)}, u32[]{:S(2)}) collective-permute-start(bf16[144,1024]{1,0:T(8,128)(2,1)S(1)} %get-tuple-element.77), channel_id=1, source_target_pairs={{0,192},{2,194},{4,196},{6,198},{8,200},{10,202},{12,204},{14,206}... | collective-permute-start | bytes 884744 | tf_op jit(solution)/shard_map/ppermute | solution.py:465
  34.4 0.1 collective-permute-start.13
  34.5 4.7 %collective-permute-start.14 = (bf16[144,1024]{1,0:T(8,128)(2,1)S(1)}, bf16[144,1024]{1,0:T(8,128)(2,1)S(1)}, u32[]{:S(2)}, u32[]{:S(2)}) collective-permute-start(bf16[144,1024]{1,0:T(8,128)(2,1)S(1)} %get-tuple-element.79), channel_id=1, source_target_pairs={{0,206},{2,196},{4,194},{6,200},{8,198},{10,204},{12,202},{14,192}... | collective-permute-start | bytes 884744 | tf_op jit(solution)/shard_map/ppermute | solution.py:465
  39.2 2.7 %first_backward.1 = (bf16[4,144,512]{2,1,0:T(8,128)(2,1)S(1)}, bf16[144,1024]{1,0:T(8,128)(2,1)S(1)}, bf16[144,1024]{1,0:T(8,128)(2,1)S(1)}, bf16[144,1024]{1,0:T(8,128)(2,1)S(1)}, bf16[144,1024]{1,0:T(8,128)(2,1)S(1)}) custom-call(s32[1]{0:T(128)} %bitcast.me, bf16[36,1024]{1,0:T(8,128)(2,1)S(1)} %collective-permute-done.3.b0, ...), custom_call_target="tpu_custom_call" | custom-call | tf_op jit(solution)/shard_map/first_backward/pallas_call | solution.py:406
  41.9 0.1 collective-permute-start.6
  42.0 0.1 collective-permute-start.7
  42.1 2.0 %collective-permute-done.12.refs_1_ = bf16[144,1024]{1,0:T(8,128)(2,1)S(1)} collective-permute-done((bf16[144,1024]{1,0:T(8,128)(2,1)S(1)}, bf16[144,1024]{1,0:T(8,128)(2,1)S(1)}, u32[]{:S(2)}, u32[]{:S(2)}) %collective-permute-start.12) | collective-permute-done | bytes 294944 | tf_op jit(solution)/shard_map/ppermute | solution.py:465
  44.2 1.3 %collective-permute-start.8 = (bf16[144,1024]{1,0:T(8,128)(2,1)S(1)}, bf16[144,1024]{1,0:T(8,128)(2,1)S(1)}, u32[]{:S(2)}, u32[]{:S(2)}) collective-permute-start(bf16[144,1024]{1,0:T(8,128)(2,1)S(1)} %get-tuple-element.67), channel_id=1, source_target_pairs={{0,66},{2,64},{4,70},{6,68},{8,74},{10,72},{12,78},{14,76},{32,98}... | collective-permute-start | bytes 884744 | tf_op jit(solution)/shard_map/ppermute | solution.py:465
  45.5 0.0 collective-permute-done.13.refs_2_
  45.5 3.5 %collective-permute-done.14.refs_3_ = bf16[144,1024]{1,0:T(8,128)(2,1)S(1)} collective-permute-done((bf16[144,1024]{1,0:T(8,128)(2,1)S(1)}, bf16[144,1024]{1,0:T(8,128)(2,1)S(1)}, u32[]{:S(2)}, u32[]{:S(2)}) %collective-permute-start.14) | collective-permute-done | bytes 294944 | tf_op jit(solution)/shard_map/ppermute | solution.py:465
  49.0 0.8 second_weights.1
  49.9 0.5 collective-permute-start.15
  50.3 1.4 %collective-permute-start.16 = (bf16[128,512]{1,0:T(8,128)(2,1)S(1)}, bf16[128,512]{1,0:T(8,128)(2,1)S(1)}, u32[]{:S(2)}, u32[]{:S(2)}) collective-permute-start(bf16[128,512]{1,0:T(8,128)(2,1)S(1)} %get-tuple-element.82), channel_id=1, source_target_pairs={{0,16},{2,18},{4,20},{6,22},{8,24},{10,26},{12,28},{14,30},{32,48}... | collective-permute-start | bytes 393224 | tf_op jit(solution)/shard_map/ppermute | solution.py:465
  51.7 0.0 collective-permute-done.6.refs_1_
  51.7 2.9 %collective-permute-start.17 = (bf16[128,512]{1,0:T(8,128)(2,1)S(1)}, bf16[128,512]{1,0:T(8,128)(2,1)S(1)}, u32[]{:S(2)}, u32[]{:S(2)}) collective-permute-start(bf16[128,512]{1,0:T(8,128)(2,1)S(1)} %get-tuple-element.83), channel_id=1, source_target_pairs={{0,48},{2,50},{4,52},{6,54},{8,56},{10,58},{12,60},{14,62},{32,16}... | collective-permute-start | bytes 393224 | tf_op jit(solution)/shard_map/ppermute | solution.py:465
  54.7 0.0 collective-permute-done.7.refs_2_
  54.7 0.0 collective-permute-done.8.refs_3_
  54.7 0.0 copy-start.3
  54.7 0.0 copy-start.5
  54.7 0.8 first_weights.1
  55.5 0.3 collective-permute-start.9
  55.8 1.6 %collective-permute-start.10 = (bf16[128,512]{1,0:T(8,128)(2,1)S(1)}, bf16[128,512]{1,0:T(8,128)(2,1)S(1)}, u32[]{:S(2)}, u32[]{:S(2)}) collective-permute-start(bf16[128,512]{1,0:T(8,128)(2,1)S(1)} %get-tuple-element.70), channel_id=1, source_target_pairs={{0,16},{2,18},{4,20},{6,22},{8,24},{10,26},{12,28},{14,30},{32,48}... | collective-permute-start | bytes 393224 | tf_op jit(solution)/shard_map/ppermute | solution.py:465
  57.4 2.9 %collective-permute-start.11 = (bf16[128,512]{1,0:T(8,128)(2,1)S(1)}, bf16[128,512]{1,0:T(8,128)(2,1)S(1)}, u32[]{:S(2)}, u32[]{:S(2)}) collective-permute-start(bf16[128,512]{1,0:T(8,128)(2,1)S(1)} %get-tuple-element.71), channel_id=1, source_target_pairs={{0,48},{2,50},{4,52},{6,54},{8,56},{10,58},{12,60},{14,62},{32,16}... | collective-permute-start | bytes 393224 | tf_op jit(solution)/shard_map/ppermute | solution.py:465
  60.3 0.6 collective-permute-done.17.b3
  60.9 1.4 %collective-permute-done.10.a2 = bf16[128,512]{1,0:T(8,128)(2,1)S(1)} collective-permute-done((bf16[128,512]{1,0:T(8,128)(2,1)S(1)}, bf16[128,512]{1,0:T(8,128)(2,1)S(1)}, u32[]{:S(2)}, u32[]{:S(2)}) %collective-permute-start.10) | collective-permute-done | bytes 131104 | tf_op jit(solution)/shard_map/ppermute | solution.py:465
  62.3 1.4 %collective-permute-done.11.a3 = bf16[128,512]{1,0:T(8,128)(2,1)S(1)} collective-permute-done((bf16[128,512]{1,0:T(8,128)(2,1)S(1)}, bf16[128,512]{1,0:T(8,128)(2,1)S(1)}, u32[]{:S(2)}, u32[]{:S(2)}) %collective-permute-start.11) | collective-permute-done | bytes 131104 | tf_op jit(solution)/shard_map/ppermute | solution.py:465
  63.7 0.2 add_rows.1
  63.9 18.0 %all_to_all.10.parts = bf16[32,32,128]{2,1,0:T(8,128)(2,1)S(1)} all-to-all(bf16[32,32,128]{2,1,0:T(8,128)(2,1)S(1)} %add_rows.1), channel_id=1, replica_groups={{0,2,4,6,8,10,12,14,64,66,68,70,72,74,76,78,128,130,132,134,136,138,140..., dimensions={0} | all-to-all | bytes 524288 | tf_op jit(solution)/shard_map/all_to_all | solution.py:478
  81.9 0.8 own_rows.1
  82.7 6.6 %all-to-all-start.1 = ((f32[128,1,128]{2,1,0:T(1,128)}), f32[128,1,128]{2,1,0:T(1,128)S(1)}, u32[]{:S(2)}, u32[]{:S(2)}) async-start(f32[128,1,128]{2,1,0:T(1,128)} %get-tuple-element.84), calls=%async_computation.1 | async-start | bytes 131072 | tf_op jit(solution)/shard_map/all_to_all | solution.py:574
  89.4 1.6 %first_rest.1 = (bf16[6,12,2,512]{3,2,1,0:T(2,128)(2,1)}, bf16[6,12,2,512]{3,2,1,0:T(2,128)(2,1)}) custom-call(bf16[36,1024]{1,0:T(8,128)(2,1)S(1)} %collective-permute-done.3.b0, bf16[36,1024]{1,0:T(8,128)(2,1)S(1)} %collective-permute-done.4.b1, bf16[36,1024]{1,0:T(8,128)(2,1)S(1)} %collective-permute-done.5.b2, ...), custom_call_target="tpu_custom_call" | custom-call | tf_op jit(solution)/shard_map/first_rest/pallas_call | solution.py:406
  91.0 10.1 %all-to-all-done.1.tiles = f32[128,1,128]{2,1,0:T(1,128)S(1)} async-done(((f32[128,1,128]{2,1,0:T(1,128)}), f32[128,1,128]{2,1,0:T(1,128)S(1)}, u32[]{:S(2)}, u32[]{:S(2)}) %all-to-all-start.1) | async-done | bytes 65568 | tf_op jit(solution)/shard_map/all_to_all | solution.py:574
  101.1 0.8 clipped.1
  (15 shorter events, 0.0 us)
Async XLA Ops:
  0.6 17.0 %copy-start.4 = (bf16[512,512]{1,0:T(8,128)(2,1)S(1)}, bf16[512,512]{1,0:T(8,128)(2,1)}, u32[]{:S(2)}) copy-start(bf16[512,512]{1,0:T(8,128)(2,1)} %wout.2) | copy-start | bytes 1572868
  0.6 17.0 %copy-start.2 = (bf16[512,1536]{1,0:T(8,128)(2,1)S(1)}, bf16[512,1536]{1,0:T(8,128)(2,1)}, u32[]{:S(2)}) copy-start(bf16[512,1536]{1,0:T(8,128)(2,1)} %wqkv.2) | copy-start | bytes 4718596
  0.7 17.0 %copy-start.6 = (f32[512]{0:T(512)S(1)}, f32[512]{0:T(512)}, u32[]{:S(2)}) copy-start(f32[512]{0:T(512)} %param.15) | copy-start | bytes 6148
  4.0 11.5 %collective-permute-start = (bf16[36,1152]{1,0:T(8,128)(2,1)S(1)}, bf16[36,1152]{1,0:T(8,128)(2,1)S(1)}, u32[]{:S(2)}, u32[]{:S(2)}) collective-permute-start(bf16[36,1152]{1,0:T(8,128)(2,1)S(1)} %get-tuple-element.48), channel_id=1, source_target_pairs={{0,254},{2,224},{4,226},{6,228},{8,230},{10,232},{12,234},{14,236}... | collective-permute-start | bytes 248840 | tf_op jit(solution)/shard_map/ppermute | solution.py:443
  12.8 4.6 %collective-permute-start.1 = (bf16[36,1152]{1,0:T(8,128)(2,1)S(1)}, bf16[36,1152]{1,0:T(8,128)(2,1)S(1)}, u32[]{:S(2)}, u32[]{:S(2)}) collective-permute-start(bf16[36,1152]{1,0:T(8,128)(2,1)S(1)} %get-tuple-element.49), channel_id=1, source_target_pairs={{0,224},{2,226},{4,228},{6,230},{8,232},{10,234},{12,236},{14,238}... | collective-permute-start | bytes 248840 | tf_op jit(solution)/shard_map/ppermute | solution.py:443
  13.0 4.7 %collective-permute-start.2 = (bf16[36,1152]{1,0:T(8,128)(2,1)S(1)}, bf16[36,1152]{1,0:T(8,128)(2,1)S(1)}, u32[]{:S(2)}, u32[]{:S(2)}) collective-permute-start(bf16[36,1152]{1,0:T(8,128)(2,1)S(1)} %get-tuple-element.50), channel_id=1, source_target_pairs={{0,30},{2,0},{4,2},{6,4},{8,6},{10,8},{12,10},{14,12},{16,14},{18,... | collective-permute-start | bytes 248840 | tf_op jit(solution)/shard_map/ppermute | solution.py:443
  17.7 21.6 %copy-start.1 = (bf16[512,512]{1,0:T(8,128)(2,1)S(1)}, bf16[512,512]{1,0:T(8,128)(2,1)}, u32[]{:S(2)}) copy-start(bf16[512,512]{1,0:T(8,128)(2,1)} %wout.3) | copy-start | bytes 1572868
  22.5 10.8 %collective-permute-start.3 = (bf16[36,1024]{1,0:T(8,128)(2,1)S(1)}, bf16[36,1024]{1,0:T(8,128)(2,1)S(1)}, u32[]{:S(2)}, u32[]{:S(2)}) collective-permute-start(bf16[36,1024]{1,0:T(8,128)(2,1)S(1)} %get-tuple-element.52), channel_id=1, source_target_pairs={{254,0},{224,2},{226,4},{228,6},{230,8},{232,10},{234,12},{236,14}... | collective-permute-start | bytes 221192 | tf_op jit(solution)/shard_map/ppermute | solution.py:443
  23.4 9.9 %collective-permute-start.4 = (bf16[36,1024]{1,0:T(8,128)(2,1)S(1)}, bf16[36,1024]{1,0:T(8,128)(2,1)S(1)}, u32[]{:S(2)}, u32[]{:S(2)}) collective-permute-start(bf16[36,1024]{1,0:T(8,128)(2,1)S(1)} %get-tuple-element.53), channel_id=1, source_target_pairs={{224,0},{226,2},{228,4},{230,6},{232,8},{234,10},{236,12},{238,14}... | collective-permute-start | bytes 221192 | tf_op jit(solution)/shard_map/ppermute | solution.py:443
  24.4 8.9 %collective-permute-start.5 = (bf16[36,1024]{1,0:T(8,128)(2,1)S(1)}, bf16[36,1024]{1,0:T(8,128)(2,1)S(1)}, u32[]{:S(2)}, u32[]{:S(2)}) collective-permute-start(bf16[36,1024]{1,0:T(8,128)(2,1)S(1)} %get-tuple-element.54), channel_id=1, source_target_pairs={{30,0},{0,2},{2,4},{4,6},{6,8},{8,10},{10,12},{12,14},{14,16},{16,... | collective-permute-start | bytes 221192 | tf_op jit(solution)/shard_map/ppermute | solution.py:443
  33.3 10.9 %collective-permute-start.12 = (bf16[144,1024]{1,0:T(8,128)(2,1)S(1)}, bf16[144,1024]{1,0:T(8,128)(2,1)S(1)}, u32[]{:S(2)}, u32[]{:S(2)}) collective-permute-start(bf16[144,1024]{1,0:T(8,128)(2,1)S(1)} %get-tuple-element.77), channel_id=1, source_target_pairs={{0,192},{2,194},{4,196},{6,198},{8,200},{10,202},{12,204},{14,206}... | collective-permute-start | bytes 884744 | tf_op jit(solution)/shard_map/ppermute | solution.py:465
  34.4 11.1 %collective-permute-start.13 = (bf16[144,1024]{1,0:T(8,128)(2,1)S(1)}, bf16[144,1024]{1,0:T(8,128)(2,1)S(1)}, u32[]{:S(2)}, u32[]{:S(2)}) collective-permute-start(bf16[144,1024]{1,0:T(8,128)(2,1)S(1)} %get-tuple-element.78), channel_id=1, source_target_pairs={{0,14},{2,4},{4,2},{6,8},{8,6},{10,12},{12,10},{14,0},{32,46},{34,... | collective-permute-start | bytes 884744 | tf_op jit(solution)/shard_map/ppermute | solution.py:465
  34.5 14.5 %collective-permute-start.14 = (bf16[144,1024]{1,0:T(8,128)(2,1)S(1)}, bf16[144,1024]{1,0:T(8,128)(2,1)S(1)}, u32[]{:S(2)}, u32[]{:S(2)}) collective-permute-start(bf16[144,1024]{1,0:T(8,128)(2,1)S(1)} %get-tuple-element.79), channel_id=1, source_target_pairs={{0,206},{2,196},{4,194},{6,200},{8,198},{10,204},{12,202},{14,192}... | collective-permute-start | bytes 884744 | tf_op jit(solution)/shard_map/ppermute | solution.py:465
  41.9 9.8 %collective-permute-start.6 = (bf16[144,1024]{1,0:T(8,128)(2,1)S(1)}, bf16[144,1024]{1,0:T(8,128)(2,1)S(1)}, u32[]{:S(2)}, u32[]{:S(2)}) collective-permute-start(bf16[144,1024]{1,0:T(8,128)(2,1)S(1)} %get-tuple-element.65), channel_id=1, source_target_pairs={{0,64},{2,66},{4,68},{6,70},{8,72},{10,74},{12,76},{14,78},{32,96}... | collective-permute-start | bytes 884744 | tf_op jit(solution)/shard_map/ppermute | solution.py:465
  42.0 12.6 %collective-permute-start.7 = (bf16[144,1024]{1,0:T(8,128)(2,1)S(1)}, bf16[144,1024]{1,0:T(8,128)(2,1)S(1)}, u32[]{:S(2)}, u32[]{:S(2)}) collective-permute-start(bf16[144,1024]{1,0:T(8,128)(2,1)S(1)} %get-tuple-element.66), channel_id=1, source_target_pairs={{0,2},{2,0},{4,6},{6,4},{8,10},{10,8},{12,14},{14,12},{32,34},{34,... | collective-permute-start | bytes 884744 | tf_op jit(solution)/shard_map/ppermute | solution.py:465
  44.2 10.5 %collective-permute-start.8 = (bf16[144,1024]{1,0:T(8,128)(2,1)S(1)}, bf16[144,1024]{1,0:T(8,128)(2,1)S(1)}, u32[]{:S(2)}, u32[]{:S(2)}) collective-permute-start(bf16[144,1024]{1,0:T(8,128)(2,1)S(1)} %get-tuple-element.67), channel_id=1, source_target_pairs={{0,66},{2,64},{4,70},{6,68},{8,74},{10,72},{12,78},{14,76},{32,98}... | collective-permute-start | bytes 884744 | tf_op jit(solution)/shard_map/ppermute | solution.py:465
  49.9 7.5 %collective-permute-start.15 = (bf16[128,512]{1,0:T(8,128)(2,1)S(1)}, bf16[128,512]{1,0:T(8,128)(2,1)S(1)}, u32[]{:S(2)}, u32[]{:S(2)}) collective-permute-start(bf16[128,512]{1,0:T(8,128)(2,1)S(1)} %get-tuple-element.81), channel_id=1, source_target_pairs={{0,32},{2,34},{4,36},{6,38},{8,40},{10,42},{12,44},{14,46},{32,0},... | collective-permute-start | bytes 393224 | tf_op jit(solution)/shard_map/ppermute | solution.py:465
  50.3 10.0 %collective-permute-start.16 = (bf16[128,512]{1,0:T(8,128)(2,1)S(1)}, bf16[128,512]{1,0:T(8,128)(2,1)S(1)}, u32[]{:S(2)}, u32[]{:S(2)}) collective-permute-start(bf16[128,512]{1,0:T(8,128)(2,1)S(1)} %get-tuple-element.82), channel_id=1, source_target_pairs={{0,16},{2,18},{4,20},{6,22},{8,24},{10,26},{12,28},{14,30},{32,48}... | collective-permute-start | bytes 393224 | tf_op jit(solution)/shard_map/ppermute | solution.py:465
  51.7 9.2 %collective-permute-start.17 = (bf16[128,512]{1,0:T(8,128)(2,1)S(1)}, bf16[128,512]{1,0:T(8,128)(2,1)S(1)}, u32[]{:S(2)}, u32[]{:S(2)}) collective-permute-start(bf16[128,512]{1,0:T(8,128)(2,1)S(1)} %get-tuple-element.83), channel_id=1, source_target_pairs={{0,48},{2,50},{4,52},{6,54},{8,56},{10,58},{12,60},{14,62},{32,16}... | collective-permute-start | bytes 393224 | tf_op jit(solution)/shard_map/ppermute | solution.py:465
  54.7 34.7 %copy-start = (bf16[512,1536]{1,0:T(8,128)(2,1)S(1)}, bf16[512,1536]{1,0:T(8,128)(2,1)}, u32[]{:S(2)}) copy-start(bf16[512,1536]{1,0:T(8,128)(2,1)} %wqkv.3) | copy-start | bytes 4718596
  54.7 34.7 %copy-start.3 = (bf16[2,6,12,512]{3,0,2,1:T(2,128)(2,1)S(1)}, bf16[2,6,12,512]{3,0,2,1:T(2,128)(2,1)}, u32[]{:S(2)}) copy-start(bf16[2,6,12,512]{3,0,2,1:T(2,128)(2,1)} %param.9) | copy-start | bytes 442372
  54.7 34.7 %copy-start.5 = (f32[512]{0:T(512)S(1)}, f32[512]{0:T(512)}, u32[]{:S(2)}) copy-start(f32[512]{0:T(512)} %param.12) | copy-start | bytes 6148
  55.5 5.4 %collective-permute-start.9 = (bf16[128,512]{1,0:T(8,128)(2,1)S(1)}, bf16[128,512]{1,0:T(8,128)(2,1)S(1)}, u32[]{:S(2)}, u32[]{:S(2)}) collective-permute-start(bf16[128,512]{1,0:T(8,128)(2,1)S(1)} %get-tuple-element.69), channel_id=1, source_target_pairs={{0,32},{2,34},{4,36},{6,38},{8,40},{10,42},{12,44},{14,46},{32,0},... | collective-permute-start | bytes 393224 | tf_op jit(solution)/shard_map/ppermute | solution.py:465
  55.8 6.5 %collective-permute-start.10 = (bf16[128,512]{1,0:T(8,128)(2,1)S(1)}, bf16[128,512]{1,0:T(8,128)(2,1)S(1)}, u32[]{:S(2)}, u32[]{:S(2)}) collective-permute-start(bf16[128,512]{1,0:T(8,128)(2,1)S(1)} %get-tuple-element.70), channel_id=1, source_target_pairs={{0,16},{2,18},{4,20},{6,22},{8,24},{10,26},{12,28},{14,30},{32,48}... | collective-permute-start | bytes 393224 | tf_op jit(solution)/shard_map/ppermute | solution.py:465
  57.4 6.3 %collective-permute-start.11 = (bf16[128,512]{1,0:T(8,128)(2,1)S(1)}, bf16[128,512]{1,0:T(8,128)(2,1)S(1)}, u32[]{:S(2)}, u32[]{:S(2)}) collective-permute-start(bf16[128,512]{1,0:T(8,128)(2,1)S(1)} %get-tuple-element.71), channel_id=1, source_target_pairs={{0,48},{2,50},{4,52},{6,54},{8,56},{10,58},{12,60},{14,62},{32,16}... | collective-permute-start | bytes 393224 | tf_op jit(solution)/shard_map/ppermute | solution.py:465
  82.7 18.3 %all-to-all-start.1 = ((f32[128,1,128]{2,1,0:T(1,128)}), f32[128,1,128]{2,1,0:T(1,128)S(1)}, u32[]{:S(2)}, u32[]{:S(2)}) async-start(f32[128,1,128]{2,1,0:T(1,128)} %get-tuple-element.84), calls=%async_computation.1 | async-start | bytes 131072 | tf_op jit(solution)/shard_map/all_to_all | solution.py:574
